TPU v7x, 32 devices: a whole 2x2x4 slice. The times are simulated.
32 devices in a mesh: row: 8 (over y, x, core), col: 4 (over z).
Axes of the slice: x: 2, y: 2, z: 4, core: 2. Of those that a mesh axis runs over, the one named last changes fastest.
Arguments:
- adj_tiles: bfloat16 [8, 4, 448, 128, 128], P('row', 'col'), may hold values from -0.046875 to 0.046875
- tile_counts: int32 [8, 4, 16], P('row', 'col'), may hold values from 5 to 32, as said below
- tile_cols: int32 [8, 4, 448], P('row', 'col'), may hold values from 0 to 31, as said below
- features: bfloat16 [16384, 256], P(('col', 'row')), may hold values from -6 to 6
- weight: bfloat16 [256, 256], replicated, may hold values from -0.375 to 0.375
- upstream: bfloat16 [16384, 256], P(('row', 'col')), may hold values from -6 to 6
Outputs:
- hidden: bfloat16 [16384, 256], P(('row', 'col'))
- weight_grad: float32 [256, 256], replicated
- feature_grad: bfloat16 [16384, 256], P(('col', 'row'))
Inputs may be any that keep to these rules, and one draw needn't show every extreme that they name: `tile_counts`: entry (r, c, t) counts the nonzero tiles of row tile t in block (r, c); the counts of one block sum to 448 or less, and to exactly 448 in at least one block. `tile_cols`: live slots are filled in order of row tile; the entries of slots past a block's total count are not used.
All inputs are finite; a program needn't handle non-finite values.
Results may differ from a plain program's by a relative error of at most 0.023.
Values may be sent and summed in bfloat16 or wider, within the bound.
No kernel may reach another device: no remote copies, remote signals or barrier semaphores. Data moves between devices by JAX's collectives and lax.ppermute only.
A program may use at most 128 MiB of HBM per device.

v0:
```python
import math

import jax
import jax.numpy as jnp
from jax import lax
from jax.sharding import PartitionSpec as P


def slot_rows(counts, slots):
    ending = jnp.cumsum(counts)
    position = jnp.arange(slots, dtype=jnp.int32)
    return jnp.sum((position[:, None] >= ending[None, :]).astype(jnp.int32), axis=1)


def split_sum(selector, product, form):
    upper = product.astype(jnp.bfloat16)
    lower = (product - upper.astype(jnp.float32)).astype(jnp.bfloat16)
    first = jnp.einsum(form, selector, upper, preferred_element_type=jnp.float32)
    return first + jnp.einsum(form, selector, lower, preferred_element_type=jnp.float32)


def forward_block(adj_block, col_ids, counts, col_block):
    rows_t = counts.shape[0]
    group_size = adj_block.shape[0] // rows_t
    tile_size = adj_block.shape[1]
    width = col_block.shape[1]
    col_tiles = col_block.shape[0] // tile_size
    row_ids = slot_rows(counts, adj_block.shape[0])
    block_tiles = col_block.reshape(col_tiles, tile_size, width)
    col_range = jnp.arange(col_tiles, dtype=jnp.int32)
    row_range = jnp.arange(rows_t, dtype=jnp.int32)

    def forward_advance(total, pieces):
        tile_g, col_g, row_g = pieces
        pick_cols = (col_g[:, None] == col_range[None, :]).astype(jnp.bfloat16)
        picked = jnp.einsum(
            "sc,cjf->sjf", pick_cols, block_tiles, preferred_element_type=jnp.float32
        ).astype(jnp.bfloat16)
        product = jnp.einsum("sij,sjf->sif", tile_g, picked, preferred_element_type=jnp.float32)
        to_rows = (row_g[:, None] == row_range[None, :]).astype(jnp.bfloat16)
        return (total + split_sum(to_rows, product, "st,sif->tif"), None)

    stacked = (
        adj_block.reshape(rows_t, group_size, tile_size, tile_size),
        col_ids.reshape(rows_t, group_size),
        row_ids.reshape(rows_t, group_size),
    )
    total, unused = lax.scan(
        forward_advance, jnp.zeros((rows_t, tile_size, width), jnp.float32), stacked
    )
    return total.reshape(rows_t * tile_size, width)


def backward_block(adj_block, col_ids, counts, row_grad, col_tiles):
    rows_t = counts.shape[0]
    group_size = adj_block.shape[0] // rows_t
    tile_size = adj_block.shape[1]
    width = row_grad.shape[1]
    row_ids = slot_rows(counts, adj_block.shape[0])
    live = row_ids < rows_t
    targets = jnp.where(live, col_ids, col_tiles)
    grad_tiles = row_grad.reshape(rows_t, tile_size, width)
    col_range = jnp.arange(col_tiles, dtype=jnp.int32)
    row_range = jnp.arange(rows_t, dtype=jnp.int32)

    def backward_advance(total, pieces):
        tile_g, target_g, row_g = pieces
        pick_rows = (row_g[:, None] == row_range[None, :]).astype(jnp.bfloat16)
        chosen = jnp.einsum(
            "st,tif->sif", pick_rows, grad_tiles, preferred_element_type=jnp.float32
        ).astype(jnp.bfloat16)
        product = jnp.einsum("sij,sif->sjf", tile_g, chosen, preferred_element_type=jnp.float32)
        to_cols = (target_g[:, None] == col_range[None, :]).astype(jnp.bfloat16)
        return (total + split_sum(to_cols, product, "sc,sjf->cjf"), None)

    stacked = (
        adj_block.reshape(rows_t, group_size, tile_size, tile_size),
        targets.reshape(rows_t, group_size),
        row_ids.reshape(rows_t, group_size),
    )
    total, unused = lax.scan(
        backward_advance, jnp.zeros((col_tiles, tile_size, width), jnp.float32), stacked
    )
    return total.reshape(col_tiles * tile_size, width)


def activate(aggregated, weight, upstream_part):
    pre = jnp.dot(aggregated, weight, preferred_element_type=jnp.float32)
    hidden = jax.nn.silu(pre).astype(jnp.bfloat16)
    sigmoid_pre = jax.nn.sigmoid(pre)
    pre_grad = (
        upstream_part.astype(jnp.float32) * sigmoid_pre * (1.0 + pre * (1.0 - sigmoid_pre))
    ).astype(jnp.bfloat16)
    return (hidden, pre_grad)


def shards(adj_tiles, tile_counts, tile_cols, features, weight, upstream):
    adj_block = adj_tiles[0, 0]
    counts = tile_counts[0, 0]
    col_ids = tile_cols[0, 0]
    tile_size = adj_block.shape[1]
    piece_rows = upstream.shape[0]
    node_count = piece_rows * lax.axis_size("row") * lax.axis_size("col")
    col_block = lax.all_gather(features, "row", axis=0, tiled=True)
    col_tiles = col_block.shape[0] // tile_size
    partial_value = forward_block(adj_block, col_ids, counts, col_block)
    aggregated = lax.psum_scatter(
        partial_value.astype(jnp.bfloat16), "col", scatter_dimension=0, tiled=True
    )
    hidden, pre_grad = activate(aggregated, weight, upstream)
    local_grad = jnp.dot(aggregated.T, pre_grad, preferred_element_type=jnp.float32)
    weight_grad = lax.psum(local_grad, ("row", "col")) / math.sqrt(node_count)
    grad_piece = jnp.dot(pre_grad, weight.T, preferred_element_type=jnp.float32).astype(
        jnp.bfloat16
    )
    row_grad = lax.all_gather(grad_piece, "col", axis=0, tiled=True)
    grads = backward_block(adj_block, col_ids, counts, row_grad, col_tiles)
    feature_grad = lax.psum_scatter(
        grads.astype(jnp.bfloat16), "row", scatter_dimension=0, tiled=True
    )
    return (hidden, weight_grad, feature_grad)


def solution(mesh):
    placed = (
        P("row", "col", None, None, None),
        P("row", "col", None),
        P("row", "col", None),
        P(("col", "row"), None),
        P(),
        P(("row", "col"), None),
    )
    return jax.shard_map(
        shards,
        mesh=mesh,
        in_specs=placed,
        out_specs=(P(("row", "col"), None), P(), P(("col", "row"), None)),
        check_vma=False,
    )
```

profile of v0, /device:TPU:0, one launch (start us, length us, event | category | flops | bytes accessed | tf_op | source)
XLA Modules:
  0.0 427.3 jit_solution(5767132302618192763)
XLA Ops:
  11.0 29.5 %all-gather.3.cloned.1.call-done = bf16[4096,256]{1,0:T(8,128)(2,1)} async-done(((bf16[512,256]{1,0:T(8,128)(2,1)}), bf16[4096,256]{1,0:T(8,128)(2,1)}) %all-gather.3.cloned.1.call-update) | async-done | bytes 2097168 | tf_op jit(solution)/shard_map/all_gather | solution.py:104
  40.5 4.1 copy.47
  44.6 121.3 %while.22 = (s32[]{:T(128)}, f32[16,128,256]{2,0,1:T(8,128)S(1)}, s32[16,28]{1,0:T(8,128)S(1)}, bf16[16,28,128,128]{3,2,1,0:T(8,128)(2,1)}, s32[16,28]{1,0:T(8,1...) while((s32[]{:T(128)}, f32[16,128,256]{2,0,1:T(8,128)S(1)}, ...), condition=%wide.region_3.4_spmd.clone, body=%wide.region_2.3_spmd.clone.sunk | while | flops 358483712 | bytes 22414208 | solution.py:48
  47.0 2.6 subtract_convert_fusion.4
  54.6 2.6 subtract_convert_fusion.4
  62.1 2.6 subtract_convert_fusion.4
  69.7 2.6 subtract_convert_fusion.4
  77.3 2.6 subtract_convert_fusion.4
  84.9 2.6 subtract_convert_fusion.4
  92.5 2.6 subtract_convert_fusion.4
  100.1 2.6 subtract_convert_fusion.4
  107.6 2.6 subtract_convert_fusion.4
  115.2 2.6 subtract_convert_fusion.4
  122.8 2.6 subtract_convert_fusion.4
  130.4 2.6 subtract_convert_fusion.4
  138.0 2.6 subtract_convert_fusion.4
  145.6 2.6 subtract_convert_fusion.4
  153.1 2.6 subtract_convert_fusion.4
  160.7 2.6 subtract_convert_fusion.4
  168.1 27.2 %reduce-scatter.3.cloned.1.call-done = bf16[512,256]{1,0:T(8,128)(2,1)} async-done(((bf16[2048,256]{1,0:T(8,128)(2,1)}), bf16[512,256]{1,0:T(8,128)(2,1)}) %reduce-scatter.3.cloned.1.call-update) | async-done | bytes 262160 | tf_op jit(solution)/shard_map/reduce_scatter | solution.py:107
  198.4 20.0 %copy.45 = bf16[1,1,448,128,128]{3,4,2,1,0:T(8,128)(2,1)} copy(bf16[1,1,448,128,128]{4,3,2,1,0:T(8,128)(2,1)} %bitcast.72) | data formatting | bytes 29360128 | tf_op args[0]
  219.6 5.5 %all-gather.5.cloned.1.call-done = bf16[2048,256]{1,0:T(8,128)(2,1)} async-done(((bf16[512,256]{1,0:T(8,128)(2,1)}), bf16[2048,256]{1,0:T(8,128)(2,1)}) %all-gather.5.cloned.1.call-update) | async-done | bytes 1048592 | tf_op jit(solution)/shard_map/all_gather | solution.py:116
  227.0 147.8 %while.23 = (s32[]{:T(128)}, f32[32,128,256]{2,0,1:T(8,128)}, s32[16,28]{1,0:T(8,128)S(1)}, bf16[16,28,128,128]{2,3,1,0:T(8,128)(2,1)}, s32[16,28]{1,0:T(8,128)S...) while((s32[]{:T(128)}, f32[32,128,256]{2,0,1:T(8,128)}, ...), condition=%wide.region_7.8_spmd.clone, body=%wide.region_6.7_spmd.clone.sunk | while | flops 389417152 | bytes 63308724 | solution.py:81
  227.7 2.5 subtract_convert_fusion.5
  237.0 2.6 subtract_convert_fusion.5
  246.2 2.6 subtract_convert_fusion.5
  255.4 2.6 subtract_convert_fusion.5
  264.7 2.5 subtract_convert_fusion.5
  273.9 2.5 subtract_convert_fusion.5
  292.4 2.6 subtract_convert_fusion.5
  310.9 2.5 subtract_convert_fusion.5
  381.5 39.2 %reduce-scatter.5.cloned.1.call-done = bf16[512,256]{1,0:T(8,128)(2,1)} async-done(((bf16[4096,256]{1,0:T(8,128)(2,1)}), bf16[512,256]{1,0:T(8,128)(2,1)}) %reduce-scatter.5.cloned.1.call-update) | async-done | bytes 262160 | tf_op jit(solution)/shard_map/reduce_scatter | solution.py:118
  (238 shorter events, 225.2 us)
Async XLA Ops:
  7.2 188.2 %copy-start = (bf16[256,256]{1,0:T(8,128)(2,1)S(1)}, bf16[256,256]{1,0:T(8,128)(2,1)}, u32[]{:S(2)}) copy-start(bf16[256,256]{1,0:T(8,128)(2,1)} %param.14) | copy-start | bytes 393220
  7.2 33.4 %all-gather.3.cloned.1.call-start = ((), (), s32[]{:S(2)}) async-start(), calls=%async_computation.2 | async-start | bytes 2359296 | tf_op jit(solution)/shard_map/all_gather | solution.py:104
  7.9 187.4 %reduce-scatter.3.cloned.1.call-start = ((), (), s32[]{:S(2)}) async-start(), calls=%async_computation.3 | async-start | bytes 1310720 | tf_op jit(solution)/shard_map/reduce_scatter | solution.py:107
  165.9 29.4 %copy-start.5 = (bf16[512,256]{1,0:T(8,128)(2,1)S(1)}, bf16[512,256]{1,0:T(8,128)(2,1)}, u32[]{:S(2)}) copy-start(bf16[512,256]{1,0:T(8,128)(2,1)} %param.15) | copy-start | bytes 786436
  168.1 57.1 %all-gather.5.cloned.1.call-start = ((), (), s32[]{:S(2)}) async-start(), calls=%async_computation.5 | async-start | bytes 1310720 | tf_op jit(solution)/shard_map/all_gather | solution.py:116
  198.4 181.5 %all-reduce.2.cloned.1.call-start = ((), (), s32[]{:S(2)}) async-start(), calls=%async_computation.4 | async-start | bytes 524288 | tf_op jit(solution)/shard_map/psum | solution.py:112
  198.4 20.0 %copy-start.4 = (bf16[512,256]{1,0:T(8,128)(2,1)S(1)}, bf16[512,256]{1,0:T(8,128)(2,1)}, u32[]{:S(2)}) copy-start(bf16[512,256]{1,0:T(8,128)(2,1)} %reduce-scatter.3.cloned.1.call-done) | copy-start | bytes 786436
  219.4 201.4 %reduce-scatter.5.cloned.1.call-start = ((), (), s32[]{:S(2)}) async-start(), calls=%async_computation.6 | async-start | bytes 2359296 | tf_op jit(solution)/shard_map/reduce_scatter | solution.py:118
  230.3 2.2 copy-start.2
  234.2 2.0 copy-start.3
  239.5 2.2 copy-start.2
  243.5 2.0 copy-start.3
  248.8 2.2 copy-start.2
  252.7 2.0 copy-start.3
  258.0 2.2 copy-start.2
  267.3 2.2 copy-start.2
  276.5 2.2 copy-start.2
  285.7 2.2 copy-start.2
  295.0 2.2 copy-start.2
  304.2 2.2 copy-start.2
  313.4 2.2 copy-start.2
  317.4 2.0 copy-start.3
  322.7 2.2 copy-start.2
  326.6 2.0 copy-start.3
  331.9 2.2 copy-start.2
  341.1 2.2 copy-start.2
  350.4 2.2 copy-start.2
  354.3 2.0 copy-start.3
  359.6 2.2 copy-start.2
  363.5 2.0 copy-start.3
  368.8 2.2 copy-start.2
  377.3 43.5 %copy-start.1 = (bf16[256,256]{1,0:T(8,128)(2,1)S(1)}, bf16[256,256]{1,0:T(8,128)(2,1)}, u32[]{:S(2)}) copy-start(bf16[256,256]{1,0:T(8,128)(2,1)} %param.14) | copy-start | bytes 393220
  (9 other events, 17.8 us)
Sparse Core Ops, SparseCore 0:
  9.9 30.5 all-gather.2
  168.2 27.1 reduce-scatter.2
  198.5 26.6 all-gather.4
  232.0 124.4 all-reduce.1
  379.9 40.7 reduce-scatter.4
where the time goes:
time: 431 us; the launch traced here: 427 us
  matrix products  224 us (52%)
  waiting for transfers between devices  102 us (24%)
  local copies, waits for them, and re-layouts  79.4 us (18%)
  between operations  13.9 us (3%)
  other arithmetic  5.78 us (1%)
    while x64, local copies, waits for them, and re-layouts  47.3 us
    dot_general x32, matrix products, split_sum(): jnp.einsum(form, selector, lower, preferred_element_type=jnp.float32)  45.8 us
    dot_general x32, matrix products, split_sum(): jnp.einsum(form, selector, upper, preferred_element_type=jnp.float32)  43.3 us
    dot_general x16, matrix products, forward_advance(): jnp.einsum('sij,sjf->sif', tile_g, picked, preferred_element_type=jnp.flo...  41 us
    dot_general x16, matrix products, backward_advance(): jnp.einsum('sij,sif->sjf', tile_g, chosen, preferred_element_type=jnp.flo...  40.8 us
    reduce_scatter x1, waiting for transfers between devices, shards(): lax.psum_scatter(grads.astype(jnp.bfloat16), 'row', scatter_dimension=0,...  39.2 us
    dot_general x16, matrix products, forward_advance(): jnp.einsum('sc,cjf->sjf', pick_cols, block_tiles, preferred_element_type=...  37.4 us
    all_gather x1, waiting for transfers between devices, shards(): col_block = lax.all_gather(features, 'row', axis=0, tiled=True)  29.5 us
  transfers between devices with their start and end apart: 5, of which 4 were waited for; matrix products, arithmetic and copies ran while one was open for 31% of the time, Pallas kernels for 0%

commit v1 on v0

v1 whole, which is shorter than its diff:
```python
import functools
import math

import jax
import jax.numpy as jnp
from jax import lax
from jax.experimental import pallas as pl
from jax.experimental.pallas import tpu as pltpu
from jax.sharding import PartitionSpec as P

VMEM_LIMIT = 40 * 1024 * 1024


def dense_kernel(counts, cols, adj_ref, out_ref, held, total, sems, *, window, slots):
    row_tiles = pl.num_programs(0)
    t = pl.program_id(0)
    tile = adj_ref.shape[1]
    width = out_ref.shape[1]

    def begin(index):
        return lax.fori_loop(0, index, lambda i, s: s + counts[i], jnp.int32(0))

    def fetch(index, slot):
        base = jnp.minimum(begin(index), slots - window)
        return pltpu.make_async_copy(adj_ref.at[pl.ds(base, window)], held.at[slot], sems.at[slot])

    slot = lax.rem(t, 2)

    @pl.when(t == 0)
    def _():
        fetch(t, slot).start()

    @pl.when(t + 1 < row_tiles)
    def _():
        fetch(t + 1, 1 - slot).start()

    start = begin(t)
    shift = start - jnp.minimum(start, slots - window)
    count = counts[t]
    out_ref[...] = jnp.zeros_like(out_ref)
    fetch(t, slot).wait()

    def place(j):
        c = cols[start + j]
        out_ref[:, pl.ds(pl.multiple_of(c * tile, tile), tile)] = held[slot, shift + j]
        return lax.shift_left(jnp.int32(1), c)

    def four(i, state):
        seen, twice = state
        for u in range(4):
            bit = place(4 * i + u)
            twice = twice | (seen & bit)
            seen = seen | bit
        return seen, twice

    def one(j, state):
        seen, twice = state
        bit = place(j)
        return seen | bit, twice | (seen & bit)

    groups = lax.div(count, 4)
    state = lax.fori_loop(0, groups, four, (jnp.int32(0), jnp.int32(0)))
    seen, twice = lax.fori_loop(4 * groups, count, one, state)
    repeated = (twice != 0) if width // tile <= 32 else (count > 0)

    @pl.when(repeated)
    def _():
        total[...] = jnp.zeros_like(total)

        def add(j, carry):
            where = pl.ds(pl.multiple_of(cols[start + j] * tile, tile), tile)
            total[:, where] += held[slot, shift + j].astype(jnp.float32)
            return carry

        lax.fori_loop(0, count, add, 0)
        out_ref[...] = total[...].astype(out_ref.dtype)


def dense_block(adj, counts, cols, col_tiles):
    slots, tile, _ = adj.shape
    row_tiles = counts.shape[0]
    window = min(col_tiles, slots)
    width = col_tiles * tile
    return pl.pallas_call(
        functools.partial(dense_kernel, window=window, slots=slots),
        out_shape=jax.ShapeDtypeStruct((row_tiles * tile, width), adj.dtype),
        grid_spec=pltpu.PrefetchScalarGridSpec(
            num_scalar_prefetch=2,
            grid=(row_tiles,),
            in_specs=[pl.BlockSpec(memory_space=pl.ANY)],
            out_specs=pl.BlockSpec((tile, width), lambda t, *_: (t, 0)),
            scratch_shapes=[
                pltpu.VMEM((2, window, tile, tile), adj.dtype),
                pltpu.VMEM((tile, width), jnp.float32),
                pltpu.SemaphoreType.DMA((2,)),
            ],
        ),
        compiler_params=pltpu.CompilerParams(vmem_limit_bytes=VMEM_LIMIT),
        cost_estimate=pl.CostEstimate(
            flops=0, bytes_accessed=adj.size * 2 + row_tiles * tile * width * 2, transcendentals=0
        ),
        name="dense_block",
    )(counts, cols, adj)


def forward_kernel(where, a_ref, *refs, first, total):
    shards, out_ref = refs[:-1], refs[-1]
    depth = shards[0].shape[0]
    value = None
    for k, shard in enumerate(shards):
        cols = pl.ds(pl.multiple_of(where[total + k] * depth, depth), depth)
        part = jnp.dot(a_ref[:, cols], shard[...], preferred_element_type=jnp.float32)
        value = part if value is None else value + part
    out_ref[0] = value.astype(out_ref.dtype)


def forward(where, dense, shards, first, last, total, rows, kind):
    width = shards[0].shape[1]
    step = min(rows, 256)
    per = rows // step
    count = last - first
    return pl.pallas_call(
        functools.partial(forward_kernel, first=first, total=total),
        out_shape=jax.ShapeDtypeStruct((count, rows, width), kind),
        grid_spec=pltpu.PrefetchScalarGridSpec(
            num_scalar_prefetch=1,
            grid=(count, per),
            in_specs=[
                pl.BlockSpec((step, dense.shape[1]), lambda i, m, where: (where[first + i] * per + m, 0))
            ]
            + [pl.BlockSpec(s.shape, lambda i, m, where: (0, 0)) for s in shards],
            out_specs=pl.BlockSpec((1, step, width), lambda i, m, where: (i, m, 0)),
        ),
        compiler_params=pltpu.CompilerParams(vmem_limit_bytes=VMEM_LIMIT),
        cost_estimate=pl.CostEstimate(
            flops=2 * count * rows * dense.shape[1] * width,
            bytes_accessed=count * rows * dense.shape[1] * 2,
            transcendentals=0,
        ),
        name="forward_rows",
    )(where, dense, *shards)


def middle_kernel(came_ref, own_ref, weight_ref, up_ref, hidden_ref, grad_ref, wgrad_ref, *, scale):
    agg = (came_ref[...].astype(jnp.float32) + own_ref[...].astype(jnp.float32)).astype(jnp.bfloat16)
    weight = weight_ref[...]
    pre = jnp.dot(agg, weight, preferred_element_type=jnp.float32)
    sig = jax.nn.sigmoid(pre)
    hidden_ref[...] = (pre * sig).astype(jnp.bfloat16)
    pre_grad = (up_ref[...].astype(jnp.float32) * sig * (1.0 + pre * (1.0 - sig))).astype(jnp.bfloat16)
    grad_ref[...] = lax.dot_general(
        weight, pre_grad, (((1,), (1,)), ((), ())), preferred_element_type=jnp.float32
    ).astype(jnp.bfloat16)
    wgrad_ref[...] = scale * lax.dot_general(
        agg, pre_grad, (((0,), (0,)), ((), ())), preferred_element_type=jnp.float32
    )


def middle(came, own, weight, upstream, scale):
    rows, width = upstream.shape
    return pl.pallas_call(
        functools.partial(middle_kernel, scale=scale),
        out_shape=(
            jax.ShapeDtypeStruct((rows, width), jnp.bfloat16),
            jax.ShapeDtypeStruct((width, rows), jnp.bfloat16),
            jax.ShapeDtypeStruct((width, width), jnp.float32),
        ),
        compiler_params=pltpu.CompilerParams(vmem_limit_bytes=VMEM_LIMIT),
        cost_estimate=pl.CostEstimate(
            flops=6 * rows * width * width, bytes_accessed=10 * rows * width, transcendentals=rows * width
        ),
        name="middle",
    )(came, own, weight, upstream)


def backward_kernel(where, *refs, count, has_sum):
    blocks, pieces = refs[:count], refs[count : 2 * count]
    out_ref = refs[-1]
    value = refs[2 * count][0] if has_sum else None
    for a_ref, piece in zip(blocks, pieces):
        part = jnp.dot(piece[...], a_ref[...], preferred_element_type=jnp.float32)
        value = part if value is None else value + part
    out_ref[0] = value.astype(out_ref.dtype)


def backward(where, dense, pieces, row_at, col_at, columns, depth, before, before_at, kind):
    count = len(pieces)
    width, rows = pieces[0].shape

    def block(i):
        return pl.BlockSpec((rows, depth), lambda j, where: (where[row_at + i], where[col_at + j]))

    in_specs = [block(i) for i in range(count)]
    in_specs += [pl.BlockSpec((width, rows), lambda j, where: (0, 0)) for _ in range(count)]
    operands = [dense] * count + list(pieces)
    if before is not None:
        in_specs.append(pl.BlockSpec((1, width, depth), lambda j, where: (before_at + j, 0, 0)))
        operands.append(before)
    return pl.pallas_call(
        functools.partial(backward_kernel, count=count, has_sum=before is not None),
        out_shape=jax.ShapeDtypeStruct((columns, width, depth), kind),
        grid_spec=pltpu.PrefetchScalarGridSpec(
            num_scalar_prefetch=1,
            grid=(columns,),
            in_specs=in_specs,
            out_specs=pl.BlockSpec((1, width, depth), lambda j, where: (j, 0, 0)),
        ),
        compiler_params=pltpu.CompilerParams(vmem_limit_bytes=VMEM_LIMIT),
        cost_estimate=pl.CostEstimate(
            flops=2 * count * rows * width * columns * depth,
            bytes_accessed=count * rows * columns * depth * 2,
            transcendentals=0,
        ),
        name="backward_cols",
    )(where, *operands)


def finish_kernel(*refs):
    parts, out_ref = refs[:-1], refs[-1]
    value = parts[0][...].astype(jnp.float32)
    for part in parts[1:]:
        value = value + part[...].astype(jnp.float32)
    out_ref[...] = value.T.astype(out_ref.dtype)


def finish(parts):
    width, rows = parts[0].shape
    return pl.pallas_call(
        finish_kernel,
        out_shape=jax.ShapeDtypeStruct((rows, width), jnp.bfloat16),
        compiler_params=pltpu.CompilerParams(vmem_limit_bytes=VMEM_LIMIT),
        cost_estimate=pl.CostEstimate(
            flops=len(parts) * rows * width, bytes_accessed=4 * len(parts) * rows * width, transcendentals=0
        ),
        name="finish",
    )(*parts)


def swap(value, axis, size, bit):
    return lax.ppermute(value, axis, [(i, i ^ bit) for i in range(size)])


def turn(value, order):
    count = len(order)
    return lax.ppermute(value, "col", [(order[p], order[(p + 1) % count]) for p in range(count)])


def gather_rows(features, size, core):
    across_x = swap(features, "row", size, 2)
    across_y = swap(features, "row", size, 4)
    beside = swap(features, "row", size, 1)
    onward = jnp.where(core == 0, across_x, across_y)
    corner = lax.ppermute(onward, "row", [(i, i ^ (4 if i % 2 == 0 else 2)) for i in range(size)])
    beside_x = swap(across_x, "row", size, 1)
    beside_y = swap(across_y, "row", size, 1)
    beside_corner = swap(corner, "row", size, 1)
    return [features, beside, across_x, beside_x, across_y, beside_y, corner, beside_corner]


def sum_all(value, n_row, n_col):
    if n_row & (n_row - 1) or n_col & (n_col - 1) or value.shape[0] % (8 * n_row):
        return lax.psum(value, ("row", "col"))
    row, col_bits, bit = lax.axis_index("row"), 1, 1
    while bit < n_row:
        half = value.shape[0] // 2
        high = ((row // bit) % 2).astype(jnp.int32)
        kept = lax.dynamic_slice_in_dim(value, high * half, half, 0)
        sent = lax.dynamic_slice_in_dim(value, (1 - high) * half, half, 0)
        value = kept + swap(sent, "row", n_row, bit)
        bit *= 2
    while col_bits < n_col:
        value = value + swap(value, "col", n_col, col_bits)
        col_bits *= 2
    while bit > 1:
        bit //= 2
        high = ((row // bit) % 2) == 1
        other = swap(value, "row", n_row, bit)
        value = jnp.concatenate([jnp.where(high, other, value), jnp.where(high, value, other)], axis=0)
    return value


def shards(adj_tiles, tile_counts, tile_cols, features, weight, upstream):
    n_row, n_col = lax.axis_size("row"), lax.axis_size("col")
    row, col = lax.axis_index("row"), lax.axis_index("col")
    adj, counts, cols = adj_tiles[0, 0], tile_counts[0, 0], tile_cols[0, 0]
    tile = adj.shape[1]
    rows, depth = upstream.shape[0], features.shape[0]
    col_tiles = depth * n_row // tile
    scale = 1.0 / math.sqrt(rows * n_row * n_col)
    paired = n_row == 8

    order = [i for i in range(0, n_col, 2)] + [i for i in range(n_col)[::-1] if i % 2]
    ring = jnp.array(order, jnp.int32)
    place = jnp.argmax(ring == col).astype(jnp.int32)
    steps = jnp.arange(n_col, dtype=jnp.int32)
    by_owner = ring[(place + n_col - 1 - steps) % n_col]
    by_arrival = ring[(place + n_col - steps) % n_col]
    core = row % 2
    if paired:
        held = row ^ jnp.arange(n_row, dtype=jnp.int32)
        even, odd = jnp.array([0, 6, 2, 4], jnp.int32), jnp.array([0, 6, 4, 2], jnp.int32)
        mine = jnp.where(core == 0, even, odd)
        others = jnp.where(core == 0, odd, even)
        targets = jnp.concatenate([(row ^ 1) ^ others, row ^ mine])
    else:
        held = jnp.arange(n_row, dtype=jnp.int32)
        targets = held
    where = jnp.concatenate([by_owner, by_arrival, held, targets]).astype(jnp.int32)
    at_arrival, at_held, at_targets = n_col, 2 * n_col, 2 * n_col + n_row

    if paired:
        parts = gather_rows(features, n_row, core)
    else:
        block = lax.all_gather(features, "row", axis=0, tiled=True)
        parts = [block[i * depth : (i + 1) * depth] for i in range(n_row)]
    dense = dense_block(adj, counts, cols, col_tiles)

    moving = forward(where, dense, parts, 0, 1, at_held, rows, jnp.bfloat16)[0]
    rest = forward(where, dense, parts, 1, n_col, at_held, rows, jnp.float32)
    for step in range(n_col - 1):
        moving = turn(moving, order)
        if step < n_col - 2:
            moving = (moving.astype(jnp.float32) + rest[step]).astype(jnp.bfloat16)
    hidden, piece, weight_part = middle(moving, rest[n_col - 2], weight, upstream, scale)

    pieces = [piece]
    for step in range(n_col - 1):
        pieces.append(turn(pieces[-1], order))
    weight_grad = sum_all(weight_part, n_row, n_col)

    early = backward(
        where, dense, pieces[:-1], at_arrival, at_targets, n_row, depth, None, 0, jnp.float32
    )
    last = functools.partial(backward, where, dense, pieces[-1:], at_arrival + n_col - 1)
    if not paired:
        grads = last(at_targets, n_row, depth, early, 0, jnp.bfloat16)
        return hidden, weight_grad, finish([lax.psum_scatter(grads, "row", scatter_dimension=0, tiled=True)[0]])

    half = n_row // 2
    sent = last(at_targets, half, depth, early, 0, jnp.bfloat16)
    kept = last(at_targets + half, half, depth, early, half, jnp.float32)
    came = swap(sent, "row", n_row, 1)
    summed = kept + came.astype(jnp.float32)
    near = [(i, i ^ (2 if i % 2 == 0 else 4)) for i in range(n_row)]
    far = [(i, i ^ (4 if i % 2 == 0 else 2)) for i in range(n_row)]
    corner = lax.ppermute(summed[1].astype(jnp.bfloat16), "row", near)
    first = lax.ppermute(summed[2].astype(jnp.bfloat16), "row", near)
    second = lax.ppermute((summed[3] + corner.astype(jnp.float32)).astype(jnp.bfloat16), "row", far)
    return hidden, weight_grad, finish([summed[0], first, second])


def solution(mesh):
    placed = (
        P("row", "col", None, None, None),
        P("row", "col", None),
        P("row", "col", None),
        P(("col", "row"), None),
        P(),
        P(("row", "col"), None),
    )
    return jax.shard_map(
        shards,
        mesh=mesh,
        in_specs=placed,
        out_specs=(P(("row", "col"), None), P(), P(("col", "row"), None)),
        check_vma=False,
    )
```

time: 431 us -> 148 us (0.34)
  matrix products: 224 us -> 0 us
  local copies, waits for them, and re-layouts: 79.4 us -> 7.31 us
  Pallas kernels: 0 us -> 50.1 us
  waiting for transfers between devices: 102 us -> 57.3 us
  starting transfers between devices: 0.38 us -> 27.2 us
  between operations: 13.9 us -> 2.36 us
    dot_general x131 -> x0, matrix products: 224 us -> none  [the longest x32 45.8 us: split_sum(): jnp.einsum(form, selector, lower, preferred_element_type=jnp.float32)]
    reduce_scatter x2 -> x0, waiting for transfers between devices: 66.5 us -> none  [the longest x1 39.2 us: shards(): lax.psum_scatter(grads.astype(jnp.bfloat16), 'row', scatter_dimension=0,...]
    ppermute x0 -> x25, waiting for transfers between devices: none -> 57.3 us  [the longest x6 23.1 us: turn(): lax.ppermute(value, 'col', [(order[p], order[(p + 1) % count]) for p in r...]
    pallas_call x0 -> x8, Pallas kernels: none -> 50.1 us  [the longest x1 18.7 us: dense_block(): pl.pallas_call(functools.partial(dense_kernel, window=window, slots=slots...]
    while x65 -> x0, local copies, waits for them, and re-layouts: 49.4 us -> none
    all_gather x2 -> x0, waiting for transfers between devices: 35 us -> none  [the longest x1 29.5 us: shards(): col_block = lax.all_gather(features, 'row', axis=0, tiled=True)]
    ppermute x0 -> x25, starting transfers between devices: none -> 27.2 us  [the longest x6 15.7 us: turn(): lax.ppermute(value, 'col', [(order[p], order[(p + 1) % count]) for p in r...]
    unnamed x12 -> x22, local copies, waits for them, and re-layouts: 26.4 us -> 4.5 us
  transfers between devices with their start and end apart: 5 -> 25, of which waited for: 4 -> 14; matrix products, arithmetic and copies ran while one was open for 31% -> 4% of each run, Pallas kernels for 0% -> 30%
where the time goes in v1:
time: 148 us; the launch traced here: 147 us
  waiting for transfers between devices  57.3 us (39%)
  Pallas kernels  50.1 us (34%)
  starting transfers between devices  27.2 us (18%)
  local copies, waits for them, and re-layouts  7.31 us (5%)
  other arithmetic  2.79 us (2%)
  between operations  2.36 us (2%)
    ppermute x6, waiting for transfers between devices, turn(): lax.ppermute(value, 'col', [(order[p], order[(p + 1) % count]) for p in r...  23.1 us
    ppermute x15, waiting for transfers between devices, swap(): return lax.ppermute(value, axis, [(i, i ^ bit) for i in range(size)])  19.4 us
    pallas_call x1, Pallas kernels, dense_block(): pl.pallas_call(functools.partial(dense_kernel, window=window, slots=slots...  18.7 us
    pallas_call x3, Pallas kernels, backward(): pl.pallas_call(functools.partial(backward_kernel, count=count, has_sum=be...  17.2 us
    ppermute x6, starting transfers between devices, turn(): lax.ppermute(value, 'col', [(order[p], order[(p + 1) % count]) for p in r...  15.7 us
    pallas_call x2, Pallas kernels, forward(): pl.pallas_call(functools.partial(forward_kernel, first=first, total=total...  12.2 us
    ppermute x15, starting transfers between devices, swap(): return lax.ppermute(value, axis, [(i, i ^ bit) for i in range(size)])  8.43 us
    ppermute x1, waiting for transfers between devices, gather_rows(): lax.ppermute(onward, 'row', [(i, i ^ (4 if i % 2 == 0 else 2)) for i in r...  5.39 us
  transfers between devices with their start and end apart: 25, of which 14 were waited for; matrix products, arithmetic and copies ran while one was open for 4% of the time, Pallas kernels for 30%

profile of v1, /device:TPU:0, one launch (start us, length us, event | category | flops | bytes accessed | tf_op | source)
XLA Modules:
  0.0 147.1 jit_solution(13260926784919515276)
XLA Ops:
  0.6 3.0 %collective-permute-start.3 = (bf16[512,256]{1,0:T(8,128)(2,1)}, bf16[512,256]{1,0:T(8,128)(2,1)S(1)}, u32[]{:S(2)}, u32[]{:S(2)}) collective-permute-start(bf16[512,256]{1,0:T(8,128)(2,1)} %refs_0_.3), channel_id=1, source_target_pairs={{0,16},{4,20},{8,24},{12,28},{16,0},{20,4},{24,8},{28,12},{1,17},{... | collective-permute-start | bytes 786440 | tf_op jit(solution)/shard_map/ppermute | solution.py:240
  3.7 1.5 %collective-permute-start.1 = (bf16[512,256]{1,0:T(8,128)(2,1)}, bf16[512,256]{1,0:T(8,128)(2,1)S(1)}, u32[]{:S(2)}, u32[]{:S(2)}) collective-permute-start(bf16[512,256]{1,0:T(8,128)(2,1)} %refs_0_.3), channel_id=1, source_target_pairs={{0,8},{4,12},{8,0},{12,4},{16,24},{20,28},{24,16},{28,20},{1,9},{5... | collective-permute-start | bytes 786440 | tf_op jit(solution)/shard_map/ppermute | solution.py:240
  5.2 1.3 compare_reduce_fusion
  7.8 2.4 %collective-permute-done.3.refs_4_ = bf16[512,256]{1,0:T(8,128)(2,1)S(1)} collective-permute-done((bf16[512,256]{1,0:T(8,128)(2,1)}, bf16[512,256]{1,0:T(8,128)(2,1)S(1)}, u32[]{:S(2)}, u32[]{:S(2)}) %collective-permute-start.3) | collective-permute-done | bytes 262176 | tf_op jit(solution)/shard_map/ppermute | solution.py:240
  10.2 1.5 collective-permute-done.1.refs_2_
  12.7 5.4 %collective-permute-done.5.refs_6_ = bf16[512,256]{1,0:T(8,128)(2,1)S(1)} collective-permute-done((bf16[512,256]{1,0:T(8,128)(2,1)S(1)}, bf16[512,256]{1,0:T(8,128)(2,1)S(1)}, u32[]{:S(2)}, u32[]{:S(2)}) %collective-permute-start.5) | collective-permute-done | bytes 262176 | tf_op jit(solution)/shard_map/ppermute | solution.py:253
  22.1 18.7 %dense_block.1.a_ref.refs_0_.refs_1_.refs_2_ = bf16[2048,4096]{1,0:T(8,128)(2,1)} custom-call(s32[16]{0:T(128)S(1)} %bitcast.36, s32[448]{0:T(512)S(1)} %bitcast.35, bf16[448,128,128]{2,1,0:T(8,128)(2,1)} %bitcast.37), custom_call_target="tpu_custom_call" | custom-call | bytes 31457280 | tf_op jit(solution)/shard_map/dense_block/pallas_call | solution.py:84
  40.9 3.6 %forward_rows.2 = bf16[1,512,256]{2,1,0:T(8,128)(2,1)S(1)} custom-call(s32[24]{0:T(128)S(1)} %concatenate.12.where, bf16[2048,4096]{1,0:T(8,128)(2,1)} %dense_block.1.a_ref.refs_0_.refs_1_.refs_2_, bf16[512,256]{1,0:T(8,128)(2,1)S(1)} %copy-done.2, bf16[512,256]{1,0:T(8,128)(2,1)S(1)} %collective-permute-done.refs_1_, ...), custom_call_target="tpu_custom_call" | custom-call | flops 1073741824 | bytes 4194304 | tf_op jit(solution)/shard_map/forward_rows/pallas_call | solution.py:122
  44.6 2.6 %collective-permute-start.7 = (bf16[512,256]{1,0:T(8,128)(2,1)S(1)}, bf16[512,256]{1,0:T(8,128)(2,1)S(1)}, u32[]{:S(2)}, u32[]{:S(2)}) collective-permute-start(bf16[512,256]{1,0:T(8,128)(2,1)S(1)} %bitcast.34), channel_id=1, source_target_pairs={{0,2},{2,3},{3,1},{1,0},{4,6},{6,7},{7,5},{5,4},{8,10},{10,11},{11... | collective-permute-start | bytes 786440 | tf_op jit(solution)/shard_map/ppermute | solution.py:245
  48.1 8.6 %forward_rows.3 = f32[3,512,256]{2,1,0:T(8,128)S(1)} custom-call(s32[24]{0:T(128)S(1)} %concatenate.12.where, bf16[2048,4096]{1,0:T(8,128)(2,1)} %dense_block.1.a_ref.refs_0_.refs_1_.refs_2_, bf16[512,256]{1,0:T(8,128)(2,1)S(1)} %copy-done.2, bf16[512,256]{1,0:T(8,128)(2,1)S(1)} %collective-permute-done.refs_1_, ...), custom_call_target="tpu_custom_call" | custom-call | flops 3221225472 | bytes 12582912 | tf_op jit(solution)/shard_map/forward_rows/pallas_call | solution.py:122
  57.9 7.6 %collective-permute-done.8 = bf16[512,256]{1,0:T(8,128)(2,1)S(1)} collective-permute-done((bf16[512,256]{1,0:T(8,128)(2,1)S(1)}, bf16[512,256]{1,0:T(8,128)(2,1)S(1)}, u32[]{:S(2)}, u32[]{:S(2)}) %collective-permute-start.8) | collective-permute-done | bytes 262176 | tf_op jit(solution)/shard_map/ppermute | solution.py:245
  65.5 2.1 %collective-permute-start.9 = (bf16[512,256]{1,0:T(8,128)(2,1)S(1)}, bf16[512,256]{1,0:T(8,128)(2,1)S(1)}, u32[]{:S(2)}, u32[]{:S(2)}) collective-permute-start(bf16[512,256]{1,0:T(8,128)(2,1)S(1)} %fusion.3), channel_id=1, source_target_pairs={{0,2},{2,3},{3,1},{1,0},{4,6},{6,7},{7,5},{5,4},{8,10},{10,11},{11... | collective-permute-start | bytes 786440 | tf_op jit(solution)/shard_map/ppermute | solution.py:245
  67.6 5.7 %collective-permute-done.9.came_ref = bf16[512,256]{1,0:T(8,128)(2,1)S(1)} collective-permute-done((bf16[512,256]{1,0:T(8,128)(2,1)S(1)}, bf16[512,256]{1,0:T(8,128)(2,1)S(1)}, u32[]{:S(2)}, u32[]{:S(2)}) %collective-permute-start.9) | collective-permute-done | bytes 262176 | tf_op jit(solution)/shard_map/ppermute | solution.py:245
  74.5 3.2 %collective-permute-start.18 = (bf16[256,512]{1,0:T(8,128)(2,1)S(1)}, bf16[256,512]{1,0:T(8,128)(2,1)S(1)}, u32[]{:S(2)}, u32[]{:S(2)}) collective-permute-start(bf16[256,512]{1,0:T(8,128)(2,1)S(1)} %get-tuple-element.10.refs_3_), channel_id=1, source_target_pairs={{0,2},{2,3},{3,1},{1,0},{4,6},{6,7},{7,5},{5,4},{8,10},{10,11},{11... | collective-permute-start | bytes 786440 | tf_op jit(solution)/shard_map/ppermute | solution.py:245
  77.8 1.5 %collective-permute-start.11 = (f32[64,256]{1,0:T(8,128)S(1)}, f32[64,256]{1,0:T(8,128)S(1)}, u32[]{:S(2)}, u32[]{:S(2)}) collective-permute-start(f32[64,256]{1,0:T(8,128)S(1)} %constant_dynamic-slice_fusion.1), channel_id=1, source_target_pairs={{0,8},{4,12},{8,0},{12,4},{16,24},{20,28},{24,16},{28,20},{1,9},{5... | collective-permute-start | bytes 196616 | tf_op jit(solution)/shard_map/ppermute | solution.py:240
  79.3 4.6 %collective-permute-done.18.refs_4_ = bf16[256,512]{1,0:T(8,128)(2,1)S(1)} collective-permute-done((bf16[256,512]{1,0:T(8,128)(2,1)S(1)}, bf16[256,512]{1,0:T(8,128)(2,1)S(1)}, u32[]{:S(2)}, u32[]{:S(2)}) %collective-permute-start.18) | collective-permute-done | bytes 262176 | tf_op jit(solution)/shard_map/ppermute | solution.py:245
  83.9 3.4 %collective-permute-start.19 = (bf16[256,512]{1,0:T(8,128)(2,1)S(1)}, bf16[256,512]{1,0:T(8,128)(2,1)S(1)}, u32[]{:S(2)}, u32[]{:S(2)}) collective-permute-start(bf16[256,512]{1,0:T(8,128)(2,1)S(1)} %collective-permute-done.18.refs_4_), channel_id=1, source_target_pairs={{0,2},{2,3},{3,1},{1,0},{4,6},{6,7},{7,5},{5,4},{8,10},{10,11},{11... | collective-permute-start | bytes 786440 | tf_op jit(solution)/shard_map/ppermute | solution.py:245
  87.4 5.3 %collective-permute-done.19.refs_5_ = bf16[256,512]{1,0:T(8,128)(2,1)S(1)} collective-permute-done((bf16[256,512]{1,0:T(8,128)(2,1)S(1)}, bf16[256,512]{1,0:T(8,128)(2,1)S(1)}, u32[]{:S(2)}, u32[]{:S(2)}) %collective-permute-start.19) | collective-permute-done | bytes 262176 | tf_op jit(solution)/shard_map/ppermute | solution.py:245
  92.6 3.4 %collective-permute-start.20 = (bf16[256,512]{1,0:T(8,128)(2,1)S(1)}, bf16[256,512]{1,0:T(8,128)(2,1)S(1)}, u32[]{:S(2)}, u32[]{:S(2)}) collective-permute-start(bf16[256,512]{1,0:T(8,128)(2,1)S(1)} %collective-permute-done.19.refs_5_), channel_id=1, source_target_pairs={{0,2},{2,3},{3,1},{1,0},{4,6},{6,7},{7,5},{5,4},{8,10},{10,11},{11... | collective-permute-start | bytes 786440 | tf_op jit(solution)/shard_map/ppermute | solution.py:245
  96.0 9.3 %backward_cols.3.refs_2_ = f32[8,256,512]{2,1,0:T(8,128)S(1)} custom-call(s32[24]{0:T(128)S(1)} %concatenate.12.where, bf16[2048,4096]{1,0:T(8,128)(2,1)} %dense_block.1.a_ref.refs_0_.refs_1_.refs_2_, bf16[2048,4096]{1,0:T(8,128)(2,1)} %dense_block.1.a_ref.refs_0_.refs_1_.refs_2_, bf16[2048,4096]{1,0:T(8,128)(2,1)} %dense_block.1.a_ref.refs_0_.refs_1_.refs_2_, ...), custom_call_target="tpu_custom_call" | custom-call | flops 3221225472 | bytes 12582912 | tf_op jit(solution)/shard_map/backward_cols/pallas_call | solution.py:199
  105.4 4.3 %backward_cols.5 = bf16[4,256,512]{2,1,0:T(8,128)(2,1)S(1)} custom-call(s32[24]{0:T(128)S(1)} %concatenate.12.where, bf16[2048,4096]{1,0:T(8,128)(2,1)} %dense_block.1.a_ref.refs_0_.refs_1_.refs_2_, bf16[256,512]{1,0:T(8,128)(2,1)S(1)} %collective-permute-done.20.refs_1_, f32[8,256,512]{2,1,0:T(8,128)S(1)} %backward_cols.3.refs_2_), custom_call_target="tpu_custom_call" | custom-call | flops 536870912 | bytes 2097152 | tf_op jit(solution)/shard_map/backward_cols/pallas_call | solution.py:199
  109.9 3.9 %collective-permute-done.13 = f32[32,256]{1,0:T(8,128)S(1)} collective-permute-done((f32[32,256]{1,0:T(8,128)S(1)}, f32[32,256]{1,0:T(8,128)S(1)}, u32[]{:S(2)}, u32[]{:S(2)}) %collective-permute-start.13) | collective-permute-done | bytes 32800 | tf_op jit(solution)/shard_map/ppermute | solution.py:240
  113.8 4.8 %collective-permute-done.14 = f32[32,256]{1,0:T(8,128)S(1)} collective-permute-done((f32[32,256]{1,0:T(8,128)S(1)}, f32[32,256]{1,0:T(8,128)S(1)}, u32[]{:S(2)}, u32[]{:S(2)}) %collective-permute-start.14) | collective-permute-done | bytes 32800 | tf_op jit(solution)/shard_map/ppermute | solution.py:240
  118.6 3.9 %collective-permute-done.15 = f32[32,256]{1,0:T(8,128)S(1)} collective-permute-done((f32[32,256]{1,0:T(8,128)S(1)}, f32[32,256]{1,0:T(8,128)S(1)}, u32[]{:S(2)}, u32[]{:S(2)}) %collective-permute-start.15) | collective-permute-done | bytes 32800 | tf_op jit(solution)/shard_map/ppermute | solution.py:240
  122.5 1.5 %collective-permute-start.16 = (f32[64,256]{1,0:T(8,128)S(1)}, f32[64,256]{1,0:T(8,128)S(1)}, u32[]{:S(2)}, u32[]{:S(2)}) collective-permute-start(f32[64,256]{1,0:T(8,128)S(1)} %pad_maximum_fusion.2), channel_id=1, source_target_pairs={{0,8},{4,12},{8,0},{12,4},{16,24},{20,28},{24,16},{28,20},{1,9},{5... | collective-permute-start | bytes 196616 | tf_op jit(solution)/shard_map/ppermute | solution.py:240
  124.0 2.8 %collective-permute-done.16 = f32[64,256]{1,0:T(8,128)S(1)} collective-permute-done((f32[64,256]{1,0:T(8,128)S(1)}, f32[64,256]{1,0:T(8,128)S(1)}, u32[]{:S(2)}, u32[]{:S(2)}) %collective-permute-start.16) | collective-permute-done | bytes 65568 | tf_op jit(solution)/shard_map/ppermute | solution.py:240
  127.0 2.2 %copy-done.1 = f32[8,256,512]{2,1,0:T(8,128)S(1)} copy-done((f32[8,256,512]{2,1,0:T(8,128)S(1)}, f32[8,256,512]{2,1,0:T(8,128)}, u32[]{:S(2)}) %copy-start.1) | copy-done | bytes 4194328
  129.2 3.6 %backward_cols.4 = f32[4,256,512]{2,1,0:T(8,128)S(1)} custom-call(s32[24]{0:T(128)S(1)} %concatenate.12.where, bf16[2048,4096]{1,0:T(8,128)(2,1)} %dense_block.1.a_ref.refs_0_.refs_1_.refs_2_, bf16[256,512]{1,0:T(8,128)(2,1)S(1)} %collective-permute-done.20.refs_1_, f32[8,256,512]{2,1,0:T(8,128)S(1)} %copy-done.1), custom_call_target="tpu_custom_call" | custom-call | flops 536870912 | bytes 2097152 | tf_op jit(solution)/shard_map/backward_cols/pallas_call | solution.py:199
  133.3 1.5 %collective-permute-start.23 = (bf16[256,512]{1,0:T(8,128)(2,1)S(1)}, bf16[256,512]{1,0:T(8,128)(2,1)S(1)}, u32[]{:S(2)}, u32[]{:S(2)}) collective-permute-start(bf16[256,512]{1,0:T(8,128)(2,1)S(1)} %get-tuple-element.13), channel_id=1, source_target_pairs={{0,8},{4,20},{8,0},{12,28},{16,24},{20,4},{24,16},{28,12},{1,9},{5... | collective-permute-start | bytes 786440 | tf_op jit(solution)/shard_map/ppermute | solution.py:346
  135.5 4.3 %collective-permute-done.23 = bf16[256,512]{1,0:T(8,128)(2,1)S(1)} collective-permute-done((bf16[256,512]{1,0:T(8,128)(2,1)S(1)}, bf16[256,512]{1,0:T(8,128)(2,1)S(1)}, u32[]{:S(2)}, u32[]{:S(2)}) %collective-permute-start.23) | collective-permute-done | bytes 262176 | tf_op jit(solution)/shard_map/ppermute | solution.py:346
  141.0 1.9 %collective-permute-done.22.refs_1_ = bf16[256,512]{1,0:T(8,128)(2,1)S(1)} collective-permute-done((bf16[256,512]{1,0:T(8,128)(2,1)S(1)}, bf16[256,512]{1,0:T(8,128)(2,1)S(1)}, u32[]{:S(2)}, u32[]{:S(2)}) %collective-permute-start.22) | collective-permute-done | bytes 262176 | tf_op jit(solution)/shard_map/ppermute | solution.py:347
  142.9 3.3 %collective-permute-done.24.refs_2_ = bf16[256,512]{1,0:T(8,128)(2,1)S(1)} collective-permute-done((bf16[256,512]{1,0:T(8,128)(2,1)S(1)}, bf16[256,512]{1,0:T(8,128)(2,1)S(1)}, u32[]{:S(2)}, u32[]{:S(2)}) %collective-permute-start.24) | collective-permute-done | bytes 262176 | tf_op jit(solution)/shard_map/ppermute | solution.py:348
  (79 shorter events, 12.1 us)
Async XLA Ops:
  0.6 9.6 %collective-permute-start.3 = (bf16[512,256]{1,0:T(8,128)(2,1)}, bf16[512,256]{1,0:T(8,128)(2,1)S(1)}, u32[]{:S(2)}, u32[]{:S(2)}) collective-permute-start(bf16[512,256]{1,0:T(8,128)(2,1)} %refs_0_.3), channel_id=1, source_target_pairs={{0,16},{4,20},{8,24},{12,28},{16,0},{20,4},{24,8},{28,12},{1,17},{... | collective-permute-start | bytes 786440 | tf_op jit(solution)/shard_map/ppermute | solution.py:240
  3.7 8.0 %collective-permute-start.1 = (bf16[512,256]{1,0:T(8,128)(2,1)}, bf16[512,256]{1,0:T(8,128)(2,1)S(1)}, u32[]{:S(2)}, u32[]{:S(2)}) collective-permute-start(bf16[512,256]{1,0:T(8,128)(2,1)} %refs_0_.3), channel_id=1, source_target_pairs={{0,8},{4,12},{8,0},{12,4},{16,24},{20,28},{24,16},{28,20},{1,9},{5... | collective-permute-start | bytes 786440 | tf_op jit(solution)/shard_map/ppermute | solution.py:240
  5.2 35.7 %collective-permute-start = (bf16[512,256]{1,0:T(8,128)(2,1)}, bf16[512,256]{1,0:T(8,128)(2,1)S(1)}, u32[]{:S(2)}, u32[]{:S(2)}) collective-permute-start(bf16[512,256]{1,0:T(8,128)(2,1)} %refs_0_.3), channel_id=1, source_target_pairs={{0,4},{4,0},{8,12},{12,8},{16,20},{20,16},{24,28},{28,24},{1,5},{5... | collective-permute-start | bytes 786440 | tf_op jit(solution)/shard_map/ppermute | solution.py:240
  11.7 6.4 %collective-permute-start.5 = (bf16[512,256]{1,0:T(8,128)(2,1)S(1)}, bf16[512,256]{1,0:T(8,128)(2,1)S(1)}, u32[]{:S(2)}, u32[]{:S(2)}) collective-permute-start(bf16[512,256]{1,0:T(8,128)(2,1)S(1)} %broadcast_select_fusion), channel_id=1, source_target_pairs={{0,16},{4,12},{8,24},{12,4},{16,0},{20,28},{24,8},{28,20},{1,17},{... | collective-permute-start | bytes 786440 | tf_op jit(solution)/shard_map/ppermute | solution.py:253
  12.1 28.7 %collective-permute-start.4 = (bf16[512,256]{1,0:T(8,128)(2,1)S(1)}, bf16[512,256]{1,0:T(8,128)(2,1)S(1)}, u32[]{:S(2)}, u32[]{:S(2)}) collective-permute-start(bf16[512,256]{1,0:T(8,128)(2,1)S(1)} %collective-permute-done.3.refs_4_), channel_id=1, source_target_pairs={{0,4},{4,0},{8,12},{12,8},{16,20},{20,16},{24,28},{28,24},{1,5},{5... | collective-permute-start | bytes 786440 | tf_op jit(solution)/shard_map/ppermute | solution.py:240
  12.2 28.6 %collective-permute-start.2 = (bf16[512,256]{1,0:T(8,128)(2,1)S(1)}, bf16[512,256]{1,0:T(8,128)(2,1)S(1)}, u32[]{:S(2)}, u32[]{:S(2)}) collective-permute-start(bf16[512,256]{1,0:T(8,128)(2,1)S(1)} %collective-permute-done.1.refs_2_), channel_id=1, source_target_pairs={{0,4},{4,0},{8,12},{12,8},{16,20},{20,16},{24,28},{28,24},{1,5},{5... | collective-permute-start | bytes 786440 | tf_op jit(solution)/shard_map/ppermute | solution.py:240
  18.1 22.8 %collective-permute-start.6 = (bf16[512,256]{1,0:T(8,128)(2,1)S(1)}, bf16[512,256]{1,0:T(8,128)(2,1)S(1)}, u32[]{:S(2)}, u32[]{:S(2)}) collective-permute-start(bf16[512,256]{1,0:T(8,128)(2,1)S(1)} %collective-permute-done.5.refs_6_), channel_id=1, source_target_pairs={{0,4},{4,0},{8,12},{12,8},{16,20},{20,16},{24,28},{28,24},{1,5},{5... | collective-permute-start | bytes 786440 | tf_op jit(solution)/shard_map/ppermute | solution.py:240
  22.0 18.7 %copy-start.9 = (s32[4]{0:T(128)S(1)}, s32[4]{0:T(128)}, u32[]{:S(2)}) copy-start(s32[4]{0:T(128)} %constant.119.clone) | copy-start | bytes 52
  22.0 18.7 %copy-start.10 = (s32[4]{0:T(128)S(1)}, s32[4]{0:T(128)}, u32[]{:S(2)}) copy-start(s32[4]{0:T(128)} %constant.118.clone) | copy-start | bytes 52
  22.0 18.8 %copy-start.2 = (bf16[512,256]{1,0:T(8,128)(2,1)S(1)}, bf16[512,256]{1,0:T(8,128)(2,1)}, u32[]{:S(2)}) copy-start(bf16[512,256]{1,0:T(8,128)(2,1)} %refs_0_.3) | copy-start | bytes 786436
  40.9 3.7 %copy-start.3 = (bf16[512,256]{1,0:T(8,128)(2,1)}, bf16[512,256]{1,0:T(8,128)(2,1)S(1)}, u32[]{:S(2)}) copy-start(bf16[512,256]{1,0:T(8,128)(2,1)S(1)} %collective-permute-done.6.refs_7_) | copy-start | bytes 786436
  44.6 12.2 %collective-permute-start.7 = (bf16[512,256]{1,0:T(8,128)(2,1)S(1)}, bf16[512,256]{1,0:T(8,128)(2,1)S(1)}, u32[]{:S(2)}, u32[]{:S(2)}) collective-permute-start(bf16[512,256]{1,0:T(8,128)(2,1)S(1)} %bitcast.34), channel_id=1, source_target_pairs={{0,2},{2,3},{3,1},{1,0},{4,6},{6,7},{7,5},{5,4},{8,10},{10,11},{11... | collective-permute-start | bytes 786440 | tf_op jit(solution)/shard_map/ppermute | solution.py:245
  56.7 16.6 %copy-start.5 = (bf16[512,256]{1,0:T(8,128)(2,1)S(1)}, bf16[512,256]{1,0:T(8,128)(2,1)}, u32[]{:S(2)}) copy-start(bf16[512,256]{1,0:T(8,128)(2,1)} %up_ref.1) | copy-start | bytes 786436
  56.7 16.6 %copy-start.6 = (bf16[256,256]{1,0:T(8,128)(2,1)S(1)}, bf16[256,256]{1,0:T(8,128)(2,1)}, u32[]{:S(2)}) copy-start(bf16[256,256]{1,0:T(8,128)(2,1)} %weight_ref.1) | copy-start | bytes 393220
  56.8 8.6 %collective-permute-start.8 = (bf16[512,256]{1,0:T(8,128)(2,1)S(1)}, bf16[512,256]{1,0:T(8,128)(2,1)S(1)}, u32[]{:S(2)}, u32[]{:S(2)}) collective-permute-start(bf16[512,256]{1,0:T(8,128)(2,1)S(1)} %fusion.5), channel_id=1, source_target_pairs={{0,2},{2,3},{3,1},{1,0},{4,6},{6,7},{7,5},{5,4},{8,10},{10,11},{11... | collective-permute-start | bytes 786440 | tf_op jit(solution)/shard_map/ppermute | solution.py:245
  65.5 7.8 %collective-permute-start.9 = (bf16[512,256]{1,0:T(8,128)(2,1)S(1)}, bf16[512,256]{1,0:T(8,128)(2,1)S(1)}, u32[]{:S(2)}, u32[]{:S(2)}) collective-permute-start(bf16[512,256]{1,0:T(8,128)(2,1)S(1)} %fusion.3), channel_id=1, source_target_pairs={{0,2},{2,3},{3,1},{1,0},{4,6},{6,7},{7,5},{5,4},{8,10},{10,11},{11... | collective-permute-start | bytes 786440 | tf_op jit(solution)/shard_map/ppermute | solution.py:245
  74.4 3.3 %collective-permute-start.10 = (f32[128,256]{1,0:T(8,128)S(1)}, f32[128,256]{1,0:T(8,128)S(1)}, u32[]{:S(2)}, u32[]{:S(2)}) collective-permute-start(f32[128,256]{1,0:T(8,128)S(1)} %constant_dynamic-slice_fusion.2), channel_id=1, source_target_pairs={{0,4},{4,0},{8,12},{12,8},{16,20},{20,16},{24,28},{28,24},{1,5},{5... | collective-permute-start | bytes 393224 | tf_op jit(solution)/shard_map/ppermute | solution.py:240
  74.5 9.4 %collective-permute-start.18 = (bf16[256,512]{1,0:T(8,128)(2,1)S(1)}, bf16[256,512]{1,0:T(8,128)(2,1)S(1)}, u32[]{:S(2)}, u32[]{:S(2)}) collective-permute-start(bf16[256,512]{1,0:T(8,128)(2,1)S(1)} %get-tuple-element.10.refs_3_), channel_id=1, source_target_pairs={{0,2},{2,3},{3,1},{1,0},{4,6},{6,7},{7,5},{5,4},{8,10},{10,11},{11... | collective-permute-start | bytes 786440 | tf_op jit(solution)/shard_map/ppermute | solution.py:245
  77.8 9.5 %collective-permute-start.11 = (f32[64,256]{1,0:T(8,128)S(1)}, f32[64,256]{1,0:T(8,128)S(1)}, u32[]{:S(2)}, u32[]{:S(2)}) collective-permute-start(f32[64,256]{1,0:T(8,128)S(1)} %constant_dynamic-slice_fusion.1), channel_id=1, source_target_pairs={{0,8},{4,12},{8,0},{12,4},{16,24},{20,28},{24,16},{28,20},{1,9},{5... | collective-permute-start | bytes 196616 | tf_op jit(solution)/shard_map/ppermute | solution.py:240
  83.9 8.7 %collective-permute-start.19 = (bf16[256,512]{1,0:T(8,128)(2,1)S(1)}, bf16[256,512]{1,0:T(8,128)(2,1)S(1)}, u32[]{:S(2)}, u32[]{:S(2)}) collective-permute-start(bf16[256,512]{1,0:T(8,128)(2,1)S(1)} %collective-permute-done.18.refs_4_), channel_id=1, source_target_pairs={{0,2},{2,3},{3,1},{1,0},{4,6},{6,7},{7,5},{5,4},{8,10},{10,11},{11... | collective-permute-start | bytes 786440 | tf_op jit(solution)/shard_map/ppermute | solution.py:245
  87.3 22.5 %collective-permute-start.12 = (f32[32,256]{1,0:T(8,128)S(1)}, f32[32,256]{1,0:T(8,128)S(1)}, u32[]{:S(2)}, u32[]{:S(2)}) collective-permute-start(f32[32,256]{1,0:T(8,128)S(1)} %constant_dynamic-slice_fusion), channel_id=1, source_target_pairs={{0,16},{4,20},{8,24},{12,28},{16,0},{20,4},{24,8},{28,12},{1,17},{... | collective-permute-start | bytes 98312 | tf_op jit(solution)/shard_map/ppermute | solution.py:240
  92.6 12.7 %collective-permute-start.20 = (bf16[256,512]{1,0:T(8,128)(2,1)S(1)}, bf16[256,512]{1,0:T(8,128)(2,1)S(1)}, u32[]{:S(2)}, u32[]{:S(2)}) collective-permute-start(bf16[256,512]{1,0:T(8,128)(2,1)S(1)} %collective-permute-done.19.refs_5_), channel_id=1, source_target_pairs={{0,2},{2,3},{3,1},{1,0},{4,6},{6,7},{7,5},{5,4},{8,10},{10,11},{11... | collective-permute-start | bytes 786440 | tf_op jit(solution)/shard_map/ppermute | solution.py:245
  105.4 4.3 %copy-start = (f32[8,256,512]{2,1,0:T(8,128)}, f32[8,256,512]{2,1,0:T(8,128)S(1)}, u32[]{:S(2)}) copy-start(f32[8,256,512]{2,1,0:T(8,128)S(1)} %backward_cols.3.refs_2_) | copy-start | bytes 12582916
  109.7 23.1 %collective-permute-start.21 = (bf16[4,256,512]{2,1,0:T(8,128)(2,1)S(1)}, bf16[4,256,512]{2,1,0:T(8,128)(2,1)S(1)}, u32[]{:S(2)}, u32[]{:S(2)}) collective-permute-start(bf16[4,256,512]{2,1,0:T(8,128)(2,1)S(1)} %backward_cols.5), channel_id=1, source_target_pairs={{0,4},{4,0},{8,12},{12,8},{16,20},{20,16},{24,28},{28,24},{1,5},{5... | collective-permute-start | bytes 3145736 | tf_op jit(solution)/shard_map/ppermute | solution.py:240
  109.8 4.0 %collective-permute-start.13 = (f32[32,256]{1,0:T(8,128)S(1)}, f32[32,256]{1,0:T(8,128)S(1)}, u32[]{:S(2)}, u32[]{:S(2)}) collective-permute-start(f32[32,256]{1,0:T(8,128)S(1)} %dynamic-slice_add_fusion.2), channel_id=1, source_target_pairs={{0,1},{1,0},{2,3},{3,2},{4,5},{5,4},{6,7},{7,6},{8,9},{9,8},{10,11... | collective-permute-start | bytes 98312 | tf_op jit(solution)/shard_map/ppermute | solution.py:240
  113.8 4.8 %collective-permute-start.14 = (f32[32,256]{1,0:T(8,128)S(1)}, f32[32,256]{1,0:T(8,128)S(1)}, u32[]{:S(2)}, u32[]{:S(2)}) collective-permute-start(f32[32,256]{1,0:T(8,128)S(1)} %add.132), channel_id=1, source_target_pairs={{0,2},{1,3},{2,0},{3,1},{4,6},{5,7},{6,4},{7,5},{8,10},{9,11},{10,... | collective-permute-start | bytes 98312 | tf_op jit(solution)/shard_map/ppermute | solution.py:240
  118.6 3.9 %collective-permute-start.15 = (f32[32,256]{1,0:T(8,128)S(1)}, f32[32,256]{1,0:T(8,128)S(1)}, u32[]{:S(2)}, u32[]{:S(2)}) collective-permute-start(f32[32,256]{1,0:T(8,128)S(1)} %add.133), channel_id=1, source_target_pairs={{0,16},{4,20},{8,24},{12,28},{16,0},{20,4},{24,8},{28,12},{1,17},{... | collective-permute-start | bytes 98312 | tf_op jit(solution)/shard_map/ppermute | solution.py:240
  122.5 4.3 %collective-permute-start.16 = (f32[64,256]{1,0:T(8,128)S(1)}, f32[64,256]{1,0:T(8,128)S(1)}, u32[]{:S(2)}, u32[]{:S(2)}) collective-permute-start(f32[64,256]{1,0:T(8,128)S(1)} %pad_maximum_fusion.2), channel_id=1, source_target_pairs={{0,8},{4,12},{8,0},{12,4},{16,24},{20,28},{24,16},{28,20},{1,9},{5... | collective-permute-start | bytes 196616 | tf_op jit(solution)/shard_map/ppermute | solution.py:240
  126.9 7.9 %collective-permute-start.17 = (f32[128,256]{1,0:T(8,128)S(1)}, f32[128,256]{1,0:T(8,128)S(1)}, u32[]{:S(2)}, u32[]{:S(2)}) collective-permute-start(f32[128,256]{1,0:T(8,128)S(1)} %pad_maximum_fusion.1), channel_id=1, source_target_pairs={{0,4},{4,0},{8,12},{12,8},{16,20},{20,16},{24,28},{28,24},{1,5},{5... | collective-permute-start | bytes 393224 | tf_op jit(solution)/shard_map/ppermute | solution.py:240
  133.3 6.4 %collective-permute-start.23 = (bf16[256,512]{1,0:T(8,128)(2,1)S(1)}, bf16[256,512]{1,0:T(8,128)(2,1)S(1)}, u32[]{:S(2)}, u32[]{:S(2)}) collective-permute-start(bf16[256,512]{1,0:T(8,128)(2,1)S(1)} %get-tuple-element.13), channel_id=1, source_target_pairs={{0,8},{4,20},{8,0},{12,28},{16,24},{20,4},{24,16},{28,12},{1,9},{5... | collective-permute-start | bytes 786440 | tf_op jit(solution)/shard_map/ppermute | solution.py:346
  134.8 8.1 %collective-permute-start.22 = (bf16[256,512]{1,0:T(8,128)(2,1)S(1)}, bf16[256,512]{1,0:T(8,128)(2,1)S(1)}, u32[]{:S(2)}, u32[]{:S(2)}) collective-permute-start(bf16[256,512]{1,0:T(8,128)(2,1)S(1)} %get-tuple-element.14), channel_id=1, source_target_pairs={{0,8},{4,20},{8,0},{12,28},{16,24},{20,4},{24,16},{28,12},{1,9},{5... | collective-permute-start | bytes 786440 | tf_op jit(solution)/shard_map/ppermute | solution.py:347
  139.8 6.4 %collective-permute-start.24 = (bf16[256,512]{1,0:T(8,128)(2,1)S(1)}, bf16[256,512]{1,0:T(8,128)(2,1)S(1)}, u32[]{:S(2)}, u32[]{:S(2)}) collective-permute-start(bf16[256,512]{1,0:T(8,128)(2,1)S(1)} %fusion.1), channel_id=1, source_target_pairs={{0,16},{4,12},{8,24},{12,4},{16,0},{20,28},{24,8},{28,20},{1,17},{... | collective-permute-start | bytes 786440 | tf_op jit(solution)/shard_map/ppermute | solution.py:348
  (4 other events, 4.5 us)

commit v2 on v0

v2 whole, which is shorter than its diff:
```python
import functools
import math

import jax
import jax.numpy as jnp
from jax import lax
from jax.experimental import pallas as pl
from jax.experimental.pallas import tpu as pltpu
from jax.sharding import PartitionSpec as P

MIB = 1024 * 1024
SCALARS = pl.BlockSpec(memory_space=pltpu.SMEM)
WHOLE = pl.BlockSpec(memory_space=pltpu.VMEM)


def params(mib):
    return pltpu.CompilerParams(vmem_limit_bytes=mib * MIB)


def cost(flops, moved, exps=0):
    return pl.CostEstimate(flops=flops, bytes_accessed=moved, transcendentals=exps)


def near(value):
    return pltpu.with_memory_space_constraint(value, pltpu.VMEM)


def dense_kernel(where, counts, cols, adj_ref, out_ref, held, total, sems, *, at, window):
    tile = adj_ref.shape[1]
    slots = adj_ref.shape[0]
    per = out_ref.shape[0] // tile
    width = out_ref.shape[1]
    first = where[at] * per

    starts = [lax.fori_loop(0, first, lambda i, s: s + counts[i], jnp.int32(0))]
    for u in range(per - 1):
        starts.append(starts[-1] + counts[first + u])
    bases = [jnp.minimum(start, slots - window) for start in starts]
    fetches = [
        pltpu.make_async_copy(adj_ref.at[pl.ds(bases[u], window)], held.at[u], sems.at[u]) for u in range(per)
    ]
    for fetch in fetches:
        fetch.start()

    out_ref[...] = jnp.zeros_like(out_ref)
    for u in range(per):
        start, shift, count = starts[u], starts[u] - bases[u], counts[first + u]
        rows = pl.ds(u * tile, tile)
        fetches[u].wait()

        def place(j):
            c = cols[start + j]
            out_ref[rows, pl.ds(pl.multiple_of(c * tile, tile), tile)] = held[u, shift + j]
            return lax.shift_left(jnp.int32(1), c)

        def four(i, state):
            seen, twice = state
            for v in range(4):
                bit = place(4 * i + v)
                twice = twice | (seen & bit)
                seen = seen | bit
            return seen, twice

        def one(j, state):
            seen, twice = state
            bit = place(j)
            return seen | bit, twice | (seen & bit)

        groups = lax.div(count, 4)
        state = lax.fori_loop(0, groups, four, (jnp.int32(0), jnp.int32(0)))
        seen, twice = lax.fori_loop(4 * groups, count, one, state)
        repeated = (twice != 0) if width // tile <= 32 else (count > 0)

        @pl.when(repeated)
        def _():
            total[...] = jnp.zeros_like(total)

            def add(j, carry):
                here = pl.ds(pl.multiple_of(cols[start + j] * tile, tile), tile)
                total[:, here] += held[u, shift + j].astype(jnp.float32)
                return carry

            lax.fori_loop(0, count, add, 0)
            out_ref[rows, :] = total[...].astype(out_ref.dtype)


def dense_rows(where, at, counts, cols, adj, rows, col_tiles):
    slots, tile, _ = adj.shape
    window = min(col_tiles, slots)
    width = col_tiles * tile
    per = rows // tile
    return pl.pallas_call(
        functools.partial(dense_kernel, at=at, window=window),
        out_shape=pltpu.VMEM((rows, width), adj.dtype),
        in_specs=[SCALARS, SCALARS, SCALARS, pl.BlockSpec(memory_space=pltpu.HBM)],
        out_specs=WHOLE,
        scratch_shapes=[
            pltpu.VMEM((per, window, tile, tile), adj.dtype),
            pltpu.VMEM((tile, width), jnp.float32),
            pltpu.SemaphoreType.DMA((per,)),
        ],
        compiler_params=params(14),
        cost_estimate=cost(0, 5 * rows * width),
        name="dense_rows",
    )(where, counts, cols, pltpu.with_memory_space_constraint(adj, pltpu.HBM))


def forward_kernel(where, *refs, blocks, at):
    dense, shards, outs = refs[:blocks], refs[blocks:-blocks], refs[-blocks:]
    depth = shards[0].shape[0]
    for a_ref, out_ref in zip(dense, outs):
        value = None
        for k, shard in enumerate(shards):
            cols = pl.ds(pl.multiple_of(where[at + k] * depth, depth), depth)
            part = jnp.dot(a_ref[:, cols], shard[...], preferred_element_type=jnp.float32)
            value = part if value is None else value + part
        out_ref[...] = value.astype(out_ref.dtype)


def forward(where, at, dense, shards, kinds):
    rows, width = dense[0].shape[0], shards[0].shape[1]
    count = len(dense)
    return pl.pallas_call(
        functools.partial(forward_kernel, blocks=count, at=at),
        out_shape=[pltpu.VMEM((rows, width), kind) for kind in kinds],
        in_specs=[SCALARS] + [WHOLE] * (count + len(shards)),
        out_specs=[WHOLE] * count,
        compiler_params=params(10),
        cost_estimate=cost(2 * count * dense[0].size * width, count * dense[0].size * 2),
        name="forward_rows",
    )(where, *map(near, dense), *map(near, shards))


def middle_kernel(*refs, scale, came):
    parts = refs[: came + 1]
    weight_ref, up_ref, hidden_ref, grad_ref, wgrad_ref = refs[came + 1 :]
    agg = parts[0][...].astype(jnp.float32)
    for part in parts[1:]:
        agg = agg + part[...].astype(jnp.float32)
    agg = agg.astype(jnp.bfloat16)
    weight = weight_ref[...]
    pre = jnp.dot(agg, weight, preferred_element_type=jnp.float32)
    sig = jax.nn.sigmoid(pre)
    hidden_ref[...] = (pre * sig).astype(jnp.bfloat16)
    pre_grad = (up_ref[...].astype(jnp.float32) * sig * (1.0 + pre * (1.0 - sig))).astype(jnp.bfloat16)
    grad_ref[...] = lax.dot_general(
        weight, pre_grad, (((1,), (1,)), ((), ())), preferred_element_type=jnp.float32
    ).astype(jnp.bfloat16)
    wgrad_ref[...] = scale * lax.dot_general(
        agg, pre_grad, (((0,), (0,)), ((), ())), preferred_element_type=jnp.float32
    )


def middle(parts, weight, upstream, scale):
    rows, width = upstream.shape
    return pl.pallas_call(
        functools.partial(middle_kernel, scale=scale, came=len(parts) - 1),
        out_shape=(
            jax.ShapeDtypeStruct((rows, width), jnp.bfloat16),
            jax.ShapeDtypeStruct((width, rows), jnp.bfloat16),
            jax.ShapeDtypeStruct((width, width), jnp.float32),
        ),
        compiler_params=params(16),
        cost_estimate=cost(6 * rows * width * width, 10 * rows * width, rows * width),
        name="middle",
    )(*parts, weight, upstream)


def backward_kernel(where, *refs, count, at, before_at):
    dense, pieces = refs[:count], refs[count : 2 * count]
    out_ref = refs[-1]
    columns, _, depth = out_ref.shape

    def one(j, carry):
        cols = pl.ds(pl.multiple_of(where[at + j] * depth, depth), depth)
        value = None if before_at is None else refs[2 * count][before_at + j]
        for a_ref, piece in zip(dense, pieces):
            part = jnp.dot(piece[...], a_ref[:, cols], preferred_element_type=jnp.float32)
            value = part if value is None else value + part
        out_ref[j] = value.astype(out_ref.dtype)
        return carry

    lax.fori_loop(0, columns, one, 0)


def backward(where, at, dense, pieces, columns, depth, before, before_at, kind, after=()):
    count = len(pieces)
    width, rows = pieces[0].shape
    operands = [near(x) for x in [*dense, *pieces] + ([] if before is None else [before])]
    return pl.pallas_call(
        functools.partial(
            backward_kernel, count=count, at=at, before_at=None if before is None else before_at
        ),
        out_shape=pltpu.VMEM((columns, width, depth), kind),
        in_specs=[SCALARS] + [WHOLE] * len(operands) + [pl.BlockSpec(memory_space=pl.ANY)] * len(after),
        out_specs=WHOLE,
        compiler_params=params(10),
        cost_estimate=cost(
            2 * count * rows * width * columns * depth, count * rows * columns * depth * 2
        ),
        name="backward_cols",
    )(where, *operands, *after)


def finish_kernel(*refs):
    parts, out_ref = refs[:-1], refs[-1]
    value = parts[0][...].astype(jnp.float32)
    for part in parts[1:]:
        value = value + part[...].astype(jnp.float32)
    out_ref[...] = value.T.astype(out_ref.dtype)


def finish(parts):
    width, rows = parts[0].shape
    return pl.pallas_call(
        finish_kernel,
        out_shape=jax.ShapeDtypeStruct((rows, width), jnp.bfloat16),
        compiler_params=params(10),
        cost_estimate=cost(len(parts) * rows * width, 4 * len(parts) * rows * width),
        name="finish",
    )(*parts)


def pick_kernel(which, even_ref, odd_ref, *refs):
    out_ref = refs[-1]

    @pl.when(which[0] == 0)
    def _():
        out_ref[...] = even_ref[...]

    @pl.when(which[0] != 0)
    def _():
        out_ref[...] = odd_ref[...]


def pick(which, even, odd, before):
    return pl.pallas_call(
        pick_kernel,
        out_shape=pltpu.VMEM(even.shape, even.dtype),
        in_specs=[SCALARS, WHOLE, WHOLE] + [pl.BlockSpec(memory_space=pl.ANY)] * len(before),
        out_specs=WHOLE,
        compiler_params=params(10),
        cost_estimate=cost(0, 4 * even.size),
        name="pick",
    )(which.reshape(1), near(even), near(odd), *before)


def join_kernel(mine, *refs, count):
    out_ref = refs[-1]
    rows = refs[0].shape[0]
    for bit in range(count):
        out_ref[pl.ds(pl.multiple_of((mine[0] ^ bit) * rows, rows), rows), :] = refs[bit][...]


def join(mine, parts, before):
    count, (rows, width) = len(parts), parts[0].shape
    return pl.pallas_call(
        functools.partial(join_kernel, count=count),
        out_shape=jax.ShapeDtypeStruct((count * rows, width), parts[0].dtype),
        in_specs=[SCALARS] + [WHOLE] * count + [pl.BlockSpec(memory_space=pl.ANY)] * len(before),
        out_specs=WHOLE,
        compiler_params=params(10),
        cost_estimate=cost(0, 8 * count * rows * width),
        name="join",
    )(mine.reshape(1), *parts, *before)


def swap(value, axis, size, bit):
    return lax.ppermute(value, axis, [(i, i ^ bit) for i in range(size)])


def corner_first(size):
    return [(i, i ^ (2 if i % 2 == 0 else 4)) for i in range(size)]


def corner_second(size):
    return [(i, i ^ (4 if i % 2 == 0 else 2)) for i in range(size)]


def gather_rows(features, size, core, beside):
    across_x = swap(features, "row", size, 2)
    across_y = swap(features, "row", size, 4)
    sibling = swap(features, "row", size, 1)
    onward = pick(core, across_x, across_y, beside)
    corner = lax.ppermute(onward, "row", corner_second(size))
    sibling_x = swap(across_x, "row", size, 1)
    sibling_y = swap(across_y, "row", size, 1)
    sibling_corner = swap(corner, "row", size, 1)
    return [features, sibling, across_x, sibling_x, across_y, sibling_y, corner, sibling_corner]


def add(value, came):
    return (value.astype(jnp.float32) + came.astype(jnp.float32)).astype(jnp.bfloat16)


def choose(index, options):
    options = dict(options) if isinstance(options, dict) else dict(enumerate(options))
    last = max(options)
    value = options[last]
    for i, option in options.items():
        if option is not value and i != last:
            value = jnp.where(index == i, option, value)
    return value


def shards(adj_tiles, tile_counts, tile_cols, features, weight, upstream):
    n_row, n_col = lax.axis_size("row"), lax.axis_size("col")
    row, col = lax.axis_index("row"), lax.axis_index("col")
    adj, counts, cols = adj_tiles[0, 0], tile_counts[0, 0], tile_cols[0, 0]
    tile = adj.shape[1]
    rows, depth = upstream.shape[0], features.shape[0]
    col_tiles = depth * n_row // tile
    scale = 1.0 / math.sqrt(rows * n_row * n_col)
    paired = n_row == 8
    core = row % 2

    order = [sorted(range(n_col), key=lambda s: (-abs(s - z), s)) for z in range(n_col)]
    owners = choose(col, [jnp.array(line, jnp.int32) for line in order])
    if paired:
        held = row ^ jnp.arange(n_row, dtype=jnp.int32)
        even, odd = jnp.array([0, 6, 2, 4], jnp.int32), jnp.array([0, 6, 4, 2], jnp.int32)
        mine = jnp.where(core == 0, even, odd)
        others = jnp.where(core == 0, odd, even)
        targets = jnp.concatenate([(row ^ 1) ^ others, row ^ mine])
    else:
        held = jnp.arange(n_row, dtype=jnp.int32)
        targets = held
    where = jnp.concatenate([owners, held, targets]).astype(jnp.int32)
    at_held, at_targets = n_col, n_col + n_row

    dense = [dense_rows(where, i, counts, cols, adj, rows, col_tiles) for i in range(n_col)]
    if paired:
        parts = gather_rows(features, n_row, core, dense[: n_col // 2])
    else:
        block = lax.all_gather(features, "row", axis=0, tiled=True)
        parts = [block[i * depth : (i + 1) * depth] for i in range(n_row)]

    sums = list(forward(where, at_held, dense[:1], parts, [jnp.bfloat16]))
    sums += forward(where, at_held, dense[1:], parts, [jnp.bfloat16] * (n_col - 2) + [jnp.float32])
    up = down = None
    for k in range(1, n_col):
        rising = {z: sums[order[z].index(z + n_col - k)] for z in range(n_col - 1) if z <= k - 1}
        falling = {z: sums[order[z].index(z - n_col + k)] for z in range(1, n_col) if z >= n_col - k}
        upward, downward = choose(col, rising), choose(col, falling)
        if k > 1:
            upward, downward = add(upward, up), add(downward, down)
        up = lax.ppermute(upward, "col", [(z, z + 1) for z in rising])
        down = lax.ppermute(downward, "col", [(z, z - 1) for z in falling])
    hidden, piece, part = middle([sums[-1], up, down], weight, upstream, scale)

    beside = paired and n_col == 4 and part.shape[0] % 64 == 0
    chip = row // 2
    below, above = [piece], [piece]
    for k in range(1, n_col):
        up, down = below[-1], above[-1]
        if beside and k > 1:
            up, down, part = lax.optimization_barrier((up, down, part))
        below.append(lax.ppermute(up, "col", [(z, z + 1) for z in range(k - 1, n_col - 1)]))
        above.append(lax.ppermute(down, "col", [(z, z - 1) for z in range(1, n_col - k + 1)]))
        if beside and k == 1:
            half = part.shape[0] // 2
            sent = lax.dynamic_slice_in_dim(part, (1 - core) * half, half, 0)
            kept = lax.dynamic_slice_in_dim(part, core * half, half, 0)
            part = kept + swap(sent, "row", n_row, 1)
        if beside and k == 2:
            quarter = part.shape[0] // 4
            whole, part = part, lax.dynamic_slice_in_dim(part, chip * quarter, quarter, 0)
            for bit in (1, 2, 3):
                sent = lax.dynamic_slice_in_dim(whole, (chip ^ bit) * quarter, quarter, 0)
                part = part + swap(sent, "row", n_row, 2 * bit)
        if beside and k == 3:
            part = sum([swap(part, "col", n_col, bit) for bit in (1, 2, 3)], part)

    def came_from(i):
        came = {z: below[z - line[i]] if line[i] <= z else above[line[i] - z] for z, line in enumerate(order)}
        return choose(col, came)

    pieces = [came_from(i) for i in range(1, n_col)]
    early = backward(where, at_targets, dense[1:], pieces, n_row, depth, None, 0, jnp.float32)
    below, above, early = lax.optimization_barrier((below, above, early))
    late = [came_from(0)]
    last = functools.partial(backward, where)
    if not paired:
        grads = last(at_targets, dense[:1], late, n_row, depth, early, 0, jnp.bfloat16)
        weight_grad = lax.psum(part, ("row", "col"))
        return hidden, weight_grad, finish([lax.psum_scatter(grads, "row", scatter_dimension=0, tiled=True)[0]])

    half = n_row // 2
    sent = last(at_targets, dense[:1], late, half, depth, early, 0, jnp.bfloat16, [part] if beside else [])
    kept = last(at_targets + half, dense[:1], late, half, depth, early, half, jnp.float32)
    came = swap(sent, "row", n_row, 1)
    if beside:
        quarters = [part] + [swap(part, "row", n_row, 2 * bit) for bit in (1, 2, 3)]
        part = join(chip, quarters, [kept])
    summed = [add(kept[i], came[i]) for i in (1, 2)]
    corner = lax.ppermute(summed[0], "row", corner_first(n_row))
    first = lax.ppermute(summed[1], "row", corner_first(n_row))
    if beside:
        other = swap(part, "row", n_row, 1)
        weight_grad = join(core, [part, other], [])
    else:
        weight_grad = lax.psum(part, ("row", "col"))
    onward = (kept[3] + came[3].astype(jnp.float32) + corner.astype(jnp.float32)).astype(jnp.bfloat16)
    second = lax.ppermute(onward, "row", corner_second(n_row))
    return hidden, weight_grad, finish([kept[0], came[0], first, second])


def solution(mesh):
    placed = (
        P("row", "col", None, None, None),
        P("row", "col", None),
        P("row", "col", None),
        P(("col", "row"), None),
        P(),
        P(("row", "col"), None),
    )
    return jax.shard_map(
        shards,
        mesh=mesh,
        in_specs=placed,
        out_specs=(P(("row", "col"), None), P(), P(("col", "row"), None)),
        check_vma=False,
    )
```

time: 431 us -> 133 us (0.31)
  matrix products: 224 us -> 0 us
  local copies, waits for them, and re-layouts: 79.4 us -> 8.44 us
  waiting for transfers between devices: 102 us -> 43.5 us
  starting transfers between devices: 0.38 us -> 47 us
  Pallas kernels: 0 us -> 30.8 us
  between operations: 13.9 us -> 1.18 us
    dot_general x131 -> x0, matrix products: 224 us -> none  [the longest x32 45.8 us: split_sum(): jnp.einsum(form, selector, lower, preferred_element_type=jnp.float32)]
    reduce_scatter x2 -> x0, waiting for transfers between devices: 66.5 us -> none  [the longest x1 39.2 us: shards(): lax.psum_scatter(grads.astype(jnp.bfloat16), 'row', scatter_dimension=0,...]
    while x65 -> x0, local copies, waits for them, and re-layouts: 49.4 us -> none
    ppermute x0 -> x34, starting transfers between devices: none -> 47 us  [the longest x18 16.7 us: swap(): return lax.ppermute(value, axis, [(i, i ^ bit) for i in range(size)])]
    ppermute x0 -> x34, waiting for transfers between devices: none -> 43.5 us  [the longest x3 9.13 us: shards(): lax.ppermute(down, 'col', [(z, z - 1) for z in range(1, n_col - k + 1)])]
    all_gather x2 -> x0, waiting for transfers between devices: 35 us -> none  [the longest x1 29.5 us: shards(): col_block = lax.all_gather(features, 'row', axis=0, tiled=True)]
    pallas_call x0 -> x14, Pallas kernels: none -> 30.8 us  [the longest x4 13.6 us: dense_rows(): pl.pallas_call(functools.partial(dense_kernel, at=at, window=window), out...]
    unnamed x12 -> x26, local copies, waits for them, and re-layouts: 26.4 us -> 8.39 us
  transfers between devices with their start and end apart: 5 -> 34, of which waited for: 4 -> 15; matrix products, arithmetic and copies ran while one was open for 31% -> 1% of each run, Pallas kernels for 0% -> 19%
where the time goes in v2:
time: 133 us
  starting transfers between devices  47 us (35%)
  waiting for transfers between devices  43.5 us (33%)
  Pallas kernels  30.8 us (23%)
  local copies, waits for them, and re-layouts  8.44 us (6%)
  other arithmetic  2.29 us (2%)
    ppermute x18, starting transfers between devices, swap(): return lax.ppermute(value, axis, [(i, i ^ bit) for i in range(size)])  16.7 us
    ppermute x3, starting transfers between devices, shards(): up = lax.ppermute(upward, 'col', [(z, z + 1) for z in rising])  14 us
    pallas_call x4, Pallas kernels, dense_rows(): pl.pallas_call(functools.partial(dense_kernel, at=at, window=window), out...  13.6 us
    ppermute x3, waiting for transfers between devices, shards(): lax.ppermute(down, 'col', [(z, z - 1) for z in range(1, n_col - k + 1)])  9.13 us
    pallas_call x3, Pallas kernels, backward(): pl.pallas_call(functools.partial(backward_kernel, count=count, at=at, bef...  8.67 us
    ppermute x3, waiting for transfers between devices, shards(): up = lax.ppermute(upward, 'col', [(z, z + 1) for z in rising])  8.64 us
    unnamed x26, local copies, waits for them, and re-layouts  8.39 us
    ppermute x18, waiting for transfers between devices, swap(): return lax.ppermute(value, axis, [(i, i ^ bit) for i in range(size)])  7.1 us
  transfers between devices with their start and end apart: 34, of which 15 were waited for; matrix products, arithmetic and copies ran while one was open for 1% of the time, Pallas kernels for 19%

profile of v2, /device:TPU:0, one launch (start us, length us, event | category | flops | bytes accessed | tf_op | source)
XLA Modules:
  0.0 133.2 jit_solution(5994037247661840774)
XLA Ops:
  0.6 3.0 %collective-permute-start.1 = (bf16[512,256]{1,0:T(8,128)(2,1)}, bf16[512,256]{1,0:T(8,128)(2,1)S(1)}, u32[]{:S(2)}, u32[]{:S(2)}) collective-permute-start(bf16[512,256]{1,0:T(8,128)(2,1)} %refs_1_.1), channel_id=1, source_target_pairs={{0,8},{4,12},{8,0},{12,4},{16,24},{20,28},{24,16},{28,20},{1,9},{5... | collective-permute-start | bytes 786440 | tf_op jit(solution)/shard_map/ppermute | solution.py:269
  3.6 1.5 %collective-permute-start.3 = (bf16[512,256]{1,0:T(8,128)(2,1)}, bf16[512,256]{1,0:T(8,128)(2,1)S(1)}, u32[]{:S(2)}, u32[]{:S(2)}) collective-permute-start(bf16[512,256]{1,0:T(8,128)(2,1)} %refs_1_.1), channel_id=1, source_target_pairs={{0,16},{4,20},{8,24},{12,28},{16,0},{20,4},{24,8},{28,12},{1,17},{... | collective-permute-start | bytes 786440 | tf_op jit(solution)/shard_map/ppermute | solution.py:269
  7.9 3.0 %dense_rows.4.refs_1_.refs_0_ = bf16[512,4096]{1,0:T(8,128)(2,1)S(1)} custom-call(s32[20]{0:T(128)S(1)} %pad_add_fusion.where, s32[16]{0:T(128)S(1)} %bitcast.23, s32[448]{0:T(512)S(1)} %bitcast.19, bf16[448,128,128]{2,1,0:T(8,128)(2,1)} %bitcast.27), custom_call_target="tpu_custom_call" | custom-call | bytes 10485760 | tf_op jit(solution)/shard_map/dense_rows/pallas_call | solution.py:92
  10.9 3.8 %dense_rows.7.refs_0_ = bf16[512,4096]{1,0:T(8,128)(2,1)S(1)} custom-call(s32[20]{0:T(128)S(1)} %pad_add_fusion.where, s32[16]{0:T(128)S(1)} %bitcast.24, s32[448]{0:T(512)S(1)} %bitcast.20, bf16[448,128,128]{2,1,0:T(8,128)(2,1)} %bitcast.28), custom_call_target="tpu_custom_call" | custom-call | bytes 10485760 | tf_op jit(solution)/shard_map/dense_rows/pallas_call | solution.py:92
  16.4 4.8 %collective-permute-done.5.refs_9_.refs_7_ = bf16[512,256]{1,0:T(8,128)(2,1)S(1)} collective-permute-done((bf16[512,256]{1,0:T(8,128)(2,1)S(1)}, bf16[512,256]{1,0:T(8,128)(2,1)S(1)}, u32[]{:S(2)}, u32[]{:S(2)}) %collective-permute-start.5) | collective-permute-done | bytes 262176 | tf_op jit(solution)/shard_map/ppermute | solution.py:285
  21.2 3.0 %dense_rows.5.refs_1_ = bf16[512,4096]{1,0:T(8,128)(2,1)S(1)} custom-call(s32[20]{0:T(128)S(1)} %pad_add_fusion.where, s32[16]{0:T(128)S(1)} %bitcast.25, s32[448]{0:T(512)S(1)} %bitcast.21, bf16[448,128,128]{2,1,0:T(8,128)(2,1)} %bitcast.29), custom_call_target="tpu_custom_call" | custom-call | bytes 10485760 | tf_op jit(solution)/shard_map/dense_rows/pallas_call | solution.py:92
  24.2 3.8 %dense_rows.6.refs_2_ = bf16[512,4096]{1,0:T(8,128)(2,1)S(1)} custom-call(s32[20]{0:T(128)S(1)} %pad_add_fusion.where, s32[16]{0:T(128)S(1)} %bitcast.26, s32[448]{0:T(512)S(1)} %bitcast.22, bf16[448,128,128]{2,1,0:T(8,128)(2,1)} %bitcast.30), custom_call_target="tpu_custom_call" | custom-call | bytes 10485760 | tf_op jit(solution)/shard_map/dense_rows/pallas_call | solution.py:92
  28.1 1.8 %forward_rows.3 = bf16[512,256]{1,0:T(8,128)(2,1)S(1)} custom-call(s32[20]{0:T(128)S(1)} %pad_add_fusion.where, bf16[512,4096]{1,0:T(8,128)(2,1)S(1)} %dense_rows.7.refs_0_, bf16[512,256]{1,0:T(8,128)(2,1)S(1)} %copy-done.8, bf16[512,256]{1,0:T(8,128)(2,1)S(1)} %collective-permute-done.refs_4_.refs_2_, ...), custom_call_target="tpu_custom_call" | custom-call | flops 1073741824 | bytes 4194304 | tf_op jit(solution)/shard_map/forward_rows/pallas_call | solution.py:123
  30.8 3.8 %collective-permute-start.7 = (bf16[512,256]{1,0:T(8,128)(2,1)S(1)}, bf16[512,256]{1,0:T(8,128)(2,1)S(1)}, u32[]{:S(2)}, u32[]{:S(2)}) collective-permute-start(bf16[512,256]{1,0:T(8,128)(2,1)S(1)} %forward_rows.3), channel_id=1, source_target_pairs={{0,1},{4,5},{8,9},{12,13},{16,17},{20,21},{24,25},{28,29}} | collective-permute-start | bytes 786440 | tf_op jit(solution)/shard_map/ppermute | solution.py:347
  34.6 4.0 %forward_rows.2 = (bf16[512,256]{1,0:T(8,128)(2,1)S(1)}, bf16[512,256]{1,0:T(8,128)(2,1)S(1)}, f32[512,256]{1,0:T(8,128)S(1)}) custom-call(s32[20]{0:T(128)S(1)} %pad_add_fusion.where, bf16[512,4096]{1,0:T(8,128)(2,1)S(1)} %dense_rows.4.refs_1_.refs_0_, bf16[512,4096]{1,0:T(8,128)(2,1)S(1)} %dense_rows.5.refs_1_, bf16[512,4096]{1,0:T(8,128)(2,1)S(1)} %dense_rows.6.refs_2_, ...), custom_call_target="tpu_custom_call" | custom-call | flops 3221225472 | bytes 12582912 | tf_op jit(solution)/shard_map/forward_rows/pallas_call | solution.py:123
  38.6 2.1 %collective-permute-done.7 = bf16[512,256]{1,0:T(8,128)(2,1)S(1)} collective-permute-done((bf16[512,256]{1,0:T(8,128)(2,1)S(1)}, bf16[512,256]{1,0:T(8,128)(2,1)S(1)}, u32[]{:S(2)}, u32[]{:S(2)}) %collective-permute-start.7) | collective-permute-done | bytes 262176 | tf_op jit(solution)/shard_map/ppermute | solution.py:347
  41.6 5.0 %collective-permute-start.8 = (bf16[512,256]{1,0:T(8,128)(2,1)S(1)}, bf16[512,256]{1,0:T(8,128)(2,1)S(1)}, u32[]{:S(2)}, u32[]{:S(2)}) collective-permute-start(bf16[512,256]{1,0:T(8,128)(2,1)S(1)} %get-tuple-element.41), channel_id=1, source_target_pairs={{0,1},{1,2},{4,5},{5,6},{8,9},{9,10},{12,13},{13,14},{16,17},{17,1... | collective-permute-start | bytes 786440 | tf_op jit(solution)/shard_map/ppermute | solution.py:347
  46.6 5.3 %collective-permute-done.8 = bf16[512,256]{1,0:T(8,128)(2,1)S(1)} collective-permute-done((bf16[512,256]{1,0:T(8,128)(2,1)S(1)}, bf16[512,256]{1,0:T(8,128)(2,1)S(1)}, u32[]{:S(2)}, u32[]{:S(2)}) %collective-permute-start.8) | collective-permute-done | bytes 262176 | tf_op jit(solution)/shard_map/ppermute | solution.py:347
  53.4 5.2 %collective-permute-start.9 = (bf16[512,256]{1,0:T(8,128)(2,1)S(1)}, bf16[512,256]{1,0:T(8,128)(2,1)S(1)}, u32[]{:S(2)}, u32[]{:S(2)}) collective-permute-start(bf16[512,256]{1,0:T(8,128)(2,1)S(1)} %get-tuple-element.45), channel_id=1, source_target_pairs={{0,1},{1,2},{2,3},{4,5},{5,6},{6,7},{8,9},{9,10},{10,11},{12,13},{... | collective-permute-start | bytes 786440 | tf_op jit(solution)/shard_map/ppermute | solution.py:347
  58.6 3.1 %collective-permute-done.12.refs_2_ = bf16[512,256]{1,0:T(8,128)(2,1)S(1)} collective-permute-done((bf16[512,256]{1,0:T(8,128)(2,1)S(1)}, bf16[512,256]{1,0:T(8,128)(2,1)S(1)}, u32[]{:S(2)}, u32[]{:S(2)}) %collective-permute-start.12) | collective-permute-done | bytes 262176 | tf_op jit(solution)/shard_map/ppermute | solution.py:348
  64.1 4.4 %collective-permute-start.13 = (bf16[256,512]{1,0:T(8,128)(2,1)S(1)}, bf16[256,512]{1,0:T(8,128)(2,1)S(1)}, u32[]{:S(2)}, u32[]{:S(2)}) collective-permute-start(bf16[256,512]{1,0:T(8,128)(2,1)S(1)} %get-tuple-element.24.refs_5_), channel_id=1, source_target_pairs={{0,1},{1,2},{2,3},{4,5},{5,6},{6,7},{8,9},{9,10},{10,11},{12,13},{... | collective-permute-start | bytes 786440 | tf_op jit(solution)/shard_map/ppermute | solution.py:358
  69.9 4.8 %collective-permute-done.13 = bf16[256,512]{1,0:T(8,128)(2,1)S(1)} collective-permute-done((bf16[256,512]{1,0:T(8,128)(2,1)S(1)}, bf16[256,512]{1,0:T(8,128)(2,1)S(1)}, u32[]{:S(2)}, u32[]{:S(2)}) %collective-permute-start.13) | collective-permute-done | bytes 262176 | tf_op jit(solution)/shard_map/ppermute | solution.py:358
  74.7 4.4 %collective-permute-done.14 = bf16[256,512]{1,0:T(8,128)(2,1)S(1)} collective-permute-done((bf16[256,512]{1,0:T(8,128)(2,1)S(1)}, bf16[256,512]{1,0:T(8,128)(2,1)S(1)}, u32[]{:S(2)}, u32[]{:S(2)}) %collective-permute-start.14) | collective-permute-done | bytes 262176 | tf_op jit(solution)/shard_map/ppermute | solution.py:359
  82.4 2.2 %collective-permute-start.20 = (f32[32,256]{1,0:T(8,128)S(1)}, f32[32,256]{1,0:T(8,128)S(1)}, u32[]{:S(2)}, u32[]{:S(2)}) collective-permute-start(f32[32,256]{1,0:T(8,128)S(1)} %get-tuple-element.47), channel_id=1, source_target_pairs={{0,24},{4,28},{8,16},{12,20},{16,8},{20,12},{24,0},{28,4},{1,25},{... | collective-permute-start | bytes 98312 | tf_op jit(solution)/shard_map/ppermute | solution.py:269
  85.6 1.7 %collective-permute-done.20 = f32[32,256]{1,0:T(8,128)S(1)} collective-permute-done((f32[32,256]{1,0:T(8,128)S(1)}, f32[32,256]{1,0:T(8,128)S(1)}, u32[]{:S(2)}, u32[]{:S(2)}) %collective-permute-start.20) | collective-permute-done | bytes 32800 | tf_op jit(solution)/shard_map/ppermute | solution.py:269
  87.3 4.7 %collective-permute-done.17 = bf16[256,512]{1,0:T(8,128)(2,1)S(1)} collective-permute-done((bf16[256,512]{1,0:T(8,128)(2,1)S(1)}, bf16[256,512]{1,0:T(8,128)(2,1)S(1)}, u32[]{:S(2)}, u32[]{:S(2)}) %collective-permute-start.17) | collective-permute-done | bytes 262176 | tf_op jit(solution)/shard_map/ppermute | solution.py:359
  92.0 1.7 %collective-permute-start.21 = (f32[32,256]{1,0:T(8,128)S(1)}, f32[32,256]{1,0:T(8,128)S(1)}, u32[]{:S(2)}, u32[]{:S(2)}) collective-permute-start(f32[32,256]{1,0:T(8,128)S(1)} %add_add_fusion.1), channel_id=1, source_target_pairs={{0,1},{1,0},{2,3},{3,2},{4,5},{5,4},{6,7},{7,6},{8,9},{9,8},{10,11... | collective-permute-start | bytes 98312 | tf_op jit(solution)/shard_map/ppermute | solution.py:269
  94.3 2.1 %collective-permute-start.23 = (f32[32,256]{1,0:T(8,128)S(1)}, f32[32,256]{1,0:T(8,128)S(1)}, u32[]{:S(2)}, u32[]{:S(2)}) collective-permute-start(f32[32,256]{1,0:T(8,128)S(1)} %add_add_fusion.1), channel_id=1, source_target_pairs={{0,3},{1,2},{2,1},{3,0},{4,7},{5,6},{6,5},{7,4},{8,11},{9,10},{10,... | collective-permute-start | bytes 98312 | tf_op jit(solution)/shard_map/ppermute | solution.py:269
  98.4 2.2 %copy-done.3 = bf16[512,4096]{1,0:T(8,128)(2,1)S(1)} copy-done((bf16[512,4096]{1,0:T(8,128)(2,1)S(1)}, bf16[512,4096]{1,0:T(8,128)(2,1)}, u32[]{:S(2)}) %copy-start.3) | copy-done | bytes 4194328
  100.6 2.2 %copy-done.5 = bf16[512,4096]{1,0:T(8,128)(2,1)S(1)} copy-done((bf16[512,4096]{1,0:T(8,128)(2,1)S(1)}, bf16[512,4096]{1,0:T(8,128)(2,1)}, u32[]{:S(2)}) %copy-start.5) | copy-done | bytes 4194328
  102.8 2.2 %copy-done.7 = bf16[512,4096]{1,0:T(8,128)(2,1)S(1)} copy-done((bf16[512,4096]{1,0:T(8,128)(2,1)S(1)}, bf16[512,4096]{1,0:T(8,128)(2,1)}, u32[]{:S(2)}) %copy-start.7) | copy-done | bytes 4194328
  105.0 5.2 %backward_cols.3.refs_2_ = f32[8,256,512]{2,1,0:T(8,128)S(1)} custom-call(s32[20]{0:T(128)S(1)} %pad_add_fusion.where, bf16[512,4096]{1,0:T(8,128)(2,1)S(1)} %copy-done.3, bf16[512,4096]{1,0:T(8,128)(2,1)S(1)} %copy-done.5, bf16[512,4096]{1,0:T(8,128)(2,1)S(1)} %copy-done.7, bf16[256,512]{1,0:T(8,128)(2,1)S(1)} %get-tuple-element.43.refs_3_, ...), custom_call_target="tpu_custom_call" | custom-call | flops 3221225472 | bytes 12582912 | tf_op jit(solution)/shard_map/backward_cols/pallas_call | solution.py:190
  110.3 1.8 %backward_cols.5 = bf16[4,256,512]{2,1,0:T(8,128)(2,1)S(1)} custom-call(s32[20]{0:T(128)S(1)} %pad_add_fusion.where, bf16[512,4096]{1,0:T(8,128)(2,1)S(1)} %copy-done.1, bf16[256,512]{1,0:T(8,128)(2,1)S(1)} %select_select_fusion.3.refs_1_, f32[8,256,512]{2,1,0:T(8,128)S(1)} %backward_cols.3.refs_2_, f32[32,256]{1,0:T(8,128)S(1)} %add_add_fusion.refs_0_.refs_3_), custom_call_target="tpu_custom_call" | custom-call | flops 536870912 | bytes 2097152 | tf_op jit(solution)/shard_map/backward_cols/pallas_call | solution.py:190
  112.1 1.8 %backward_cols.4.refs_4_ = f32[4,256,512]{2,1,0:T(8,128)S(1)} custom-call(s32[20]{0:T(128)S(1)} %pad_add_fusion.where, bf16[512,4096]{1,0:T(8,128)(2,1)S(1)} %copy-done.1, bf16[256,512]{1,0:T(8,128)(2,1)S(1)} %select_select_fusion.3.refs_1_, f32[8,256,512]{2,1,0:T(8,128)S(1)} %backward_cols.3.refs_2_), custom_call_target="tpu_custom_call" | custom-call | flops 536870912 | bytes 2097152 | tf_op jit(solution)/shard_map/backward_cols/pallas_call | solution.py:190
  118.1 1.5 %collective-permute-start.26 = (f32[32,256]{1,0:T(8,128)S(1)}, f32[32,256]{1,0:T(8,128)S(1)}, u32[]{:S(2)}, u32[]{:S(2)}) collective-permute-start(f32[32,256]{1,0:T(8,128)S(1)} %add_add_fusion.refs_0_.refs_3_), channel_id=1, source_target_pairs={{0,24},{4,28},{8,16},{12,20},{16,8},{20,12},{24,0},{28,4},{1,25},{... | collective-permute-start | bytes 98312 | tf_op jit(solution)/shard_map/ppermute | solution.py:269
  119.6 2.8 %collective-permute-done.24.refs_1_ = f32[32,256]{1,0:T(8,128)S(1)} collective-permute-done((f32[32,256]{1,0:T(8,128)S(1)}, f32[32,256]{1,0:T(8,128)S(1)}, u32[]{:S(2)}, u32[]{:S(2)}) %collective-permute-start.24) | collective-permute-done | bytes 32800 | tf_op jit(solution)/shard_map/ppermute | solution.py:269
  126.4 5.9 %collective-permute-done.31.refs_2_ = bf16[256,512]{1,0:T(8,128)(2,1)S(1)} collective-permute-done((bf16[256,512]{1,0:T(8,128)(2,1)S(1)}, bf16[256,512]{1,0:T(8,128)(2,1)S(1)}, u32[]{:S(2)}, u32[]{:S(2)}) %collective-permute-start.31) | collective-permute-done | bytes 262176 | tf_op jit(solution)/shard_map/ppermute | solution.py:397
  (92 shorter events, 27.2 us)
Async XLA Ops:
  0.6 14.1 %collective-permute-start.1 = (bf16[512,256]{1,0:T(8,128)(2,1)}, bf16[512,256]{1,0:T(8,128)(2,1)S(1)}, u32[]{:S(2)}, u32[]{:S(2)}) collective-permute-start(bf16[512,256]{1,0:T(8,128)(2,1)} %refs_1_.1), channel_id=1, source_target_pairs={{0,8},{4,12},{8,0},{12,4},{16,24},{20,28},{24,16},{28,20},{1,9},{5... | collective-permute-start | bytes 786440 | tf_op jit(solution)/shard_map/ppermute | solution.py:269
  3.6 11.1 %collective-permute-start.3 = (bf16[512,256]{1,0:T(8,128)(2,1)}, bf16[512,256]{1,0:T(8,128)(2,1)S(1)}, u32[]{:S(2)}, u32[]{:S(2)}) collective-permute-start(bf16[512,256]{1,0:T(8,128)(2,1)} %refs_1_.1), channel_id=1, source_target_pairs={{0,16},{4,20},{8,24},{12,28},{16,0},{20,4},{24,8},{28,12},{1,17},{... | collective-permute-start | bytes 786440 | tf_op jit(solution)/shard_map/ppermute | solution.py:269
  14.8 6.4 %collective-permute-start.5 = (bf16[512,256]{1,0:T(8,128)(2,1)S(1)}, bf16[512,256]{1,0:T(8,128)(2,1)S(1)}, u32[]{:S(2)}, u32[]{:S(2)}) collective-permute-start(bf16[512,256]{1,0:T(8,128)(2,1)S(1)} %pick.1), channel_id=1, source_target_pairs={{0,16},{4,12},{8,24},{12,4},{16,0},{20,28},{24,8},{28,20},{1,17},{... | collective-permute-start | bytes 786440 | tf_op jit(solution)/shard_map/ppermute | solution.py:285
  15.9 12.2 %collective-permute-start = (bf16[512,256]{1,0:T(8,128)(2,1)S(1)}, bf16[512,256]{1,0:T(8,128)(2,1)S(1)}, u32[]{:S(2)}, u32[]{:S(2)}) collective-permute-start(bf16[512,256]{1,0:T(8,128)(2,1)S(1)} %copy-done.8), channel_id=1, source_target_pairs={{0,4},{4,0},{8,12},{12,8},{16,20},{20,16},{24,28},{28,24},{1,5},{5... | collective-permute-start | bytes 786440 | tf_op jit(solution)/shard_map/ppermute | solution.py:269
  15.9 12.2 %collective-permute-start.2 = (bf16[512,256]{1,0:T(8,128)(2,1)S(1)}, bf16[512,256]{1,0:T(8,128)(2,1)S(1)}, u32[]{:S(2)}, u32[]{:S(2)}) collective-permute-start(bf16[512,256]{1,0:T(8,128)(2,1)S(1)} %collective-permute-done.1.even_ref.refs_5_.refs_3_), channel_id=1, source_target_pairs={{0,4},{4,0},{8,12},{12,8},{16,20},{20,16},{24,28},{28,24},{1,5},{5... | collective-permute-start | bytes 786440 | tf_op jit(solution)/shard_map/ppermute | solution.py:269
  16.4 11.7 %collective-permute-start.4 = (bf16[512,256]{1,0:T(8,128)(2,1)S(1)}, bf16[512,256]{1,0:T(8,128)(2,1)S(1)}, u32[]{:S(2)}, u32[]{:S(2)}) collective-permute-start(bf16[512,256]{1,0:T(8,128)(2,1)S(1)} %collective-permute-done.3.odd_ref.refs_7_.refs_5_), channel_id=1, source_target_pairs={{0,4},{4,0},{8,12},{12,8},{16,20},{20,16},{24,28},{28,24},{1,5},{5... | collective-permute-start | bytes 786440 | tf_op jit(solution)/shard_map/ppermute | solution.py:269
  21.2 6.9 %collective-permute-start.6 = (bf16[512,256]{1,0:T(8,128)(2,1)S(1)}, bf16[512,256]{1,0:T(8,128)(2,1)S(1)}, u32[]{:S(2)}, u32[]{:S(2)}) collective-permute-start(bf16[512,256]{1,0:T(8,128)(2,1)S(1)} %collective-permute-done.5.refs_9_.refs_7_), channel_id=1, source_target_pairs={{0,4},{4,0},{8,12},{12,8},{16,20},{20,16},{24,28},{28,24},{1,5},{5... | collective-permute-start | bytes 786440 | tf_op jit(solution)/shard_map/ppermute | solution.py:269
  30.0 8.6 %collective-permute-start.10 = (bf16[512,256]{1,0:T(8,128)(2,1)S(1)}, bf16[512,256]{1,0:T(8,128)(2,1)S(1)}, u32[]{:S(2)}, u32[]{:S(2)}) collective-permute-start(bf16[512,256]{1,0:T(8,128)(2,1)S(1)} %forward_rows.3), channel_id=1, source_target_pairs={{3,2},{7,6},{11,10},{15,14},{19,18},{23,22},{27,26},{31,30}} | collective-permute-start | bytes 786440 | tf_op jit(solution)/shard_map/ppermute | solution.py:348
  30.8 9.9 %collective-permute-start.7 = (bf16[512,256]{1,0:T(8,128)(2,1)S(1)}, bf16[512,256]{1,0:T(8,128)(2,1)S(1)}, u32[]{:S(2)}, u32[]{:S(2)}) collective-permute-start(bf16[512,256]{1,0:T(8,128)(2,1)S(1)} %forward_rows.3), channel_id=1, source_target_pairs={{0,1},{4,5},{8,9},{12,13},{16,17},{20,21},{24,25},{28,29}} | collective-permute-start | bytes 786440 | tf_op jit(solution)/shard_map/ppermute | solution.py:347
  40.9 5.7 %collective-permute-start.11 = (bf16[512,256]{1,0:T(8,128)(2,1)S(1)}, bf16[512,256]{1,0:T(8,128)(2,1)S(1)}, u32[]{:S(2)}, u32[]{:S(2)}) collective-permute-start(bf16[512,256]{1,0:T(8,128)(2,1)S(1)} %get-tuple-element.40), channel_id=1, source_target_pairs={{2,1},{3,2},{6,5},{7,6},{10,9},{11,10},{14,13},{15,14},{18,17},{19... | collective-permute-start | bytes 786440 | tf_op jit(solution)/shard_map/ppermute | solution.py:348
  41.6 10.4 %collective-permute-start.8 = (bf16[512,256]{1,0:T(8,128)(2,1)S(1)}, bf16[512,256]{1,0:T(8,128)(2,1)S(1)}, u32[]{:S(2)}, u32[]{:S(2)}) collective-permute-start(bf16[512,256]{1,0:T(8,128)(2,1)S(1)} %get-tuple-element.41), channel_id=1, source_target_pairs={{0,1},{1,2},{4,5},{5,6},{8,9},{9,10},{12,13},{13,14},{16,17},{17,1... | collective-permute-start | bytes 786440 | tf_op jit(solution)/shard_map/ppermute | solution.py:347
  52.1 9.6 %collective-permute-start.12 = (bf16[512,256]{1,0:T(8,128)(2,1)S(1)}, bf16[512,256]{1,0:T(8,128)(2,1)S(1)}, u32[]{:S(2)}, u32[]{:S(2)}) collective-permute-start(bf16[512,256]{1,0:T(8,128)(2,1)S(1)} %get-tuple-element.44), channel_id=1, source_target_pairs={{1,0},{2,1},{3,2},{5,4},{6,5},{7,6},{9,8},{10,9},{11,10},{13,12},{... | collective-permute-start | bytes 786440 | tf_op jit(solution)/shard_map/ppermute | solution.py:348
  53.4 9.5 %collective-permute-start.9 = (bf16[512,256]{1,0:T(8,128)(2,1)S(1)}, bf16[512,256]{1,0:T(8,128)(2,1)S(1)}, u32[]{:S(2)}, u32[]{:S(2)}) collective-permute-start(bf16[512,256]{1,0:T(8,128)(2,1)S(1)} %get-tuple-element.45), channel_id=1, source_target_pairs={{0,1},{1,2},{2,3},{4,5},{5,6},{6,7},{8,9},{9,10},{10,11},{12,13},{... | collective-permute-start | bytes 786440 | tf_op jit(solution)/shard_map/ppermute | solution.py:347
  64.0 5.8 %collective-permute-start.15 = (f32[128,256]{1,0:T(8,128)S(1)}, f32[128,256]{1,0:T(8,128)S(1)}, u32[]{:S(2)}, u32[]{:S(2)}) collective-permute-start(f32[128,256]{1,0:T(8,128)S(1)} %constant_dynamic-slice_fusion.3), channel_id=1, source_target_pairs={{0,4},{4,0},{8,12},{12,8},{16,20},{20,16},{24,28},{28,24},{1,5},{5... | collective-permute-start | bytes 393224 | tf_op jit(solution)/shard_map/ppermute | solution.py:269
  64.1 10.6 %collective-permute-start.13 = (bf16[256,512]{1,0:T(8,128)(2,1)S(1)}, bf16[256,512]{1,0:T(8,128)(2,1)S(1)}, u32[]{:S(2)}, u32[]{:S(2)}) collective-permute-start(bf16[256,512]{1,0:T(8,128)(2,1)S(1)} %get-tuple-element.24.refs_5_), channel_id=1, source_target_pairs={{0,1},{1,2},{2,3},{4,5},{5,6},{6,7},{8,9},{9,10},{10,11},{12,13},{... | collective-permute-start | bytes 786440 | tf_op jit(solution)/shard_map/ppermute | solution.py:358
  68.5 10.6 %collective-permute-start.14 = (bf16[256,512]{1,0:T(8,128)(2,1)S(1)}, bf16[256,512]{1,0:T(8,128)(2,1)S(1)}, u32[]{:S(2)}, u32[]{:S(2)}) collective-permute-start(bf16[256,512]{1,0:T(8,128)(2,1)S(1)} %get-tuple-element.24.refs_5_), channel_id=1, source_target_pairs={{1,0},{2,1},{3,2},{5,4},{6,5},{7,6},{9,8},{10,9},{11,10},{13,12},{... | collective-permute-start | bytes 786440 | tf_op jit(solution)/shard_map/ppermute | solution.py:359
  79.1 8.2 %collective-permute-start.16 = (bf16[256,512]{1,0:T(8,128)(2,1)S(1)}, bf16[256,512]{1,0:T(8,128)(2,1)S(1)}, u32[]{:S(2)}, u32[]{:S(2)}) collective-permute-start(bf16[256,512]{1,0:T(8,128)(2,1)S(1)} %collective-permute-done.13), channel_id=1, source_target_pairs={{1,2},{2,3},{5,6},{6,7},{9,10},{10,11},{13,14},{14,15},{17,18},{18... | collective-permute-start | bytes 786440 | tf_op jit(solution)/shard_map/ppermute | solution.py:358
  79.8 12.2 %collective-permute-start.17 = (bf16[256,512]{1,0:T(8,128)(2,1)S(1)}, bf16[256,512]{1,0:T(8,128)(2,1)S(1)}, u32[]{:S(2)}, u32[]{:S(2)}) collective-permute-start(bf16[256,512]{1,0:T(8,128)(2,1)S(1)} %collective-permute-done.14), channel_id=1, source_target_pairs={{1,0},{2,1},{5,4},{6,5},{9,8},{10,9},{13,12},{14,13},{17,16},{18,1... | collective-permute-start | bytes 786440 | tf_op jit(solution)/shard_map/ppermute | solution.py:359
  81.1 4.3 %collective-permute-start.18 = (f32[32,256]{1,0:T(8,128)S(1)}, f32[32,256]{1,0:T(8,128)S(1)}, u32[]{:S(2)}, u32[]{:S(2)}) collective-permute-start(f32[32,256]{1,0:T(8,128)S(1)} %get-tuple-element.46), channel_id=1, source_target_pairs={{0,8},{4,12},{8,0},{12,4},{16,24},{20,28},{24,16},{28,20},{1,9},{5... | collective-permute-start | bytes 98312 | tf_op jit(solution)/shard_map/ppermute | solution.py:269
  81.5 4.1 %collective-permute-start.19 = (f32[32,256]{1,0:T(8,128)S(1)}, f32[32,256]{1,0:T(8,128)S(1)}, u32[]{:S(2)}, u32[]{:S(2)}) collective-permute-start(f32[32,256]{1,0:T(8,128)S(1)} %get-tuple-element.48), channel_id=1, source_target_pairs={{0,16},{4,20},{8,24},{12,28},{16,0},{20,4},{24,8},{28,12},{1,17},{... | collective-permute-start | bytes 98312 | tf_op jit(solution)/shard_map/ppermute | solution.py:269
  82.4 4.8 %collective-permute-start.20 = (f32[32,256]{1,0:T(8,128)S(1)}, f32[32,256]{1,0:T(8,128)S(1)}, u32[]{:S(2)}, u32[]{:S(2)}) collective-permute-start(f32[32,256]{1,0:T(8,128)S(1)} %get-tuple-element.47), channel_id=1, source_target_pairs={{0,24},{4,28},{8,16},{12,20},{16,8},{20,12},{24,0},{28,4},{1,25},{... | collective-permute-start | bytes 98312 | tf_op jit(solution)/shard_map/ppermute | solution.py:269
  92.0 18.2 %collective-permute-start.21 = (f32[32,256]{1,0:T(8,128)S(1)}, f32[32,256]{1,0:T(8,128)S(1)}, u32[]{:S(2)}, u32[]{:S(2)}) collective-permute-start(f32[32,256]{1,0:T(8,128)S(1)} %add_add_fusion.1), channel_id=1, source_target_pairs={{0,1},{1,0},{2,3},{3,2},{4,5},{5,4},{6,7},{7,6},{8,9},{9,8},{10,11... | collective-permute-start | bytes 98312 | tf_op jit(solution)/shard_map/ppermute | solution.py:269
  93.7 16.4 %collective-permute-start.22 = (f32[32,256]{1,0:T(8,128)S(1)}, f32[32,256]{1,0:T(8,128)S(1)}, u32[]{:S(2)}, u32[]{:S(2)}) collective-permute-start(f32[32,256]{1,0:T(8,128)S(1)} %add_add_fusion.1), channel_id=1, source_target_pairs={{0,2},{1,3},{2,0},{3,1},{4,6},{5,7},{6,4},{7,5},{8,10},{9,11},{10,... | collective-permute-start | bytes 98312 | tf_op jit(solution)/shard_map/ppermute | solution.py:269
  94.3 15.9 %collective-permute-start.23 = (f32[32,256]{1,0:T(8,128)S(1)}, f32[32,256]{1,0:T(8,128)S(1)}, u32[]{:S(2)}, u32[]{:S(2)}) collective-permute-start(f32[32,256]{1,0:T(8,128)S(1)} %add_add_fusion.1), channel_id=1, source_target_pairs={{0,3},{1,2},{2,1},{3,0},{4,7},{5,6},{6,5},{7,4},{8,11},{9,10},{10,... | collective-permute-start | bytes 98312 | tf_op jit(solution)/shard_map/ppermute | solution.py:269
  96.4 13.8 %collective-permute-start.27 = (bf16[256,512]{1,0:T(8,128)(2,1)S(1)}, bf16[256,512]{1,0:T(8,128)(2,1)S(1)}, u32[]{:S(2)}, u32[]{:S(2)}) collective-permute-start(bf16[256,512]{1,0:T(8,128)(2,1)S(1)} %collective-permute-done.16), channel_id=1, source_target_pairs={{2,3},{6,7},{10,11},{14,15},{18,19},{22,23},{26,27},{30,31}} | collective-permute-start | bytes 786440 | tf_op jit(solution)/shard_map/ppermute | solution.py:358
  97.0 13.2 %collective-permute-start.28 = (bf16[256,512]{1,0:T(8,128)(2,1)S(1)}, bf16[256,512]{1,0:T(8,128)(2,1)S(1)}, u32[]{:S(2)}, u32[]{:S(2)}) collective-permute-start(bf16[256,512]{1,0:T(8,128)(2,1)S(1)} %collective-permute-done.17), channel_id=1, source_target_pairs={{1,0},{5,4},{9,8},{13,12},{17,16},{21,20},{25,24},{29,28}} | collective-permute-start | bytes 786440 | tf_op jit(solution)/shard_map/ppermute | solution.py:359
  115.0 9.4 %collective-permute-start.32 = (bf16[256,512]{1,0:T(8,128)(2,1)S(1)}, bf16[256,512]{1,0:T(8,128)(2,1)S(1)}, u32[]{:S(2)}, u32[]{:S(2)}) collective-permute-start(bf16[256,512]{1,0:T(8,128)(2,1)S(1)} %get-tuple-element.37), channel_id=1, source_target_pairs={{0,8},{4,20},{8,0},{12,28},{16,24},{20,4},{24,16},{28,12},{1,9},{5... | collective-permute-start | bytes 786440 | tf_op jit(solution)/shard_map/ppermute | solution.py:396
  116.1 6.3 %collective-permute-start.24 = (f32[32,256]{1,0:T(8,128)S(1)}, f32[32,256]{1,0:T(8,128)S(1)}, u32[]{:S(2)}, u32[]{:S(2)}) collective-permute-start(f32[32,256]{1,0:T(8,128)S(1)} %add_add_fusion.refs_0_.refs_3_), channel_id=1, source_target_pairs={{0,8},{4,12},{8,0},{12,4},{16,24},{20,28},{24,16},{28,20},{1,9},{5... | collective-permute-start | bytes 98312 | tf_op jit(solution)/shard_map/ppermute | solution.py:269
  117.1 5.3 %collective-permute-start.25 = (f32[32,256]{1,0:T(8,128)S(1)}, f32[32,256]{1,0:T(8,128)S(1)}, u32[]{:S(2)}, u32[]{:S(2)}) collective-permute-start(f32[32,256]{1,0:T(8,128)S(1)} %add_add_fusion.refs_0_.refs_3_), channel_id=1, source_target_pairs={{0,16},{4,20},{8,24},{12,28},{16,0},{20,4},{24,8},{28,12},{1,17},{... | collective-permute-start | bytes 98312 | tf_op jit(solution)/shard_map/ppermute | solution.py:269
  118.1 5.1 %collective-permute-start.26 = (f32[32,256]{1,0:T(8,128)S(1)}, f32[32,256]{1,0:T(8,128)S(1)}, u32[]{:S(2)}, u32[]{:S(2)}) collective-permute-start(f32[32,256]{1,0:T(8,128)S(1)} %add_add_fusion.refs_0_.refs_3_), channel_id=1, source_target_pairs={{0,24},{4,28},{8,16},{12,20},{16,8},{20,12},{24,0},{28,4},{1,25},{... | collective-permute-start | bytes 98312 | tf_op jit(solution)/shard_map/ppermute | solution.py:269
  123.3 9.0 %collective-permute-start.31 = (bf16[256,512]{1,0:T(8,128)(2,1)S(1)}, bf16[256,512]{1,0:T(8,128)(2,1)S(1)}, u32[]{:S(2)}, u32[]{:S(2)}) collective-permute-start(bf16[256,512]{1,0:T(8,128)(2,1)S(1)} %get-tuple-element.38), channel_id=1, source_target_pairs={{0,8},{4,20},{8,0},{12,28},{16,24},{20,4},{24,16},{28,12},{1,9},{5... | collective-permute-start | bytes 786440 | tf_op jit(solution)/shard_map/ppermute | solution.py:397
  124.5 7.8 %collective-permute-start.33 = (bf16[256,512]{1,0:T(8,128)(2,1)S(1)}, bf16[256,512]{1,0:T(8,128)(2,1)S(1)}, u32[]{:S(2)}, u32[]{:S(2)}) collective-permute-start(bf16[256,512]{1,0:T(8,128)(2,1)S(1)} %fusion.3), channel_id=1, source_target_pairs={{0,16},{4,12},{8,24},{12,4},{16,0},{20,28},{24,8},{28,20},{1,17},{... | collective-permute-start | bytes 786440 | tf_op jit(solution)/shard_map/ppermute | solution.py:404
  (15 other events, 143.4 us)

commit v3 on v2

v3 whole, which is shorter than its diff:
```python
import functools
import math

import jax
import jax.numpy as jnp
from jax import lax
from jax.experimental import pallas as pl
from jax.experimental.pallas import tpu as pltpu
from jax.sharding import PartitionSpec as P


MIB = 1024 * 1024
SCALARS = pl.BlockSpec(memory_space=pltpu.SMEM)
WHOLE = pl.BlockSpec(memory_space=pltpu.VMEM)
UNREAD = pl.BlockSpec(memory_space=pl.ANY)


def params(mib):
    return pltpu.CompilerParams(vmem_limit_bytes=mib * MIB)


def cost(flops, moved, exps=0):
    return pl.CostEstimate(flops=flops, bytes_accessed=moved, transcendentals=exps)


def near(value):
    return pltpu.with_memory_space_constraint(value, pltpu.VMEM)


def dense_kernel(where, counts, cols, adj_ref, *refs, steps, window):
    outs, (held, total, sems) = refs[: len(steps)], refs[len(steps) :]
    slots, tile, _ = adj_ref.shape
    per = outs[0].shape[0] // tile
    width = outs[0].shape[1]

    plans = []
    for i, step in enumerate(steps):
        first = (where[1] ^ step) * per
        start = lax.fori_loop(0, first, lambda t, s: s + counts[t], jnp.int32(0))
        for u in range(per):
            count = counts[first + u]
            base = jnp.minimum(start, slots - window)
            fetch = pltpu.make_async_copy(
                adj_ref.at[pl.ds(base, window)], held.at[i * per + u], sems.at[i * per + u]
            )
            fetch.start()
            plans.append((start, start - base, count, fetch))
            start = start + count

    for i, out_ref in enumerate(outs):
        out_ref[...] = jnp.zeros_like(out_ref)
    for n, (start, shift, count, fetch) in enumerate(plans):
        out_ref = outs[n // per]
        rows = pl.ds((n % per) * tile, tile)
        fetch.wait()

        def place(j):
            c = cols[start + j]
            out_ref[rows, pl.ds(pl.multiple_of(c * tile, tile), tile)] = held[n, shift + j]
            return lax.shift_left(jnp.int32(1), c)

        def four(i, state):
            seen, twice = state
            for v in range(4):
                bit = place(4 * i + v)
                twice = twice | (seen & bit)
                seen = seen | bit
            return seen, twice

        def one(j, state):
            seen, twice = state
            bit = place(j)
            return seen | bit, twice | (seen & bit)

        groups = lax.div(count, 4)
        state = lax.fori_loop(0, groups, four, (jnp.int32(0), jnp.int32(0)))
        seen, twice = lax.fori_loop(4 * groups, count, one, state)
        repeated = (twice != 0) if width // tile <= 32 else (count > 0)

        @pl.when(repeated)
        def _():
            total[...] = jnp.zeros_like(total)

            def add(j, carry):
                here = pl.ds(pl.multiple_of(cols[start + j] * tile, tile), tile)
                total[:, here] += held[n, shift + j].astype(jnp.float32)
                return carry

            lax.fori_loop(0, count, add, 0)
            out_ref[rows, :] = total[...].astype(out_ref.dtype)


def dense_rows(where, steps, counts, cols, adj, rows, col_tiles):
    slots, tile, _ = adj.shape
    window = min(col_tiles, slots)
    width = col_tiles * tile
    tiles = rows // tile * len(steps)
    return pl.pallas_call(
        functools.partial(dense_kernel, steps=steps, window=window),
        out_shape=[pltpu.VMEM((rows, width), adj.dtype) for _ in steps],
        in_specs=[SCALARS, SCALARS, SCALARS, pl.BlockSpec(memory_space=pltpu.HBM)],
        out_specs=[WHOLE] * len(steps),
        scratch_shapes=[
            pltpu.VMEM((tiles, window, tile, tile), adj.dtype),
            pltpu.VMEM((tile, width), jnp.float32),
            pltpu.SemaphoreType.DMA((tiles,)),
        ],
        compiler_params=params(16),
        cost_estimate=cost(0, 5 * len(steps) * rows * width),
        name="dense_rows",
    )(where, counts, cols, pltpu.with_memory_space_constraint(adj, pltpu.HBM))


def forward_kernel(where, *refs, blocks, count, odd, before):
    dense, shards, sums = refs[:blocks], refs[blocks : blocks + count], refs[blocks + count :]
    depth = shards[0].shape[0]
    for i, a_ref in enumerate(dense):
        value = sums[i][...] if before else None
        for k, shard in enumerate(shards):
            cols = pl.ds(pl.multiple_of((where[0] ^ (2 * k + odd)) * depth, depth), depth)
            part = jnp.dot(a_ref[:, cols], shard[...], preferred_element_type=jnp.float32)
            value = part if value is None else value + part
        out_ref = sums[blocks + i if before else i]
        out_ref[...] = value.astype(out_ref.dtype)


def forward(where, dense, shards, odd, before, kind):
    rows, width = dense[0].shape[0], shards[0].shape[1]
    blocks, count = len(dense), len(shards)
    operands = [near(x) for x in [*dense, *shards, *before]]
    return pl.pallas_call(
        functools.partial(forward_kernel, blocks=blocks, count=count, odd=odd, before=bool(before)),
        out_shape=[pltpu.VMEM((rows, width), kind)] * blocks,
        in_specs=[SCALARS] + [WHOLE] * len(operands),
        out_specs=[WHOLE] * blocks,
        compiler_params=params(10),
        cost_estimate=cost(blocks * dense[0].size * width, blocks * dense[0].size),
        name="forward_rows",
    )(where, *operands)


def middle_kernel(*refs, scale, came):
    parts = refs[: came + 1]
    weight_ref, up_ref, hidden_ref, grad_ref, wgrad_ref = refs[came + 1 :]
    agg = parts[0][...].astype(jnp.float32)
    for part in parts[1:]:
        agg = agg + part[...].astype(jnp.float32)
    agg = agg.astype(jnp.bfloat16)
    weight = weight_ref[...]
    pre = jnp.dot(agg, weight, preferred_element_type=jnp.float32)
    sig = jax.nn.sigmoid(pre)
    hidden_ref[...] = (pre * sig).astype(jnp.bfloat16)
    pre_grad = (up_ref[...].astype(jnp.float32) * sig * (1.0 + pre * (1.0 - sig))).astype(jnp.bfloat16)
    grad_ref[...] = lax.dot_general(
        weight, pre_grad, (((1,), (1,)), ((), ())), preferred_element_type=jnp.float32
    ).astype(jnp.bfloat16)
    wgrad_ref[...] = scale * lax.dot_general(
        agg, pre_grad, (((0,), (0,)), ((), ())), preferred_element_type=jnp.float32
    )


def middle(parts, weight, upstream, scale):
    rows, width = upstream.shape
    return pl.pallas_call(
        functools.partial(middle_kernel, scale=scale, came=len(parts) - 1),
        out_shape=(
            jax.ShapeDtypeStruct((rows, width), jnp.bfloat16),
            jax.ShapeDtypeStruct((width, rows), jnp.bfloat16),
            jax.ShapeDtypeStruct((width, width), jnp.float32),
        ),
        compiler_params=params(16),
        cost_estimate=cost(6 * rows * width * width, 10 * rows * width, rows * width),
        name="middle",
    )(*parts, weight, upstream)


def backward_kernel(where, *refs, count, first, before, n_row):
    dense, pieces = refs[:count], refs[count : 2 * count]
    out_ref = refs[-1]
    columns, _, depth = out_ref.shape
    half = n_row // 2

    def one(j, carry):
        at = first + j
        step = 2 * lax.rem(at, half) + (at < half).astype(jnp.int32)
        cols = pl.ds(pl.multiple_of((where[0] ^ step) * depth, depth), depth)
        value = refs[2 * count][at] if before else None
        for a_ref, piece in zip(dense, pieces):
            part = jnp.dot(piece[...], a_ref[:, cols], preferred_element_type=jnp.float32)
            value = part if value is None else value + part
        out_ref[j] = value.astype(out_ref.dtype)
        return carry

    lax.fori_loop(0, columns, one, 0)


def backward(where, dense, pieces, first, columns, n_row, depth, before, kind, after=()):
    count = len(pieces)
    width, rows = pieces[0].shape
    operands = [near(x) for x in [*dense, *pieces] + ([] if before is None else [before])]
    return pl.pallas_call(
        functools.partial(
            backward_kernel, count=count, first=first, before=before is not None, n_row=n_row
        ),
        out_shape=pltpu.VMEM((columns, width, depth), kind),
        in_specs=[SCALARS] + [WHOLE] * len(operands) + [UNREAD] * len(after),
        out_specs=WHOLE,
        compiler_params=params(10),
        cost_estimate=cost(0, 0),
        name="backward_cols",
    )(where, *operands, *after)


def finish_kernel(*refs):
    parts, out_ref = refs[:-1], refs[-1]
    value = parts[0][0].astype(jnp.float32) + parts[1][0].astype(jnp.float32)
    for part in parts[2:]:
        value = value + part[...].astype(jnp.float32)
    out_ref[...] = value.T.astype(out_ref.dtype)


def finish(kept, came, parts):
    _, width, rows = kept.shape
    own = pl.BlockSpec((1, width, rows), lambda i: (0, 0, 0))
    part = pl.BlockSpec((width, rows), lambda i: (0, 0))
    return pl.pallas_call(
        finish_kernel,
        out_shape=jax.ShapeDtypeStruct((rows, width), jnp.bfloat16),
        grid=(1,),
        in_specs=[own, own] + [part] * len(parts),
        out_specs=pl.BlockSpec((rows, width), lambda i: (0, 0)),
        compiler_params=params(12),
        cost_estimate=cost(len(parts) * rows * width, 4 * len(parts) * rows * width),
        name="finish",
    )(kept, came, *parts)


def gate(values, after):
    count = len(values)
    return pl.pallas_call(
        lambda *refs: None,
        out_shape=[pltpu.VMEM(x.shape, x.dtype) for x in values],
        in_specs=[WHOLE] * count + [UNREAD] * len(after),
        out_specs=[WHOLE] * count,
        input_output_aliases={i: i for i in range(count)},
        compiler_params=params(4),
        cost_estimate=cost(0, 0),
        name="gate",
    )(*map(near, values), *after)


def split_kernel(where, *refs, by_core):
    outs = refs[1:] if by_core else refs[2:]
    rows = outs[0].shape[0]
    place = where[0] & 1 if by_core else lax.div(where[0], 2)
    for step, out_ref in enumerate(outs):
        at = pl.ds(pl.multiple_of((place ^ step) * rows, rows), rows)
        out_ref[...] = refs[0][at, :] if by_core else refs[0][at, :] + refs[1][at, :]


def split(where, values, count, by_core):
    rows, width = values[0].shape
    return pl.pallas_call(
        functools.partial(split_kernel, by_core=by_core),
        out_shape=[jax.ShapeDtypeStruct((rows // count, width), values[0].dtype)] * count,
        in_specs=[SCALARS] + [WHOLE] * len(values),
        compiler_params=params(10),
        cost_estimate=cost(0, 0),
        name="split",
    )(where, *values)


def join_kernel(where, *refs, by_core):
    parts, out_ref = refs[:-1], refs[-1]
    rows = parts[0].shape[0]
    place = where[0] & 1 if by_core else lax.div(where[0], 2)
    for step, part in enumerate(parts):
        out_ref[pl.ds(pl.multiple_of((place ^ step) * rows, rows), rows), :] = part[...]


def join(where, parts, by_core):
    count, (rows, width) = len(parts), parts[0].shape
    return pl.pallas_call(
        functools.partial(join_kernel, by_core=by_core),
        out_shape=jax.ShapeDtypeStruct((count * rows, width), parts[0].dtype),
        in_specs=[SCALARS] + [WHOLE] * count,
        compiler_params=params(10),
        cost_estimate=cost(0, 0),
        name="join",
    )(where, *parts)


def swap(value, axis, size, step):
    return lax.ppermute(value, axis, [(i, i ^ step) for i in range(size)])


def shards(adj_tiles, tile_counts, tile_cols, features, weight, upstream):
    n_row, n_col = lax.axis_size("row"), lax.axis_size("col")
    assert n_row & (n_row - 1) == 0 and n_col & (n_col - 1) == 0 and n_row > 1
    adj, counts, cols = adj_tiles[0, 0], tile_counts[0, 0], tile_cols[0, 0]
    rows, depth = upstream.shape[0], features.shape[0]
    col_tiles = depth * n_row // adj.shape[1]
    chips = n_row // 2
    where = jnp.stack([lax.axis_index("row"), lax.axis_index("col")]).astype(jnp.int32)
    steps = [*range(n_col - 1, 0, -1), 0]

    dense = {}
    for i in range(0, n_col, 2):
        group = steps[i : i + 2]
        dense.update(zip(group, dense_rows(where, group, counts, cols, adj, rows, col_tiles)))
    blocks = [dense[s] for s in steps]

    away = gate([swap(features, "row", n_row, 2 * s) for s in range(chips - 1, 0, -1)], blocks)
    even = [features, *away[::-1]]
    odd = [swap(shard, "row", n_row, 1) for shard in even]
    halves = forward(where, blocks, even, 0, [], jnp.float32)

    came = []
    for s, block, half in zip(steps[:-1], blocks, halves):
        share = forward(where, [block], odd, 1, [half], jnp.bfloat16)[0]
        came.append(swap(share, "col", n_col, s))
    own = forward(where, blocks[-1:], odd, 1, halves[-1:], jnp.float32)
    scale = 1.0 / math.sqrt(rows * n_row * n_col)
    hidden, piece, part = middle([*own, *came], weight, upstream, scale)

    pieces = {s: swap(piece, "col", n_col, s) for s in steps[:-1]}
    pieces[0] = piece
    kept, sent = split(where, [part], 2, True)
    part, *others = split(where, [kept, swap(sent, "row", n_row, 1)], chips, False)

    soon, late = [0, 1], steps[:-2]
    early = backward(
        where, [dense[s] for s in soon], [pieces[s] for s in soon], 0, n_row, n_row, depth, None, jnp.float32
    )
    last = functools.partial(backward, where, [dense[s] for s in late], [pieces[s] for s in late])
    sent = last(0, chips, n_row, depth, early, jnp.bfloat16, [part])
    kept = last(chips, chips, n_row, depth, early, jnp.float32)
    came = swap(sent, "row", n_row, 1)
    summed = [(kept[s] + came[s].astype(jnp.float32)).astype(jnp.bfloat16) for s in range(1, chips)]
    parts = [swap(summed[s - 1], "row", n_row, 2 * s) for s in range(chips - 1, 0, -1)]

    others = gate([swap(other, "row", n_row, 2 * s) for s, other in enumerate(others, 1)], [kept])
    part = sum(others, part)
    part = sum([swap(part, "col", n_col, s) for s in range(1, n_col)], part)
    half = join(where, [part] + [swap(part, "row", n_row, 2 * s) for s in range(1, chips)], False)
    weight_grad = join(where, [half, swap(half, "row", n_row, 1)], True)
    return hidden, weight_grad, finish(kept, came, parts)


def solution(mesh):
    placed = (
        P("row", "col", None, None, None),
        P("row", "col", None),
        P("row", "col", None),
        P(("col", "row"), None),
        P(),
        P(("row", "col"), None),
    )
    return jax.shard_map(
        shards,
        mesh=mesh,
        in_specs=placed,
        out_specs=(P(("row", "col"), None), P(), P(("col", "row"), None)),
        check_vma=False,
    )
```

time: 133 us -> 109 us (0.82)
  starting transfers between devices: 47 us -> 30.8 us
  local copies, waits for them, and re-layouts: 8.44 us -> 1.78 us
  other arithmetic: 2.29 us -> 0.37 us
    ppermute x34 -> x28, starting transfers between devices: 47 us -> 30.8 us  [swap(): return lax.ppermute(value, axis, [(i, i ^ step) for i in range(size)])]
    unnamed x26 -> x10, local copies, waits for them, and re-layouts: 8.39 us -> 1.78 us
    ppermute x34 -> x28, waiting for transfers between devices: 43.5 us -> 43.9 us  [swap(): return lax.ppermute(value, axis, [(i, i ^ step) for i in range(size)])]
    pallas_call x12 -> x16, Pallas kernels: 28.8 us -> 29 us  [the longest x2 9.38 us: dense_rows(): pl.pallas_call(functools.partial(dense_kernel, steps=steps, window=window...]
  transfers between devices with their start and end apart: 34 -> 28, of which waited for: 15 -> 11; matrix products, arithmetic and copies ran while one was open for 1% -> 0% of each run, Pallas kernels for 19% -> 23%
where the time goes in v3:
time: 109 us
  waiting for transfers between devices  43.9 us (40%)
  Pallas kernels  30.9 us (28%)
  starting transfers between devices  30.8 us (28%)
  local copies, waits for them, and re-layouts  1.78 us (2%)
    ppermute x28, waiting for transfers between devices, swap(): return lax.ppermute(value, axis, [(i, i ^ step) for i in range(size)])  43.9 us
    ppermute x28, starting transfers between devices, swap(): return lax.ppermute(value, axis, [(i, i ^ step) for i in range(size)])  30.8 us
    pallas_call x2, Pallas kernels, dense_rows(): pl.pallas_call(functools.partial(dense_kernel, steps=steps, window=window...  9.38 us
    pallas_call x3, Pallas kernels, backward(): pl.pallas_call(functools.partial(backward_kernel, count=count, first=firs...  8.67 us
    pallas_call x5, Pallas kernels, forward(): pl.pallas_call(functools.partial(forward_kernel, blocks=blocks, count=cou...  7.96 us
  transfers between devices with their start and end apart: 28, of which 11 were waited for; matrix products, arithmetic and copies ran while one was open for 0% of the time, Pallas kernels for 23%

profile of v3, /device:TPU:0, one launch (start us, length us, event | category | flops | bytes accessed | tf_op | source)
XLA Modules:
  0.0 108.6 jit_solution(2729362164813469697)
XLA Ops:
  0.6 3.0 %collective-permute-start.2 = (bf16[512,256]{1,0:T(8,128)(2,1)}, bf16[512,256]{1,0:T(8,128)(2,1)S(1)}, u32[]{:S(2)}, u32[]{:S(2)}) collective-permute-start(bf16[512,256]{1,0:T(8,128)(2,1)} %refs_4_.2), channel_id=1, source_target_pairs={{0,16},{4,20},{8,24},{12,28},{16,0},{20,4},{24,8},{28,12},{1,17},{... | collective-permute-start | bytes 786440 | tf_op jit(solution)/shard_map/ppermute | solution.py:294
  3.7 1.4 %collective-permute-start.1 = (bf16[512,256]{1,0:T(8,128)(2,1)}, bf16[512,256]{1,0:T(8,128)(2,1)S(1)}, u32[]{:S(2)}, u32[]{:S(2)}) collective-permute-start(bf16[512,256]{1,0:T(8,128)(2,1)} %refs_4_.2), channel_id=1, source_target_pairs={{0,24},{4,28},{8,16},{12,20},{16,8},{20,12},{24,0},{28,4},{1,25},{... | collective-permute-start | bytes 786440 | tf_op jit(solution)/shard_map/ppermute | solution.py:294
  6.6 4.8 %dense_rows.3 = (bf16[512,4096]{1,0:T(8,128)(2,1)S(1)}, bf16[512,4096]{1,0:T(8,128)(2,1)S(1)}) custom-call(s32[2]{0:T(128)S(1)} %pad_add_fusion.where, s32[16]{0:T(128)S(1)} %bitcast.13, s32[448]{0:T(512)S(1)} %bitcast.11, bf16[448,128,128]{2,1,0:T(8,128)(2,1)} %bitcast.15), custom_call_target="tpu_custom_call" | custom-call | bytes 20971520 | tf_op jit(solution)/shard_map/dense_rows/pallas_call | solution.py:98
  11.5 4.5 %dense_rows.2 = (bf16[512,4096]{1,0:T(8,128)(2,1)S(1)}, bf16[512,4096]{1,0:T(8,128)(2,1)S(1)}) custom-call(s32[2]{0:T(128)S(1)} %pad_add_fusion.where, s32[16]{0:T(128)S(1)} %bitcast.14, s32[448]{0:T(512)S(1)} %bitcast.12, bf16[448,128,128]{2,1,0:T(8,128)(2,1)} %bitcast.16), custom_call_target="tpu_custom_call" | custom-call | bytes 20971520 | tf_op jit(solution)/shard_map/dense_rows/pallas_call | solution.py:98
  18.1 2.9 %forward_rows.5 = (f32[512,256]{1,0:T(8,128)S(1)}, f32[512,256]{1,0:T(8,128)S(1)}, f32[512,256]{1,0:T(8,128)S(1)}, f32[512,256]{1,0:T(8,128)S(1)}) custom-call(s32[2]{0:T(128)S(1)} %pad_add_fusion.where, bf16[512,4096]{1,0:T(8,128)(2,1)S(1)} %get-tuple-element.27.refs_3_.refs_0_, bf16[512,4096]{1,0:T(8,128)(2,1)S(1)} %get-tuple-element.28.refs_4_.refs_1_.refs_0_, ...), custom_call_target="tpu_custom_call" | custom-call | flops 2147483648 | bytes 8388608 | tf_op jit(solution)/shard_map/forward_rows/pallas_call | solution.py:131
  21.0 1.3 %forward_rows.7 = bf16[512,256]{1,0:T(8,128)(2,1)S(1)} custom-call(s32[2]{0:T(128)S(1)} %pad_add_fusion.where, bf16[512,4096]{1,0:T(8,128)(2,1)S(1)} %get-tuple-element.27.refs_3_.refs_0_, bf16[512,256]{1,0:T(8,128)(2,1)S(1)} %collective-permute-done.refs_1_, bf16[512,256]{1,0:T(8,128)(2,1)S(1)} %collective-permute-done.4.refs_2_, ...), custom_call_target="tpu_custom_call" | custom-call | flops 536870912 | bytes 2097152 | tf_op jit(solution)/shard_map/forward_rows/pallas_call | solution.py:131
  22.3 3.8 %collective-permute-start.7 = (bf16[512,256]{1,0:T(8,128)(2,1)S(1)}, bf16[512,256]{1,0:T(8,128)(2,1)S(1)}, u32[]{:S(2)}, u32[]{:S(2)}) collective-permute-start(bf16[512,256]{1,0:T(8,128)(2,1)S(1)} %forward_rows.7), channel_id=1, source_target_pairs={{0,3},{1,2},{2,1},{3,0},{4,7},{5,6},{6,5},{7,4},{8,11},{9,10},{10,... | collective-permute-start | bytes 786440 | tf_op jit(solution)/shard_map/ppermute | solution.py:294
  26.1 1.3 %forward_rows.8 = bf16[512,256]{1,0:T(8,128)(2,1)S(1)} custom-call(s32[2]{0:T(128)S(1)} %pad_add_fusion.where, bf16[512,4096]{1,0:T(8,128)(2,1)S(1)} %get-tuple-element.28.refs_4_.refs_1_.refs_0_, bf16[512,256]{1,0:T(8,128)(2,1)S(1)} %collective-permute-done.refs_1_, bf16[512,256]{1,0:T(8,128)(2,1)S(1)} %collective-permute-done.4.refs_2_, ...), custom_call_target="tpu_custom_call" | custom-call | flops 536870912 | bytes 2097152 | tf_op jit(solution)/shard_map/forward_rows/pallas_call | solution.py:131
  27.4 1.3 %forward_rows.9 = bf16[512,256]{1,0:T(8,128)(2,1)S(1)} custom-call(s32[2]{0:T(128)S(1)} %pad_add_fusion.where, bf16[512,4096]{1,0:T(8,128)(2,1)S(1)} %get-tuple-element.29.refs_5_.refs_2_.refs_0_.refs_1_, bf16[512,256]{1,0:T(8,128)(2,1)S(1)} %collective-permute-done.refs_1_, bf16[512,256]{1,0:T(8,128)(2,1)S(1)} %collective-permute-done.4.refs_2_, ...), custom_call_target="tpu_custom_call" | custom-call | flops 536870912 | bytes 2097152 | tf_op jit(solution)/shard_map/forward_rows/pallas_call | solution.py:131
  29.4 1.3 %forward_rows.6.refs_0_ = f32[512,256]{1,0:T(8,128)S(1)} custom-call(s32[2]{0:T(128)S(1)} %pad_add_fusion.where, bf16[512,4096]{1,0:T(8,128)(2,1)S(1)} %get-tuple-element.26.refs_6_.refs_3_.refs_0_, bf16[512,256]{1,0:T(8,128)(2,1)S(1)} %collective-permute-done.refs_1_, bf16[512,256]{1,0:T(8,128)(2,1)S(1)} %collective-permute-done.4.refs_2_, ...), custom_call_target="tpu_custom_call" | custom-call | flops 536870912 | bytes 2097152 | tf_op jit(solution)/shard_map/forward_rows/pallas_call | solution.py:131
  30.7 2.7 %collective-permute-done.7.refs_1_ = bf16[512,256]{1,0:T(8,128)(2,1)S(1)} collective-permute-done((bf16[512,256]{1,0:T(8,128)(2,1)S(1)}, bf16[512,256]{1,0:T(8,128)(2,1)S(1)}, u32[]{:S(2)}, u32[]{:S(2)}) %collective-permute-start.7) | collective-permute-done | bytes 262176 | tf_op jit(solution)/shard_map/ppermute | solution.py:294
  33.4 15.2 %collective-permute-done.8.refs_2_ = bf16[512,256]{1,0:T(8,128)(2,1)S(1)} collective-permute-done((bf16[512,256]{1,0:T(8,128)(2,1)S(1)}, bf16[512,256]{1,0:T(8,128)(2,1)S(1)}, u32[]{:S(2)}, u32[]{:S(2)}) %collective-permute-start.8) | collective-permute-done | bytes 262176 | tf_op jit(solution)/shard_map/ppermute | solution.py:294
  49.7 3.0 %collective-permute-start.15 = (bf16[256,512]{1,0:T(8,128)(2,1)S(1)}, bf16[256,512]{1,0:T(8,128)(2,1)S(1)}, u32[]{:S(2)}, u32[]{:S(2)}) collective-permute-start(bf16[256,512]{1,0:T(8,128)(2,1)S(1)} %get-tuple-element.45.refs_2_), channel_id=1, source_target_pairs={{0,2},{1,3},{2,0},{3,1},{4,6},{5,7},{6,4},{7,5},{8,10},{9,11},{10,... | collective-permute-start | bytes 786440 | tf_op jit(solution)/shard_map/ppermute | solution.py:294
  52.7 1.3 %collective-permute-start.14 = (bf16[256,512]{1,0:T(8,128)(2,1)S(1)}, bf16[256,512]{1,0:T(8,128)(2,1)S(1)}, u32[]{:S(2)}, u32[]{:S(2)}) collective-permute-start(bf16[256,512]{1,0:T(8,128)(2,1)S(1)} %get-tuple-element.45.refs_2_), channel_id=1, source_target_pairs={{0,3},{1,2},{2,1},{3,0},{4,7},{5,6},{6,5},{7,4},{8,11},{9,10},{10,... | collective-permute-start | bytes 786440 | tf_op jit(solution)/shard_map/ppermute | solution.py:294
  54.7 1.3 %collective-permute-done.10.refs_1_ = f32[128,256]{1,0:T(8,128)S(1)} collective-permute-done((f32[128,256]{1,0:T(8,128)S(1)}, f32[128,256]{1,0:T(8,128)S(1)}, u32[]{:S(2)}, u32[]{:S(2)}) %collective-permute-start.10) | collective-permute-done | bytes 131104 | tf_op jit(solution)/shard_map/ppermute | solution.py:294
  56.6 5.1 %collective-permute-done.16.refs_3_ = bf16[256,512]{1,0:T(8,128)(2,1)S(1)} collective-permute-done((bf16[256,512]{1,0:T(8,128)(2,1)S(1)}, bf16[256,512]{1,0:T(8,128)(2,1)S(1)}, u32[]{:S(2)}, u32[]{:S(2)}) %collective-permute-start.16) | collective-permute-done | bytes 262176 | tf_op jit(solution)/shard_map/ppermute | solution.py:294
  61.8 4.1 %backward_cols.3.refs_4_ = f32[8,256,512]{2,1,0:T(8,128)S(1)} custom-call(s32[2]{0:T(128)S(1)} %pad_add_fusion.where, bf16[512,4096]{1,0:T(8,128)(2,1)S(1)} %get-tuple-element.26.refs_6_.refs_3_.refs_0_, bf16[512,4096]{1,0:T(8,128)(2,1)S(1)} %get-tuple-element.29.refs_5_.refs_2_.refs_0_.refs_1_, bf16[256,512]{1,0:T(8,128)(2,1)S(1)} %get-tuple-element.45.refs_2_, ...), custom_call_target="tpu_custom_call" | custom-call | tf_op jit(solution)/shard_map/backward_cols/pallas_call | solution.py:201
  65.8 5.4 %collective-permute-done.15.refs_3_ = bf16[256,512]{1,0:T(8,128)(2,1)S(1)} collective-permute-done((bf16[256,512]{1,0:T(8,128)(2,1)S(1)}, bf16[256,512]{1,0:T(8,128)(2,1)S(1)}, u32[]{:S(2)}, u32[]{:S(2)}) %collective-permute-start.15) | collective-permute-done | bytes 262176 | tf_op jit(solution)/shard_map/ppermute | solution.py:294
  71.2 2.3 %backward_cols.5 = bf16[4,256,512]{2,1,0:T(8,128)(2,1)S(1)} custom-call(s32[2]{0:T(128)S(1)} %pad_add_fusion.where, bf16[512,4096]{1,0:T(8,128)(2,1)S(1)} %get-tuple-element.27.refs_3_.refs_0_, bf16[512,4096]{1,0:T(8,128)(2,1)S(1)} %get-tuple-element.28.refs_4_.refs_1_.refs_0_, bf16[256,512]{1,0:T(8,128)(2,1)S(1)} %collective-permute-done.14.refs_2_, ...), custom_call_target="tpu_custom_call" | custom-call | tf_op jit(solution)/shard_map/backward_cols/pallas_call | solution.py:201
  73.6 1.6 %collective-permute-start.11 = (f32[32,256]{1,0:T(8,128)S(1)}, f32[32,256]{1,0:T(8,128)S(1)}, u32[]{:S(2)}, u32[]{:S(2)}) collective-permute-start(f32[32,256]{1,0:T(8,128)S(1)} %get-tuple-element.42), channel_id=1, source_target_pairs={{0,8},{4,12},{8,0},{12,4},{16,24},{20,28},{24,16},{28,20},{1,9},{5... | collective-permute-start | bytes 98312 | tf_op jit(solution)/shard_map/ppermute | solution.py:294
  75.1 1.5 %collective-permute-start.12 = (f32[32,256]{1,0:T(8,128)S(1)}, f32[32,256]{1,0:T(8,128)S(1)}, u32[]{:S(2)}, u32[]{:S(2)}) collective-permute-start(f32[32,256]{1,0:T(8,128)S(1)} %get-tuple-element.43), channel_id=1, source_target_pairs={{0,16},{4,20},{8,24},{12,28},{16,0},{20,4},{24,8},{28,12},{1,17},{... | collective-permute-start | bytes 98312 | tf_op jit(solution)/shard_map/ppermute | solution.py:294
  77.1 2.3 %backward_cols.4.refs_3_.refs_0_ = f32[4,256,512]{2,1,0:T(8,128)S(1)} custom-call(s32[2]{0:T(128)S(1)} %pad_add_fusion.where, bf16[512,4096]{1,0:T(8,128)(2,1)S(1)} %get-tuple-element.27.refs_3_.refs_0_, bf16[512,4096]{1,0:T(8,128)(2,1)S(1)} %get-tuple-element.28.refs_4_.refs_1_.refs_0_, bf16[256,512]{1,0:T(8,128)(2,1)S(1)} %collective-permute-done.14.refs_2_, ...), custom_call_target="tpu_custom_call" | custom-call | tf_op jit(solution)/shard_map/backward_cols/pallas_call | solution.py:201
  79.5 2.0 %collective-permute-done.13.refs_2_ = f32[32,256]{1,0:T(8,128)S(1)} collective-permute-done((f32[32,256]{1,0:T(8,128)S(1)}, f32[32,256]{1,0:T(8,128)S(1)}, u32[]{:S(2)}, u32[]{:S(2)}) %collective-permute-start.13) | collective-permute-done | bytes 32800 | tf_op jit(solution)/shard_map/ppermute | solution.py:294
  81.5 2.4 %collective-permute-start.19 = (f32[32,256]{1,0:T(8,128)S(1)}, f32[32,256]{1,0:T(8,128)S(1)}, u32[]{:S(2)}, u32[]{:S(2)}) collective-permute-start(f32[32,256]{1,0:T(8,128)S(1)} %add_add_fusion.1), channel_id=1, source_target_pairs={{0,3},{1,2},{2,1},{3,0},{4,7},{5,6},{6,5},{7,4},{8,11},{9,10},{10,... | collective-permute-start | bytes 98312 | tf_op jit(solution)/shard_map/ppermute | solution.py:294
  83.9 3.5 %collective-permute-start.18 = (f32[32,256]{1,0:T(8,128)S(1)}, f32[32,256]{1,0:T(8,128)S(1)}, u32[]{:S(2)}, u32[]{:S(2)}) collective-permute-start(f32[32,256]{1,0:T(8,128)S(1)} %add_add_fusion.1), channel_id=1, source_target_pairs={{0,2},{1,3},{2,0},{3,1},{4,6},{5,7},{6,4},{7,5},{8,10},{9,11},{10,... | collective-permute-start | bytes 98312 | tf_op jit(solution)/shard_map/ppermute | solution.py:294
  88.8 2.4 %collective-permute-start.25 = (bf16[256,512]{1,0:T(8,128)(2,1)S(1)}, bf16[256,512]{1,0:T(8,128)(2,1)S(1)}, u32[]{:S(2)}, u32[]{:S(2)}) collective-permute-start(bf16[256,512]{1,0:T(8,128)(2,1)S(1)} %get-tuple-element.51), channel_id=1, source_target_pairs={{0,24},{4,28},{8,16},{12,20},{16,8},{20,12},{24,0},{28,4},{1,25},{... | collective-permute-start | bytes 786440 | tf_op jit(solution)/shard_map/ppermute | solution.py:294
  91.9 1.5 %collective-permute-start.21 = (f32[32,256]{1,0:T(8,128)S(1)}, f32[32,256]{1,0:T(8,128)S(1)}, u32[]{:S(2)}, u32[]{:S(2)}) collective-permute-start(f32[32,256]{1,0:T(8,128)S(1)} %add_add_fusion.refs_0_), channel_id=1, source_target_pairs={{0,16},{4,20},{8,24},{12,28},{16,0},{20,4},{24,8},{28,12},{1,17},{... | collective-permute-start | bytes 98312 | tf_op jit(solution)/shard_map/ppermute | solution.py:294
  93.4 7.1 %collective-permute-done.22.refs_3_ = f32[32,256]{1,0:T(8,128)S(1)} collective-permute-done((f32[32,256]{1,0:T(8,128)S(1)}, f32[32,256]{1,0:T(8,128)S(1)}, u32[]{:S(2)}, u32[]{:S(2)}) %collective-permute-start.22) | collective-permute-done | bytes 32800 | tf_op jit(solution)/shard_map/ppermute | solution.py:294
  100.5 1.4 %collective-permute-start.20 = (f32[32,256]{1,0:T(8,128)S(1)}, f32[32,256]{1,0:T(8,128)S(1)}, u32[]{:S(2)}, u32[]{:S(2)}) collective-permute-start(f32[32,256]{1,0:T(8,128)S(1)} %add_add_fusion.refs_0_), channel_id=1, source_target_pairs={{0,8},{4,12},{8,0},{12,4},{16,24},{20,28},{24,16},{28,20},{1,9},{5... | collective-permute-start | bytes 98312 | tf_op jit(solution)/shard_map/ppermute | solution.py:294
  101.9 2.5 %collective-permute-done.20.refs_1_ = f32[32,256]{1,0:T(8,128)S(1)} collective-permute-done((f32[32,256]{1,0:T(8,128)S(1)}, f32[32,256]{1,0:T(8,128)S(1)}, u32[]{:S(2)}, u32[]{:S(2)}) %collective-permute-start.20) | collective-permute-done | bytes 32800 | tf_op jit(solution)/shard_map/ppermute | solution.py:294
  105.1 1.3 %collective-permute-done.23.refs_1_ = f32[128,256]{1,0:T(8,128)S(1)} collective-permute-done((f32[128,256]{1,0:T(8,128)S(1)}, f32[128,256]{1,0:T(8,128)S(1)}, u32[]{:S(2)}, u32[]{:S(2)}) %collective-permute-start.23) | collective-permute-done | bytes 131104 | tf_op jit(solution)/shard_map/ppermute | solution.py:294
  106.4 1.3 %join.3 = f32[256,256]{1,0:T(8,128)} custom-call(s32[2]{0:T(128)S(1)} %pad_add_fusion.where, f32[128,256]{1,0:T(8,128)S(1)} %join.2.refs_0_, f32[128,256]{1,0:T(8,128)S(1)} %collective-permute-done.23.refs_1_), custom_call_target="tpu_custom_call" | custom-call | tf_op jit(solution)/shard_map/join/pallas_call | solution.py:283
  (56 shorter events, 10.8 us)
Async XLA Ops:
  0.6 15.4 %collective-permute-start.2 = (bf16[512,256]{1,0:T(8,128)(2,1)}, bf16[512,256]{1,0:T(8,128)(2,1)S(1)}, u32[]{:S(2)}, u32[]{:S(2)}) collective-permute-start(bf16[512,256]{1,0:T(8,128)(2,1)} %refs_4_.2), channel_id=1, source_target_pairs={{0,16},{4,20},{8,24},{12,28},{16,0},{20,4},{24,8},{28,12},{1,17},{... | collective-permute-start | bytes 786440 | tf_op jit(solution)/shard_map/ppermute | solution.py:294
  3.7 12.4 %collective-permute-start.1 = (bf16[512,256]{1,0:T(8,128)(2,1)}, bf16[512,256]{1,0:T(8,128)(2,1)S(1)}, u32[]{:S(2)}, u32[]{:S(2)}) collective-permute-start(bf16[512,256]{1,0:T(8,128)(2,1)} %refs_4_.2), channel_id=1, source_target_pairs={{0,24},{4,28},{8,16},{12,20},{16,8},{20,12},{24,0},{28,4},{1,25},{... | collective-permute-start | bytes 786440 | tf_op jit(solution)/shard_map/ppermute | solution.py:294
  5.1 12.0 %collective-permute-start.3 = (bf16[512,256]{1,0:T(8,128)(2,1)}, bf16[512,256]{1,0:T(8,128)(2,1)S(1)}, u32[]{:S(2)}, u32[]{:S(2)}) collective-permute-start(bf16[512,256]{1,0:T(8,128)(2,1)} %refs_4_.2), channel_id=1, source_target_pairs={{0,8},{4,12},{8,0},{12,4},{16,24},{20,28},{24,16},{28,20},{1,9},{5... | collective-permute-start | bytes 786440 | tf_op jit(solution)/shard_map/ppermute | solution.py:294
  5.2 15.7 %collective-permute-start = (bf16[512,256]{1,0:T(8,128)(2,1)}, bf16[512,256]{1,0:T(8,128)(2,1)S(1)}, u32[]{:S(2)}, u32[]{:S(2)}) collective-permute-start(bf16[512,256]{1,0:T(8,128)(2,1)} %refs_4_.2), channel_id=1, source_target_pairs={{0,4},{4,0},{8,12},{12,8},{16,20},{20,16},{24,28},{28,24},{1,5},{5... | collective-permute-start | bytes 786440 | tf_op jit(solution)/shard_map/ppermute | solution.py:294
  5.3 0.7 copy-start.3
  17.1 1.0 copy-start
  17.1 3.8 %collective-permute-start.4 = (bf16[512,256]{1,0:T(8,128)(2,1)S(1)}, bf16[512,256]{1,0:T(8,128)(2,1)S(1)}, u32[]{:S(2)}, u32[]{:S(2)}) collective-permute-start(bf16[512,256]{1,0:T(8,128)(2,1)S(1)} %get-tuple-element.30.refs_5_), channel_id=1, source_target_pairs={{0,4},{4,0},{8,12},{12,8},{16,20},{20,16},{24,28},{28,24},{1,5},{5... | collective-permute-start | bytes 786440 | tf_op jit(solution)/shard_map/ppermute | solution.py:294
  17.1 3.8 %collective-permute-start.5 = (bf16[512,256]{1,0:T(8,128)(2,1)S(1)}, bf16[512,256]{1,0:T(8,128)(2,1)S(1)}, u32[]{:S(2)}, u32[]{:S(2)}) collective-permute-start(bf16[512,256]{1,0:T(8,128)(2,1)S(1)} %get-tuple-element.31.refs_6_), channel_id=1, source_target_pairs={{0,4},{4,0},{8,12},{12,8},{16,20},{20,16},{24,28},{28,24},{1,5},{5... | collective-permute-start | bytes 786440 | tf_op jit(solution)/shard_map/ppermute | solution.py:294
  17.6 3.3 %collective-permute-start.6 = (bf16[512,256]{1,0:T(8,128)(2,1)S(1)}, bf16[512,256]{1,0:T(8,128)(2,1)S(1)}, u32[]{:S(2)}, u32[]{:S(2)}) collective-permute-start(bf16[512,256]{1,0:T(8,128)(2,1)S(1)} %get-tuple-element.32.refs_7_), channel_id=1, source_target_pairs={{0,4},{4,0},{8,12},{12,8},{16,20},{20,16},{24,28},{28,24},{1,5},{5... | collective-permute-start | bytes 786440 | tf_op jit(solution)/shard_map/ppermute | solution.py:294
  22.3 11.1 %collective-permute-start.7 = (bf16[512,256]{1,0:T(8,128)(2,1)S(1)}, bf16[512,256]{1,0:T(8,128)(2,1)S(1)}, u32[]{:S(2)}, u32[]{:S(2)}) collective-permute-start(bf16[512,256]{1,0:T(8,128)(2,1)S(1)} %forward_rows.7), channel_id=1, source_target_pairs={{0,3},{1,2},{2,1},{3,0},{4,7},{5,6},{6,5},{7,4},{8,11},{9,10},{10,... | collective-permute-start | bytes 786440 | tf_op jit(solution)/shard_map/ppermute | solution.py:294
  27.3 21.3 %collective-permute-start.8 = (bf16[512,256]{1,0:T(8,128)(2,1)S(1)}, bf16[512,256]{1,0:T(8,128)(2,1)S(1)}, u32[]{:S(2)}, u32[]{:S(2)}) collective-permute-start(bf16[512,256]{1,0:T(8,128)(2,1)S(1)} %forward_rows.8), channel_id=1, source_target_pairs={{0,2},{1,3},{2,0},{3,1},{4,6},{5,7},{6,4},{7,5},{8,10},{9,11},{10,... | collective-permute-start | bytes 786440 | tf_op jit(solution)/shard_map/ppermute | solution.py:294
  28.7 19.9 %copy-start.1 = (bf16[512,256]{1,0:T(8,128)(2,1)S(1)}, bf16[512,256]{1,0:T(8,128)(2,1)}, u32[]{:S(2)}) copy-start(bf16[512,256]{1,0:T(8,128)(2,1)} %refs_5_.1) | copy-start | bytes 786436
  28.7 19.9 %copy-start.2 = (bf16[256,256]{1,0:T(8,128)(2,1)S(1)}, bf16[256,256]{1,0:T(8,128)(2,1)}, u32[]{:S(2)}) copy-start(bf16[256,256]{1,0:T(8,128)(2,1)} %refs_4_.3) | copy-start | bytes 393220
  28.7 19.9 %collective-permute-start.9 = (bf16[512,256]{1,0:T(8,128)(2,1)S(1)}, bf16[512,256]{1,0:T(8,128)(2,1)S(1)}, u32[]{:S(2)}, u32[]{:S(2)}) collective-permute-start(bf16[512,256]{1,0:T(8,128)(2,1)S(1)} %forward_rows.9), channel_id=1, source_target_pairs={{0,1},{1,0},{2,3},{3,2},{4,5},{5,4},{6,7},{7,6},{8,9},{9,8},{10,11... | collective-permute-start | bytes 786440 | tf_op jit(solution)/shard_map/ppermute | solution.py:294
  49.7 12.1 %collective-permute-start.16 = (bf16[256,512]{1,0:T(8,128)(2,1)S(1)}, bf16[256,512]{1,0:T(8,128)(2,1)S(1)}, u32[]{:S(2)}, u32[]{:S(2)}) collective-permute-start(bf16[256,512]{1,0:T(8,128)(2,1)S(1)} %get-tuple-element.45.refs_2_), channel_id=1, source_target_pairs={{0,1},{1,0},{2,3},{3,2},{4,5},{5,4},{6,7},{7,6},{8,9},{9,8},{10,11... | collective-permute-start | bytes 786440 | tf_op jit(solution)/shard_map/ppermute | solution.py:294
  49.7 21.5 %collective-permute-start.15 = (bf16[256,512]{1,0:T(8,128)(2,1)S(1)}, bf16[256,512]{1,0:T(8,128)(2,1)S(1)}, u32[]{:S(2)}, u32[]{:S(2)}) collective-permute-start(bf16[256,512]{1,0:T(8,128)(2,1)S(1)} %get-tuple-element.45.refs_2_), channel_id=1, source_target_pairs={{0,2},{1,3},{2,0},{3,1},{4,6},{5,7},{6,4},{7,5},{8,10},{9,11},{10,... | collective-permute-start | bytes 786440 | tf_op jit(solution)/shard_map/ppermute | solution.py:294
  52.7 18.5 %collective-permute-start.14 = (bf16[256,512]{1,0:T(8,128)(2,1)S(1)}, bf16[256,512]{1,0:T(8,128)(2,1)S(1)}, u32[]{:S(2)}, u32[]{:S(2)}) collective-permute-start(bf16[256,512]{1,0:T(8,128)(2,1)S(1)} %get-tuple-element.45.refs_2_), channel_id=1, source_target_pairs={{0,3},{1,2},{2,1},{3,0},{4,7},{5,6},{6,5},{7,4},{8,11},{9,10},{10,... | collective-permute-start | bytes 786440 | tf_op jit(solution)/shard_map/ppermute | solution.py:294
  54.6 1.4 %collective-permute-start.10 = (f32[128,256]{1,0:T(8,128)S(1)}, f32[128,256]{1,0:T(8,128)S(1)}, u32[]{:S(2)}, u32[]{:S(2)}) collective-permute-start(f32[128,256]{1,0:T(8,128)S(1)} %get-tuple-element.40), channel_id=1, source_target_pairs={{0,4},{4,0},{8,12},{12,8},{16,20},{20,16},{24,28},{28,24},{1,5},{5... | collective-permute-start | bytes 393224 | tf_op jit(solution)/shard_map/ppermute | solution.py:294
  73.5 13.9 %collective-permute-start.24 = (bf16[4,256,512]{2,1,0:T(8,128)(2,1)S(1)}, bf16[4,256,512]{2,1,0:T(8,128)(2,1)S(1)}, u32[]{:S(2)}, u32[]{:S(2)}) collective-permute-start(bf16[4,256,512]{2,1,0:T(8,128)(2,1)S(1)} %backward_cols.5), channel_id=1, source_target_pairs={{0,4},{4,0},{8,12},{12,8},{16,20},{20,16},{24,28},{28,24},{1,5},{5... | collective-permute-start | bytes 3145736 | tf_op jit(solution)/shard_map/ppermute | solution.py:294
  73.6 5.9 %collective-permute-start.11 = (f32[32,256]{1,0:T(8,128)S(1)}, f32[32,256]{1,0:T(8,128)S(1)}, u32[]{:S(2)}, u32[]{:S(2)}) collective-permute-start(f32[32,256]{1,0:T(8,128)S(1)} %get-tuple-element.42), channel_id=1, source_target_pairs={{0,8},{4,12},{8,0},{12,4},{16,24},{20,28},{24,16},{28,20},{1,9},{5... | collective-permute-start | bytes 98312 | tf_op jit(solution)/shard_map/ppermute | solution.py:294
  75.1 4.3 %collective-permute-start.12 = (f32[32,256]{1,0:T(8,128)S(1)}, f32[32,256]{1,0:T(8,128)S(1)}, u32[]{:S(2)}, u32[]{:S(2)}) collective-permute-start(f32[32,256]{1,0:T(8,128)S(1)} %get-tuple-element.43), channel_id=1, source_target_pairs={{0,16},{4,20},{8,24},{12,28},{16,0},{20,4},{24,8},{28,12},{1,17},{... | collective-permute-start | bytes 98312 | tf_op jit(solution)/shard_map/ppermute | solution.py:294
  76.6 4.8 %collective-permute-start.13 = (f32[32,256]{1,0:T(8,128)S(1)}, f32[32,256]{1,0:T(8,128)S(1)}, u32[]{:S(2)}, u32[]{:S(2)}) collective-permute-start(f32[32,256]{1,0:T(8,128)S(1)} %get-tuple-element.44), channel_id=1, source_target_pairs={{0,24},{4,28},{8,16},{12,20},{16,8},{20,12},{24,0},{28,4},{1,25},{... | collective-permute-start | bytes 98312 | tf_op jit(solution)/shard_map/ppermute | solution.py:294
  81.5 7.3 %collective-permute-start.19 = (f32[32,256]{1,0:T(8,128)S(1)}, f32[32,256]{1,0:T(8,128)S(1)}, u32[]{:S(2)}, u32[]{:S(2)}) collective-permute-start(f32[32,256]{1,0:T(8,128)S(1)} %add_add_fusion.1), channel_id=1, source_target_pairs={{0,3},{1,2},{2,1},{3,0},{4,7},{5,6},{6,5},{7,4},{8,11},{9,10},{10,... | collective-permute-start | bytes 98312 | tf_op jit(solution)/shard_map/ppermute | solution.py:294
  83.9 7.4 %collective-permute-start.18 = (f32[32,256]{1,0:T(8,128)S(1)}, f32[32,256]{1,0:T(8,128)S(1)}, u32[]{:S(2)}, u32[]{:S(2)}) collective-permute-start(f32[32,256]{1,0:T(8,128)S(1)} %add_add_fusion.1), channel_id=1, source_target_pairs={{0,2},{1,3},{2,0},{3,1},{4,6},{5,7},{6,4},{7,5},{8,10},{9,11},{10,... | collective-permute-start | bytes 98312 | tf_op jit(solution)/shard_map/ppermute | solution.py:294
  87.4 3.9 %collective-permute-start.17 = (f32[32,256]{1,0:T(8,128)S(1)}, f32[32,256]{1,0:T(8,128)S(1)}, u32[]{:S(2)}, u32[]{:S(2)}) collective-permute-start(f32[32,256]{1,0:T(8,128)S(1)} %add_add_fusion.1), channel_id=1, source_target_pairs={{0,1},{1,0},{2,3},{3,2},{4,5},{5,4},{6,7},{7,6},{8,9},{9,8},{10,11... | collective-permute-start | bytes 98312 | tf_op jit(solution)/shard_map/ppermute | solution.py:294
  87.7 20.0 %collective-permute-start.27 = (bf16[256,512]{1,0:T(8,128)(2,1)S(1)}, bf16[256,512]{1,0:T(8,128)(2,1)S(1)}, u32[]{:S(2)}, u32[]{:S(2)}) collective-permute-start(bf16[256,512]{1,0:T(8,128)(2,1)S(1)} %get-tuple-element.49), channel_id=1, source_target_pairs={{0,8},{4,12},{8,0},{12,4},{16,24},{20,28},{24,16},{28,20},{1,9},{5... | collective-permute-start | bytes 786440 | tf_op jit(solution)/shard_map/ppermute | solution.py:294
  88.3 19.4 %collective-permute-start.26 = (bf16[256,512]{1,0:T(8,128)(2,1)S(1)}, bf16[256,512]{1,0:T(8,128)(2,1)S(1)}, u32[]{:S(2)}, u32[]{:S(2)}) collective-permute-start(bf16[256,512]{1,0:T(8,128)(2,1)S(1)} %get-tuple-element.50), channel_id=1, source_target_pairs={{0,16},{4,20},{8,24},{12,28},{16,0},{20,4},{24,8},{28,12},{1,17},{... | collective-permute-start | bytes 786440 | tf_op jit(solution)/shard_map/ppermute | solution.py:294
  88.8 18.9 %collective-permute-start.25 = (bf16[256,512]{1,0:T(8,128)(2,1)S(1)}, bf16[256,512]{1,0:T(8,128)(2,1)S(1)}, u32[]{:S(2)}, u32[]{:S(2)}) collective-permute-start(bf16[256,512]{1,0:T(8,128)(2,1)S(1)} %get-tuple-element.51), channel_id=1, source_target_pairs={{0,24},{4,28},{8,16},{12,20},{16,8},{20,12},{24,0},{28,4},{1,25},{... | collective-permute-start | bytes 786440 | tf_op jit(solution)/shard_map/ppermute | solution.py:294
  91.4 9.2 %collective-permute-start.22 = (f32[32,256]{1,0:T(8,128)S(1)}, f32[32,256]{1,0:T(8,128)S(1)}, u32[]{:S(2)}, u32[]{:S(2)}) collective-permute-start(f32[32,256]{1,0:T(8,128)S(1)} %add_add_fusion.refs_0_), channel_id=1, source_target_pairs={{0,24},{4,28},{8,16},{12,20},{16,8},{20,12},{24,0},{28,4},{1,25},{... | collective-permute-start | bytes 98312 | tf_op jit(solution)/shard_map/ppermute | solution.py:294
  91.9 10.0 %collective-permute-start.21 = (f32[32,256]{1,0:T(8,128)S(1)}, f32[32,256]{1,0:T(8,128)S(1)}, u32[]{:S(2)}, u32[]{:S(2)}) collective-permute-start(f32[32,256]{1,0:T(8,128)S(1)} %add_add_fusion.refs_0_), channel_id=1, source_target_pairs={{0,16},{4,20},{8,24},{12,28},{16,0},{20,4},{24,8},{28,12},{1,17},{... | collective-permute-start | bytes 98312 | tf_op jit(solution)/shard_map/ppermute | solution.py:294
  100.5 3.9 %collective-permute-start.20 = (f32[32,256]{1,0:T(8,128)S(1)}, f32[32,256]{1,0:T(8,128)S(1)}, u32[]{:S(2)}, u32[]{:S(2)}) collective-permute-start(f32[32,256]{1,0:T(8,128)S(1)} %add_add_fusion.refs_0_), channel_id=1, source_target_pairs={{0,8},{4,12},{8,0},{12,4},{16,24},{20,28},{24,16},{28,20},{1,9},{5... | collective-permute-start | bytes 98312 | tf_op jit(solution)/shard_map/ppermute | solution.py:294
  105.0 1.4 %collective-permute-start.23 = (f32[128,256]{1,0:T(8,128)S(1)}, f32[128,256]{1,0:T(8,128)S(1)}, u32[]{:S(2)}, u32[]{:S(2)}) collective-permute-start(f32[128,256]{1,0:T(8,128)S(1)} %join.2.refs_0_), channel_id=1, source_target_pairs={{0,4},{4,0},{8,12},{12,8},{16,20},{20,16},{24,28},{28,24},{1,5},{5... | collective-permute-start | bytes 393224 | tf_op jit(solution)/shard_map/ppermute | solution.py:294
  (1 other events, 0.7 us)

commit v4 on v3

--- a/solution.py
+++ b/solution.py
@@ -249,45 +249,59 @@
     )(*map(near, values), *after)
 
 
-def split_kernel(where, *refs, by_core):
-    outs = refs[1:] if by_core else refs[2:]
-    rows = outs[0].shape[0]
-    place = where[0] & 1 if by_core else lax.div(where[0], 2)
-    for step, out_ref in enumerate(outs):
-        at = pl.ds(pl.multiple_of((place ^ step) * rows, rows), rows)
-        out_ref[...] = refs[0][at, :] if by_core else refs[0][at, :] + refs[1][at, :]
-
-
-def split(where, values, count, by_core):
-    rows, width = values[0].shape
-    return pl.pallas_call(
-        functools.partial(split_kernel, by_core=by_core),
-        out_shape=[jax.ShapeDtypeStruct((rows // count, width), values[0].dtype)] * count,
-        in_specs=[SCALARS] + [WHOLE] * len(values),
+def split_kernel(where, value_ref, kept_ref, sent_ref, *, rows):
+    core = where[0] & 1
+    for i in range(kept_ref.shape[0] // rows):
+        at = pl.ds(i * rows, rows)
+        kept_ref[at, :] = value_ref[pl.ds(pl.multiple_of((2 * i + core) * rows, rows), rows), :]
+        sent_ref[at, :] = value_ref[pl.ds(pl.multiple_of((2 * i + 1 - core) * rows, rows), rows), :]
+
+
+def split(where, value, count):
+    rows, width = value.shape
+    half = jax.ShapeDtypeStruct((rows // 2, width), value.dtype)
+    return pl.pallas_call(
+        functools.partial(split_kernel, rows=rows // count),
+        out_shape=[half, half],
+        in_specs=[SCALARS, WHOLE],
         compiler_params=params(10),
         cost_estimate=cost(0, 0),
         name="split",
-    )(where, *values)
-
-
-def join_kernel(where, *refs, by_core):
-    parts, out_ref = refs[:-1], refs[-1]
-    rows = parts[0].shape[0]
-    place = where[0] & 1 if by_core else lax.div(where[0], 2)
-    for step, part in enumerate(parts):
-        out_ref[pl.ds(pl.multiple_of((place ^ step) * rows, rows), rows), :] = part[...]
-
-
-def join(where, parts, by_core):
-    count, (rows, width) = len(parts), parts[0].shape
-    return pl.pallas_call(
-        functools.partial(join_kernel, by_core=by_core),
-        out_shape=jax.ShapeDtypeStruct((count * rows, width), parts[0].dtype),
-        in_specs=[SCALARS] + [WHOLE] * count,
-        compiler_params=params(10),
-        cost_estimate=cost(0, 0),
-        name="join",
-    )(where, *parts)
+    )(where, value)
+
+
+def own_kernel(where, values_ref, out_ref):
+    rows = out_ref.shape[0]
+    at = pl.ds(pl.multiple_of(lax.div(where[0], 2) * rows, rows), rows)
+    value = values_ref[0, at, :]
+    for i in range(1, values_ref.shape[0]):
+        value = value + values_ref[i, at, :]
+    out_ref[...] = value
+
+
+def own(where, values, rows):
+    return pl.pallas_call(
+        own_kernel,
+        out_shape=jax.ShapeDtypeStruct((rows, values.shape[2]), values.dtype),
+        in_specs=[SCALARS, WHOLE],
+        compiler_params=params(10),
+        cost_estimate=cost(0, 0),
+        name="own",
+    )(where, values)
+
+
+def keep_kernel(value_ref, out_ref):
+    out_ref[...] = value_ref[...]
+
+
+def keep(value):
+    return pl.pallas_call(
+        keep_kernel,
+        out_shape=jax.ShapeDtypeStruct(value.shape, value.dtype),
+        compiler_params=params(10),
+        cost_estimate=cost(0, 0),
+        name="keep",
+    )(value)
 
 
 def swap(value, axis, size, step):
@@ -319,31 +333,30 @@
     for s, block, half in zip(steps[:-1], blocks, halves):
         share = forward(where, [block], odd, 1, [half], jnp.bfloat16)[0]
         came.append(swap(share, "col", n_col, s))
-    own = forward(where, blocks[-1:], odd, 1, halves[-1:], jnp.float32)
+    mine = forward(where, blocks[-1:], odd, 1, halves[-1:], jnp.float32)
     scale = 1.0 / math.sqrt(rows * n_row * n_col)
-    hidden, piece, part = middle([*own, *came], weight, upstream, scale)
+    hidden, piece, part = middle([*mine, *came], weight, upstream, scale)
 
     pieces = {s: swap(piece, "col", n_col, s) for s in steps[:-1]}
     pieces[0] = piece
-    kept, sent = split(where, [part], 2, True)
-    part, *others = split(where, [kept, swap(sent, "row", n_row, 1)], chips, False)
+    kept, sent = split(where, part, n_row)
+    cores = [[i for i in range(n_row) if i % 2 == core] for core in range(2)]
+    part = lax.all_gather(kept + swap(sent, "row", n_row, 1), "row", axis_index_groups=cores)
+    part = lax.all_gather(own(where, part, part.shape[1] // chips), "col")
+    part = lax.all_gather(sum([part[i] for i in range(1, n_col)], part[0]), "row", axis=0, tiled=True)
+    weight_grad = keep(part)
 
     soon, late = [0, 1], steps[:-2]
     early = backward(
         where, [dense[s] for s in soon], [pieces[s] for s in soon], 0, n_row, n_row, depth, None, jnp.float32
     )
     last = functools.partial(backward, where, [dense[s] for s in late], [pieces[s] for s in late])
-    sent = last(0, chips, n_row, depth, early, jnp.bfloat16, [part])
+    sent = last(0, chips, n_row, depth, early, jnp.bfloat16, [weight_grad])
     kept = last(chips, chips, n_row, depth, early, jnp.float32)
     came = swap(sent, "row", n_row, 1)
     summed = [(kept[s] + came[s].astype(jnp.float32)).astype(jnp.bfloat16) for s in range(1, chips)]
     parts = [swap(summed[s - 1], "row", n_row, 2 * s) for s in range(chips - 1, 0, -1)]
 
-    others = gate([swap(other, "row", n_row, 2 * s) for s, other in enumerate(others, 1)], [kept])
-    part = sum(others, part)
-    part = sum([swap(part, "col", n_col, s) for s in range(1, n_col)], part)
-    half = join(where, [part] + [swap(part, "row", n_row, 2 * s) for s in range(1, chips)], False)
-    weight_grad = join(where, [half, swap(half, "row", n_row, 1)], True)
     return hidden, weight_grad, finish(kept, came, parts)
 
 

time: 109 us -> 120 us (1.10)
  blocking collectives: 0 us -> 38.2 us
  starting transfers between devices: 30.8 us -> 18.1 us
  waiting for transfers between devices: 43.9 us -> 31.3 us
  Pallas kernels: 30.9 us -> 29.5 us
    all_gather x0 -> x3, blocking collectives: none -> 38.2 us  [the longest x1 18.7 us: shards(): part = lax.all_gather(own(where, part, part.shape[1] // chips), 'col')]
    ppermute x28 -> x18, starting transfers between devices: 30.8 us -> 18.1 us  [swap(): return lax.ppermute(value, axis, [(i, i ^ step) for i in range(size)])]
    ppermute x28 -> x18, waiting for transfers between devices: 43.9 us -> 31.3 us  [swap(): return lax.ppermute(value, axis, [(i, i ^ step) for i in range(size)])]
    pallas_call x4 -> x3, Pallas kernels: 2.95 us -> 1.84 us  [the longest x1 0.72 us: keep(): pl.pallas_call(keep_kernel, out_shape=jax.ShapeDtypeStruct(value.shape, v...]
  transfers between devices with their start and end apart: 28 -> 18, of which waited for: 11 -> 6; matrix products, arithmetic and copies ran while one was open for 0% -> 0% of each run, Pallas kernels for 23% -> 19%
where the time goes in v4:
time: 120 us
  blocking collectives  38.2 us (32%)
  waiting for transfers between devices  31.3 us (26%)
  Pallas kernels  29.5 us (25%)
  starting transfers between devices  18.1 us (15%)
  local copies, waits for them, and re-layouts  1.79 us (1%)
    ppermute x18, waiting for transfers between devices, swap(): return lax.ppermute(value, axis, [(i, i ^ step) for i in range(size)])  31.3 us
    all_gather x1, blocking collectives, shards(): part = lax.all_gather(own(where, part, part.shape[1] // chips), 'col')  18.7 us
    ppermute x18, starting transfers between devices, swap(): return lax.ppermute(value, axis, [(i, i ^ step) for i in range(size)])  18.1 us
    all_gather x1, blocking collectives, shards(): lax.all_gather(kept + swap(sent, 'row', n_row, 1), 'row', axis_index_grou...  10.2 us
    all_gather x1, blocking collectives, shards(): lax.all_gather(sum([part[i] for i in range(1, n_col)], part[0]), 'row', a...  9.3 us
    pallas_call x2, Pallas kernels, dense_rows(): pl.pallas_call(functools.partial(dense_kernel, steps=steps, window=window...  9 us
    pallas_call x3, Pallas kernels, backward(): pl.pallas_call(functools.partial(backward_kernel, count=count, first=firs...  8.68 us
    pallas_call x5, Pallas kernels, forward(): pl.pallas_call(functools.partial(forward_kernel, blocks=blocks, count=cou...  7.96 us
  transfers between devices with their start and end apart: 18, of which 6 were waited for; matrix products, arithmetic and copies ran while one was open for 0% of the time, Pallas kernels for 19%

profile of v4, /device:TPU:0, one launch (start us, length us, event | category | flops | bytes accessed | tf_op | source)
XLA Modules:
  0.0 120.1 jit_solution(14127930576081037908)
XLA Ops:
  0.6 3.0 %collective-permute-start.2 = (bf16[512,256]{1,0:T(8,128)(2,1)}, bf16[512,256]{1,0:T(8,128)(2,1)S(1)}, u32[]{:S(2)}, u32[]{:S(2)}) collective-permute-start(bf16[512,256]{1,0:T(8,128)(2,1)} %refs_4_.2), channel_id=1, source_target_pairs={{0,16},{4,20},{8,24},{12,28},{16,0},{20,4},{24,8},{28,12},{1,17},{... | collective-permute-start | bytes 786440 | tf_op jit(solution)/shard_map/ppermute | solution.py:308
  3.7 1.4 %collective-permute-start.1 = (bf16[512,256]{1,0:T(8,128)(2,1)}, bf16[512,256]{1,0:T(8,128)(2,1)S(1)}, u32[]{:S(2)}, u32[]{:S(2)}) collective-permute-start(bf16[512,256]{1,0:T(8,128)(2,1)} %refs_4_.2), channel_id=1, source_target_pairs={{0,24},{4,28},{8,16},{12,20},{16,8},{20,12},{24,0},{28,4},{1,25},{... | collective-permute-start | bytes 786440 | tf_op jit(solution)/shard_map/ppermute | solution.py:308
  5.3 0.7 copy-done.4
  6.0 0.7 copy-done.5
  6.6 4.5 %dense_rows.3 = (bf16[512,4096]{1,0:T(8,128)(2,1)S(1)}, bf16[512,4096]{1,0:T(8,128)(2,1)S(1)}) custom-call(s32[2]{0:T(128)S(1)} %pad_add_fusion.where, s32[16]{0:T(128)S(1)} %bitcast.19, s32[448]{0:T(512)S(1)} %bitcast.17, bf16[448,128,128]{2,1,0:T(8,128)(2,1)} %bitcast.21), custom_call_target="tpu_custom_call" | custom-call | bytes 20971520 | tf_op jit(solution)/shard_map/dense_rows/pallas_call | solution.py:98
  11.2 4.5 %dense_rows.2 = (bf16[512,4096]{1,0:T(8,128)(2,1)S(1)}, bf16[512,4096]{1,0:T(8,128)(2,1)S(1)}) custom-call(s32[2]{0:T(128)S(1)} %pad_add_fusion.where, s32[16]{0:T(128)S(1)} %bitcast.20, s32[448]{0:T(512)S(1)} %bitcast.18, bf16[448,128,128]{2,1,0:T(8,128)(2,1)} %bitcast.22), custom_call_target="tpu_custom_call" | custom-call | bytes 20971520 | tf_op jit(solution)/shard_map/dense_rows/pallas_call | solution.py:98
  15.8 1.3 %collective-permute-done.3.refs_2_ = bf16[512,256]{1,0:T(8,128)(2,1)S(1)} collective-permute-done((bf16[512,256]{1,0:T(8,128)(2,1)}, bf16[512,256]{1,0:T(8,128)(2,1)S(1)}, u32[]{:S(2)}, u32[]{:S(2)}) %collective-permute-start.3) | collective-permute-done | bytes 262176 | tf_op jit(solution)/shard_map/ppermute | solution.py:308
  18.1 2.9 %forward_rows.5 = (f32[512,256]{1,0:T(8,128)S(1)}, f32[512,256]{1,0:T(8,128)S(1)}, f32[512,256]{1,0:T(8,128)S(1)}, f32[512,256]{1,0:T(8,128)S(1)}) custom-call(s32[2]{0:T(128)S(1)} %pad_add_fusion.where, bf16[512,4096]{1,0:T(8,128)(2,1)S(1)} %get-tuple-element.20.refs_3_.refs_0_, bf16[512,4096]{1,0:T(8,128)(2,1)S(1)} %get-tuple-element.21.refs_4_.refs_1_.refs_0_, ...), custom_call_target="tpu_custom_call" | custom-call | flops 2147483648 | bytes 8388608 | tf_op jit(solution)/shard_map/forward_rows/pallas_call | solution.py:131
  21.0 1.3 %forward_rows.7 = bf16[512,256]{1,0:T(8,128)(2,1)S(1)} custom-call(s32[2]{0:T(128)S(1)} %pad_add_fusion.where, bf16[512,4096]{1,0:T(8,128)(2,1)S(1)} %get-tuple-element.20.refs_3_.refs_0_, bf16[512,256]{1,0:T(8,128)(2,1)S(1)} %collective-permute-done.refs_1_, bf16[512,256]{1,0:T(8,128)(2,1)S(1)} %collective-permute-done.4.refs_2_, ...), custom_call_target="tpu_custom_call" | custom-call | flops 536870912 | bytes 2097152 | tf_op jit(solution)/shard_map/forward_rows/pallas_call | solution.py:131
  22.3 3.8 %collective-permute-start.7 = (bf16[512,256]{1,0:T(8,128)(2,1)S(1)}, bf16[512,256]{1,0:T(8,128)(2,1)S(1)}, u32[]{:S(2)}, u32[]{:S(2)}) collective-permute-start(bf16[512,256]{1,0:T(8,128)(2,1)S(1)} %forward_rows.7), channel_id=1, source_target_pairs={{0,3},{1,2},{2,1},{3,0},{4,7},{5,6},{6,5},{7,4},{8,11},{9,10},{10,... | collective-permute-start | bytes 786440 | tf_op jit(solution)/shard_map/ppermute | solution.py:308
  26.1 1.3 %forward_rows.8 = bf16[512,256]{1,0:T(8,128)(2,1)S(1)} custom-call(s32[2]{0:T(128)S(1)} %pad_add_fusion.where, bf16[512,4096]{1,0:T(8,128)(2,1)S(1)} %get-tuple-element.21.refs_4_.refs_1_.refs_0_, bf16[512,256]{1,0:T(8,128)(2,1)S(1)} %collective-permute-done.refs_1_, bf16[512,256]{1,0:T(8,128)(2,1)S(1)} %collective-permute-done.4.refs_2_, ...), custom_call_target="tpu_custom_call" | custom-call | flops 536870912 | bytes 2097152 | tf_op jit(solution)/shard_map/forward_rows/pallas_call | solution.py:131
  27.4 1.3 %forward_rows.9 = bf16[512,256]{1,0:T(8,128)(2,1)S(1)} custom-call(s32[2]{0:T(128)S(1)} %pad_add_fusion.where, bf16[512,4096]{1,0:T(8,128)(2,1)S(1)} %get-tuple-element.22.refs_5_.refs_2_.refs_0_.refs_1_, bf16[512,256]{1,0:T(8,128)(2,1)S(1)} %collective-permute-done.refs_1_, bf16[512,256]{1,0:T(8,128)(2,1)S(1)} %collective-permute-done.4.refs_2_, ...), custom_call_target="tpu_custom_call" | custom-call | flops 536870912 | bytes 2097152 | tf_op jit(solution)/shard_map/forward_rows/pallas_call | solution.py:131
  28.7 0.7 collective-permute-start.9
  29.4 1.3 %forward_rows.6.refs_0_ = f32[512,256]{1,0:T(8,128)S(1)} custom-call(s32[2]{0:T(128)S(1)} %pad_add_fusion.where, bf16[512,4096]{1,0:T(8,128)(2,1)S(1)} %get-tuple-element.19.refs_6_.refs_3_.refs_0_, bf16[512,256]{1,0:T(8,128)(2,1)S(1)} %collective-permute-done.refs_1_, bf16[512,256]{1,0:T(8,128)(2,1)S(1)} %collective-permute-done.4.refs_2_, ...), custom_call_target="tpu_custom_call" | custom-call | flops 536870912 | bytes 2097152 | tf_op jit(solution)/shard_map/forward_rows/pallas_call | solution.py:131
  30.7 2.7 %collective-permute-done.7.refs_1_ = bf16[512,256]{1,0:T(8,128)(2,1)S(1)} collective-permute-done((bf16[512,256]{1,0:T(8,128)(2,1)S(1)}, bf16[512,256]{1,0:T(8,128)(2,1)S(1)}, u32[]{:S(2)}, u32[]{:S(2)}) %collective-permute-start.7) | collective-permute-done | bytes 262176 | tf_op jit(solution)/shard_map/ppermute | solution.py:308
  33.4 15.2 %collective-permute-done.8.refs_2_ = bf16[512,256]{1,0:T(8,128)(2,1)S(1)} collective-permute-done((bf16[512,256]{1,0:T(8,128)(2,1)S(1)}, bf16[512,256]{1,0:T(8,128)(2,1)S(1)}, u32[]{:S(2)}, u32[]{:S(2)}) %collective-permute-start.8) | collective-permute-done | bytes 262176 | tf_op jit(solution)/shard_map/ppermute | solution.py:308
  48.6 1.1 middle.1
  49.7 0.6 split.1
  50.4 3.0 %collective-permute-start.12 = (bf16[256,512]{1,0:T(8,128)(2,1)S(1)}, bf16[256,512]{1,0:T(8,128)(2,1)S(1)}, u32[]{:S(2)}, u32[]{:S(2)}) collective-permute-start(bf16[256,512]{1,0:T(8,128)(2,1)S(1)} %get-tuple-element.34.refs_2_), channel_id=1, source_target_pairs={{0,2},{1,3},{2,0},{3,1},{4,6},{5,7},{6,4},{7,5},{8,10},{9,11},{10,... | collective-permute-start | bytes 786440 | tf_op jit(solution)/shard_map/ppermute | solution.py:308
  53.4 1.3 %collective-permute-start.11 = (bf16[256,512]{1,0:T(8,128)(2,1)S(1)}, bf16[256,512]{1,0:T(8,128)(2,1)S(1)}, u32[]{:S(2)}, u32[]{:S(2)}) collective-permute-start(bf16[256,512]{1,0:T(8,128)(2,1)S(1)} %get-tuple-element.34.refs_2_), channel_id=1, source_target_pairs={{0,3},{1,2},{2,1},{3,0},{4,7},{5,6},{6,5},{7,4},{8,11},{9,10},{10,... | collective-permute-start | bytes 786440 | tf_op jit(solution)/shard_map/ppermute | solution.py:308
  54.8 10.2 %all-gather = f32[512,256]{1,0:T(8,128)S(1)} all-gather(f32[128,256]{1,0:T(8,128)S(1)} %add.29), channel_id=2, replica_groups={{0,8,16,24},{4,12,20,28},{1,9,17,25},{5,13,21,29},{2,10,18,26},{6,14,22..., dimensions={0}, use_global_device_ids=true | all-gather | bytes 655360 | tf_op jit(solution)/shard_map/all_gather | solution.py:344
  65.6 18.7 %all-gather.1 = f32[128,256]{1,0:T(8,128)S(1)} all-gather(f32[32,256]{1,0:T(8,128)S(1)} %own.1), channel_id=3, replica_groups=mesh['row'=8,'col'=4] {'col'}, dimensions={0}, use_global_device_ids=true | all-gather | bytes 163840 | tf_op jit(solution)/shard_map/all_gather | solution.py:345
  84.3 9.3 %all-gather.2 = f32[1,256,256]{2,1,0:T(8,128)S(1)} all-gather(f32[1,32,256]{2,1,0:T(8,128)S(1)} %fusion.6), channel_id=4, replica_groups=mesh['row'=8,'col'=4] {'row'}, dimensions={1}, use_global_device_ids=true | all-gather | bytes 294912 | tf_op jit(solution)/shard_map/all_gather | solution.py:346
  93.6 0.7 keep.1.refs_5_
  94.3 4.1 %backward_cols.3.refs_4_ = f32[8,256,512]{2,1,0:T(8,128)S(1)} custom-call(s32[2]{0:T(128)S(1)} %pad_add_fusion.where, bf16[512,4096]{1,0:T(8,128)(2,1)S(1)} %get-tuple-element.19.refs_6_.refs_3_.refs_0_, bf16[512,4096]{1,0:T(8,128)(2,1)S(1)} %get-tuple-element.22.refs_5_.refs_2_.refs_0_.refs_1_, bf16[256,512]{1,0:T(8,128)(2,1)S(1)} %get-tuple-element.34.refs_2_, ...), custom_call_target="tpu_custom_call" | custom-call | tf_op jit(solution)/shard_map/backward_cols/pallas_call | solution.py:201
  98.4 2.3 %backward_cols.5 = bf16[4,256,512]{2,1,0:T(8,128)(2,1)S(1)} custom-call(s32[2]{0:T(128)S(1)} %pad_add_fusion.where, bf16[512,4096]{1,0:T(8,128)(2,1)S(1)} %get-tuple-element.20.refs_3_.refs_0_, bf16[512,4096]{1,0:T(8,128)(2,1)S(1)} %get-tuple-element.21.refs_4_.refs_1_.refs_0_, bf16[256,512]{1,0:T(8,128)(2,1)S(1)} %collective-permute-done.11.refs_2_, ...), custom_call_target="tpu_custom_call" | custom-call | tf_op jit(solution)/shard_map/backward_cols/pallas_call | solution.py:201
  101.1 2.3 %backward_cols.4.refs_0_ = f32[4,256,512]{2,1,0:T(8,128)S(1)} custom-call(s32[2]{0:T(128)S(1)} %pad_add_fusion.where, bf16[512,4096]{1,0:T(8,128)(2,1)S(1)} %get-tuple-element.20.refs_3_.refs_0_, bf16[512,4096]{1,0:T(8,128)(2,1)S(1)} %get-tuple-element.21.refs_4_.refs_1_.refs_0_, bf16[256,512]{1,0:T(8,128)(2,1)S(1)} %collective-permute-done.11.refs_2_, ...), custom_call_target="tpu_custom_call" | custom-call | tf_op jit(solution)/shard_map/backward_cols/pallas_call | solution.py:201
  103.7 1.6 %collective-permute-start.17 = (bf16[256,512]{1,0:T(8,128)(2,1)S(1)}, bf16[256,512]{1,0:T(8,128)(2,1)S(1)}, u32[]{:S(2)}, u32[]{:S(2)}) collective-permute-start(bf16[256,512]{1,0:T(8,128)(2,1)S(1)} %get-tuple-element.35), channel_id=1, source_target_pairs={{0,8},{4,12},{8,0},{12,4},{16,24},{20,28},{24,16},{28,20},{1,9},{5... | collective-permute-start | bytes 786440 | tf_op jit(solution)/shard_map/ppermute | solution.py:308
  105.8 1.5 %collective-permute-start.15 = (bf16[256,512]{1,0:T(8,128)(2,1)S(1)}, bf16[256,512]{1,0:T(8,128)(2,1)S(1)}, u32[]{:S(2)}, u32[]{:S(2)}) collective-permute-start(bf16[256,512]{1,0:T(8,128)(2,1)S(1)} %get-tuple-element.37), channel_id=1, source_target_pairs={{0,24},{4,28},{8,16},{12,20},{16,8},{20,12},{24,0},{28,4},{1,25},{... | collective-permute-start | bytes 786440 | tf_op jit(solution)/shard_map/ppermute | solution.py:308
  107.3 5.6 %collective-permute-done.17.refs_4_ = bf16[256,512]{1,0:T(8,128)(2,1)S(1)} collective-permute-done((bf16[256,512]{1,0:T(8,128)(2,1)S(1)}, bf16[256,512]{1,0:T(8,128)(2,1)S(1)}, u32[]{:S(2)}, u32[]{:S(2)}) %collective-permute-start.17) | collective-permute-done | bytes 262176 | tf_op jit(solution)/shard_map/ppermute | solution.py:308
  112.9 6.3 %collective-permute-done.16.refs_3_ = bf16[256,512]{1,0:T(8,128)(2,1)S(1)} collective-permute-done((bf16[256,512]{1,0:T(8,128)(2,1)S(1)}, bf16[256,512]{1,0:T(8,128)(2,1)S(1)}, u32[]{:S(2)}, u32[]{:S(2)}) %collective-permute-start.16) | collective-permute-done | bytes 262176 | tf_op jit(solution)/shard_map/ppermute | solution.py:308
  119.2 0.9 finish.1
  (39 shorter events, 3.4 us)
Async XLA Ops:
  0.6 15.2 %collective-permute-start.2 = (bf16[512,256]{1,0:T(8,128)(2,1)}, bf16[512,256]{1,0:T(8,128)(2,1)S(1)}, u32[]{:S(2)}, u32[]{:S(2)}) collective-permute-start(bf16[512,256]{1,0:T(8,128)(2,1)} %refs_4_.2), channel_id=1, source_target_pairs={{0,16},{4,20},{8,24},{12,28},{16,0},{20,4},{24,8},{28,12},{1,17},{... | collective-permute-start | bytes 786440 | tf_op jit(solution)/shard_map/ppermute | solution.py:308
  3.7 12.1 %collective-permute-start.1 = (bf16[512,256]{1,0:T(8,128)(2,1)}, bf16[512,256]{1,0:T(8,128)(2,1)S(1)}, u32[]{:S(2)}, u32[]{:S(2)}) collective-permute-start(bf16[512,256]{1,0:T(8,128)(2,1)} %refs_4_.2), channel_id=1, source_target_pairs={{0,24},{4,28},{8,16},{12,20},{16,8},{20,12},{24,0},{28,4},{1,25},{... | collective-permute-start | bytes 786440 | tf_op jit(solution)/shard_map/ppermute | solution.py:308
  5.1 12.0 %collective-permute-start.3 = (bf16[512,256]{1,0:T(8,128)(2,1)}, bf16[512,256]{1,0:T(8,128)(2,1)S(1)}, u32[]{:S(2)}, u32[]{:S(2)}) collective-permute-start(bf16[512,256]{1,0:T(8,128)(2,1)} %refs_4_.2), channel_id=1, source_target_pairs={{0,8},{4,12},{8,0},{12,4},{16,24},{20,28},{24,16},{28,20},{1,9},{5... | collective-permute-start | bytes 786440 | tf_op jit(solution)/shard_map/ppermute | solution.py:308
  5.2 15.7 %collective-permute-start = (bf16[512,256]{1,0:T(8,128)(2,1)}, bf16[512,256]{1,0:T(8,128)(2,1)S(1)}, u32[]{:S(2)}, u32[]{:S(2)}) collective-permute-start(bf16[512,256]{1,0:T(8,128)(2,1)} %refs_4_.2), channel_id=1, source_target_pairs={{0,4},{4,0},{8,12},{12,8},{16,20},{20,16},{24,28},{28,24},{1,5},{5... | collective-permute-start | bytes 786440 | tf_op jit(solution)/shard_map/ppermute | solution.py:308
  5.3 0.7 copy-start.4
  6.0 0.7 copy-start.5
  17.1 1.0 copy-start.1
  17.1 3.8 %collective-permute-start.4 = (bf16[512,256]{1,0:T(8,128)(2,1)S(1)}, bf16[512,256]{1,0:T(8,128)(2,1)S(1)}, u32[]{:S(2)}, u32[]{:S(2)}) collective-permute-start(bf16[512,256]{1,0:T(8,128)(2,1)S(1)} %get-tuple-element.23.refs_5_), channel_id=1, source_target_pairs={{0,4},{4,0},{8,12},{12,8},{16,20},{20,16},{24,28},{28,24},{1,5},{5... | collective-permute-start | bytes 786440 | tf_op jit(solution)/shard_map/ppermute | solution.py:308
  17.1 3.8 %collective-permute-start.5 = (bf16[512,256]{1,0:T(8,128)(2,1)S(1)}, bf16[512,256]{1,0:T(8,128)(2,1)S(1)}, u32[]{:S(2)}, u32[]{:S(2)}) collective-permute-start(bf16[512,256]{1,0:T(8,128)(2,1)S(1)} %get-tuple-element.24.refs_6_), channel_id=1, source_target_pairs={{0,4},{4,0},{8,12},{12,8},{16,20},{20,16},{24,28},{28,24},{1,5},{5... | collective-permute-start | bytes 786440 | tf_op jit(solution)/shard_map/ppermute | solution.py:308
  17.6 3.3 %collective-permute-start.6 = (bf16[512,256]{1,0:T(8,128)(2,1)S(1)}, bf16[512,256]{1,0:T(8,128)(2,1)S(1)}, u32[]{:S(2)}, u32[]{:S(2)}) collective-permute-start(bf16[512,256]{1,0:T(8,128)(2,1)S(1)} %get-tuple-element.25.refs_7_), channel_id=1, source_target_pairs={{0,4},{4,0},{8,12},{12,8},{16,20},{20,16},{24,28},{28,24},{1,5},{5... | collective-permute-start | bytes 786440 | tf_op jit(solution)/shard_map/ppermute | solution.py:308
  22.3 11.1 %collective-permute-start.7 = (bf16[512,256]{1,0:T(8,128)(2,1)S(1)}, bf16[512,256]{1,0:T(8,128)(2,1)S(1)}, u32[]{:S(2)}, u32[]{:S(2)}) collective-permute-start(bf16[512,256]{1,0:T(8,128)(2,1)S(1)} %forward_rows.7), channel_id=1, source_target_pairs={{0,3},{1,2},{2,1},{3,0},{4,7},{5,6},{6,5},{7,4},{8,11},{9,10},{10,... | collective-permute-start | bytes 786440 | tf_op jit(solution)/shard_map/ppermute | solution.py:308
  27.3 21.3 %collective-permute-start.8 = (bf16[512,256]{1,0:T(8,128)(2,1)S(1)}, bf16[512,256]{1,0:T(8,128)(2,1)S(1)}, u32[]{:S(2)}, u32[]{:S(2)}) collective-permute-start(bf16[512,256]{1,0:T(8,128)(2,1)S(1)} %forward_rows.8), channel_id=1, source_target_pairs={{0,2},{1,3},{2,0},{3,1},{4,6},{5,7},{6,4},{7,5},{8,10},{9,11},{10,... | collective-permute-start | bytes 786440 | tf_op jit(solution)/shard_map/ppermute | solution.py:308
  28.7 19.9 %copy-start.2 = (bf16[512,256]{1,0:T(8,128)(2,1)S(1)}, bf16[512,256]{1,0:T(8,128)(2,1)}, u32[]{:S(2)}) copy-start(bf16[512,256]{1,0:T(8,128)(2,1)} %refs_5_.1) | copy-start | bytes 786436
  28.7 19.9 %copy-start.3 = (bf16[256,256]{1,0:T(8,128)(2,1)S(1)}, bf16[256,256]{1,0:T(8,128)(2,1)}, u32[]{:S(2)}) copy-start(bf16[256,256]{1,0:T(8,128)(2,1)} %refs_4_.3) | copy-start | bytes 393220
  28.7 19.9 %collective-permute-start.9 = (bf16[512,256]{1,0:T(8,128)(2,1)S(1)}, bf16[512,256]{1,0:T(8,128)(2,1)S(1)}, u32[]{:S(2)}, u32[]{:S(2)}) collective-permute-start(bf16[512,256]{1,0:T(8,128)(2,1)S(1)} %forward_rows.9), channel_id=1, source_target_pairs={{0,1},{1,0},{2,3},{3,2},{4,5},{5,4},{6,7},{7,6},{8,9},{9,8},{10,11... | collective-permute-start | bytes 786440 | tf_op jit(solution)/shard_map/ppermute | solution.py:308
  50.2 4.5 %collective-permute-start.10 = (f32[128,256]{1,0:T(8,128)S(1)}, f32[128,256]{1,0:T(8,128)S(1)}, u32[]{:S(2)}, u32[]{:S(2)}) collective-permute-start(f32[128,256]{1,0:T(8,128)S(1)} %get-tuple-element.33), channel_id=1, source_target_pairs={{0,4},{4,0},{8,12},{12,8},{16,20},{20,16},{24,28},{28,24},{1,5},{5... | collective-permute-start | bytes 393224 | tf_op jit(solution)/shard_map/ppermute | solution.py:308
  50.3 44.0 %collective-permute-start.13 = (bf16[256,512]{1,0:T(8,128)(2,1)S(1)}, bf16[256,512]{1,0:T(8,128)(2,1)S(1)}, u32[]{:S(2)}, u32[]{:S(2)}) collective-permute-start(bf16[256,512]{1,0:T(8,128)(2,1)S(1)} %get-tuple-element.34.refs_2_), channel_id=1, source_target_pairs={{0,1},{1,0},{2,3},{3,2},{4,5},{5,4},{6,7},{7,6},{8,9},{9,8},{10,11... | collective-permute-start | bytes 786440 | tf_op jit(solution)/shard_map/ppermute | solution.py:308
  50.4 48.0 %collective-permute-start.12 = (bf16[256,512]{1,0:T(8,128)(2,1)S(1)}, bf16[256,512]{1,0:T(8,128)(2,1)S(1)}, u32[]{:S(2)}, u32[]{:S(2)}) collective-permute-start(bf16[256,512]{1,0:T(8,128)(2,1)S(1)} %get-tuple-element.34.refs_2_), channel_id=1, source_target_pairs={{0,2},{1,3},{2,0},{3,1},{4,6},{5,7},{6,4},{7,5},{8,10},{9,11},{10,... | collective-permute-start | bytes 786440 | tf_op jit(solution)/shard_map/ppermute | solution.py:308
  53.4 45.0 %collective-permute-start.11 = (bf16[256,512]{1,0:T(8,128)(2,1)S(1)}, bf16[256,512]{1,0:T(8,128)(2,1)S(1)}, u32[]{:S(2)}, u32[]{:S(2)}) collective-permute-start(bf16[256,512]{1,0:T(8,128)(2,1)S(1)} %get-tuple-element.34.refs_2_), channel_id=1, source_target_pairs={{0,3},{1,2},{2,1},{3,0},{4,7},{5,6},{6,5},{7,4},{8,11},{9,10},{10,... | collective-permute-start | bytes 786440 | tf_op jit(solution)/shard_map/ppermute | solution.py:308
  94.3 4.1 %copy-start = (f32[256,256]{1,0:T(8,128)S(1)}, f32[256,256]{1,0:T(8,128)}, u32[]{:S(2)}) copy-start(f32[256,256]{1,0:T(8,128)} %keep.1.refs_5_) | copy-start | bytes 786436
  100.7 2.7 %collective-permute-start.14 = (bf16[4,256,512]{2,1,0:T(8,128)(2,1)S(1)}, bf16[4,256,512]{2,1,0:T(8,128)(2,1)S(1)}, u32[]{:S(2)}, u32[]{:S(2)}) collective-permute-start(bf16[4,256,512]{2,1,0:T(8,128)(2,1)S(1)} %backward_cols.5), channel_id=1, source_target_pairs={{0,4},{4,0},{8,12},{12,8},{16,20},{20,16},{24,28},{28,24},{1,5},{5... | collective-permute-start | bytes 3145736 | tf_op jit(solution)/shard_map/ppermute | solution.py:308
  103.7 9.2 %collective-permute-start.17 = (bf16[256,512]{1,0:T(8,128)(2,1)S(1)}, bf16[256,512]{1,0:T(8,128)(2,1)S(1)}, u32[]{:S(2)}, u32[]{:S(2)}) collective-permute-start(bf16[256,512]{1,0:T(8,128)(2,1)S(1)} %get-tuple-element.35), channel_id=1, source_target_pairs={{0,8},{4,12},{8,0},{12,4},{16,24},{20,28},{24,16},{28,20},{1,9},{5... | collective-permute-start | bytes 786440 | tf_op jit(solution)/shard_map/ppermute | solution.py:308
  105.3 13.9 %collective-permute-start.16 = (bf16[256,512]{1,0:T(8,128)(2,1)S(1)}, bf16[256,512]{1,0:T(8,128)(2,1)S(1)}, u32[]{:S(2)}, u32[]{:S(2)}) collective-permute-start(bf16[256,512]{1,0:T(8,128)(2,1)S(1)} %get-tuple-element.36), channel_id=1, source_target_pairs={{0,16},{4,20},{8,24},{12,28},{16,0},{20,4},{24,8},{28,12},{1,17},{... | collective-permute-start | bytes 786440 | tf_op jit(solution)/shard_map/ppermute | solution.py:308
  105.8 13.4 %collective-permute-start.15 = (bf16[256,512]{1,0:T(8,128)(2,1)S(1)}, bf16[256,512]{1,0:T(8,128)(2,1)S(1)}, u32[]{:S(2)}, u32[]{:S(2)}) collective-permute-start(bf16[256,512]{1,0:T(8,128)(2,1)S(1)} %get-tuple-element.37), channel_id=1, source_target_pairs={{0,24},{4,28},{8,16},{12,20},{16,8},{20,12},{24,0},{28,4},{1,25},{... | collective-permute-start | bytes 786440 | tf_op jit(solution)/shard_map/ppermute | solution.py:308

commit v5 on v3

--- a/solution.py
+++ b/solution.py
@@ -249,45 +249,25 @@
     )(*map(near, values), *after)
 
 
-def split_kernel(where, *refs, by_core):
-    outs = refs[1:] if by_core else refs[2:]
-    rows = outs[0].shape[0]
-    place = where[0] & 1 if by_core else lax.div(where[0], 2)
-    for step, out_ref in enumerate(outs):
-        at = pl.ds(pl.multiple_of((place ^ step) * rows, rows), rows)
-        out_ref[...] = refs[0][at, :] if by_core else refs[0][at, :] + refs[1][at, :]
-
-
-def split(where, values, count, by_core):
-    rows, width = values[0].shape
-    return pl.pallas_call(
-        functools.partial(split_kernel, by_core=by_core),
-        out_shape=[jax.ShapeDtypeStruct((rows // count, width), values[0].dtype)] * count,
-        in_specs=[SCALARS] + [WHOLE] * len(values),
+def total_kernel(*refs):
+    parts, out_ref = refs[:-1], refs[-1]
+    rows = out_ref.shape[0]
+    value = None
+    for part in parts:
+        for i in range(part.shape[0] // rows):
+            term = part[pl.ds(i * rows, rows), :].astype(jnp.float32)
+            value = term if value is None else value + term
+    out_ref[...] = value.astype(out_ref.dtype)
+
+
+def total(parts, rows, kind):
+    return pl.pallas_call(
+        total_kernel,
+        out_shape=jax.ShapeDtypeStruct((rows, parts[0].shape[1]), kind),
         compiler_params=params(10),
         cost_estimate=cost(0, 0),
-        name="split",
-    )(where, *values)
-
-
-def join_kernel(where, *refs, by_core):
-    parts, out_ref = refs[:-1], refs[-1]
-    rows = parts[0].shape[0]
-    place = where[0] & 1 if by_core else lax.div(where[0], 2)
-    for step, part in enumerate(parts):
-        out_ref[pl.ds(pl.multiple_of((place ^ step) * rows, rows), rows), :] = part[...]
-
-
-def join(where, parts, by_core):
-    count, (rows, width) = len(parts), parts[0].shape
-    return pl.pallas_call(
-        functools.partial(join_kernel, by_core=by_core),
-        out_shape=jax.ShapeDtypeStruct((count * rows, width), parts[0].dtype),
-        in_specs=[SCALARS] + [WHOLE] * count,
-        compiler_params=params(10),
-        cost_estimate=cost(0, 0),
-        name="join",
-    )(where, *parts)
+        name="total",
+    )(*parts)
 
 
 def swap(value, axis, size, step):
@@ -325,8 +305,10 @@
 
     pieces = {s: swap(piece, "col", n_col, s) for s in steps[:-1]}
     pieces[0] = piece
-    kept, sent = split(where, [part], 2, True)
-    part, *others = split(where, [kept, swap(sent, "row", n_row, 1)], chips, False)
+    cores = [[i for i in range(n_row) if i % 2 == core] for core in range(2)]
+    part = (part + swap(part, "row", n_row, 1)).astype(jnp.bfloat16)
+    gathered = lax.all_gather(part, "row", axis_index_groups=cores, tiled=True)
+    part = total([gathered], part.shape[0], jnp.bfloat16)
 
     soon, late = [0, 1], steps[:-2]
     early = backward(
@@ -339,11 +321,8 @@
     summed = [(kept[s] + came[s].astype(jnp.float32)).astype(jnp.bfloat16) for s in range(1, chips)]
     parts = [swap(summed[s - 1], "row", n_row, 2 * s) for s in range(chips - 1, 0, -1)]
 
-    others = gate([swap(other, "row", n_row, 2 * s) for s, other in enumerate(others, 1)], [kept])
-    part = sum(others, part)
-    part = sum([swap(part, "col", n_col, s) for s in range(1, n_col)], part)
-    half = join(where, [part] + [swap(part, "row", n_row, 2 * s) for s in range(1, chips)], False)
-    weight_grad = join(where, [half, swap(half, "row", n_row, 1)], True)
+    part = gate([part], [kept])[0]
+    weight_grad = total([part] + [swap(part, "col", n_col, s) for s in steps[:-1]], part.shape[0], jnp.float32)
     return hidden, weight_grad, finish(kept, came, parts)
 
 

time: 109 us -> 98.9 us (0.907)
  waiting for transfers between devices: 43.9 us -> 30.7 us
  blocking collectives: 0 us -> 10 us
  starting transfers between devices: 30.8 us -> 26.2 us
  Pallas kernels: 30.9 us -> 28.5 us
    ppermute x28 -> x21, waiting for transfers between devices: 43.9 us -> 30.7 us  [swap(): return lax.ppermute(value, axis, [(i, i ^ step) for i in range(size)])]
    all_gather x0 -> x1, blocking collectives: none -> 10 us  [shards(): gathered = lax.all_gather(part, 'row', axis_index_groups=cores, tiled=True)]
    ppermute x28 -> x21, starting transfers between devices: 30.8 us -> 26.2 us  [swap(): return lax.ppermute(value, axis, [(i, i ^ step) for i in range(size)])]
    pallas_call x4 -> x2, Pallas kernels: 2.95 us -> 0.84 us  [total(): pl.pallas_call(total_kernel, out_shape=jax.ShapeDtypeStruct((rows, parts[...]
  transfers between devices with their start and end apart: 28 -> 21, of which waited for: 11 -> 6; matrix products, arithmetic and copies ran while one was open for 0% -> 0% of each run, Pallas kernels for 23% -> 23%
where the time goes in v5:
time: 98.9 us; the launch traced here: 98.4 us
  waiting for transfers between devices  30.7 us (31%)
  Pallas kernels  28.5 us (29%)
  starting transfers between devices  26.2 us (26%)
  blocking collectives  10 us (10%)
  local copies, waits for them, and re-layouts  1.78 us (2%)
    ppermute x21, waiting for transfers between devices, swap(): return lax.ppermute(value, axis, [(i, i ^ step) for i in range(size)])  30.7 us
    ppermute x21, starting transfers between devices, swap(): return lax.ppermute(value, axis, [(i, i ^ step) for i in range(size)])  26.2 us
    all_gather x1, blocking collectives, shards(): gathered = lax.all_gather(part, 'row', axis_index_groups=cores, tiled=True)  10 us
    pallas_call x2, Pallas kernels, dense_rows(): pl.pallas_call(functools.partial(dense_kernel, steps=steps, window=window...  8.99 us
    pallas_call x3, Pallas kernels, backward(): pl.pallas_call(functools.partial(backward_kernel, count=count, first=firs...  8.68 us
    pallas_call x5, Pallas kernels, forward(): pl.pallas_call(functools.partial(forward_kernel, blocks=blocks, count=cou...  7.96 us
  transfers between devices with their start and end apart: 21, of which 6 were waited for; matrix products, arithmetic and copies ran while one was open for 0% of the time, Pallas kernels for 23%

profile of v5, /device:TPU:0, one launch (start us, length us, event | category | flops | bytes accessed | tf_op | source)
XLA Modules:
  0.0 98.4 jit_solution(6102514127451932492)
XLA Ops:
  0.6 3.0 %collective-permute-start.2 = (bf16[512,256]{1,0:T(8,128)(2,1)}, bf16[512,256]{1,0:T(8,128)(2,1)S(1)}, u32[]{:S(2)}, u32[]{:S(2)}) collective-permute-start(bf16[512,256]{1,0:T(8,128)(2,1)} %refs_4_.2), channel_id=1, source_target_pairs={{0,16},{4,20},{8,24},{12,28},{16,0},{20,4},{24,8},{28,12},{1,17},{... | collective-permute-start | bytes 786440 | tf_op jit(solution)/shard_map/ppermute | solution.py:274
  3.7 1.4 %collective-permute-start.1 = (bf16[512,256]{1,0:T(8,128)(2,1)}, bf16[512,256]{1,0:T(8,128)(2,1)S(1)}, u32[]{:S(2)}, u32[]{:S(2)}) collective-permute-start(bf16[512,256]{1,0:T(8,128)(2,1)} %refs_4_.2), channel_id=1, source_target_pairs={{0,24},{4,28},{8,16},{12,20},{16,8},{20,12},{24,0},{28,4},{1,25},{... | collective-permute-start | bytes 786440 | tf_op jit(solution)/shard_map/ppermute | solution.py:274
  5.3 0.7 copy-done.3
  6.0 0.7 copy-done.4
  6.6 4.5 %dense_rows.3 = (bf16[512,4096]{1,0:T(8,128)(2,1)S(1)}, bf16[512,4096]{1,0:T(8,128)(2,1)S(1)}) custom-call(s32[2]{0:T(128)S(1)} %pad_add_fusion.where, s32[16]{0:T(128)S(1)} %bitcast.13, s32[448]{0:T(512)S(1)} %bitcast.11, bf16[448,128,128]{2,1,0:T(8,128)(2,1)} %bitcast.15), custom_call_target="tpu_custom_call" | custom-call | bytes 20971520 | tf_op jit(solution)/shard_map/dense_rows/pallas_call | solution.py:98
  11.1 4.5 %dense_rows.2 = (bf16[512,4096]{1,0:T(8,128)(2,1)S(1)}, bf16[512,4096]{1,0:T(8,128)(2,1)S(1)}) custom-call(s32[2]{0:T(128)S(1)} %pad_add_fusion.where, s32[16]{0:T(128)S(1)} %bitcast.14, s32[448]{0:T(512)S(1)} %bitcast.12, bf16[448,128,128]{2,1,0:T(8,128)(2,1)} %bitcast.16), custom_call_target="tpu_custom_call" | custom-call | bytes 20971520 | tf_op jit(solution)/shard_map/dense_rows/pallas_call | solution.py:98
  15.8 1.3 %collective-permute-done.3.refs_2_ = bf16[512,256]{1,0:T(8,128)(2,1)S(1)} collective-permute-done((bf16[512,256]{1,0:T(8,128)(2,1)}, bf16[512,256]{1,0:T(8,128)(2,1)S(1)}, u32[]{:S(2)}, u32[]{:S(2)}) %collective-permute-start.3) | collective-permute-done | bytes 262176 | tf_op jit(solution)/shard_map/ppermute | solution.py:274
  18.1 2.9 %forward_rows.5 = (f32[512,256]{1,0:T(8,128)S(1)}, f32[512,256]{1,0:T(8,128)S(1)}, f32[512,256]{1,0:T(8,128)S(1)}, f32[512,256]{1,0:T(8,128)S(1)}) custom-call(s32[2]{0:T(128)S(1)} %pad_add_fusion.where, bf16[512,4096]{1,0:T(8,128)(2,1)S(1)} %get-tuple-element.18.refs_3_.refs_0_, bf16[512,4096]{1,0:T(8,128)(2,1)S(1)} %get-tuple-element.19.refs_4_.refs_1_.refs_0_, ...), custom_call_target="tpu_custom_call" | custom-call | flops 2147483648 | bytes 8388608 | tf_op jit(solution)/shard_map/forward_rows/pallas_call | solution.py:131
  21.0 1.3 %forward_rows.7 = bf16[512,256]{1,0:T(8,128)(2,1)S(1)} custom-call(s32[2]{0:T(128)S(1)} %pad_add_fusion.where, bf16[512,4096]{1,0:T(8,128)(2,1)S(1)} %get-tuple-element.18.refs_3_.refs_0_, bf16[512,256]{1,0:T(8,128)(2,1)S(1)} %collective-permute-done.refs_1_, bf16[512,256]{1,0:T(8,128)(2,1)S(1)} %collective-permute-done.4.refs_2_, ...), custom_call_target="tpu_custom_call" | custom-call | flops 536870912 | bytes 2097152 | tf_op jit(solution)/shard_map/forward_rows/pallas_call | solution.py:131
  22.3 3.8 %collective-permute-start.7 = (bf16[512,256]{1,0:T(8,128)(2,1)S(1)}, bf16[512,256]{1,0:T(8,128)(2,1)S(1)}, u32[]{:S(2)}, u32[]{:S(2)}) collective-permute-start(bf16[512,256]{1,0:T(8,128)(2,1)S(1)} %forward_rows.7), channel_id=1, source_target_pairs={{0,3},{1,2},{2,1},{3,0},{4,7},{5,6},{6,5},{7,4},{8,11},{9,10},{10,... | collective-permute-start | bytes 786440 | tf_op jit(solution)/shard_map/ppermute | solution.py:274
  26.1 1.3 %forward_rows.8 = bf16[512,256]{1,0:T(8,128)(2,1)S(1)} custom-call(s32[2]{0:T(128)S(1)} %pad_add_fusion.where, bf16[512,4096]{1,0:T(8,128)(2,1)S(1)} %get-tuple-element.19.refs_4_.refs_1_.refs_0_, bf16[512,256]{1,0:T(8,128)(2,1)S(1)} %collective-permute-done.refs_1_, bf16[512,256]{1,0:T(8,128)(2,1)S(1)} %collective-permute-done.4.refs_2_, ...), custom_call_target="tpu_custom_call" | custom-call | flops 536870912 | bytes 2097152 | tf_op jit(solution)/shard_map/forward_rows/pallas_call | solution.py:131
  27.4 1.3 %forward_rows.9 = bf16[512,256]{1,0:T(8,128)(2,1)S(1)} custom-call(s32[2]{0:T(128)S(1)} %pad_add_fusion.where, bf16[512,4096]{1,0:T(8,128)(2,1)S(1)} %get-tuple-element.20.refs_5_.refs_2_.refs_0_.refs_1_, bf16[512,256]{1,0:T(8,128)(2,1)S(1)} %collective-permute-done.refs_1_, bf16[512,256]{1,0:T(8,128)(2,1)S(1)} %collective-permute-done.4.refs_2_, ...), custom_call_target="tpu_custom_call" | custom-call | flops 536870912 | bytes 2097152 | tf_op jit(solution)/shard_map/forward_rows/pallas_call | solution.py:131
  28.7 0.7 collective-permute-start.9
  29.4 1.3 %forward_rows.6.refs_0_ = f32[512,256]{1,0:T(8,128)S(1)} custom-call(s32[2]{0:T(128)S(1)} %pad_add_fusion.where, bf16[512,4096]{1,0:T(8,128)(2,1)S(1)} %get-tuple-element.17.refs_6_.refs_3_.refs_0_, bf16[512,256]{1,0:T(8,128)(2,1)S(1)} %collective-permute-done.refs_1_, bf16[512,256]{1,0:T(8,128)(2,1)S(1)} %collective-permute-done.4.refs_2_, ...), custom_call_target="tpu_custom_call" | custom-call | flops 536870912 | bytes 2097152 | tf_op jit(solution)/shard_map/forward_rows/pallas_call | solution.py:131
  30.7 2.7 %collective-permute-done.7.refs_1_ = bf16[512,256]{1,0:T(8,128)(2,1)S(1)} collective-permute-done((bf16[512,256]{1,0:T(8,128)(2,1)S(1)}, bf16[512,256]{1,0:T(8,128)(2,1)S(1)}, u32[]{:S(2)}, u32[]{:S(2)}) %collective-permute-start.7) | collective-permute-done | bytes 262176 | tf_op jit(solution)/shard_map/ppermute | solution.py:274
  33.4 15.2 %collective-permute-done.8.refs_2_ = bf16[512,256]{1,0:T(8,128)(2,1)S(1)} collective-permute-done((bf16[512,256]{1,0:T(8,128)(2,1)S(1)}, bf16[512,256]{1,0:T(8,128)(2,1)S(1)}, u32[]{:S(2)}, u32[]{:S(2)}) %collective-permute-start.8) | collective-permute-done | bytes 262176 | tf_op jit(solution)/shard_map/ppermute | solution.py:274
  48.6 1.1 %middle.1 = (bf16[512,256]{1,0:T(8,128)(2,1)}, bf16[256,512]{1,0:T(8,128)(2,1)S(1)}, f32[256,256]{1,0:T(8,128)S(1)}) custom-call(f32[512,256]{1,0:T(8,128)S(1)} %forward_rows.6.refs_0_, bf16[512,256]{1,0:T(8,128)(2,1)S(1)} %collective-permute-done.7.refs_1_, bf16[512,256]{1,0:T(8,128)(2,1)S(1)} %collective-permute-done.8.refs_2_, ...), custom_call_target="tpu_custom_call" | custom-call | flops 201326592 | bytes 1310720 | tf_op jit(solution)/shard_map/middle/pallas_call | solution.py:164
  49.7 3.0 %collective-permute-start.12 = (bf16[256,512]{1,0:T(8,128)(2,1)S(1)}, bf16[256,512]{1,0:T(8,128)(2,1)S(1)}, u32[]{:S(2)}, u32[]{:S(2)}) collective-permute-start(bf16[256,512]{1,0:T(8,128)(2,1)S(1)} %get-tuple-element.30.refs_2_), channel_id=1, source_target_pairs={{0,2},{1,3},{2,0},{3,1},{4,6},{5,7},{6,4},{7,5},{8,10},{9,11},{10,... | collective-permute-start | bytes 786440 | tf_op jit(solution)/shard_map/ppermute | solution.py:274
  52.7 1.4 %collective-permute-start.11 = (bf16[256,512]{1,0:T(8,128)(2,1)S(1)}, bf16[256,512]{1,0:T(8,128)(2,1)S(1)}, u32[]{:S(2)}, u32[]{:S(2)}) collective-permute-start(bf16[256,512]{1,0:T(8,128)(2,1)S(1)} %get-tuple-element.30.refs_2_), channel_id=1, source_target_pairs={{0,3},{1,2},{2,1},{3,0},{4,7},{5,6},{6,5},{7,4},{8,11},{9,10},{10,... | collective-permute-start | bytes 786440 | tf_op jit(solution)/shard_map/ppermute | solution.py:274
  54.1 10.0 %all_gather.3.refs_0_ = bf16[1024,256]{1,0:T(8,128)(2,1)S(1)} all-gather(bf16[256,256]{1,0:T(8,128)(2,1)S(1)} %add_convert_fusion), channel_id=1, replica_groups={{0,8,16,24},{4,12,20,28},{1,9,17,25},{5,13,21,29},{2,10,18,26},{6,14,22..., dimensions={0}, use_global_device_ids=true | all-gather | bytes 655360 | tf_op jit(solution)/shard_map/all_gather | solution.py:310
  64.2 4.1 %backward_cols.3.refs_4_ = f32[8,256,512]{2,1,0:T(8,128)S(1)} custom-call(s32[2]{0:T(128)S(1)} %pad_add_fusion.where, bf16[512,4096]{1,0:T(8,128)(2,1)S(1)} %get-tuple-element.17.refs_6_.refs_3_.refs_0_, bf16[512,4096]{1,0:T(8,128)(2,1)S(1)} %get-tuple-element.20.refs_5_.refs_2_.refs_0_.refs_1_, bf16[256,512]{1,0:T(8,128)(2,1)S(1)} %get-tuple-element.30.refs_2_, ...), custom_call_target="tpu_custom_call" | custom-call | tf_op jit(solution)/shard_map/backward_cols/pallas_call | solution.py:201
  68.3 2.8 %collective-permute-done.12.refs_3_ = bf16[256,512]{1,0:T(8,128)(2,1)S(1)} collective-permute-done((bf16[256,512]{1,0:T(8,128)(2,1)S(1)}, bf16[256,512]{1,0:T(8,128)(2,1)S(1)}, u32[]{:S(2)}, u32[]{:S(2)}) %collective-permute-start.12) | collective-permute-done | bytes 262176 | tf_op jit(solution)/shard_map/ppermute | solution.py:274
  71.1 2.3 %backward_cols.5 = bf16[4,256,512]{2,1,0:T(8,128)(2,1)S(1)} custom-call(s32[2]{0:T(128)S(1)} %pad_add_fusion.where, bf16[512,4096]{1,0:T(8,128)(2,1)S(1)} %get-tuple-element.18.refs_3_.refs_0_, bf16[512,4096]{1,0:T(8,128)(2,1)S(1)} %get-tuple-element.19.refs_4_.refs_1_.refs_0_, bf16[256,512]{1,0:T(8,128)(2,1)S(1)} %collective-permute-done.11.refs_2_, ...), custom_call_target="tpu_custom_call" | custom-call | tf_op jit(solution)/shard_map/backward_cols/pallas_call | solution.py:201
  73.5 2.3 %backward_cols.4.refs_1_.refs_0_ = f32[4,256,512]{2,1,0:T(8,128)S(1)} custom-call(s32[2]{0:T(128)S(1)} %pad_add_fusion.where, bf16[512,4096]{1,0:T(8,128)(2,1)S(1)} %get-tuple-element.18.refs_3_.refs_0_, bf16[512,4096]{1,0:T(8,128)(2,1)S(1)} %get-tuple-element.19.refs_4_.refs_1_.refs_0_, bf16[256,512]{1,0:T(8,128)(2,1)S(1)} %collective-permute-done.11.refs_2_, ...), custom_call_target="tpu_custom_call" | custom-call | tf_op jit(solution)/shard_map/backward_cols/pallas_call | solution.py:201
  75.8 5.9 %collective-permute-start.16 = (bf16[256,256]{1,0:T(8,128)(2,1)S(1)}, bf16[256,256]{1,0:T(8,128)(2,1)S(1)}, u32[]{:S(2)}, u32[]{:S(2)}) collective-permute-start(bf16[256,256]{1,0:T(8,128)(2,1)S(1)} %gate.3.refs_0_), channel_id=1, source_target_pairs={{0,1},{1,0},{2,3},{3,2},{4,5},{5,4},{6,7},{7,6},{8,9},{9,8},{10,11... | collective-permute-start | bytes 393224 | tf_op jit(solution)/shard_map/ppermute | solution.py:274
  81.9 1.6 %collective-permute-start.20 = (bf16[256,512]{1,0:T(8,128)(2,1)S(1)}, bf16[256,512]{1,0:T(8,128)(2,1)S(1)}, u32[]{:S(2)}, u32[]{:S(2)}) collective-permute-start(bf16[256,512]{1,0:T(8,128)(2,1)S(1)} %get-tuple-element.31), channel_id=1, source_target_pairs={{0,8},{4,12},{8,0},{12,4},{16,24},{20,28},{24,16},{28,20},{1,9},{5... | collective-permute-start | bytes 786440 | tf_op jit(solution)/shard_map/ppermute | solution.py:274
  83.5 1.5 %collective-permute-start.19 = (bf16[256,512]{1,0:T(8,128)(2,1)S(1)}, bf16[256,512]{1,0:T(8,128)(2,1)S(1)}, u32[]{:S(2)}, u32[]{:S(2)}) collective-permute-start(bf16[256,512]{1,0:T(8,128)(2,1)S(1)} %get-tuple-element.32), channel_id=1, source_target_pairs={{0,16},{4,20},{8,24},{12,28},{16,0},{20,4},{24,8},{28,12},{1,17},{... | collective-permute-start | bytes 786440 | tf_op jit(solution)/shard_map/ppermute | solution.py:274
  85.5 1.1 %collective-permute-start.15 = (bf16[256,256]{1,0:T(8,128)(2,1)S(1)}, bf16[256,256]{1,0:T(8,128)(2,1)S(1)}, u32[]{:S(2)}, u32[]{:S(2)}) collective-permute-start(bf16[256,256]{1,0:T(8,128)(2,1)S(1)} %gate.3.refs_0_), channel_id=1, source_target_pairs={{0,2},{1,3},{2,0},{3,1},{4,6},{5,7},{6,4},{7,5},{8,10},{9,11},{10,... | collective-permute-start | bytes 393224 | tf_op jit(solution)/shard_map/ppermute | solution.py:274
  86.6 1.5 %collective-permute-start.14 = (bf16[256,256]{1,0:T(8,128)(2,1)S(1)}, bf16[256,256]{1,0:T(8,128)(2,1)S(1)}, u32[]{:S(2)}, u32[]{:S(2)}) collective-permute-start(bf16[256,256]{1,0:T(8,128)(2,1)S(1)} %gate.3.refs_0_), channel_id=1, source_target_pairs={{0,3},{1,2},{2,1},{3,0},{4,7},{5,6},{6,5},{7,4},{8,11},{9,10},{10,... | collective-permute-start | bytes 393224 | tf_op jit(solution)/shard_map/ppermute | solution.py:274
  88.2 8.5 %collective-permute-done.15.refs_2_ = bf16[256,256]{1,0:T(8,128)(2,1)S(1)} collective-permute-done((bf16[256,256]{1,0:T(8,128)(2,1)S(1)}, bf16[256,256]{1,0:T(8,128)(2,1)S(1)}, u32[]{:S(2)}, u32[]{:S(2)}) %collective-permute-start.15) | collective-permute-done | bytes 131104 | tf_op jit(solution)/shard_map/ppermute | solution.py:274
  96.7 0.8 total.3
  97.4 0.9 finish.1
  (40 shorter events, 2.4 us)
Async XLA Ops:
  0.6 15.2 %collective-permute-start.2 = (bf16[512,256]{1,0:T(8,128)(2,1)}, bf16[512,256]{1,0:T(8,128)(2,1)S(1)}, u32[]{:S(2)}, u32[]{:S(2)}) collective-permute-start(bf16[512,256]{1,0:T(8,128)(2,1)} %refs_4_.2), channel_id=1, source_target_pairs={{0,16},{4,20},{8,24},{12,28},{16,0},{20,4},{24,8},{28,12},{1,17},{... | collective-permute-start | bytes 786440 | tf_op jit(solution)/shard_map/ppermute | solution.py:274
  3.7 12.1 %collective-permute-start.1 = (bf16[512,256]{1,0:T(8,128)(2,1)}, bf16[512,256]{1,0:T(8,128)(2,1)S(1)}, u32[]{:S(2)}, u32[]{:S(2)}) collective-permute-start(bf16[512,256]{1,0:T(8,128)(2,1)} %refs_4_.2), channel_id=1, source_target_pairs={{0,24},{4,28},{8,16},{12,20},{16,8},{20,12},{24,0},{28,4},{1,25},{... | collective-permute-start | bytes 786440 | tf_op jit(solution)/shard_map/ppermute | solution.py:274
  5.1 12.0 %collective-permute-start.3 = (bf16[512,256]{1,0:T(8,128)(2,1)}, bf16[512,256]{1,0:T(8,128)(2,1)S(1)}, u32[]{:S(2)}, u32[]{:S(2)}) collective-permute-start(bf16[512,256]{1,0:T(8,128)(2,1)} %refs_4_.2), channel_id=1, source_target_pairs={{0,8},{4,12},{8,0},{12,4},{16,24},{20,28},{24,16},{28,20},{1,9},{5... | collective-permute-start | bytes 786440 | tf_op jit(solution)/shard_map/ppermute | solution.py:274
  5.2 15.7 %collective-permute-start = (bf16[512,256]{1,0:T(8,128)(2,1)}, bf16[512,256]{1,0:T(8,128)(2,1)S(1)}, u32[]{:S(2)}, u32[]{:S(2)}) collective-permute-start(bf16[512,256]{1,0:T(8,128)(2,1)} %refs_4_.2), channel_id=1, source_target_pairs={{0,4},{4,0},{8,12},{12,8},{16,20},{20,16},{24,28},{28,24},{1,5},{5... | collective-permute-start | bytes 786440 | tf_op jit(solution)/shard_map/ppermute | solution.py:274
  5.3 0.7 copy-start.3
  6.0 0.7 copy-start.4
  17.1 1.0 copy-start
  17.1 3.8 %collective-permute-start.4 = (bf16[512,256]{1,0:T(8,128)(2,1)S(1)}, bf16[512,256]{1,0:T(8,128)(2,1)S(1)}, u32[]{:S(2)}, u32[]{:S(2)}) collective-permute-start(bf16[512,256]{1,0:T(8,128)(2,1)S(1)} %get-tuple-element.21.refs_5_), channel_id=1, source_target_pairs={{0,4},{4,0},{8,12},{12,8},{16,20},{20,16},{24,28},{28,24},{1,5},{5... | collective-permute-start | bytes 786440 | tf_op jit(solution)/shard_map/ppermute | solution.py:274
  17.1 3.8 %collective-permute-start.5 = (bf16[512,256]{1,0:T(8,128)(2,1)S(1)}, bf16[512,256]{1,0:T(8,128)(2,1)S(1)}, u32[]{:S(2)}, u32[]{:S(2)}) collective-permute-start(bf16[512,256]{1,0:T(8,128)(2,1)S(1)} %get-tuple-element.22.refs_6_), channel_id=1, source_target_pairs={{0,4},{4,0},{8,12},{12,8},{16,20},{20,16},{24,28},{28,24},{1,5},{5... | collective-permute-start | bytes 786440 | tf_op jit(solution)/shard_map/ppermute | solution.py:274
  17.6 3.3 %collective-permute-start.6 = (bf16[512,256]{1,0:T(8,128)(2,1)S(1)}, bf16[512,256]{1,0:T(8,128)(2,1)S(1)}, u32[]{:S(2)}, u32[]{:S(2)}) collective-permute-start(bf16[512,256]{1,0:T(8,128)(2,1)S(1)} %get-tuple-element.23.refs_7_), channel_id=1, source_target_pairs={{0,4},{4,0},{8,12},{12,8},{16,20},{20,16},{24,28},{28,24},{1,5},{5... | collective-permute-start | bytes 786440 | tf_op jit(solution)/shard_map/ppermute | solution.py:274
  22.3 11.1 %collective-permute-start.7 = (bf16[512,256]{1,0:T(8,128)(2,1)S(1)}, bf16[512,256]{1,0:T(8,128)(2,1)S(1)}, u32[]{:S(2)}, u32[]{:S(2)}) collective-permute-start(bf16[512,256]{1,0:T(8,128)(2,1)S(1)} %forward_rows.7), channel_id=1, source_target_pairs={{0,3},{1,2},{2,1},{3,0},{4,7},{5,6},{6,5},{7,4},{8,11},{9,10},{10,... | collective-permute-start | bytes 786440 | tf_op jit(solution)/shard_map/ppermute | solution.py:274
  27.3 21.3 %collective-permute-start.8 = (bf16[512,256]{1,0:T(8,128)(2,1)S(1)}, bf16[512,256]{1,0:T(8,128)(2,1)S(1)}, u32[]{:S(2)}, u32[]{:S(2)}) collective-permute-start(bf16[512,256]{1,0:T(8,128)(2,1)S(1)} %forward_rows.8), channel_id=1, source_target_pairs={{0,2},{1,3},{2,0},{3,1},{4,6},{5,7},{6,4},{7,5},{8,10},{9,11},{10,... | collective-permute-start | bytes 786440 | tf_op jit(solution)/shard_map/ppermute | solution.py:274
  28.7 19.9 %copy-start.1 = (bf16[512,256]{1,0:T(8,128)(2,1)S(1)}, bf16[512,256]{1,0:T(8,128)(2,1)}, u32[]{:S(2)}) copy-start(bf16[512,256]{1,0:T(8,128)(2,1)} %refs_5_.1) | copy-start | bytes 786436
  28.7 19.9 %copy-start.2 = (bf16[256,256]{1,0:T(8,128)(2,1)S(1)}, bf16[256,256]{1,0:T(8,128)(2,1)}, u32[]{:S(2)}) copy-start(bf16[256,256]{1,0:T(8,128)(2,1)} %refs_4_.3) | copy-start | bytes 393220
  28.7 19.9 %collective-permute-start.9 = (bf16[512,256]{1,0:T(8,128)(2,1)S(1)}, bf16[512,256]{1,0:T(8,128)(2,1)S(1)}, u32[]{:S(2)}, u32[]{:S(2)}) collective-permute-start(bf16[512,256]{1,0:T(8,128)(2,1)S(1)} %forward_rows.9), channel_id=1, source_target_pairs={{0,1},{1,0},{2,3},{3,2},{4,5},{5,4},{6,7},{7,6},{8,9},{9,8},{10,11... | collective-permute-start | bytes 786440 | tf_op jit(solution)/shard_map/ppermute | solution.py:274
  49.7 4.4 %collective-permute-start.10 = (f32[256,256]{1,0:T(8,128)S(1)}, f32[256,256]{1,0:T(8,128)S(1)}, u32[]{:S(2)}, u32[]{:S(2)}) collective-permute-start(f32[256,256]{1,0:T(8,128)S(1)} %get-tuple-element.29), channel_id=1, source_target_pairs={{0,4},{4,0},{8,12},{12,8},{16,20},{20,16},{24,28},{28,24},{1,5},{5... | collective-permute-start | bytes 786440 | tf_op jit(solution)/shard_map/ppermute | solution.py:274
  49.7 14.6 %collective-permute-start.13 = (bf16[256,512]{1,0:T(8,128)(2,1)S(1)}, bf16[256,512]{1,0:T(8,128)(2,1)S(1)}, u32[]{:S(2)}, u32[]{:S(2)}) collective-permute-start(bf16[256,512]{1,0:T(8,128)(2,1)S(1)} %get-tuple-element.30.refs_2_), channel_id=1, source_target_pairs={{0,1},{1,0},{2,3},{3,2},{4,5},{5,4},{6,7},{7,6},{8,9},{9,8},{10,11... | collective-permute-start | bytes 786440 | tf_op jit(solution)/shard_map/ppermute | solution.py:274
  49.7 21.4 %collective-permute-start.12 = (bf16[256,512]{1,0:T(8,128)(2,1)S(1)}, bf16[256,512]{1,0:T(8,128)(2,1)S(1)}, u32[]{:S(2)}, u32[]{:S(2)}) collective-permute-start(bf16[256,512]{1,0:T(8,128)(2,1)S(1)} %get-tuple-element.30.refs_2_), channel_id=1, source_target_pairs={{0,2},{1,3},{2,0},{3,1},{4,6},{5,7},{6,4},{7,5},{8,10},{9,11},{10,... | collective-permute-start | bytes 786440 | tf_op jit(solution)/shard_map/ppermute | solution.py:274
  52.7 18.4 %collective-permute-start.11 = (bf16[256,512]{1,0:T(8,128)(2,1)S(1)}, bf16[256,512]{1,0:T(8,128)(2,1)S(1)}, u32[]{:S(2)}, u32[]{:S(2)}) collective-permute-start(bf16[256,512]{1,0:T(8,128)(2,1)S(1)} %get-tuple-element.30.refs_2_), channel_id=1, source_target_pairs={{0,3},{1,2},{2,1},{3,0},{4,7},{5,6},{6,5},{7,4},{8,11},{9,10},{10,... | collective-permute-start | bytes 786440 | tf_op jit(solution)/shard_map/ppermute | solution.py:274
  73.4 8.3 %collective-permute-start.17 = (bf16[4,256,512]{2,1,0:T(8,128)(2,1)S(1)}, bf16[4,256,512]{2,1,0:T(8,128)(2,1)S(1)}, u32[]{:S(2)}, u32[]{:S(2)}) collective-permute-start(bf16[4,256,512]{2,1,0:T(8,128)(2,1)S(1)} %backward_cols.5), channel_id=1, source_target_pairs={{0,4},{4,0},{8,12},{12,8},{16,20},{20,16},{24,28},{28,24},{1,5},{5... | collective-permute-start | bytes 3145736 | tf_op jit(solution)/shard_map/ppermute | solution.py:274
  75.8 10.8 %collective-permute-start.16 = (bf16[256,256]{1,0:T(8,128)(2,1)S(1)}, bf16[256,256]{1,0:T(8,128)(2,1)S(1)}, u32[]{:S(2)}, u32[]{:S(2)}) collective-permute-start(bf16[256,256]{1,0:T(8,128)(2,1)S(1)} %gate.3.refs_0_), channel_id=1, source_target_pairs={{0,1},{1,0},{2,3},{3,2},{4,5},{5,4},{6,7},{7,6},{8,9},{9,8},{10,11... | collective-permute-start | bytes 393224 | tf_op jit(solution)/shard_map/ppermute | solution.py:274
  81.9 15.5 %collective-permute-start.20 = (bf16[256,512]{1,0:T(8,128)(2,1)S(1)}, bf16[256,512]{1,0:T(8,128)(2,1)S(1)}, u32[]{:S(2)}, u32[]{:S(2)}) collective-permute-start(bf16[256,512]{1,0:T(8,128)(2,1)S(1)} %get-tuple-element.31), channel_id=1, source_target_pairs={{0,8},{4,12},{8,0},{12,4},{16,24},{20,28},{24,16},{28,20},{1,9},{5... | collective-permute-start | bytes 786440 | tf_op jit(solution)/shard_map/ppermute | solution.py:274
  83.5 13.9 %collective-permute-start.19 = (bf16[256,512]{1,0:T(8,128)(2,1)S(1)}, bf16[256,512]{1,0:T(8,128)(2,1)S(1)}, u32[]{:S(2)}, u32[]{:S(2)}) collective-permute-start(bf16[256,512]{1,0:T(8,128)(2,1)S(1)} %get-tuple-element.32), channel_id=1, source_target_pairs={{0,16},{4,20},{8,24},{12,28},{16,0},{20,4},{24,8},{28,12},{1,17},{... | collective-permute-start | bytes 786440 | tf_op jit(solution)/shard_map/ppermute | solution.py:274
  85.0 12.4 %collective-permute-start.18 = (bf16[256,512]{1,0:T(8,128)(2,1)S(1)}, bf16[256,512]{1,0:T(8,128)(2,1)S(1)}, u32[]{:S(2)}, u32[]{:S(2)}) collective-permute-start(bf16[256,512]{1,0:T(8,128)(2,1)S(1)} %get-tuple-element.33), channel_id=1, source_target_pairs={{0,24},{4,28},{8,16},{12,20},{16,8},{20,12},{24,0},{28,4},{1,25},{... | collective-permute-start | bytes 786440 | tf_op jit(solution)/shard_map/ppermute | solution.py:274
  85.5 11.2 %collective-permute-start.15 = (bf16[256,256]{1,0:T(8,128)(2,1)S(1)}, bf16[256,256]{1,0:T(8,128)(2,1)S(1)}, u32[]{:S(2)}, u32[]{:S(2)}) collective-permute-start(bf16[256,256]{1,0:T(8,128)(2,1)S(1)} %gate.3.refs_0_), channel_id=1, source_target_pairs={{0,2},{1,3},{2,0},{3,1},{4,6},{5,7},{6,4},{7,5},{8,10},{9,11},{10,... | collective-permute-start | bytes 393224 | tf_op jit(solution)/shard_map/ppermute | solution.py:274
  86.6 10.0 %collective-permute-start.14 = (bf16[256,256]{1,0:T(8,128)(2,1)S(1)}, bf16[256,256]{1,0:T(8,128)(2,1)S(1)}, u32[]{:S(2)}, u32[]{:S(2)}) collective-permute-start(bf16[256,256]{1,0:T(8,128)(2,1)S(1)} %gate.3.refs_0_), channel_id=1, source_target_pairs={{0,3},{1,2},{2,1},{3,0},{4,7},{5,6},{6,5},{7,4},{8,11},{9,10},{10,... | collective-permute-start | bytes 393224 | tf_op jit(solution)/shard_map/ppermute | solution.py:274

commit v6 on v5

--- a/solution.py
+++ b/solution.py
@@ -105,36 +105,36 @@
             pltpu.VMEM((tile, width), jnp.float32),
             pltpu.SemaphoreType.DMA((tiles,)),
         ],
-        compiler_params=params(16),
+        compiler_params=params(26),
         cost_estimate=cost(0, 5 * len(steps) * rows * width),
         name="dense_rows",
     )(where, counts, cols, pltpu.with_memory_space_constraint(adj, pltpu.HBM))
 
 
-def forward_kernel(where, *refs, blocks, count, odd, before):
-    dense, shards, sums = refs[:blocks], refs[blocks : blocks + count], refs[blocks + count :]
+def forward_kernel(where, a_ref, *refs, first, step):
+    shards, out_ref, before = refs[:-1], refs[-1], None
+    if first:
+        shards, before = shards[:-1], shards[-1]
     depth = shards[0].shape[0]
-    for i, a_ref in enumerate(dense):
-        value = sums[i][...] if before else None
-        for k, shard in enumerate(shards):
-            cols = pl.ds(pl.multiple_of((where[0] ^ (2 * k + odd)) * depth, depth), depth)
-            part = jnp.dot(a_ref[:, cols], shard[...], preferred_element_type=jnp.float32)
-            value = part if value is None else value + part
-        out_ref = sums[blocks + i if before else i]
-        out_ref[...] = value.astype(out_ref.dtype)
-
-
-def forward(where, dense, shards, odd, before, kind):
-    rows, width = dense[0].shape[0], shards[0].shape[1]
-    blocks, count = len(dense), len(shards)
-    operands = [near(x) for x in [*dense, *shards, *before]]
-    return pl.pallas_call(
-        functools.partial(forward_kernel, blocks=blocks, count=count, odd=odd, before=bool(before)),
-        out_shape=[pltpu.VMEM((rows, width), kind)] * blocks,
+    value = None if before is None else before[...]
+    for k, shard in enumerate(shards):
+        cols = pl.ds(pl.multiple_of((where[0] ^ (first + step * k)) * depth, depth), depth)
+        part = jnp.dot(a_ref[:, cols], shard[...], preferred_element_type=jnp.float32)
+        value = part if value is None else value + part
+    out_ref[...] = value.astype(out_ref.dtype)
+
+
+def forward(where, dense, shards, first, step, before, kind):
+    rows, width = dense.shape[0], shards[0].shape[1]
+    operands = [near(x) for x in [dense, *shards, *before]]
+    flops = 2 * rows * dense.shape[1] * width
+    return pl.pallas_call(
+        functools.partial(forward_kernel, first=first, step=step),
+        out_shape=pltpu.VMEM((rows, width), kind),
         in_specs=[SCALARS] + [WHOLE] * len(operands),
-        out_specs=[WHOLE] * blocks,
+        out_specs=WHOLE,
         compiler_params=params(10),
-        cost_estimate=cost(blocks * dense[0].size * width, blocks * dense[0].size),
+        cost_estimate=cost(flops, dense.size * 2),
         name="forward_rows",
     )(where, *operands)
 
@@ -249,8 +249,8 @@
     )(*map(near, values), *after)
 
 
-def total_kernel(*refs):
-    parts, out_ref = refs[:-1], refs[-1]
+def total_kernel(*refs, count):
+    parts, out_ref = refs[:count], refs[-1]
     rows = out_ref.shape[0]
     value = None
     for part in parts:
@@ -260,14 +260,15 @@
     out_ref[...] = value.astype(out_ref.dtype)
 
 
-def total(parts, rows, kind):
-    return pl.pallas_call(
-        total_kernel,
+def total(parts, rows, kind, after=()):
+    return pl.pallas_call(
+        functools.partial(total_kernel, count=len(parts)),
         out_shape=jax.ShapeDtypeStruct((rows, parts[0].shape[1]), kind),
+        in_specs=[WHOLE] * len(parts) + [UNREAD] * len(after),
         compiler_params=params(10),
         cost_estimate=cost(0, 0),
         name="total",
-    )(*parts)
+    )(*parts, *after)
 
 
 def swap(value, axis, size, step):
@@ -284,24 +285,21 @@
     where = jnp.stack([lax.axis_index("row"), lax.axis_index("col")]).astype(jnp.int32)
     steps = [*range(n_col - 1, 0, -1), 0]
 
-    dense = {}
-    for i in range(0, n_col, 2):
-        group = steps[i : i + 2]
-        dense.update(zip(group, dense_rows(where, group, counts, cols, adj, rows, col_tiles)))
-    blocks = [dense[s] for s in steps]
+    blocks = dense_rows(where, steps, counts, cols, adj, rows, col_tiles)
+    dense = dict(zip(steps, blocks))
 
     away = gate([swap(features, "row", n_row, 2 * s) for s in range(chips - 1, 0, -1)], blocks)
     even = [features, *away[::-1]]
     odd = [swap(shard, "row", n_row, 1) for shard in even]
-    halves = forward(where, blocks, even, 0, [], jnp.float32)
-
-    came = []
-    for s, block, half in zip(steps[:-1], blocks, halves):
-        share = forward(where, [block], odd, 1, [half], jnp.bfloat16)[0]
-        came.append(swap(share, "col", n_col, s))
-    own = forward(where, blocks[-1:], odd, 1, halves[-1:], jnp.float32)
+    parts = [shard for pair in zip(even, odd) for shard in pair]
+
+    half = forward(where, blocks[0], even, 0, 2, [], jnp.float32)
+    shares = [forward(where, blocks[0], odd, 1, 2, [half], jnp.bfloat16)]
+    shares += [forward(where, block, parts, 0, 1, [], jnp.bfloat16) for block in blocks[1:-1]]
+    came = [swap(share, "col", n_col, s) for s, share in zip(steps, shares)]
+    mine = forward(where, blocks[-1], parts, 0, 1, [], jnp.float32)
     scale = 1.0 / math.sqrt(rows * n_row * n_col)
-    hidden, piece, part = middle([*own, *came], weight, upstream, scale)
+    hidden, piece, part = middle([mine, *came], weight, upstream, scale)
 
     pieces = {s: swap(piece, "col", n_col, s) for s in steps[:-1]}
     pieces[0] = piece
@@ -321,9 +319,13 @@
     summed = [(kept[s] + came[s].astype(jnp.float32)).astype(jnp.bfloat16) for s in range(1, chips)]
     parts = [swap(summed[s - 1], "row", n_row, 2 * s) for s in range(chips - 1, 0, -1)]
 
-    part = gate([part], [kept])[0]
-    weight_grad = total([part] + [swap(part, "col", n_col, s) for s in steps[:-1]], part.shape[0], jnp.float32)
-    return hidden, weight_grad, finish(kept, came, parts)
+    feature_grad = finish(kept, came, parts)
+    for s in range(n_col.bit_length() - 2):
+        part = total([part, swap(part, "col", n_col, 1 << s)], part.shape[0], jnp.bfloat16, [kept])
+    came = swap(part, "col", n_col, n_col // 2)
+    done = pltpu.with_memory_space_constraint(feature_grad, pltpu.HBM)
+    weight_grad = total([part, came], part.shape[0], jnp.float32, [done])
+    return hidden, weight_grad, feature_grad
 
 
 def solution(mesh):

time: 98.9 us -> 98 us (level)
  starting transfers between devices: 26.2 us -> 28.6 us
  waiting for transfers between devices: 30.7 us -> 29 us
  Pallas kernels: 28.5 us -> 27.3 us
    ppermute x21 -> x20, starting transfers between devices: 26.2 us -> 28.6 us  [swap(): return lax.ppermute(value, axis, [(i, i ^ step) for i in range(size)])]
    ppermute x21 -> x20, waiting for transfers between devices: 30.7 us -> 29 us  [swap(): return lax.ppermute(value, axis, [(i, i ^ step) for i in range(size)])]
    pallas_call x2 -> x1, Pallas kernels: 8.99 us -> 7.79 us  [dense_rows(): pl.pallas_call(functools.partial(dense_kernel, steps=steps, window=window...]
    pallas_call x7 -> x8, Pallas kernels: 8.79 us -> 8.76 us  [the longest x5 7.93 us: forward(): pl.pallas_call(functools.partial(forward_kernel, first=first, step=step),...]
  transfers between devices with their start and end apart: 21 -> 20, of which waited for: 6 -> 7; matrix products, arithmetic and copies ran while one was open for 0% -> 0% of each run, Pallas kernels for 23% -> 22%
where the time goes in v6:
time: 98 us; the launch traced here: 97.8 us
  waiting for transfers between devices  29 us (30%)
  starting transfers between devices  28.6 us (29%)
  Pallas kernels  27.3 us (28%)
  blocking collectives  10.1 us (10%)
  local copies, waits for them, and re-layouts  1.71 us (2%)
    ppermute x20, waiting for transfers between devices, swap(): return lax.ppermute(value, axis, [(i, i ^ step) for i in range(size)])  29 us
    ppermute x20, starting transfers between devices, swap(): return lax.ppermute(value, axis, [(i, i ^ step) for i in range(size)])  28.6 us
    all_gather x1, blocking collectives, shards(): gathered = lax.all_gather(part, 'row', axis_index_groups=cores, tiled=True)  10.1 us
    pallas_call x3, Pallas kernels, backward(): pl.pallas_call(functools.partial(backward_kernel, count=count, first=firs...  8.76 us
    pallas_call x5, Pallas kernels, forward(): pl.pallas_call(functools.partial(forward_kernel, first=first, step=step),...  7.93 us
    pallas_call x1, Pallas kernels, dense_rows(): pl.pallas_call(functools.partial(dense_kernel, steps=steps, window=window...  7.79 us
  transfers between devices with their start and end apart: 20, of which 7 were waited for; matrix products, arithmetic and copies ran while one was open for 0% of the time, Pallas kernels for 22%

profile of v6, /device:TPU:0, one launch (start us, length us, event | category | flops | bytes accessed | tf_op | source)
XLA Modules:
  0.0 97.8 jit_solution(15319630278024887062)
XLA Ops:
  0.6 3.0 %collective-permute-start.3 = (bf16[512,256]{1,0:T(8,128)(2,1)}, bf16[512,256]{1,0:T(8,128)(2,1)S(1)}, u32[]{:S(2)}, u32[]{:S(2)}) collective-permute-start(bf16[512,256]{1,0:T(8,128)(2,1)} %refs_0_.7), channel_id=1, source_target_pairs={{0,8},{4,12},{8,0},{12,4},{16,24},{20,28},{24,16},{28,20},{1,9},{5... | collective-permute-start | bytes 786440 | tf_op jit(solution)/shard_map/ppermute | solution.py:275
  3.6 1.5 %collective-permute-start.2 = (bf16[512,256]{1,0:T(8,128)(2,1)}, bf16[512,256]{1,0:T(8,128)(2,1)S(1)}, u32[]{:S(2)}, u32[]{:S(2)}) collective-permute-start(bf16[512,256]{1,0:T(8,128)(2,1)} %refs_0_.7), channel_id=1, source_target_pairs={{0,16},{4,20},{8,24},{12,28},{16,0},{20,4},{24,8},{28,12},{1,17},{... | collective-permute-start | bytes 786440 | tf_op jit(solution)/shard_map/ppermute | solution.py:275
  6.6 7.8 %dense_rows.1 = (bf16[512,4096]{1,0:T(8,128)(2,1)S(1)}, bf16[512,4096]{1,0:T(8,128)(2,1)S(1)}, bf16[512,4096]{1,0:T(8,128)(2,1)S(1)}, bf16[512,4096]{1,0:T(8,128)(2,1)S(1)}) custom-call(s32[2]{0:T(128)S(1)} %pad_add_fusion.where, s32[16]{0:T(128)S(1)} %bitcast.12, s32[448]{0:T(512)S(1)} %bitcast.11, bf16[448,128,128]{2,1,0:T(8,128)(2,1)} %bitcast.13), custom_call_target="tpu_custom_call" | custom-call | bytes 41943040 | tf_op jit(solution)/shard_map/dense_rows/pallas_call | solution.py:98
  14.4 2.8 %collective-permute-done.2.refs_1_ = bf16[512,256]{1,0:T(8,128)(2,1)S(1)} collective-permute-done((bf16[512,256]{1,0:T(8,128)(2,1)}, bf16[512,256]{1,0:T(8,128)(2,1)S(1)}, u32[]{:S(2)}, u32[]{:S(2)}) %collective-permute-start.2) | collective-permute-done | bytes 262176 | tf_op jit(solution)/shard_map/ppermute | solution.py:275
  18.2 1.3 %forward_rows.6.refs_4_ = f32[512,256]{1,0:T(8,128)S(1)} custom-call(s32[2]{0:T(128)S(1)} %pad_add_fusion.where, bf16[512,4096]{1,0:T(8,128)(2,1)S(1)} %get-tuple-element.14.refs_3_.a_ref.refs_0_, bf16[512,256]{1,0:T(8,128)(2,1)S(1)} %copy-done, bf16[512,256]{1,0:T(8,128)(2,1)S(1)} %get-tuple-element.17.refs_2_.refs_1_, ...), custom_call_target="tpu_custom_call" | custom-call | flops 1073741824 | bytes 4194304 | tf_op jit(solution)/shard_map/forward_rows/pallas_call | solution.py:131
  19.5 1.8 %forward_rows.8 = bf16[512,256]{1,0:T(8,128)(2,1)S(1)} custom-call(s32[2]{0:T(128)S(1)} %pad_add_fusion.where, bf16[512,4096]{1,0:T(8,128)(2,1)S(1)} %get-tuple-element.15.refs_4_.a_ref.refs_1_, bf16[512,256]{1,0:T(8,128)(2,1)S(1)} %copy-done, bf16[512,256]{1,0:T(8,128)(2,1)S(1)} %collective-permute-done.refs_1_.refs_0_, ...), custom_call_target="tpu_custom_call" | custom-call | flops 1073741824 | bytes 4194304 | tf_op jit(solution)/shard_map/forward_rows/pallas_call | solution.py:131
  21.3 2.7 %collective-permute-start.8 = (bf16[512,256]{1,0:T(8,128)(2,1)S(1)}, bf16[512,256]{1,0:T(8,128)(2,1)S(1)}, u32[]{:S(2)}, u32[]{:S(2)}) collective-permute-start(bf16[512,256]{1,0:T(8,128)(2,1)S(1)} %forward_rows.8), channel_id=1, source_target_pairs={{0,2},{1,3},{2,0},{3,1},{4,6},{5,7},{6,4},{7,5},{8,10},{9,11},{10,... | collective-permute-start | bytes 786440 | tf_op jit(solution)/shard_map/ppermute | solution.py:275
  24.0 1.8 %forward_rows.9 = bf16[512,256]{1,0:T(8,128)(2,1)S(1)} custom-call(s32[2]{0:T(128)S(1)} %pad_add_fusion.where, bf16[512,4096]{1,0:T(8,128)(2,1)S(1)} %get-tuple-element.16.refs_5_.a_ref.refs_1_, bf16[512,256]{1,0:T(8,128)(2,1)S(1)} %copy-done, bf16[512,256]{1,0:T(8,128)(2,1)S(1)} %collective-permute-done.refs_1_.refs_0_, ...), custom_call_target="tpu_custom_call" | custom-call | flops 1073741824 | bytes 4194304 | tf_op jit(solution)/shard_map/forward_rows/pallas_call | solution.py:131
  25.8 1.6 %collective-permute-start.9 = (bf16[512,256]{1,0:T(8,128)(2,1)S(1)}, bf16[512,256]{1,0:T(8,128)(2,1)S(1)}, u32[]{:S(2)}, u32[]{:S(2)}) collective-permute-start(bf16[512,256]{1,0:T(8,128)(2,1)S(1)} %forward_rows.9), channel_id=1, source_target_pairs={{0,1},{1,0},{2,3},{3,2},{4,5},{5,4},{6,7},{7,6},{8,9},{9,8},{10,11... | collective-permute-start | bytes 786440 | tf_op jit(solution)/shard_map/ppermute | solution.py:275
  27.4 1.3 %forward_rows.7 = bf16[512,256]{1,0:T(8,128)(2,1)S(1)} custom-call(s32[2]{0:T(128)S(1)} %pad_add_fusion.where, bf16[512,4096]{1,0:T(8,128)(2,1)S(1)} %get-tuple-element.14.refs_3_.a_ref.refs_0_, bf16[512,256]{1,0:T(8,128)(2,1)S(1)} %collective-permute-done.refs_1_.refs_0_, bf16[512,256]{1,0:T(8,128)(2,1)S(1)} %collective-permute-done.4.refs_3_.refs_1_, ...), custom_call_target="tpu_custom_call" | custom-call | flops 1073741824 | bytes 4194304 | tf_op jit(solution)/shard_map/forward_rows/pallas_call | solution.py:131
  29.0 1.8 %forward_rows.5.refs_0_ = f32[512,256]{1,0:T(8,128)S(1)} custom-call(s32[2]{0:T(128)S(1)} %pad_add_fusion.where, bf16[512,4096]{1,0:T(8,128)(2,1)S(1)} %get-tuple-element.13.refs_6_.a_ref.refs_0_, bf16[512,256]{1,0:T(8,128)(2,1)S(1)} %copy-done, bf16[512,256]{1,0:T(8,128)(2,1)S(1)} %collective-permute-done.refs_1_.refs_0_, ...), custom_call_target="tpu_custom_call" | custom-call | flops 1073741824 | bytes 4194304 | tf_op jit(solution)/shard_map/forward_rows/pallas_call | solution.py:131
  30.8 6.9 %collective-permute-done.8.refs_2_ = bf16[512,256]{1,0:T(8,128)(2,1)S(1)} collective-permute-done((bf16[512,256]{1,0:T(8,128)(2,1)S(1)}, bf16[512,256]{1,0:T(8,128)(2,1)S(1)}, u32[]{:S(2)}, u32[]{:S(2)}) %collective-permute-start.8) | collective-permute-done | bytes 262176 | tf_op jit(solution)/shard_map/ppermute | solution.py:275
  37.7 6.3 %collective-permute-done.9.refs_3_ = bf16[512,256]{1,0:T(8,128)(2,1)S(1)} collective-permute-done((bf16[512,256]{1,0:T(8,128)(2,1)S(1)}, bf16[512,256]{1,0:T(8,128)(2,1)S(1)}, u32[]{:S(2)}, u32[]{:S(2)}) %collective-permute-start.9) | collective-permute-done | bytes 262176 | tf_op jit(solution)/shard_map/ppermute | solution.py:275
  44.1 1.1 %middle.1 = (bf16[512,256]{1,0:T(8,128)(2,1)}, bf16[256,512]{1,0:T(8,128)(2,1)S(1)}, f32[256,256]{1,0:T(8,128)S(1)}) custom-call(f32[512,256]{1,0:T(8,128)S(1)} %forward_rows.5.refs_0_, bf16[512,256]{1,0:T(8,128)(2,1)S(1)} %collective-permute-done.7.refs_1_, bf16[512,256]{1,0:T(8,128)(2,1)S(1)} %collective-permute-done.8.refs_2_, ...), custom_call_target="tpu_custom_call" | custom-call | flops 201326592 | bytes 1310720 | tf_op jit(solution)/shard_map/middle/pallas_call | solution.py:164
  45.1 4.2 %collective-permute-start.14 = (bf16[256,512]{1,0:T(8,128)(2,1)S(1)}, bf16[256,512]{1,0:T(8,128)(2,1)S(1)}, u32[]{:S(2)}, u32[]{:S(2)}) collective-permute-start(bf16[256,512]{1,0:T(8,128)(2,1)S(1)} %get-tuple-element.22.refs_2_), channel_id=1, source_target_pairs={{0,1},{1,0},{2,3},{3,2},{4,5},{5,4},{6,7},{7,6},{8,9},{9,8},{10,11... | collective-permute-start | bytes 786440 | tf_op jit(solution)/shard_map/ppermute | solution.py:275
  49.3 1.9 %collective-permute-start.13 = (bf16[256,512]{1,0:T(8,128)(2,1)S(1)}, bf16[256,512]{1,0:T(8,128)(2,1)S(1)}, u32[]{:S(2)}, u32[]{:S(2)}) collective-permute-start(bf16[256,512]{1,0:T(8,128)(2,1)S(1)} %get-tuple-element.22.refs_2_), channel_id=1, source_target_pairs={{0,2},{1,3},{2,0},{3,1},{4,6},{5,7},{6,4},{7,5},{8,10},{9,11},{10,... | collective-permute-start | bytes 786440 | tf_op jit(solution)/shard_map/ppermute | solution.py:275
  51.2 1.5 %collective-permute-start.12 = (bf16[256,512]{1,0:T(8,128)(2,1)S(1)}, bf16[256,512]{1,0:T(8,128)(2,1)S(1)}, u32[]{:S(2)}, u32[]{:S(2)}) collective-permute-start(bf16[256,512]{1,0:T(8,128)(2,1)S(1)} %get-tuple-element.22.refs_2_), channel_id=1, source_target_pairs={{0,3},{1,2},{2,1},{3,0},{4,7},{5,6},{6,5},{7,4},{8,11},{9,10},{10,... | collective-permute-start | bytes 786440 | tf_op jit(solution)/shard_map/ppermute | solution.py:275
  52.7 10.1 %all_gather.3.refs_0_ = bf16[1024,256]{1,0:T(8,128)(2,1)S(1)} all-gather(bf16[256,256]{1,0:T(8,128)(2,1)S(1)} %add_convert_fusion), channel_id=1, replica_groups={{0,8,16,24},{4,12,20,28},{1,9,17,25},{5,13,21,29},{2,10,18,26},{6,14,22..., dimensions={0}, use_global_device_ids=true | all-gather | bytes 655360 | tf_op jit(solution)/shard_map/all_gather | solution.py:308
  62.9 4.1 %backward_cols.3.refs_4_ = f32[8,256,512]{2,1,0:T(8,128)S(1)} custom-call(s32[2]{0:T(128)S(1)} %pad_add_fusion.where, bf16[512,4096]{1,0:T(8,128)(2,1)S(1)} %get-tuple-element.13.refs_6_.a_ref.refs_0_, bf16[512,4096]{1,0:T(8,128)(2,1)S(1)} %get-tuple-element.16.refs_5_.a_ref.refs_1_, bf16[256,512]{1,0:T(8,128)(2,1)S(1)} %get-tuple-element.22.refs_2_, ...), custom_call_target="tpu_custom_call" | custom-call | tf_op jit(solution)/shard_map/backward_cols/pallas_call | solution.py:201
  67.0 3.7 %collective-permute-done.12.refs_2_ = bf16[256,512]{1,0:T(8,128)(2,1)S(1)} collective-permute-done((bf16[256,512]{1,0:T(8,128)(2,1)S(1)}, bf16[256,512]{1,0:T(8,128)(2,1)S(1)}, u32[]{:S(2)}, u32[]{:S(2)}) %collective-permute-start.12) | collective-permute-done | bytes 262176 | tf_op jit(solution)/shard_map/ppermute | solution.py:275
  70.7 2.3 %backward_cols.5 = bf16[4,256,512]{2,1,0:T(8,128)(2,1)S(1)} custom-call(s32[2]{0:T(128)S(1)} %pad_add_fusion.where, bf16[512,4096]{1,0:T(8,128)(2,1)S(1)} %get-tuple-element.14.refs_3_.a_ref.refs_0_, bf16[512,4096]{1,0:T(8,128)(2,1)S(1)} %get-tuple-element.15.refs_4_.a_ref.refs_1_, bf16[256,512]{1,0:T(8,128)(2,1)S(1)} %collective-permute-done.12.refs_2_, ...), custom_call_target="tpu_custom_call" | custom-call | tf_op jit(solution)/shard_map/backward_cols/pallas_call | solution.py:201
  73.1 5.5 %collective-permute-start.11 = (bf16[256,256]{1,0:T(8,128)(2,1)S(1)}, bf16[256,256]{1,0:T(8,128)(2,1)S(1)}, u32[]{:S(2)}, u32[]{:S(2)}) collective-permute-start(bf16[256,256]{1,0:T(8,128)(2,1)S(1)} %total.3.refs_0_.refs_5_), channel_id=1, source_target_pairs={{0,1},{1,0},{2,3},{3,2},{4,5},{5,4},{6,7},{7,6},{8,9},{9,8},{10,11... | collective-permute-start | bytes 393224 | tf_op jit(solution)/shard_map/ppermute | solution.py:275
  78.5 2.3 %backward_cols.4.refs_2_.refs_0_ = f32[4,256,512]{2,1,0:T(8,128)S(1)} custom-call(s32[2]{0:T(128)S(1)} %pad_add_fusion.where, bf16[512,4096]{1,0:T(8,128)(2,1)S(1)} %get-tuple-element.14.refs_3_.a_ref.refs_0_, bf16[512,4096]{1,0:T(8,128)(2,1)S(1)} %get-tuple-element.15.refs_4_.a_ref.refs_1_, bf16[256,512]{1,0:T(8,128)(2,1)S(1)} %collective-permute-done.12.refs_2_, ...), custom_call_target="tpu_custom_call" | custom-call | tf_op jit(solution)/shard_map/backward_cols/pallas_call | solution.py:201
  81.1 1.3 %collective-permute-start.19 = (bf16[256,512]{1,0:T(8,128)(2,1)S(1)}, bf16[256,512]{1,0:T(8,128)(2,1)S(1)}, u32[]{:S(2)}, u32[]{:S(2)}) collective-permute-start(bf16[256,512]{1,0:T(8,128)(2,1)S(1)} %get-tuple-element.23), channel_id=1, source_target_pairs={{0,8},{4,12},{8,0},{12,4},{16,24},{20,28},{24,16},{28,20},{1,9},{5... | collective-permute-start | bytes 786440 | tf_op jit(solution)/shard_map/ppermute | solution.py:275
  82.4 0.8 collective-permute-start.18
  83.3 1.4 %collective-permute-start.17 = (bf16[256,512]{1,0:T(8,128)(2,1)S(1)}, bf16[256,512]{1,0:T(8,128)(2,1)S(1)}, u32[]{:S(2)}, u32[]{:S(2)}) collective-permute-start(bf16[256,512]{1,0:T(8,128)(2,1)S(1)} %get-tuple-element.25), channel_id=1, source_target_pairs={{0,24},{4,28},{8,16},{12,20},{16,8},{20,12},{24,0},{28,4},{1,25},{... | collective-permute-start | bytes 786440 | tf_op jit(solution)/shard_map/ppermute | solution.py:275
  84.7 2.2 %collective-permute-start.15 = (bf16[256,256]{1,0:T(8,128)(2,1)S(1)}, bf16[256,256]{1,0:T(8,128)(2,1)S(1)}, u32[]{:S(2)}, u32[]{:S(2)}) collective-permute-start(bf16[256,256]{1,0:T(8,128)(2,1)S(1)} %total.4.refs_0_), channel_id=1, source_target_pairs={{0,2},{1,3},{2,0},{3,1},{4,6},{5,7},{6,4},{7,5},{8,10},{9,11},{10,... | collective-permute-start | bytes 393224 | tf_op jit(solution)/shard_map/ppermute | solution.py:275
  87.0 3.4 %collective-permute-done.19.refs_4_ = bf16[256,512]{1,0:T(8,128)(2,1)S(1)} collective-permute-done((bf16[256,512]{1,0:T(8,128)(2,1)S(1)}, bf16[256,512]{1,0:T(8,128)(2,1)S(1)}, u32[]{:S(2)}, u32[]{:S(2)}) %collective-permute-start.19) | collective-permute-done | bytes 262176 | tf_op jit(solution)/shard_map/ppermute | solution.py:275
  90.4 4.2 %collective-permute-done.18.refs_3_ = bf16[256,512]{1,0:T(8,128)(2,1)S(1)} collective-permute-done((bf16[256,512]{1,0:T(8,128)(2,1)S(1)}, bf16[256,512]{1,0:T(8,128)(2,1)S(1)}, u32[]{:S(2)}, u32[]{:S(2)}) %collective-permute-start.18) | collective-permute-done | bytes 262176 | tf_op jit(solution)/shard_map/ppermute | solution.py:275
  94.5 1.6 %collective-permute-done.17.refs_2_ = bf16[256,512]{1,0:T(8,128)(2,1)S(1)} collective-permute-done((bf16[256,512]{1,0:T(8,128)(2,1)S(1)}, bf16[256,512]{1,0:T(8,128)(2,1)S(1)}, u32[]{:S(2)}, u32[]{:S(2)}) %collective-permute-start.17) | collective-permute-done | bytes 262176 | tf_op jit(solution)/shard_map/ppermute | solution.py:275
  96.2 0.9 finish.1.refs_2_
  97.1 0.7 total.5
  (37 shorter events, 3.2 us)
Async XLA Ops:
  0.6 13.8 %collective-permute-start.3 = (bf16[512,256]{1,0:T(8,128)(2,1)}, bf16[512,256]{1,0:T(8,128)(2,1)S(1)}, u32[]{:S(2)}, u32[]{:S(2)}) collective-permute-start(bf16[512,256]{1,0:T(8,128)(2,1)} %refs_0_.7), channel_id=1, source_target_pairs={{0,8},{4,12},{8,0},{12,4},{16,24},{20,28},{24,16},{28,20},{1,9},{5... | collective-permute-start | bytes 786440 | tf_op jit(solution)/shard_map/ppermute | solution.py:275
  3.6 13.6 %collective-permute-start.2 = (bf16[512,256]{1,0:T(8,128)(2,1)}, bf16[512,256]{1,0:T(8,128)(2,1)S(1)}, u32[]{:S(2)}, u32[]{:S(2)}) collective-permute-start(bf16[512,256]{1,0:T(8,128)(2,1)} %refs_0_.7), channel_id=1, source_target_pairs={{0,16},{4,20},{8,24},{12,28},{16,0},{20,4},{24,8},{28,12},{1,17},{... | collective-permute-start | bytes 786440 | tf_op jit(solution)/shard_map/ppermute | solution.py:275
  5.2 12.1 %collective-permute-start.1 = (bf16[512,256]{1,0:T(8,128)(2,1)}, bf16[512,256]{1,0:T(8,128)(2,1)S(1)}, u32[]{:S(2)}, u32[]{:S(2)}) collective-permute-start(bf16[512,256]{1,0:T(8,128)(2,1)} %refs_0_.7), channel_id=1, source_target_pairs={{0,24},{4,28},{8,16},{12,20},{16,8},{20,12},{24,0},{28,4},{1,25},{... | collective-permute-start | bytes 786440 | tf_op jit(solution)/shard_map/ppermute | solution.py:275
  5.2 14.3 %collective-permute-start = (bf16[512,256]{1,0:T(8,128)(2,1)}, bf16[512,256]{1,0:T(8,128)(2,1)S(1)}, u32[]{:S(2)}, u32[]{:S(2)}) collective-permute-start(bf16[512,256]{1,0:T(8,128)(2,1)} %refs_0_.7), channel_id=1, source_target_pairs={{0,4},{4,0},{8,12},{12,8},{16,20},{20,16},{24,28},{28,24},{1,5},{5... | collective-permute-start | bytes 786440 | tf_op jit(solution)/shard_map/ppermute | solution.py:275
  5.3 0.7 copy-start.3
  5.9 0.7 copy-start.4
  17.2 1.0 copy-start
  17.2 2.2 %collective-permute-start.4 = (bf16[512,256]{1,0:T(8,128)(2,1)S(1)}, bf16[512,256]{1,0:T(8,128)(2,1)S(1)}, u32[]{:S(2)}, u32[]{:S(2)}) collective-permute-start(bf16[512,256]{1,0:T(8,128)(2,1)S(1)} %get-tuple-element.17.refs_2_.refs_1_), channel_id=1, source_target_pairs={{0,4},{4,0},{8,12},{12,8},{16,20},{20,16},{24,28},{28,24},{1,5},{5... | collective-permute-start | bytes 786440 | tf_op jit(solution)/shard_map/ppermute | solution.py:275
  17.2 2.2 %collective-permute-start.5 = (bf16[512,256]{1,0:T(8,128)(2,1)S(1)}, bf16[512,256]{1,0:T(8,128)(2,1)S(1)}, u32[]{:S(2)}, u32[]{:S(2)}) collective-permute-start(bf16[512,256]{1,0:T(8,128)(2,1)S(1)} %get-tuple-element.18.refs_4_.refs_2_), channel_id=1, source_target_pairs={{0,4},{4,0},{8,12},{12,8},{16,20},{20,16},{24,28},{28,24},{1,5},{5... | collective-permute-start | bytes 786440 | tf_op jit(solution)/shard_map/ppermute | solution.py:275
  17.7 1.8 %collective-permute-start.6 = (bf16[512,256]{1,0:T(8,128)(2,1)S(1)}, bf16[512,256]{1,0:T(8,128)(2,1)S(1)}, u32[]{:S(2)}, u32[]{:S(2)}) collective-permute-start(bf16[512,256]{1,0:T(8,128)(2,1)S(1)} %get-tuple-element.19.refs_6_.refs_3_), channel_id=1, source_target_pairs={{0,4},{4,0},{8,12},{12,8},{16,20},{20,16},{24,28},{28,24},{1,5},{5... | collective-permute-start | bytes 786440 | tf_op jit(solution)/shard_map/ppermute | solution.py:275
  21.3 16.4 %collective-permute-start.8 = (bf16[512,256]{1,0:T(8,128)(2,1)S(1)}, bf16[512,256]{1,0:T(8,128)(2,1)S(1)}, u32[]{:S(2)}, u32[]{:S(2)}) collective-permute-start(bf16[512,256]{1,0:T(8,128)(2,1)S(1)} %forward_rows.8), channel_id=1, source_target_pairs={{0,2},{1,3},{2,0},{3,1},{4,6},{5,7},{6,4},{7,5},{8,10},{9,11},{10,... | collective-permute-start | bytes 786440 | tf_op jit(solution)/shard_map/ppermute | solution.py:275
  25.8 18.3 %collective-permute-start.9 = (bf16[512,256]{1,0:T(8,128)(2,1)S(1)}, bf16[512,256]{1,0:T(8,128)(2,1)S(1)}, u32[]{:S(2)}, u32[]{:S(2)}) collective-permute-start(bf16[512,256]{1,0:T(8,128)(2,1)S(1)} %forward_rows.9), channel_id=1, source_target_pairs={{0,1},{1,0},{2,3},{3,2},{4,5},{5,4},{6,7},{7,6},{8,9},{9,8},{10,11... | collective-permute-start | bytes 786440 | tf_op jit(solution)/shard_map/ppermute | solution.py:275
  28.7 15.4 %copy-start.1 = (bf16[512,256]{1,0:T(8,128)(2,1)S(1)}, bf16[512,256]{1,0:T(8,128)(2,1)}, u32[]{:S(2)}) copy-start(bf16[512,256]{1,0:T(8,128)(2,1)} %refs_5_.1) | copy-start | bytes 786436
  28.7 15.3 %copy-start.2 = (bf16[256,256]{1,0:T(8,128)(2,1)S(1)}, bf16[256,256]{1,0:T(8,128)(2,1)}, u32[]{:S(2)}) copy-start(bf16[256,256]{1,0:T(8,128)(2,1)} %refs_4_.1) | copy-start | bytes 393220
  28.7 15.3 %collective-permute-start.7 = (bf16[512,256]{1,0:T(8,128)(2,1)S(1)}, bf16[512,256]{1,0:T(8,128)(2,1)S(1)}, u32[]{:S(2)}, u32[]{:S(2)}) collective-permute-start(bf16[512,256]{1,0:T(8,128)(2,1)S(1)} %forward_rows.7), channel_id=1, source_target_pairs={{0,3},{1,2},{2,1},{3,0},{4,7},{5,6},{6,5},{7,4},{8,11},{9,10},{10,... | collective-permute-start | bytes 786440 | tf_op jit(solution)/shard_map/ppermute | solution.py:275
  45.1 7.6 %collective-permute-start.10 = (f32[256,256]{1,0:T(8,128)S(1)}, f32[256,256]{1,0:T(8,128)S(1)}, u32[]{:S(2)}, u32[]{:S(2)}) collective-permute-start(f32[256,256]{1,0:T(8,128)S(1)} %get-tuple-element.21), channel_id=1, source_target_pairs={{0,4},{4,0},{8,12},{12,8},{16,20},{20,16},{24,28},{28,24},{1,5},{5... | collective-permute-start | bytes 786440 | tf_op jit(solution)/shard_map/ppermute | solution.py:275
  45.1 17.7 %collective-permute-start.14 = (bf16[256,512]{1,0:T(8,128)(2,1)S(1)}, bf16[256,512]{1,0:T(8,128)(2,1)S(1)}, u32[]{:S(2)}, u32[]{:S(2)}) collective-permute-start(bf16[256,512]{1,0:T(8,128)(2,1)S(1)} %get-tuple-element.22.refs_2_), channel_id=1, source_target_pairs={{0,1},{1,0},{2,3},{3,2},{4,5},{5,4},{6,7},{7,6},{8,9},{9,8},{10,11... | collective-permute-start | bytes 786440 | tf_op jit(solution)/shard_map/ppermute | solution.py:275
  49.3 17.7 %collective-permute-start.13 = (bf16[256,512]{1,0:T(8,128)(2,1)S(1)}, bf16[256,512]{1,0:T(8,128)(2,1)S(1)}, u32[]{:S(2)}, u32[]{:S(2)}) collective-permute-start(bf16[256,512]{1,0:T(8,128)(2,1)S(1)} %get-tuple-element.22.refs_2_), channel_id=1, source_target_pairs={{0,2},{1,3},{2,0},{3,1},{4,6},{5,7},{6,4},{7,5},{8,10},{9,11},{10,... | collective-permute-start | bytes 786440 | tf_op jit(solution)/shard_map/ppermute | solution.py:275
  51.2 19.5 %collective-permute-start.12 = (bf16[256,512]{1,0:T(8,128)(2,1)S(1)}, bf16[256,512]{1,0:T(8,128)(2,1)S(1)}, u32[]{:S(2)}, u32[]{:S(2)}) collective-permute-start(bf16[256,512]{1,0:T(8,128)(2,1)S(1)} %get-tuple-element.22.refs_2_), channel_id=1, source_target_pairs={{0,3},{1,2},{2,1},{3,0},{4,7},{5,6},{6,5},{7,4},{8,11},{9,10},{10,... | collective-permute-start | bytes 786440 | tf_op jit(solution)/shard_map/ppermute | solution.py:275
  73.0 7.9 %collective-permute-start.16 = (bf16[4,256,512]{2,1,0:T(8,128)(2,1)S(1)}, bf16[4,256,512]{2,1,0:T(8,128)(2,1)S(1)}, u32[]{:S(2)}, u32[]{:S(2)}) collective-permute-start(bf16[4,256,512]{2,1,0:T(8,128)(2,1)S(1)} %backward_cols.5), channel_id=1, source_target_pairs={{0,4},{4,0},{8,12},{12,8},{16,20},{20,16},{24,28},{28,24},{1,5},{5... | collective-permute-start | bytes 3145736 | tf_op jit(solution)/shard_map/ppermute | solution.py:275
  73.1 11.6 %collective-permute-start.11 = (bf16[256,256]{1,0:T(8,128)(2,1)S(1)}, bf16[256,256]{1,0:T(8,128)(2,1)S(1)}, u32[]{:S(2)}, u32[]{:S(2)}) collective-permute-start(bf16[256,256]{1,0:T(8,128)(2,1)S(1)} %total.3.refs_0_.refs_5_), channel_id=1, source_target_pairs={{0,1},{1,0},{2,3},{3,2},{4,5},{5,4},{6,7},{7,6},{8,9},{9,8},{10,11... | collective-permute-start | bytes 393224 | tf_op jit(solution)/shard_map/ppermute | solution.py:275
  81.1 9.2 %collective-permute-start.19 = (bf16[256,512]{1,0:T(8,128)(2,1)S(1)}, bf16[256,512]{1,0:T(8,128)(2,1)S(1)}, u32[]{:S(2)}, u32[]{:S(2)}) collective-permute-start(bf16[256,512]{1,0:T(8,128)(2,1)S(1)} %get-tuple-element.23), channel_id=1, source_target_pairs={{0,8},{4,12},{8,0},{12,4},{16,24},{20,28},{24,16},{28,20},{1,9},{5... | collective-permute-start | bytes 786440 | tf_op jit(solution)/shard_map/ppermute | solution.py:275
  82.4 12.1 %collective-permute-start.18 = (bf16[256,512]{1,0:T(8,128)(2,1)S(1)}, bf16[256,512]{1,0:T(8,128)(2,1)S(1)}, u32[]{:S(2)}, u32[]{:S(2)}) collective-permute-start(bf16[256,512]{1,0:T(8,128)(2,1)S(1)} %get-tuple-element.24), channel_id=1, source_target_pairs={{0,16},{4,20},{8,24},{12,28},{16,0},{20,4},{24,8},{28,12},{1,17},{... | collective-permute-start | bytes 786440 | tf_op jit(solution)/shard_map/ppermute | solution.py:275
  83.3 12.9 %collective-permute-start.17 = (bf16[256,512]{1,0:T(8,128)(2,1)S(1)}, bf16[256,512]{1,0:T(8,128)(2,1)S(1)}, u32[]{:S(2)}, u32[]{:S(2)}) collective-permute-start(bf16[256,512]{1,0:T(8,128)(2,1)S(1)} %get-tuple-element.25), channel_id=1, source_target_pairs={{0,24},{4,28},{8,16},{12,20},{16,8},{20,12},{24,0},{28,4},{1,25},{... | collective-permute-start | bytes 786440 | tf_op jit(solution)/shard_map/ppermute | solution.py:275
  84.7 12.4 %collective-permute-start.15 = (bf16[256,256]{1,0:T(8,128)(2,1)S(1)}, bf16[256,256]{1,0:T(8,128)(2,1)S(1)}, u32[]{:S(2)}, u32[]{:S(2)}) collective-permute-start(bf16[256,256]{1,0:T(8,128)(2,1)S(1)} %total.4.refs_0_), channel_id=1, source_target_pairs={{0,2},{1,3},{2,0},{3,1},{4,6},{5,7},{6,4},{7,5},{8,10},{9,11},{10,... | collective-permute-start | bytes 393224 | tf_op jit(solution)/shard_map/ppermute | solution.py:275

commit v7 on v6

--- a/solution.py
+++ b/solution.py
@@ -108,7 +108,7 @@
         compiler_params=params(26),
         cost_estimate=cost(0, 5 * len(steps) * rows * width),
         name="dense_rows",
-    )(where, counts, cols, pltpu.with_memory_space_constraint(adj, pltpu.HBM))
+    )(where, *[pltpu.with_memory_space_constraint(x, pltpu.HBM) for x in (counts, cols, adj)])
 
 
 def forward_kernel(where, a_ref, *refs, first, step):
@@ -174,17 +174,17 @@
     )(*parts, weight, upstream)
 
 
-def backward_kernel(where, *refs, count, first, before, n_row):
+def backward_kernel(where, *refs, count, steps, before):
     dense, pieces = refs[:count], refs[count : 2 * count]
     out_ref = refs[-1]
     columns, _, depth = out_ref.shape
-    half = n_row // 2
 
     def one(j, carry):
-        at = first + j
-        step = 2 * lax.rem(at, half) + (at < half).astype(jnp.int32)
+        step = jnp.int32(steps[0])
+        for i in range(1, len(steps)):
+            step = jnp.where(j == i, steps[i], step)
         cols = pl.ds(pl.multiple_of((where[0] ^ step) * depth, depth), depth)
-        value = refs[2 * count][at] if before else None
+        value = refs[2 * count][step] if before else None
         for a_ref, piece in zip(dense, pieces):
             part = jnp.dot(piece[...], a_ref[:, cols], preferred_element_type=jnp.float32)
             value = part if value is None else value + part
@@ -194,15 +194,13 @@
     lax.fori_loop(0, columns, one, 0)
 
 
-def backward(where, dense, pieces, first, columns, n_row, depth, before, kind, after=()):
+def backward(where, dense, pieces, steps, depth, before, kind, after=()):
     count = len(pieces)
-    width, rows = pieces[0].shape
+    width, _ = pieces[0].shape
     operands = [near(x) for x in [*dense, *pieces] + ([] if before is None else [before])]
     return pl.pallas_call(
-        functools.partial(
-            backward_kernel, count=count, first=first, before=before is not None, n_row=n_row
-        ),
-        out_shape=pltpu.VMEM((columns, width, depth), kind),
+        functools.partial(backward_kernel, count=count, steps=steps, before=before is not None),
+        out_shape=pltpu.VMEM((len(steps), width, depth), kind),
         in_specs=[SCALARS] + [WHOLE] * len(operands) + [UNREAD] * len(after),
         out_specs=WHOLE,
         compiler_params=params(10),
@@ -308,16 +306,16 @@
     gathered = lax.all_gather(part, "row", axis_index_groups=cores, tiled=True)
     part = total([gathered], part.shape[0], jnp.bfloat16)
 
-    soon, late = [0, 1], steps[:-2]
-    early = backward(
-        where, [dense[s] for s in soon], [pieces[s] for s in soon], 0, n_row, n_row, depth, None, jnp.float32
-    )
-    last = functools.partial(backward, where, [dense[s] for s in late], [pieces[s] for s in late])
-    sent = last(0, chips, n_row, depth, early, jnp.bfloat16, [part])
-    kept = last(chips, chips, n_row, depth, early, jnp.float32)
+    every = list(range(n_row))
+    sums = None
+    for group in [[0, 1], *[[s] for s in range(2, n_col - 1)]]:
+        sums = backward(where, [dense[s] for s in group], [pieces[s] for s in group], every, depth, sums, jnp.float32)
+    last = functools.partial(backward, where, [dense[n_col - 1]], [pieces[n_col - 1]])
+    sent = last(every[1::2], depth, sums, jnp.bfloat16, [part])
+    kept = last(every[::2], depth, sums, jnp.float32)
     came = swap(sent, "row", n_row, 1)
-    summed = [(kept[s] + came[s].astype(jnp.float32)).astype(jnp.bfloat16) for s in range(1, chips)]
-    parts = [swap(summed[s - 1], "row", n_row, 2 * s) for s in range(chips - 1, 0, -1)]
+    summed = [(kept[c] + came[c].astype(jnp.float32)).astype(jnp.bfloat16) for c in range(1, chips)]
+    parts = [swap(summed[c - 1], "row", n_row, 2 * c) for c in range(chips - 1, 0, -1)]
 
     feature_grad = finish(kept, came, parts)
     for s in range(n_col.bit_length() - 2):

time: 98 us -> 96.9 us (0.989)
  waiting for transfers between devices: 29 us -> 27.3 us
  Pallas kernels: 27.3 us -> 28.7 us
  local copies, waits for them, and re-layouts: 1.71 us -> 0.38 us
    pallas_call x3 -> x4, Pallas kernels: 8.76 us -> 10.6 us  [backward(): pl.pallas_call(functools.partial(backward_kernel, count=count, steps=step...]
    ppermute x20, waiting for transfers between devices: 29 us -> 27.3 us  [swap(): return lax.ppermute(value, axis, [(i, i ^ step) for i in range(size)])]
    unnamed x10 -> x6, local copies, waits for them, and re-layouts: 1.71 us -> 0.38 us
  transfers between devices with their start and end apart: 20 -> 20, of which waited for: 7 -> 7; matrix products, arithmetic and copies ran while one was open for 0% -> 0% of each run, Pallas kernels for 22% -> 24%
where the time goes in v7:
time: 96.9 us; the launch traced here: 96.7 us
  starting transfers between devices  29.1 us (30%)
  Pallas kernels  28.7 us (30%)
  waiting for transfers between devices  27.3 us (28%)
  blocking collectives  10.1 us (10%)
    ppermute x20, starting transfers between devices, swap(): return lax.ppermute(value, axis, [(i, i ^ step) for i in range(size)])  29.1 us
    ppermute x20, waiting for transfers between devices, swap(): return lax.ppermute(value, axis, [(i, i ^ step) for i in range(size)])  27.3 us
    pallas_call x4, Pallas kernels, backward(): pl.pallas_call(functools.partial(backward_kernel, count=count, steps=step...  10.6 us
    all_gather x1, blocking collectives, shards(): gathered = lax.all_gather(part, 'row', axis_index_groups=cores, tiled=True)  10.1 us
    pallas_call x5, Pallas kernels, forward(): pl.pallas_call(functools.partial(forward_kernel, first=first, step=step),...  7.94 us
    pallas_call x1, Pallas kernels, dense_rows(): pl.pallas_call(functools.partial(dense_kernel, steps=steps, window=window...  7.32 us
  transfers between devices with their start and end apart: 20, of which 7 were waited for; matrix products, arithmetic and copies ran while one was open for 0% of the time, Pallas kernels for 24%

profile of v7, /device:TPU:0, one launch (start us, length us, event | category | flops | bytes accessed | tf_op | source)
XLA Modules:
  0.0 96.7 jit_solution(843612724353983247)
XLA Ops:
  0.6 3.0 %collective-permute-start.3 = (bf16[512,256]{1,0:T(8,128)(2,1)}, bf16[512,256]{1,0:T(8,128)(2,1)S(1)}, u32[]{:S(2)}, u32[]{:S(2)}) collective-permute-start(bf16[512,256]{1,0:T(8,128)(2,1)} %refs_0_.7), channel_id=1, source_target_pairs={{0,8},{4,12},{8,0},{12,4},{16,24},{20,28},{24,16},{28,20},{1,9},{5... | collective-permute-start | bytes 786440 | tf_op jit(solution)/shard_map/ppermute | solution.py:273
  3.6 1.5 %collective-permute-start.2 = (bf16[512,256]{1,0:T(8,128)(2,1)}, bf16[512,256]{1,0:T(8,128)(2,1)S(1)}, u32[]{:S(2)}, u32[]{:S(2)}) collective-permute-start(bf16[512,256]{1,0:T(8,128)(2,1)} %refs_0_.7), channel_id=1, source_target_pairs={{0,16},{4,20},{8,24},{12,28},{16,0},{20,4},{24,8},{28,12},{1,17},{... | collective-permute-start | bytes 786440 | tf_op jit(solution)/shard_map/ppermute | solution.py:273
  5.3 7.3 %dense_rows.1 = (bf16[512,4096]{1,0:T(8,128)(2,1)S(1)}, bf16[512,4096]{1,0:T(8,128)(2,1)S(1)}, bf16[512,4096]{1,0:T(8,128)(2,1)S(1)}, bf16[512,4096]{1,0:T(8,128)(2,1)S(1)}) custom-call(s32[2]{0:T(128)S(1)} %pad_add_fusion.where, s32[16]{0:T(128)} %bitcast.13, s32[448]{0:T(512)} %bitcast.12, bf16[448,128,128]{2,1,0:T(8,128)(2,1)} %bitcast.11), custom_call_target="tpu_custom_call" | custom-call | bytes 41943040 | tf_op jit(solution)/shard_map/dense_rows/pallas_call | solution.py:98
  12.6 4.6 %collective-permute-done.2.refs_1_ = bf16[512,256]{1,0:T(8,128)(2,1)S(1)} collective-permute-done((bf16[512,256]{1,0:T(8,128)(2,1)}, bf16[512,256]{1,0:T(8,128)(2,1)S(1)}, u32[]{:S(2)}, u32[]{:S(2)}) %collective-permute-start.2) | collective-permute-done | bytes 262176 | tf_op jit(solution)/shard_map/ppermute | solution.py:273
  18.2 1.3 %forward_rows.6.refs_4_ = f32[512,256]{1,0:T(8,128)S(1)} custom-call(s32[2]{0:T(128)S(1)} %pad_add_fusion.where, bf16[512,4096]{1,0:T(8,128)(2,1)S(1)} %get-tuple-element.14.refs_3_.a_ref.refs_0_, bf16[512,256]{1,0:T(8,128)(2,1)S(1)} %copy-done, bf16[512,256]{1,0:T(8,128)(2,1)S(1)} %get-tuple-element.17.refs_2_.refs_1_, ...), custom_call_target="tpu_custom_call" | custom-call | flops 1073741824 | bytes 4194304 | tf_op jit(solution)/shard_map/forward_rows/pallas_call | solution.py:131
  19.5 1.8 %forward_rows.8 = bf16[512,256]{1,0:T(8,128)(2,1)S(1)} custom-call(s32[2]{0:T(128)S(1)} %pad_add_fusion.where, bf16[512,4096]{1,0:T(8,128)(2,1)S(1)} %get-tuple-element.15.refs_4_.a_ref.refs_0_, bf16[512,256]{1,0:T(8,128)(2,1)S(1)} %copy-done, bf16[512,256]{1,0:T(8,128)(2,1)S(1)} %collective-permute-done.refs_1_.refs_0_, ...), custom_call_target="tpu_custom_call" | custom-call | flops 1073741824 | bytes 4194304 | tf_op jit(solution)/shard_map/forward_rows/pallas_call | solution.py:131
  21.3 2.7 %collective-permute-start.8 = (bf16[512,256]{1,0:T(8,128)(2,1)S(1)}, bf16[512,256]{1,0:T(8,128)(2,1)S(1)}, u32[]{:S(2)}, u32[]{:S(2)}) collective-permute-start(bf16[512,256]{1,0:T(8,128)(2,1)S(1)} %forward_rows.8), channel_id=1, source_target_pairs={{0,2},{1,3},{2,0},{3,1},{4,6},{5,7},{6,4},{7,5},{8,10},{9,11},{10,... | collective-permute-start | bytes 786440 | tf_op jit(solution)/shard_map/ppermute | solution.py:273
  24.0 1.8 %forward_rows.9 = bf16[512,256]{1,0:T(8,128)(2,1)S(1)} custom-call(s32[2]{0:T(128)S(1)} %pad_add_fusion.where, bf16[512,4096]{1,0:T(8,128)(2,1)S(1)} %get-tuple-element.16.refs_5_.a_ref.refs_1_, bf16[512,256]{1,0:T(8,128)(2,1)S(1)} %copy-done, bf16[512,256]{1,0:T(8,128)(2,1)S(1)} %collective-permute-done.refs_1_.refs_0_, ...), custom_call_target="tpu_custom_call" | custom-call | flops 1073741824 | bytes 4194304 | tf_op jit(solution)/shard_map/forward_rows/pallas_call | solution.py:131
  25.8 1.6 %collective-permute-start.9 = (bf16[512,256]{1,0:T(8,128)(2,1)S(1)}, bf16[512,256]{1,0:T(8,128)(2,1)S(1)}, u32[]{:S(2)}, u32[]{:S(2)}) collective-permute-start(bf16[512,256]{1,0:T(8,128)(2,1)S(1)} %forward_rows.9), channel_id=1, source_target_pairs={{0,1},{1,0},{2,3},{3,2},{4,5},{5,4},{6,7},{7,6},{8,9},{9,8},{10,11... | collective-permute-start | bytes 786440 | tf_op jit(solution)/shard_map/ppermute | solution.py:273
  27.4 1.3 %forward_rows.7 = bf16[512,256]{1,0:T(8,128)(2,1)S(1)} custom-call(s32[2]{0:T(128)S(1)} %pad_add_fusion.where, bf16[512,4096]{1,0:T(8,128)(2,1)S(1)} %get-tuple-element.14.refs_3_.a_ref.refs_0_, bf16[512,256]{1,0:T(8,128)(2,1)S(1)} %collective-permute-done.refs_1_.refs_0_, bf16[512,256]{1,0:T(8,128)(2,1)S(1)} %collective-permute-done.4.refs_3_.refs_1_, ...), custom_call_target="tpu_custom_call" | custom-call | flops 1073741824 | bytes 4194304 | tf_op jit(solution)/shard_map/forward_rows/pallas_call | solution.py:131
  29.0 1.8 %forward_rows.5.refs_0_ = f32[512,256]{1,0:T(8,128)S(1)} custom-call(s32[2]{0:T(128)S(1)} %pad_add_fusion.where, bf16[512,4096]{1,0:T(8,128)(2,1)S(1)} %get-tuple-element.13.refs_6_.a_ref.refs_0_, bf16[512,256]{1,0:T(8,128)(2,1)S(1)} %copy-done, bf16[512,256]{1,0:T(8,128)(2,1)S(1)} %collective-permute-done.refs_1_.refs_0_, ...), custom_call_target="tpu_custom_call" | custom-call | flops 1073741824 | bytes 4194304 | tf_op jit(solution)/shard_map/forward_rows/pallas_call | solution.py:131
  30.8 6.9 %collective-permute-done.8.refs_2_ = bf16[512,256]{1,0:T(8,128)(2,1)S(1)} collective-permute-done((bf16[512,256]{1,0:T(8,128)(2,1)S(1)}, bf16[512,256]{1,0:T(8,128)(2,1)S(1)}, u32[]{:S(2)}, u32[]{:S(2)}) %collective-permute-start.8) | collective-permute-done | bytes 262176 | tf_op jit(solution)/shard_map/ppermute | solution.py:273
  37.7 6.3 %collective-permute-done.9.refs_3_ = bf16[512,256]{1,0:T(8,128)(2,1)S(1)} collective-permute-done((bf16[512,256]{1,0:T(8,128)(2,1)S(1)}, bf16[512,256]{1,0:T(8,128)(2,1)S(1)}, u32[]{:S(2)}, u32[]{:S(2)}) %collective-permute-start.9) | collective-permute-done | bytes 262176 | tf_op jit(solution)/shard_map/ppermute | solution.py:273
  44.1 1.1 %middle.1 = (bf16[512,256]{1,0:T(8,128)(2,1)}, bf16[256,512]{1,0:T(8,128)(2,1)S(1)}, f32[256,256]{1,0:T(8,128)S(1)}) custom-call(f32[512,256]{1,0:T(8,128)S(1)} %forward_rows.5.refs_0_, bf16[512,256]{1,0:T(8,128)(2,1)S(1)} %collective-permute-done.7.refs_1_, bf16[512,256]{1,0:T(8,128)(2,1)S(1)} %collective-permute-done.8.refs_2_, ...), custom_call_target="tpu_custom_call" | custom-call | flops 201326592 | bytes 1310720 | tf_op jit(solution)/shard_map/middle/pallas_call | solution.py:164
  45.1 4.2 %collective-permute-start.14 = (bf16[256,512]{1,0:T(8,128)(2,1)S(1)}, bf16[256,512]{1,0:T(8,128)(2,1)S(1)}, u32[]{:S(2)}, u32[]{:S(2)}) collective-permute-start(bf16[256,512]{1,0:T(8,128)(2,1)S(1)} %get-tuple-element.22.refs_2_), channel_id=1, source_target_pairs={{0,1},{1,0},{2,3},{3,2},{4,5},{5,4},{6,7},{7,6},{8,9},{9,8},{10,11... | collective-permute-start | bytes 786440 | tf_op jit(solution)/shard_map/ppermute | solution.py:273
  49.3 1.9 %collective-permute-start.13 = (bf16[256,512]{1,0:T(8,128)(2,1)S(1)}, bf16[256,512]{1,0:T(8,128)(2,1)S(1)}, u32[]{:S(2)}, u32[]{:S(2)}) collective-permute-start(bf16[256,512]{1,0:T(8,128)(2,1)S(1)} %get-tuple-element.22.refs_2_), channel_id=1, source_target_pairs={{0,2},{1,3},{2,0},{3,1},{4,6},{5,7},{6,4},{7,5},{8,10},{9,11},{10,... | collective-permute-start | bytes 786440 | tf_op jit(solution)/shard_map/ppermute | solution.py:273
  51.2 1.5 %collective-permute-start.12 = (bf16[256,512]{1,0:T(8,128)(2,1)S(1)}, bf16[256,512]{1,0:T(8,128)(2,1)S(1)}, u32[]{:S(2)}, u32[]{:S(2)}) collective-permute-start(bf16[256,512]{1,0:T(8,128)(2,1)S(1)} %get-tuple-element.22.refs_2_), channel_id=1, source_target_pairs={{0,3},{1,2},{2,1},{3,0},{4,7},{5,6},{6,5},{7,4},{8,11},{9,10},{10,... | collective-permute-start | bytes 786440 | tf_op jit(solution)/shard_map/ppermute | solution.py:273
  52.7 10.1 %all_gather.3.refs_0_ = bf16[1024,256]{1,0:T(8,128)(2,1)S(1)} all-gather(bf16[256,256]{1,0:T(8,128)(2,1)S(1)} %add_convert_fusion), channel_id=1, replica_groups={{0,8,16,24},{4,12,20,28},{1,9,17,25},{5,13,21,29},{2,10,18,26},{6,14,22..., dimensions={0}, use_global_device_ids=true | all-gather | bytes 655360 | tf_op jit(solution)/shard_map/all_gather | solution.py:306
  62.9 4.1 %backward_cols.4.refs_2_ = f32[8,256,512]{2,1,0:T(8,128)S(1)} custom-call(s32[2]{0:T(128)S(1)} %pad_add_fusion.where, bf16[512,4096]{1,0:T(8,128)(2,1)S(1)} %get-tuple-element.13.refs_6_.a_ref.refs_0_, bf16[512,4096]{1,0:T(8,128)(2,1)S(1)} %get-tuple-element.16.refs_5_.a_ref.refs_1_, bf16[256,512]{1,0:T(8,128)(2,1)S(1)} %get-tuple-element.22.refs_2_, ...), custom_call_target="tpu_custom_call" | custom-call | tf_op jit(solution)/shard_map/backward_cols/pallas_call | solution.py:201
  66.9 3.0 %backward_cols.5.refs_2_ = f32[8,256,512]{2,1,0:T(8,128)S(1)} custom-call(s32[2]{0:T(128)S(1)} %pad_add_fusion.where, bf16[512,4096]{1,0:T(8,128)(2,1)S(1)} %get-tuple-element.15.refs_4_.a_ref.refs_0_, bf16[256,512]{1,0:T(8,128)(2,1)S(1)} %collective-permute-done.13.refs_1_, f32[8,256,512]{2,1,0:T(8,128)S(1)} %backward_cols.4.refs_2_), custom_call_target="tpu_custom_call" | custom-call | tf_op jit(solution)/shard_map/backward_cols/pallas_call | solution.py:201
  70.0 0.7 collective-permute-done.12.refs_1_
  70.7 1.8 %backward_cols.7 = bf16[4,256,512]{2,1,0:T(8,128)(2,1)S(1)} custom-call(s32[2]{0:T(128)S(1)} %pad_add_fusion.where, bf16[512,4096]{1,0:T(8,128)(2,1)S(1)} %get-tuple-element.14.refs_3_.a_ref.refs_0_, bf16[256,512]{1,0:T(8,128)(2,1)S(1)} %collective-permute-done.12.refs_1_, f32[8,256,512]{2,1,0:T(8,128)S(1)} %backward_cols.5.refs_2_, ...), custom_call_target="tpu_custom_call" | custom-call | tf_op jit(solution)/shard_map/backward_cols/pallas_call | solution.py:201
  72.5 5.5 %collective-permute-start.11 = (bf16[256,256]{1,0:T(8,128)(2,1)S(1)}, bf16[256,256]{1,0:T(8,128)(2,1)S(1)}, u32[]{:S(2)}, u32[]{:S(2)}) collective-permute-start(bf16[256,256]{1,0:T(8,128)(2,1)S(1)} %total.3.refs_0_.refs_3_), channel_id=1, source_target_pairs={{0,1},{1,0},{2,3},{3,2},{4,5},{5,4},{6,7},{7,6},{8,9},{9,8},{10,11... | collective-permute-start | bytes 393224 | tf_op jit(solution)/shard_map/ppermute | solution.py:273
  78.0 1.8 %backward_cols.6.refs_2_.refs_0_ = f32[4,256,512]{2,1,0:T(8,128)S(1)} custom-call(s32[2]{0:T(128)S(1)} %pad_add_fusion.where, bf16[512,4096]{1,0:T(8,128)(2,1)S(1)} %get-tuple-element.14.refs_3_.a_ref.refs_0_, bf16[256,512]{1,0:T(8,128)(2,1)S(1)} %collective-permute-done.12.refs_1_, f32[8,256,512]{2,1,0:T(8,128)S(1)} %backward_cols.5.refs_2_), custom_call_target="tpu_custom_call" | custom-call | tf_op jit(solution)/shard_map/backward_cols/pallas_call | solution.py:201
  80.0 1.3 %collective-permute-start.19 = (bf16[256,512]{1,0:T(8,128)(2,1)S(1)}, bf16[256,512]{1,0:T(8,128)(2,1)S(1)}, u32[]{:S(2)}, u32[]{:S(2)}) collective-permute-start(bf16[256,512]{1,0:T(8,128)(2,1)S(1)} %get-tuple-element.23), channel_id=1, source_target_pairs={{0,8},{4,12},{8,0},{12,4},{16,24},{20,28},{24,16},{28,20},{1,9},{5... | collective-permute-start | bytes 786440 | tf_op jit(solution)/shard_map/ppermute | solution.py:273
  81.4 0.8 collective-permute-start.18
  82.2 1.4 %collective-permute-start.17 = (bf16[256,512]{1,0:T(8,128)(2,1)S(1)}, bf16[256,512]{1,0:T(8,128)(2,1)S(1)}, u32[]{:S(2)}, u32[]{:S(2)}) collective-permute-start(bf16[256,512]{1,0:T(8,128)(2,1)S(1)} %get-tuple-element.25), channel_id=1, source_target_pairs={{0,24},{4,28},{8,16},{12,20},{16,8},{20,12},{24,0},{28,4},{1,25},{... | collective-permute-start | bytes 786440 | tf_op jit(solution)/shard_map/ppermute | solution.py:273
  83.6 2.8 %collective-permute-start.15 = (bf16[256,256]{1,0:T(8,128)(2,1)S(1)}, bf16[256,256]{1,0:T(8,128)(2,1)S(1)}, u32[]{:S(2)}, u32[]{:S(2)}) collective-permute-start(bf16[256,256]{1,0:T(8,128)(2,1)S(1)} %total.4.refs_0_), channel_id=1, source_target_pairs={{0,2},{1,3},{2,0},{3,1},{4,6},{5,7},{6,4},{7,5},{8,10},{9,11},{10,... | collective-permute-start | bytes 393224 | tf_op jit(solution)/shard_map/ppermute | solution.py:273
  86.4 2.8 %collective-permute-done.19.refs_4_ = bf16[256,512]{1,0:T(8,128)(2,1)S(1)} collective-permute-done((bf16[256,512]{1,0:T(8,128)(2,1)S(1)}, bf16[256,512]{1,0:T(8,128)(2,1)S(1)}, u32[]{:S(2)}, u32[]{:S(2)}) %collective-permute-start.19) | collective-permute-done | bytes 262176 | tf_op jit(solution)/shard_map/ppermute | solution.py:273
  89.3 4.2 %collective-permute-done.18.refs_3_ = bf16[256,512]{1,0:T(8,128)(2,1)S(1)} collective-permute-done((bf16[256,512]{1,0:T(8,128)(2,1)S(1)}, bf16[256,512]{1,0:T(8,128)(2,1)S(1)}, u32[]{:S(2)}, u32[]{:S(2)}) %collective-permute-start.18) | collective-permute-done | bytes 262176 | tf_op jit(solution)/shard_map/ppermute | solution.py:273
  93.4 1.6 %collective-permute-done.17.refs_2_ = bf16[256,512]{1,0:T(8,128)(2,1)S(1)} collective-permute-done((bf16[256,512]{1,0:T(8,128)(2,1)S(1)}, bf16[256,512]{1,0:T(8,128)(2,1)S(1)}, u32[]{:S(2)}, u32[]{:S(2)}) %collective-permute-start.17) | collective-permute-done | bytes 262176 | tf_op jit(solution)/shard_map/ppermute | solution.py:273
  95.1 0.9 finish.1.refs_2_
  (34 shorter events, 2.6 us)
Async XLA Ops:
  0.6 12.0 %collective-permute-start.3 = (bf16[512,256]{1,0:T(8,128)(2,1)}, bf16[512,256]{1,0:T(8,128)(2,1)S(1)}, u32[]{:S(2)}, u32[]{:S(2)}) collective-permute-start(bf16[512,256]{1,0:T(8,128)(2,1)} %refs_0_.7), channel_id=1, source_target_pairs={{0,8},{4,12},{8,0},{12,4},{16,24},{20,28},{24,16},{28,20},{1,9},{5... | collective-permute-start | bytes 786440 | tf_op jit(solution)/shard_map/ppermute | solution.py:273
  3.6 13.6 %collective-permute-start.2 = (bf16[512,256]{1,0:T(8,128)(2,1)}, bf16[512,256]{1,0:T(8,128)(2,1)S(1)}, u32[]{:S(2)}, u32[]{:S(2)}) collective-permute-start(bf16[512,256]{1,0:T(8,128)(2,1)} %refs_0_.7), channel_id=1, source_target_pairs={{0,16},{4,20},{8,24},{12,28},{16,0},{20,4},{24,8},{28,12},{1,17},{... | collective-permute-start | bytes 786440 | tf_op jit(solution)/shard_map/ppermute | solution.py:273
  5.2 12.1 %collective-permute-start.1 = (bf16[512,256]{1,0:T(8,128)(2,1)}, bf16[512,256]{1,0:T(8,128)(2,1)S(1)}, u32[]{:S(2)}, u32[]{:S(2)}) collective-permute-start(bf16[512,256]{1,0:T(8,128)(2,1)} %refs_0_.7), channel_id=1, source_target_pairs={{0,24},{4,28},{8,16},{12,20},{16,8},{20,12},{24,0},{28,4},{1,25},{... | collective-permute-start | bytes 786440 | tf_op jit(solution)/shard_map/ppermute | solution.py:273
  5.2 14.3 %collective-permute-start = (bf16[512,256]{1,0:T(8,128)(2,1)}, bf16[512,256]{1,0:T(8,128)(2,1)S(1)}, u32[]{:S(2)}, u32[]{:S(2)}) collective-permute-start(bf16[512,256]{1,0:T(8,128)(2,1)} %refs_0_.7), channel_id=1, source_target_pairs={{0,4},{4,0},{8,12},{12,8},{16,20},{20,16},{24,28},{28,24},{1,5},{5... | collective-permute-start | bytes 786440 | tf_op jit(solution)/shard_map/ppermute | solution.py:273
  17.2 1.0 copy-start
  17.2 2.2 %collective-permute-start.4 = (bf16[512,256]{1,0:T(8,128)(2,1)S(1)}, bf16[512,256]{1,0:T(8,128)(2,1)S(1)}, u32[]{:S(2)}, u32[]{:S(2)}) collective-permute-start(bf16[512,256]{1,0:T(8,128)(2,1)S(1)} %get-tuple-element.17.refs_2_.refs_1_), channel_id=1, source_target_pairs={{0,4},{4,0},{8,12},{12,8},{16,20},{20,16},{24,28},{28,24},{1,5},{5... | collective-permute-start | bytes 786440 | tf_op jit(solution)/shard_map/ppermute | solution.py:273
  17.2 2.2 %collective-permute-start.5 = (bf16[512,256]{1,0:T(8,128)(2,1)S(1)}, bf16[512,256]{1,0:T(8,128)(2,1)S(1)}, u32[]{:S(2)}, u32[]{:S(2)}) collective-permute-start(bf16[512,256]{1,0:T(8,128)(2,1)S(1)} %get-tuple-element.18.refs_4_.refs_2_), channel_id=1, source_target_pairs={{0,4},{4,0},{8,12},{12,8},{16,20},{20,16},{24,28},{28,24},{1,5},{5... | collective-permute-start | bytes 786440 | tf_op jit(solution)/shard_map/ppermute | solution.py:273
  17.7 1.8 %collective-permute-start.6 = (bf16[512,256]{1,0:T(8,128)(2,1)S(1)}, bf16[512,256]{1,0:T(8,128)(2,1)S(1)}, u32[]{:S(2)}, u32[]{:S(2)}) collective-permute-start(bf16[512,256]{1,0:T(8,128)(2,1)S(1)} %get-tuple-element.19.refs_6_.refs_3_), channel_id=1, source_target_pairs={{0,4},{4,0},{8,12},{12,8},{16,20},{20,16},{24,28},{28,24},{1,5},{5... | collective-permute-start | bytes 786440 | tf_op jit(solution)/shard_map/ppermute | solution.py:273
  21.3 16.4 %collective-permute-start.8 = (bf16[512,256]{1,0:T(8,128)(2,1)S(1)}, bf16[512,256]{1,0:T(8,128)(2,1)S(1)}, u32[]{:S(2)}, u32[]{:S(2)}) collective-permute-start(bf16[512,256]{1,0:T(8,128)(2,1)S(1)} %forward_rows.8), channel_id=1, source_target_pairs={{0,2},{1,3},{2,0},{3,1},{4,6},{5,7},{6,4},{7,5},{8,10},{9,11},{10,... | collective-permute-start | bytes 786440 | tf_op jit(solution)/shard_map/ppermute | solution.py:273
  25.8 18.3 %collective-permute-start.9 = (bf16[512,256]{1,0:T(8,128)(2,1)S(1)}, bf16[512,256]{1,0:T(8,128)(2,1)S(1)}, u32[]{:S(2)}, u32[]{:S(2)}) collective-permute-start(bf16[512,256]{1,0:T(8,128)(2,1)S(1)} %forward_rows.9), channel_id=1, source_target_pairs={{0,1},{1,0},{2,3},{3,2},{4,5},{5,4},{6,7},{7,6},{8,9},{9,8},{10,11... | collective-permute-start | bytes 786440 | tf_op jit(solution)/shard_map/ppermute | solution.py:273
  28.7 15.3 %copy-start.1 = (bf16[512,256]{1,0:T(8,128)(2,1)S(1)}, bf16[512,256]{1,0:T(8,128)(2,1)}, u32[]{:S(2)}) copy-start(bf16[512,256]{1,0:T(8,128)(2,1)} %refs_5_.1) | copy-start | bytes 786436
  28.7 15.3 %copy-start.2 = (bf16[256,256]{1,0:T(8,128)(2,1)S(1)}, bf16[256,256]{1,0:T(8,128)(2,1)}, u32[]{:S(2)}) copy-start(bf16[256,256]{1,0:T(8,128)(2,1)} %refs_4_.1) | copy-start | bytes 393220
  28.7 15.3 %collective-permute-start.7 = (bf16[512,256]{1,0:T(8,128)(2,1)S(1)}, bf16[512,256]{1,0:T(8,128)(2,1)S(1)}, u32[]{:S(2)}, u32[]{:S(2)}) collective-permute-start(bf16[512,256]{1,0:T(8,128)(2,1)S(1)} %forward_rows.7), channel_id=1, source_target_pairs={{0,3},{1,2},{2,1},{3,0},{4,7},{5,6},{6,5},{7,4},{8,11},{9,10},{10,... | collective-permute-start | bytes 786440 | tf_op jit(solution)/shard_map/ppermute | solution.py:273
  45.1 7.6 %collective-permute-start.10 = (f32[256,256]{1,0:T(8,128)S(1)}, f32[256,256]{1,0:T(8,128)S(1)}, u32[]{:S(2)}, u32[]{:S(2)}) collective-permute-start(f32[256,256]{1,0:T(8,128)S(1)} %get-tuple-element.21), channel_id=1, source_target_pairs={{0,4},{4,0},{8,12},{12,8},{16,20},{20,16},{24,28},{28,24},{1,5},{5... | collective-permute-start | bytes 786440 | tf_op jit(solution)/shard_map/ppermute | solution.py:273
  45.1 17.7 %collective-permute-start.14 = (bf16[256,512]{1,0:T(8,128)(2,1)S(1)}, bf16[256,512]{1,0:T(8,128)(2,1)S(1)}, u32[]{:S(2)}, u32[]{:S(2)}) collective-permute-start(bf16[256,512]{1,0:T(8,128)(2,1)S(1)} %get-tuple-element.22.refs_2_), channel_id=1, source_target_pairs={{0,1},{1,0},{2,3},{3,2},{4,5},{5,4},{6,7},{7,6},{8,9},{9,8},{10,11... | collective-permute-start | bytes 786440 | tf_op jit(solution)/shard_map/ppermute | solution.py:273
  49.3 17.6 %collective-permute-start.13 = (bf16[256,512]{1,0:T(8,128)(2,1)S(1)}, bf16[256,512]{1,0:T(8,128)(2,1)S(1)}, u32[]{:S(2)}, u32[]{:S(2)}) collective-permute-start(bf16[256,512]{1,0:T(8,128)(2,1)S(1)} %get-tuple-element.22.refs_2_), channel_id=1, source_target_pairs={{0,2},{1,3},{2,0},{3,1},{4,6},{5,7},{6,4},{7,5},{8,10},{9,11},{10,... | collective-permute-start | bytes 786440 | tf_op jit(solution)/shard_map/ppermute | solution.py:273
  51.2 19.5 %collective-permute-start.12 = (bf16[256,512]{1,0:T(8,128)(2,1)S(1)}, bf16[256,512]{1,0:T(8,128)(2,1)S(1)}, u32[]{:S(2)}, u32[]{:S(2)}) collective-permute-start(bf16[256,512]{1,0:T(8,128)(2,1)S(1)} %get-tuple-element.22.refs_2_), channel_id=1, source_target_pairs={{0,3},{1,2},{2,1},{3,0},{4,7},{5,6},{6,5},{7,4},{8,11},{9,10},{10,... | collective-permute-start | bytes 786440 | tf_op jit(solution)/shard_map/ppermute | solution.py:273
  72.5 7.3 %collective-permute-start.16 = (bf16[4,256,512]{2,1,0:T(8,128)(2,1)S(1)}, bf16[4,256,512]{2,1,0:T(8,128)(2,1)S(1)}, u32[]{:S(2)}, u32[]{:S(2)}) collective-permute-start(bf16[4,256,512]{2,1,0:T(8,128)(2,1)S(1)} %backward_cols.7), channel_id=1, source_target_pairs={{0,4},{4,0},{8,12},{12,8},{16,20},{20,16},{24,28},{28,24},{1,5},{5... | collective-permute-start | bytes 3145736 | tf_op jit(solution)/shard_map/ppermute | solution.py:273
  72.5 11.1 %collective-permute-start.11 = (bf16[256,256]{1,0:T(8,128)(2,1)S(1)}, bf16[256,256]{1,0:T(8,128)(2,1)S(1)}, u32[]{:S(2)}, u32[]{:S(2)}) collective-permute-start(bf16[256,256]{1,0:T(8,128)(2,1)S(1)} %total.3.refs_0_.refs_3_), channel_id=1, source_target_pairs={{0,1},{1,0},{2,3},{3,2},{4,5},{5,4},{6,7},{7,6},{8,9},{9,8},{10,11... | collective-permute-start | bytes 393224 | tf_op jit(solution)/shard_map/ppermute | solution.py:273
  80.0 9.2 %collective-permute-start.19 = (bf16[256,512]{1,0:T(8,128)(2,1)S(1)}, bf16[256,512]{1,0:T(8,128)(2,1)S(1)}, u32[]{:S(2)}, u32[]{:S(2)}) collective-permute-start(bf16[256,512]{1,0:T(8,128)(2,1)S(1)} %get-tuple-element.23), channel_id=1, source_target_pairs={{0,8},{4,12},{8,0},{12,4},{16,24},{20,28},{24,16},{28,20},{1,9},{5... | collective-permute-start | bytes 786440 | tf_op jit(solution)/shard_map/ppermute | solution.py:273
  81.4 12.1 %collective-permute-start.18 = (bf16[256,512]{1,0:T(8,128)(2,1)S(1)}, bf16[256,512]{1,0:T(8,128)(2,1)S(1)}, u32[]{:S(2)}, u32[]{:S(2)}) collective-permute-start(bf16[256,512]{1,0:T(8,128)(2,1)S(1)} %get-tuple-element.24), channel_id=1, source_target_pairs={{0,16},{4,20},{8,24},{12,28},{16,0},{20,4},{24,8},{28,12},{1,17},{... | collective-permute-start | bytes 786440 | tf_op jit(solution)/shard_map/ppermute | solution.py:273
  82.2 12.9 %collective-permute-start.17 = (bf16[256,512]{1,0:T(8,128)(2,1)S(1)}, bf16[256,512]{1,0:T(8,128)(2,1)S(1)}, u32[]{:S(2)}, u32[]{:S(2)}) collective-permute-start(bf16[256,512]{1,0:T(8,128)(2,1)S(1)} %get-tuple-element.25), channel_id=1, source_target_pairs={{0,24},{4,28},{8,16},{12,20},{16,8},{20,12},{24,0},{28,4},{1,25},{... | collective-permute-start | bytes 786440 | tf_op jit(solution)/shard_map/ppermute | solution.py:273
  83.6 12.4 %collective-permute-start.15 = (bf16[256,256]{1,0:T(8,128)(2,1)S(1)}, bf16[256,256]{1,0:T(8,128)(2,1)S(1)}, u32[]{:S(2)}, u32[]{:S(2)}) collective-permute-start(bf16[256,256]{1,0:T(8,128)(2,1)S(1)} %total.4.refs_0_), channel_id=1, source_target_pairs={{0,2},{1,3},{2,0},{3,1},{4,6},{5,7},{6,4},{7,5},{8,10},{9,11},{10,... | collective-permute-start | bytes 393224 | tf_op jit(solution)/shard_map/ppermute | solution.py:273

commit v8 on v7

--- a/solution.py
+++ b/solution.py
@@ -27,8 +27,8 @@
     return pltpu.with_memory_space_constraint(value, pltpu.VMEM)
 
 
-def dense_kernel(where, counts, cols, adj_ref, *refs, steps, window):
-    outs, (held, total, sems) = refs[: len(steps)], refs[len(steps) :]
+def dense_kernel(where, counts, cols, adj_ref, features_ref, *refs, steps, window):
+    outs, (copied_ref, held, total, sems) = refs[: len(steps)], refs[len(steps) :]
     slots, tile, _ = adj_ref.shape
     per = outs[0].shape[0] // tile
     width = outs[0].shape[1]
@@ -46,6 +46,8 @@
             fetch.start()
             plans.append((start, start - base, count, fetch))
             start = start + count
+    copied = pltpu.make_async_copy(features_ref, copied_ref, sems.at[len(plans)])
+    copied.start()
 
     for i, out_ref in enumerate(outs):
         out_ref[...] = jnp.zeros_like(out_ref)
@@ -89,26 +91,29 @@
             lax.fori_loop(0, count, add, 0)
             out_ref[rows, :] = total[...].astype(out_ref.dtype)
 
-
-def dense_rows(where, steps, counts, cols, adj, rows, col_tiles):
+    copied.wait()
+
+
+def dense_rows(where, steps, counts, cols, adj, features, rows, col_tiles):
     slots, tile, _ = adj.shape
     window = min(col_tiles, slots)
     width = col_tiles * tile
     tiles = rows // tile * len(steps)
     return pl.pallas_call(
         functools.partial(dense_kernel, steps=steps, window=window),
-        out_shape=[pltpu.VMEM((rows, width), adj.dtype) for _ in steps],
-        in_specs=[SCALARS, SCALARS, SCALARS, pl.BlockSpec(memory_space=pltpu.HBM)],
-        out_specs=[WHOLE] * len(steps),
+        out_shape=[pltpu.VMEM((rows, width), adj.dtype) for _ in steps]
+        + [pltpu.VMEM(features.shape, features.dtype)],
+        in_specs=[SCALARS] * 3 + [pl.BlockSpec(memory_space=pltpu.HBM)] * 2,
+        out_specs=[WHOLE] * (len(steps) + 1),
         scratch_shapes=[
             pltpu.VMEM((tiles, window, tile, tile), adj.dtype),
             pltpu.VMEM((tile, width), jnp.float32),
-            pltpu.SemaphoreType.DMA((tiles,)),
+            pltpu.SemaphoreType.DMA((tiles + 1,)),
         ],
         compiler_params=params(26),
         cost_estimate=cost(0, 5 * len(steps) * rows * width),
         name="dense_rows",
-    )(where, *[pltpu.with_memory_space_constraint(x, pltpu.HBM) for x in (counts, cols, adj)])
+    )(where, *[pltpu.with_memory_space_constraint(x, pltpu.HBM) for x in (counts, cols, adj, features)])
 
 
 def forward_kernel(where, a_ref, *refs, first, step):
@@ -283,17 +288,17 @@
     where = jnp.stack([lax.axis_index("row"), lax.axis_index("col")]).astype(jnp.int32)
     steps = [*range(n_col - 1, 0, -1), 0]
 
-    blocks = dense_rows(where, steps, counts, cols, adj, rows, col_tiles)
+    *blocks, near_features = dense_rows(where, steps, counts, cols, adj, features, rows, col_tiles)
     dense = dict(zip(steps, blocks))
 
     away = gate([swap(features, "row", n_row, 2 * s) for s in range(chips - 1, 0, -1)], blocks)
-    even = [features, *away[::-1]]
-    odd = [swap(shard, "row", n_row, 1) for shard in even]
+    odd = [swap(shard, "row", n_row, 1) for shard in [features, *away[::-1]]]
+    even = [near_features, *away[::-1]]
     parts = [shard for pair in zip(even, odd) for shard in pair]
 
-    half = forward(where, blocks[0], even, 0, 2, [], jnp.float32)
-    shares = [forward(where, blocks[0], odd, 1, 2, [half], jnp.bfloat16)]
-    shares += [forward(where, block, parts, 0, 1, [], jnp.bfloat16) for block in blocks[1:-1]]
+    half = forward(where, blocks[2], even, 0, 2, [], jnp.float32)
+    shares = [forward(where, block, parts, 0, 1, [], jnp.bfloat16) for block in blocks[:-1]]
+    shares[2] = forward(where, blocks[2], odd, 1, 2, [half], jnp.bfloat16)
     came = [swap(share, "col", n_col, s) for s, share in zip(steps, shares)]
     mine = forward(where, blocks[-1], parts, 0, 1, [], jnp.float32)
     scale = 1.0 / math.sqrt(rows * n_row * n_col)
@@ -307,10 +312,10 @@
     part = total([gathered], part.shape[0], jnp.bfloat16)
 
     every = list(range(n_row))
-    sums = None
-    for group in [[0, 1], *[[s] for s in range(2, n_col - 1)]]:
+    sums, latest = None, n_col // 2
+    for group in [[0, 1], *[[s] for s in range(n_col - 1, 1, -1) if s != latest]]:
         sums = backward(where, [dense[s] for s in group], [pieces[s] for s in group], every, depth, sums, jnp.float32)
-    last = functools.partial(backward, where, [dense[n_col - 1]], [pieces[n_col - 1]])
+    last = functools.partial(backward, where, [dense[latest]], [pieces[latest]])
     sent = last(every[1::2], depth, sums, jnp.bfloat16, [part])
     kept = last(every[::2], depth, sums, jnp.float32)
     came = swap(sent, "row", n_row, 1)

time: 96.9 us -> 97.1 us (level)
  starting transfers between devices: 29.1 us -> 19.2 us
  waiting for transfers between devices: 27.3 us -> 37.2 us
    ppermute x20, waiting for transfers between devices: 27.3 us -> 37.2 us  [swap(): return lax.ppermute(value, axis, [(i, i ^ step) for i in range(size)])]
    ppermute x20, starting transfers between devices: 29.1 us -> 19.2 us  [swap(): return lax.ppermute(value, axis, [(i, i ^ step) for i in range(size)])]
  transfers between devices with their start and end apart: 20 -> 20, of which waited for: 7 -> 9; matrix products, arithmetic and copies ran while one was open for 0% -> 0% of each run, Pallas kernels for 24% -> 25%
where the time goes in v8:
time: 97.1 us; the launch traced here: 96.9 us
  waiting for transfers between devices  37.2 us (38%)
  Pallas kernels  29.2 us (30%)
  starting transfers between devices  19.2 us (20%)
  blocking collectives  10 us (10%)
    ppermute x20, waiting for transfers between devices, swap(): return lax.ppermute(value, axis, [(i, i ^ step) for i in range(size)])  37.2 us
    ppermute x20, starting transfers between devices, swap(): return lax.ppermute(value, axis, [(i, i ^ step) for i in range(size)])  19.2 us
    pallas_call x4, Pallas kernels, backward(): pl.pallas_call(functools.partial(backward_kernel, count=count, steps=step...  10.6 us
    all_gather x1, blocking collectives, shards(): gathered = lax.all_gather(part, 'row', axis_index_groups=cores, tiled=True)  10 us
    pallas_call x5, Pallas kernels, forward(): pl.pallas_call(functools.partial(forward_kernel, first=first, step=step),...  7.94 us
    pallas_call x1, Pallas kernels, dense_rows(): pl.pallas_call(functools.partial(dense_kernel, steps=steps, window=window...  7.85 us
  transfers between devices with their start and end apart: 20, of which 9 were waited for; matrix products, arithmetic and copies ran while one was open for 0% of the time, Pallas kernels for 25%

profile of v8, /device:TPU:0, one launch (start us, length us, event | category | flops | bytes accessed | tf_op | source)
XLA Modules:
  0.0 96.9 jit_solution(13587461153462260585)
XLA Ops:
  0.6 4.0 %collective-permute-start.1 = (bf16[512,256]{1,0:T(8,128)(2,1)}, bf16[512,256]{1,0:T(8,128)(2,1)S(1)}, u32[]{:S(2)}, u32[]{:S(2)}) collective-permute-start(bf16[512,256]{1,0:T(8,128)(2,1)} %features_ref.1), channel_id=1, source_target_pairs={{0,24},{4,28},{8,16},{12,20},{16,8},{20,12},{24,0},{28,4},{1,25},{... | collective-permute-start | bytes 786440 | tf_op jit(solution)/shard_map/ppermute | solution.py:278
  4.6 0.5 collective-permute-start.3
  5.3 7.9 %dense_rows.1 = (bf16[512,4096]{1,0:T(8,128)(2,1)S(1)}, bf16[512,4096]{1,0:T(8,128)(2,1)S(1)}, bf16[512,4096]{1,0:T(8,128)(2,1)S(1)}, bf16[512,4096]{1,0:T(8,128)(2,1)S(1)}, bf16[512,256]{1,0:T(8,128)(2,1)S(1)}) custom-call(s32[2]{0:T(128)S(1)} %pad_add_fusion.where, s32[16]{0:T(128)} %bitcast.13, s32[448]{0:T(512)} %bitcast.12, ...), custom_call_target="tpu_custom_call" | custom-call | bytes 41943040 | tf_op jit(solution)/shard_map/dense_rows/pallas_call | solution.py:102
  13.2 3.8 %collective-permute-done.3.refs_2_ = bf16[512,256]{1,0:T(8,128)(2,1)S(1)} collective-permute-done((bf16[512,256]{1,0:T(8,128)(2,1)}, bf16[512,256]{1,0:T(8,128)(2,1)S(1)}, u32[]{:S(2)}, u32[]{:S(2)}) %collective-permute-start.3) | collective-permute-done | bytes 262176 | tf_op jit(solution)/shard_map/ppermute | solution.py:278
  17.0 0.5 collective-permute-start.5
  17.6 1.2 %forward_rows.8.refs_4_ = f32[512,256]{1,0:T(8,128)S(1)} custom-call(s32[2]{0:T(128)S(1)} %pad_add_fusion.where, bf16[512,4096]{1,0:T(8,128)(2,1)S(1)} %get-tuple-element.18.refs_5_.a_ref.refs_1_, bf16[512,256]{1,0:T(8,128)(2,1)S(1)} %get-tuple-element.15.refs_0_, bf16[512,256]{1,0:T(8,128)(2,1)S(1)} %get-tuple-element.19.refs_2_.refs_1_, ...), custom_call_target="tpu_custom_call" | custom-call | flops 1073741824 | bytes 4194304 | tf_op jit(solution)/shard_map/forward_rows/pallas_call | solution.py:136
  19.3 1.8 %forward_rows.6 = bf16[512,256]{1,0:T(8,128)(2,1)S(1)} custom-call(s32[2]{0:T(128)S(1)} %pad_add_fusion.where, bf16[512,4096]{1,0:T(8,128)(2,1)S(1)} %get-tuple-element.16.refs_3_.a_ref.refs_0_, bf16[512,256]{1,0:T(8,128)(2,1)S(1)} %get-tuple-element.15.refs_0_, bf16[512,256]{1,0:T(8,128)(2,1)S(1)} %collective-permute-done.refs_1_.refs_0_, ...), custom_call_target="tpu_custom_call" | custom-call | flops 1073741824 | bytes 4194304 | tf_op jit(solution)/shard_map/forward_rows/pallas_call | solution.py:136
  21.1 3.7 %collective-permute-start.7 = (bf16[512,256]{1,0:T(8,128)(2,1)S(1)}, bf16[512,256]{1,0:T(8,128)(2,1)S(1)}, u32[]{:S(2)}, u32[]{:S(2)}) collective-permute-start(bf16[512,256]{1,0:T(8,128)(2,1)S(1)} %forward_rows.6), channel_id=1, source_target_pairs={{0,3},{1,2},{2,1},{3,0},{4,7},{5,6},{6,5},{7,4},{8,11},{9,10},{10,... | collective-permute-start | bytes 786440 | tf_op jit(solution)/shard_map/ppermute | solution.py:278
  24.8 1.8 %forward_rows.7 = bf16[512,256]{1,0:T(8,128)(2,1)S(1)} custom-call(s32[2]{0:T(128)S(1)} %pad_add_fusion.where, bf16[512,4096]{1,0:T(8,128)(2,1)S(1)} %get-tuple-element.17.refs_4_.a_ref.refs_0_, bf16[512,256]{1,0:T(8,128)(2,1)S(1)} %get-tuple-element.15.refs_0_, bf16[512,256]{1,0:T(8,128)(2,1)S(1)} %collective-permute-done.refs_1_.refs_0_, ...), custom_call_target="tpu_custom_call" | custom-call | flops 1073741824 | bytes 4194304 | tf_op jit(solution)/shard_map/forward_rows/pallas_call | solution.py:136
  26.7 1.3 %forward_rows.9 = bf16[512,256]{1,0:T(8,128)(2,1)S(1)} custom-call(s32[2]{0:T(128)S(1)} %pad_add_fusion.where, bf16[512,4096]{1,0:T(8,128)(2,1)S(1)} %get-tuple-element.18.refs_5_.a_ref.refs_1_, bf16[512,256]{1,0:T(8,128)(2,1)S(1)} %collective-permute-done.refs_1_.refs_0_, bf16[512,256]{1,0:T(8,128)(2,1)S(1)} %collective-permute-done.4.refs_3_.refs_1_, ...), custom_call_target="tpu_custom_call" | custom-call | flops 1073741824 | bytes 4194304 | tf_op jit(solution)/shard_map/forward_rows/pallas_call | solution.py:136
  28.0 0.8 collective-permute-start.9
  28.8 1.8 %forward_rows.5.refs_0_ = f32[512,256]{1,0:T(8,128)S(1)} custom-call(s32[2]{0:T(128)S(1)} %pad_add_fusion.where, bf16[512,4096]{1,0:T(8,128)(2,1)S(1)} %get-tuple-element.14.refs_6_.a_ref.refs_0_, bf16[512,256]{1,0:T(8,128)(2,1)S(1)} %get-tuple-element.15.refs_0_, bf16[512,256]{1,0:T(8,128)(2,1)S(1)} %collective-permute-done.refs_1_.refs_0_, ...), custom_call_target="tpu_custom_call" | custom-call | flops 1073741824 | bytes 4194304 | tf_op jit(solution)/shard_map/forward_rows/pallas_call | solution.py:136
  30.6 1.6 %collective-permute-done.7.refs_1_ = bf16[512,256]{1,0:T(8,128)(2,1)S(1)} collective-permute-done((bf16[512,256]{1,0:T(8,128)(2,1)S(1)}, bf16[512,256]{1,0:T(8,128)(2,1)S(1)}, u32[]{:S(2)}, u32[]{:S(2)}) %collective-permute-start.7) | collective-permute-done | bytes 262176 | tf_op jit(solution)/shard_map/ppermute | solution.py:278
  32.2 15.2 %collective-permute-done.8.refs_2_ = bf16[512,256]{1,0:T(8,128)(2,1)S(1)} collective-permute-done((bf16[512,256]{1,0:T(8,128)(2,1)S(1)}, bf16[512,256]{1,0:T(8,128)(2,1)S(1)}, u32[]{:S(2)}, u32[]{:S(2)}) %collective-permute-start.8) | collective-permute-done | bytes 262176 | tf_op jit(solution)/shard_map/ppermute | solution.py:278
  47.4 1.1 %middle.1 = (bf16[512,256]{1,0:T(8,128)(2,1)}, bf16[256,512]{1,0:T(8,128)(2,1)S(1)}, f32[256,256]{1,0:T(8,128)S(1)}) custom-call(f32[512,256]{1,0:T(8,128)S(1)} %forward_rows.5.refs_0_, bf16[512,256]{1,0:T(8,128)(2,1)S(1)} %collective-permute-done.7.refs_1_, bf16[512,256]{1,0:T(8,128)(2,1)S(1)} %collective-permute-done.8.refs_2_, ...), custom_call_target="tpu_custom_call" | custom-call | flops 201326592 | bytes 1310720 | tf_op jit(solution)/shard_map/middle/pallas_call | solution.py:169
  48.5 2.5 %collective-permute-start.13 = (bf16[256,512]{1,0:T(8,128)(2,1)S(1)}, bf16[256,512]{1,0:T(8,128)(2,1)S(1)}, u32[]{:S(2)}, u32[]{:S(2)}) collective-permute-start(bf16[256,512]{1,0:T(8,128)(2,1)S(1)} %get-tuple-element.24.refs_2_), channel_id=1, source_target_pairs={{0,3},{1,2},{2,1},{3,0},{4,7},{5,6},{6,5},{7,4},{8,11},{9,10},{10,... | collective-permute-start | bytes 786440 | tf_op jit(solution)/shard_map/ppermute | solution.py:278
  51.0 1.0 %collective-permute-start.12 = (bf16[256,512]{1,0:T(8,128)(2,1)S(1)}, bf16[256,512]{1,0:T(8,128)(2,1)S(1)}, u32[]{:S(2)}, u32[]{:S(2)}) collective-permute-start(bf16[256,512]{1,0:T(8,128)(2,1)S(1)} %get-tuple-element.24.refs_2_), channel_id=1, source_target_pairs={{0,2},{1,3},{2,0},{3,1},{4,6},{5,7},{6,4},{7,5},{8,10},{9,11},{10,... | collective-permute-start | bytes 786440 | tf_op jit(solution)/shard_map/ppermute | solution.py:278
  52.0 10.0 %all_gather.3.refs_0_ = bf16[1024,256]{1,0:T(8,128)(2,1)S(1)} all-gather(bf16[256,256]{1,0:T(8,128)(2,1)S(1)} %add_convert_fusion), channel_id=1, replica_groups={{0,8,16,24},{4,12,20,28},{1,9,17,25},{5,13,21,29},{2,10,18,26},{6,14,22..., dimensions={0}, use_global_device_ids=true | all-gather | bytes 655360 | tf_op jit(solution)/shard_map/all_gather | solution.py:311
  62.1 4.1 %backward_cols.4.refs_2_ = f32[8,256,512]{2,1,0:T(8,128)S(1)} custom-call(s32[2]{0:T(128)S(1)} %pad_add_fusion.where, bf16[512,4096]{1,0:T(8,128)(2,1)S(1)} %get-tuple-element.14.refs_6_.a_ref.refs_0_, bf16[512,4096]{1,0:T(8,128)(2,1)S(1)} %get-tuple-element.18.refs_5_.a_ref.refs_1_, bf16[256,512]{1,0:T(8,128)(2,1)S(1)} %get-tuple-element.24.refs_2_, ...), custom_call_target="tpu_custom_call" | custom-call | tf_op jit(solution)/shard_map/backward_cols/pallas_call | solution.py:206
  66.2 3.0 %backward_cols.5.refs_2_ = f32[8,256,512]{2,1,0:T(8,128)S(1)} custom-call(s32[2]{0:T(128)S(1)} %pad_add_fusion.where, bf16[512,4096]{1,0:T(8,128)(2,1)S(1)} %get-tuple-element.16.refs_3_.a_ref.refs_0_, bf16[256,512]{1,0:T(8,128)(2,1)S(1)} %collective-permute-done.13.refs_1_, f32[8,256,512]{2,1,0:T(8,128)S(1)} %backward_cols.4.refs_2_), custom_call_target="tpu_custom_call" | custom-call | tf_op jit(solution)/shard_map/backward_cols/pallas_call | solution.py:206
  69.2 6.0 %collective-permute-done.12.refs_1_ = bf16[256,512]{1,0:T(8,128)(2,1)S(1)} collective-permute-done((bf16[256,512]{1,0:T(8,128)(2,1)S(1)}, bf16[256,512]{1,0:T(8,128)(2,1)S(1)}, u32[]{:S(2)}, u32[]{:S(2)}) %collective-permute-start.12) | collective-permute-done | bytes 262176 | tf_op jit(solution)/shard_map/ppermute | solution.py:278
  75.2 1.8 %backward_cols.7 = bf16[4,256,512]{2,1,0:T(8,128)(2,1)S(1)} custom-call(s32[2]{0:T(128)S(1)} %pad_add_fusion.where, bf16[512,4096]{1,0:T(8,128)(2,1)S(1)} %get-tuple-element.17.refs_4_.a_ref.refs_0_, bf16[256,512]{1,0:T(8,128)(2,1)S(1)} %collective-permute-done.12.refs_1_, f32[8,256,512]{2,1,0:T(8,128)S(1)} %backward_cols.5.refs_2_, ...), custom_call_target="tpu_custom_call" | custom-call | tf_op jit(solution)/shard_map/backward_cols/pallas_call | solution.py:206
  77.2 1.8 %backward_cols.6.refs_2_.refs_0_ = f32[4,256,512]{2,1,0:T(8,128)S(1)} custom-call(s32[2]{0:T(128)S(1)} %pad_add_fusion.where, bf16[512,4096]{1,0:T(8,128)(2,1)S(1)} %get-tuple-element.17.refs_4_.a_ref.refs_0_, bf16[256,512]{1,0:T(8,128)(2,1)S(1)} %collective-permute-done.12.refs_1_, f32[8,256,512]{2,1,0:T(8,128)S(1)} %backward_cols.5.refs_2_), custom_call_target="tpu_custom_call" | custom-call | tf_op jit(solution)/shard_map/backward_cols/pallas_call | solution.py:206
  78.9 0.8 collective-permute-done.16.refs_1_
  80.0 1.6 %collective-permute-start.19 = (bf16[256,512]{1,0:T(8,128)(2,1)S(1)}, bf16[256,512]{1,0:T(8,128)(2,1)S(1)}, u32[]{:S(2)}, u32[]{:S(2)}) collective-permute-start(bf16[256,512]{1,0:T(8,128)(2,1)S(1)} %get-tuple-element.25), channel_id=1, source_target_pairs={{0,8},{4,12},{8,0},{12,4},{16,24},{20,28},{24,16},{28,20},{1,9},{5... | collective-permute-start | bytes 786440 | tf_op jit(solution)/shard_map/ppermute | solution.py:278
  81.6 1.4 %collective-permute-start.18 = (bf16[256,512]{1,0:T(8,128)(2,1)S(1)}, bf16[256,512]{1,0:T(8,128)(2,1)S(1)}, u32[]{:S(2)}, u32[]{:S(2)}) collective-permute-start(bf16[256,512]{1,0:T(8,128)(2,1)S(1)} %get-tuple-element.26), channel_id=1, source_target_pairs={{0,16},{4,20},{8,24},{12,28},{16,0},{20,4},{24,8},{28,12},{1,17},{... | collective-permute-start | bytes 786440 | tf_op jit(solution)/shard_map/ppermute | solution.py:278
  83.0 0.6 collective-permute-start.17
  83.6 2.3 %collective-permute-start.15 = (bf16[256,256]{1,0:T(8,128)(2,1)S(1)}, bf16[256,256]{1,0:T(8,128)(2,1)S(1)}, u32[]{:S(2)}, u32[]{:S(2)}) collective-permute-start(bf16[256,256]{1,0:T(8,128)(2,1)S(1)} %total.4.refs_0_), channel_id=1, source_target_pairs={{0,2},{1,3},{2,0},{3,1},{4,6},{5,7},{6,4},{7,5},{8,10},{9,11},{10,... | collective-permute-start | bytes 393224 | tf_op jit(solution)/shard_map/ppermute | solution.py:278
  85.9 3.3 %collective-permute-done.19.refs_4_ = bf16[256,512]{1,0:T(8,128)(2,1)S(1)} collective-permute-done((bf16[256,512]{1,0:T(8,128)(2,1)S(1)}, bf16[256,512]{1,0:T(8,128)(2,1)S(1)}, u32[]{:S(2)}, u32[]{:S(2)}) %collective-permute-start.19) | collective-permute-done | bytes 262176 | tf_op jit(solution)/shard_map/ppermute | solution.py:278
  89.2 6.0 %collective-permute-done.18.refs_3_ = bf16[256,512]{1,0:T(8,128)(2,1)S(1)} collective-permute-done((bf16[256,512]{1,0:T(8,128)(2,1)S(1)}, bf16[256,512]{1,0:T(8,128)(2,1)S(1)}, u32[]{:S(2)}, u32[]{:S(2)}) %collective-permute-start.18) | collective-permute-done | bytes 262176 | tf_op jit(solution)/shard_map/ppermute | solution.py:278
  95.2 0.9 finish.1.refs_2_
  96.2 0.7 total.5
  (32 shorter events, 1.3 us)
Async XLA Ops:
  0.6 12.5 %collective-permute-start.1 = (bf16[512,256]{1,0:T(8,128)(2,1)}, bf16[512,256]{1,0:T(8,128)(2,1)S(1)}, u32[]{:S(2)}, u32[]{:S(2)}) collective-permute-start(bf16[512,256]{1,0:T(8,128)(2,1)} %features_ref.1), channel_id=1, source_target_pairs={{0,24},{4,28},{8,16},{12,20},{16,8},{20,12},{24,0},{28,4},{1,25},{... | collective-permute-start | bytes 786440 | tf_op jit(solution)/shard_map/ppermute | solution.py:278
  4.6 12.4 %collective-permute-start.3 = (bf16[512,256]{1,0:T(8,128)(2,1)}, bf16[512,256]{1,0:T(8,128)(2,1)S(1)}, u32[]{:S(2)}, u32[]{:S(2)}) collective-permute-start(bf16[512,256]{1,0:T(8,128)(2,1)} %features_ref.1), channel_id=1, source_target_pairs={{0,8},{4,12},{8,0},{12,4},{16,24},{20,28},{24,16},{28,20},{1,9},{5... | collective-permute-start | bytes 786440 | tf_op jit(solution)/shard_map/ppermute | solution.py:278
  5.1 11.9 %collective-permute-start.2 = (bf16[512,256]{1,0:T(8,128)(2,1)}, bf16[512,256]{1,0:T(8,128)(2,1)S(1)}, u32[]{:S(2)}, u32[]{:S(2)}) collective-permute-start(bf16[512,256]{1,0:T(8,128)(2,1)} %features_ref.1), channel_id=1, source_target_pairs={{0,16},{4,20},{8,24},{12,28},{16,0},{20,4},{24,8},{28,12},{1,17},{... | collective-permute-start | bytes 786440 | tf_op jit(solution)/shard_map/ppermute | solution.py:278
  5.2 13.6 %collective-permute-start = (bf16[512,256]{1,0:T(8,128)(2,1)}, bf16[512,256]{1,0:T(8,128)(2,1)S(1)}, u32[]{:S(2)}, u32[]{:S(2)}) collective-permute-start(bf16[512,256]{1,0:T(8,128)(2,1)} %features_ref.1), channel_id=1, source_target_pairs={{0,4},{4,0},{8,12},{12,8},{16,20},{20,16},{24,28},{28,24},{1,5},{5... | collective-permute-start | bytes 786440 | tf_op jit(solution)/shard_map/ppermute | solution.py:278
  17.0 1.8 %collective-permute-start.4 = (bf16[512,256]{1,0:T(8,128)(2,1)S(1)}, bf16[512,256]{1,0:T(8,128)(2,1)S(1)}, u32[]{:S(2)}, u32[]{:S(2)}) collective-permute-start(bf16[512,256]{1,0:T(8,128)(2,1)S(1)} %get-tuple-element.19.refs_2_.refs_1_), channel_id=1, source_target_pairs={{0,4},{4,0},{8,12},{12,8},{16,20},{20,16},{24,28},{28,24},{1,5},{5... | collective-permute-start | bytes 786440 | tf_op jit(solution)/shard_map/ppermute | solution.py:278
  17.0 1.9 %collective-permute-start.5 = (bf16[512,256]{1,0:T(8,128)(2,1)S(1)}, bf16[512,256]{1,0:T(8,128)(2,1)S(1)}, u32[]{:S(2)}, u32[]{:S(2)}) collective-permute-start(bf16[512,256]{1,0:T(8,128)(2,1)S(1)} %get-tuple-element.20.refs_4_.refs_2_), channel_id=1, source_target_pairs={{0,4},{4,0},{8,12},{12,8},{16,20},{20,16},{24,28},{28,24},{1,5},{5... | collective-permute-start | bytes 786440 | tf_op jit(solution)/shard_map/ppermute | solution.py:278
  17.5 1.8 %collective-permute-start.6 = (bf16[512,256]{1,0:T(8,128)(2,1)S(1)}, bf16[512,256]{1,0:T(8,128)(2,1)S(1)}, u32[]{:S(2)}, u32[]{:S(2)}) collective-permute-start(bf16[512,256]{1,0:T(8,128)(2,1)S(1)} %get-tuple-element.21.refs_6_.refs_3_), channel_id=1, source_target_pairs={{0,4},{4,0},{8,12},{12,8},{16,20},{20,16},{24,28},{28,24},{1,5},{5... | collective-permute-start | bytes 786440 | tf_op jit(solution)/shard_map/ppermute | solution.py:278
  21.1 11.1 %collective-permute-start.7 = (bf16[512,256]{1,0:T(8,128)(2,1)S(1)}, bf16[512,256]{1,0:T(8,128)(2,1)S(1)}, u32[]{:S(2)}, u32[]{:S(2)}) collective-permute-start(bf16[512,256]{1,0:T(8,128)(2,1)S(1)} %forward_rows.6), channel_id=1, source_target_pairs={{0,3},{1,2},{2,1},{3,0},{4,7},{5,6},{6,5},{7,4},{8,11},{9,10},{10,... | collective-permute-start | bytes 786440 | tf_op jit(solution)/shard_map/ppermute | solution.py:278
  26.6 20.8 %collective-permute-start.8 = (bf16[512,256]{1,0:T(8,128)(2,1)S(1)}, bf16[512,256]{1,0:T(8,128)(2,1)S(1)}, u32[]{:S(2)}, u32[]{:S(2)}) collective-permute-start(bf16[512,256]{1,0:T(8,128)(2,1)S(1)} %forward_rows.7), channel_id=1, source_target_pairs={{0,2},{1,3},{2,0},{3,1},{4,6},{5,7},{6,4},{7,5},{8,10},{9,11},{10,... | collective-permute-start | bytes 786440 | tf_op jit(solution)/shard_map/ppermute | solution.py:278
  28.0 19.4 %copy-start = (bf16[512,256]{1,0:T(8,128)(2,1)S(1)}, bf16[512,256]{1,0:T(8,128)(2,1)}, u32[]{:S(2)}) copy-start(bf16[512,256]{1,0:T(8,128)(2,1)} %refs_5_.1) | copy-start | bytes 786436
  28.0 19.4 %copy-start.1 = (bf16[256,256]{1,0:T(8,128)(2,1)S(1)}, bf16[256,256]{1,0:T(8,128)(2,1)}, u32[]{:S(2)}) copy-start(bf16[256,256]{1,0:T(8,128)(2,1)} %refs_4_.1) | copy-start | bytes 393220
  28.0 19.4 %collective-permute-start.9 = (bf16[512,256]{1,0:T(8,128)(2,1)S(1)}, bf16[512,256]{1,0:T(8,128)(2,1)S(1)}, u32[]{:S(2)}, u32[]{:S(2)}) collective-permute-start(bf16[512,256]{1,0:T(8,128)(2,1)S(1)} %forward_rows.9), channel_id=1, source_target_pairs={{0,1},{1,0},{2,3},{3,2},{4,5},{5,4},{6,7},{7,6},{8,9},{9,8},{10,11... | collective-permute-start | bytes 786440 | tf_op jit(solution)/shard_map/ppermute | solution.py:278
  48.5 3.5 %collective-permute-start.10 = (f32[256,256]{1,0:T(8,128)S(1)}, f32[256,256]{1,0:T(8,128)S(1)}, u32[]{:S(2)}, u32[]{:S(2)}) collective-permute-start(f32[256,256]{1,0:T(8,128)S(1)} %get-tuple-element.23), channel_id=1, source_target_pairs={{0,4},{4,0},{8,12},{12,8},{16,20},{20,16},{24,28},{28,24},{1,5},{5... | collective-permute-start | bytes 786440 | tf_op jit(solution)/shard_map/ppermute | solution.py:278
  48.5 13.6 %collective-permute-start.14 = (bf16[256,512]{1,0:T(8,128)(2,1)S(1)}, bf16[256,512]{1,0:T(8,128)(2,1)S(1)}, u32[]{:S(2)}, u32[]{:S(2)}) collective-permute-start(bf16[256,512]{1,0:T(8,128)(2,1)S(1)} %get-tuple-element.24.refs_2_), channel_id=1, source_target_pairs={{0,1},{1,0},{2,3},{3,2},{4,5},{5,4},{6,7},{7,6},{8,9},{9,8},{10,11... | collective-permute-start | bytes 786440 | tf_op jit(solution)/shard_map/ppermute | solution.py:278
  48.5 17.7 %collective-permute-start.13 = (bf16[256,512]{1,0:T(8,128)(2,1)S(1)}, bf16[256,512]{1,0:T(8,128)(2,1)S(1)}, u32[]{:S(2)}, u32[]{:S(2)}) collective-permute-start(bf16[256,512]{1,0:T(8,128)(2,1)S(1)} %get-tuple-element.24.refs_2_), channel_id=1, source_target_pairs={{0,3},{1,2},{2,1},{3,0},{4,7},{5,6},{6,5},{7,4},{8,11},{9,10},{10,... | collective-permute-start | bytes 786440 | tf_op jit(solution)/shard_map/ppermute | solution.py:278
  51.0 24.3 %collective-permute-start.12 = (bf16[256,512]{1,0:T(8,128)(2,1)S(1)}, bf16[256,512]{1,0:T(8,128)(2,1)S(1)}, u32[]{:S(2)}, u32[]{:S(2)}) collective-permute-start(bf16[256,512]{1,0:T(8,128)(2,1)S(1)} %get-tuple-element.24.refs_2_), channel_id=1, source_target_pairs={{0,2},{1,3},{2,0},{3,1},{4,6},{5,7},{6,4},{7,5},{8,10},{9,11},{10,... | collective-permute-start | bytes 786440 | tf_op jit(solution)/shard_map/ppermute | solution.py:278
  77.0 2.7 %collective-permute-start.16 = (bf16[4,256,512]{2,1,0:T(8,128)(2,1)S(1)}, bf16[4,256,512]{2,1,0:T(8,128)(2,1)S(1)}, u32[]{:S(2)}, u32[]{:S(2)}) collective-permute-start(bf16[4,256,512]{2,1,0:T(8,128)(2,1)S(1)} %backward_cols.7), channel_id=1, source_target_pairs={{0,4},{4,0},{8,12},{12,8},{16,20},{20,16},{24,28},{28,24},{1,5},{5... | collective-permute-start | bytes 3145736 | tf_op jit(solution)/shard_map/ppermute | solution.py:278
  77.1 6.5 %collective-permute-start.11 = (bf16[256,256]{1,0:T(8,128)(2,1)S(1)}, bf16[256,256]{1,0:T(8,128)(2,1)S(1)}, u32[]{:S(2)}, u32[]{:S(2)}) collective-permute-start(bf16[256,256]{1,0:T(8,128)(2,1)S(1)} %total.3.refs_0_.refs_3_), channel_id=1, source_target_pairs={{0,1},{1,0},{2,3},{3,2},{4,5},{5,4},{6,7},{7,6},{8,9},{9,8},{10,11... | collective-permute-start | bytes 393224 | tf_op jit(solution)/shard_map/ppermute | solution.py:278
  80.0 9.2 %collective-permute-start.19 = (bf16[256,512]{1,0:T(8,128)(2,1)S(1)}, bf16[256,512]{1,0:T(8,128)(2,1)S(1)}, u32[]{:S(2)}, u32[]{:S(2)}) collective-permute-start(bf16[256,512]{1,0:T(8,128)(2,1)S(1)} %get-tuple-element.25), channel_id=1, source_target_pairs={{0,8},{4,12},{8,0},{12,4},{16,24},{20,28},{24,16},{28,20},{1,9},{5... | collective-permute-start | bytes 786440 | tf_op jit(solution)/shard_map/ppermute | solution.py:278
  81.6 13.7 %collective-permute-start.18 = (bf16[256,512]{1,0:T(8,128)(2,1)S(1)}, bf16[256,512]{1,0:T(8,128)(2,1)S(1)}, u32[]{:S(2)}, u32[]{:S(2)}) collective-permute-start(bf16[256,512]{1,0:T(8,128)(2,1)S(1)} %get-tuple-element.26), channel_id=1, source_target_pairs={{0,16},{4,20},{8,24},{12,28},{16,0},{20,4},{24,8},{28,12},{1,17},{... | collective-permute-start | bytes 786440 | tf_op jit(solution)/shard_map/ppermute | solution.py:278
  83.0 12.3 %collective-permute-start.17 = (bf16[256,512]{1,0:T(8,128)(2,1)S(1)}, bf16[256,512]{1,0:T(8,128)(2,1)S(1)}, u32[]{:S(2)}, u32[]{:S(2)}) collective-permute-start(bf16[256,512]{1,0:T(8,128)(2,1)S(1)} %get-tuple-element.27), channel_id=1, source_target_pairs={{0,24},{4,28},{8,16},{12,20},{16,8},{20,12},{24,0},{28,4},{1,25},{... | collective-permute-start | bytes 786440 | tf_op jit(solution)/shard_map/ppermute | solution.py:278
  83.6 12.6 %collective-permute-start.15 = (bf16[256,256]{1,0:T(8,128)(2,1)S(1)}, bf16[256,256]{1,0:T(8,128)(2,1)S(1)}, u32[]{:S(2)}, u32[]{:S(2)}) collective-permute-start(bf16[256,256]{1,0:T(8,128)(2,1)S(1)} %total.4.refs_0_), channel_id=1, source_target_pairs={{0,2},{1,3},{2,0},{3,1},{4,6},{5,7},{6,4},{7,5},{8,10},{9,11},{10,... | collective-permute-start | bytes 393224 | tf_op jit(solution)/shard_map/ppermute | solution.py:278

commit v9 on v8

--- a/solution.py
+++ b/solution.py
@@ -219,7 +219,7 @@
     value = parts[0][0].astype(jnp.float32) + parts[1][0].astype(jnp.float32)
     for part in parts[2:]:
         value = value + part[...].astype(jnp.float32)
-    out_ref[...] = value.T.astype(out_ref.dtype)
+    out_ref[...] = value.astype(out_ref.dtype).T
 
 
 def finish(kept, came, parts):
@@ -312,22 +312,21 @@
     part = total([gathered], part.shape[0], jnp.bfloat16)
 
     every = list(range(n_row))
-    sums, latest = None, n_col // 2
-    for group in [[0, 1], *[[s] for s in range(n_col - 1, 1, -1) if s != latest]]:
+    sums, latest = None, n_col - 1
+    for group in [[0, 1], *[[s] for s in range(2, n_col - 1)]]:
         sums = backward(where, [dense[s] for s in group], [pieces[s] for s in group], every, depth, sums, jnp.float32)
     last = functools.partial(backward, where, [dense[latest]], [pieces[latest]])
     sent = last(every[1::2], depth, sums, jnp.bfloat16, [part])
     kept = last(every[::2], depth, sums, jnp.float32)
     came = swap(sent, "row", n_row, 1)
     summed = [(kept[c] + came[c].astype(jnp.float32)).astype(jnp.bfloat16) for c in range(1, chips)]
-    parts = [swap(summed[c - 1], "row", n_row, 2 * c) for c in range(chips - 1, 0, -1)]
+    parts = [swap(summed[c - 1], "row", n_row, 2 * c) for c in range(1, chips)]
 
     feature_grad = finish(kept, came, parts)
     for s in range(n_col.bit_length() - 2):
         part = total([part, swap(part, "col", n_col, 1 << s)], part.shape[0], jnp.bfloat16, [kept])
     came = swap(part, "col", n_col, n_col // 2)
-    done = pltpu.with_memory_space_constraint(feature_grad, pltpu.HBM)
-    weight_grad = total([part, came], part.shape[0], jnp.float32, [done])
+    weight_grad = total([part, came], part.shape[0], jnp.float32)
     return hidden, weight_grad, feature_grad
 
 

time: 97.1 us -> 95.7 us (0.986)
  waiting for transfers between devices: 37.2 us -> 33.2 us
  starting transfers between devices: 19.2 us -> 22.4 us
    ppermute x20, waiting for transfers between devices: 37.2 us -> 33.2 us  [swap(): return lax.ppermute(value, axis, [(i, i ^ step) for i in range(size)])]
    ppermute x20, starting transfers between devices: 19.2 us -> 22.4 us  [swap(): return lax.ppermute(value, axis, [(i, i ^ step) for i in range(size)])]
  transfers between devices with their start and end apart: 20 -> 20, of which waited for: 9 -> 8; matrix products, arithmetic and copies ran while one was open for 0% -> 0% of each run, Pallas kernels for 25% -> 24%
where the time goes in v9:
time: 95.7 us; the launch traced here: 95.5 us
  waiting for transfers between devices  33.2 us (35%)
  Pallas kernels  28.8 us (30%)
  starting transfers between devices  22.4 us (23%)
  blocking collectives  10 us (10%)
    ppermute x20, waiting for transfers between devices, swap(): return lax.ppermute(value, axis, [(i, i ^ step) for i in range(size)])  33.2 us
    ppermute x20, starting transfers between devices, swap(): return lax.ppermute(value, axis, [(i, i ^ step) for i in range(size)])  22.4 us
    pallas_call x4, Pallas kernels, backward(): pl.pallas_call(functools.partial(backward_kernel, count=count, steps=step...  10.6 us
    all_gather x1, blocking collectives, shards(): gathered = lax.all_gather(part, 'row', axis_index_groups=cores, tiled=True)  10 us
    pallas_call x5, Pallas kernels, forward(): pl.pallas_call(functools.partial(forward_kernel, first=first, step=step),...  7.94 us
    pallas_call x1, Pallas kernels, dense_rows(): pl.pallas_call(functools.partial(dense_kernel, steps=steps, window=window...  7.42 us
  transfers between devices with their start and end apart: 20, of which 8 were waited for; matrix products, arithmetic and copies ran while one was open for 0% of the time, Pallas kernels for 24%

profile of v9, /device:TPU:0, one launch (start us, length us, event | category | flops | bytes accessed | tf_op | source)
XLA Modules:
  0.0 95.5 jit_solution(17099305305411945757)
XLA Ops:
  0.6 4.0 %collective-permute-start.1 = (bf16[512,256]{1,0:T(8,128)(2,1)}, bf16[512,256]{1,0:T(8,128)(2,1)S(1)}, u32[]{:S(2)}, u32[]{:S(2)}) collective-permute-start(bf16[512,256]{1,0:T(8,128)(2,1)} %features_ref.1), channel_id=1, source_target_pairs={{0,24},{4,28},{8,16},{12,20},{16,8},{20,12},{24,0},{28,4},{1,25},{... | collective-permute-start | bytes 786440 | tf_op jit(solution)/shard_map/ppermute | solution.py:278
  4.6 0.5 collective-permute-start.3
  5.3 7.4 %dense_rows.1 = (bf16[512,4096]{1,0:T(8,128)(2,1)S(1)}, bf16[512,4096]{1,0:T(8,128)(2,1)S(1)}, bf16[512,4096]{1,0:T(8,128)(2,1)S(1)}, bf16[512,4096]{1,0:T(8,128)(2,1)S(1)}, bf16[512,256]{1,0:T(8,128)(2,1)S(1)}) custom-call(s32[2]{0:T(128)S(1)} %pad_add_fusion.where, s32[16]{0:T(128)} %bitcast.13, s32[448]{0:T(512)} %bitcast.12, ...), custom_call_target="tpu_custom_call" | custom-call | bytes 41943040 | tf_op jit(solution)/shard_map/dense_rows/pallas_call | solution.py:102
  12.7 4.3 %collective-permute-done.3.refs_2_ = bf16[512,256]{1,0:T(8,128)(2,1)S(1)} collective-permute-done((bf16[512,256]{1,0:T(8,128)(2,1)}, bf16[512,256]{1,0:T(8,128)(2,1)S(1)}, u32[]{:S(2)}, u32[]{:S(2)}) %collective-permute-start.3) | collective-permute-done | bytes 262176 | tf_op jit(solution)/shard_map/ppermute | solution.py:278
  17.0 0.5 collective-permute-start.5
  17.6 1.2 %forward_rows.8.refs_4_ = f32[512,256]{1,0:T(8,128)S(1)} custom-call(s32[2]{0:T(128)S(1)} %pad_add_fusion.where, bf16[512,4096]{1,0:T(8,128)(2,1)S(1)} %get-tuple-element.18.refs_5_.a_ref.refs_1_, bf16[512,256]{1,0:T(8,128)(2,1)S(1)} %get-tuple-element.15.refs_0_, bf16[512,256]{1,0:T(8,128)(2,1)S(1)} %get-tuple-element.19.refs_2_.refs_1_, ...), custom_call_target="tpu_custom_call" | custom-call | flops 1073741824 | bytes 4194304 | tf_op jit(solution)/shard_map/forward_rows/pallas_call | solution.py:136
  19.3 1.8 %forward_rows.6 = bf16[512,256]{1,0:T(8,128)(2,1)S(1)} custom-call(s32[2]{0:T(128)S(1)} %pad_add_fusion.where, bf16[512,4096]{1,0:T(8,128)(2,1)S(1)} %get-tuple-element.16.refs_3_.a_ref.refs_0_, bf16[512,256]{1,0:T(8,128)(2,1)S(1)} %get-tuple-element.15.refs_0_, bf16[512,256]{1,0:T(8,128)(2,1)S(1)} %collective-permute-done.refs_1_.refs_0_, ...), custom_call_target="tpu_custom_call" | custom-call | flops 1073741824 | bytes 4194304 | tf_op jit(solution)/shard_map/forward_rows/pallas_call | solution.py:136
  21.1 3.7 %collective-permute-start.7 = (bf16[512,256]{1,0:T(8,128)(2,1)S(1)}, bf16[512,256]{1,0:T(8,128)(2,1)S(1)}, u32[]{:S(2)}, u32[]{:S(2)}) collective-permute-start(bf16[512,256]{1,0:T(8,128)(2,1)S(1)} %forward_rows.6), channel_id=1, source_target_pairs={{0,3},{1,2},{2,1},{3,0},{4,7},{5,6},{6,5},{7,4},{8,11},{9,10},{10,... | collective-permute-start | bytes 786440 | tf_op jit(solution)/shard_map/ppermute | solution.py:278
  24.8 1.8 %forward_rows.7 = bf16[512,256]{1,0:T(8,128)(2,1)S(1)} custom-call(s32[2]{0:T(128)S(1)} %pad_add_fusion.where, bf16[512,4096]{1,0:T(8,128)(2,1)S(1)} %get-tuple-element.17.refs_4_.a_ref.refs_0_, bf16[512,256]{1,0:T(8,128)(2,1)S(1)} %get-tuple-element.15.refs_0_, bf16[512,256]{1,0:T(8,128)(2,1)S(1)} %collective-permute-done.refs_1_.refs_0_, ...), custom_call_target="tpu_custom_call" | custom-call | flops 1073741824 | bytes 4194304 | tf_op jit(solution)/shard_map/forward_rows/pallas_call | solution.py:136
  26.7 1.3 %forward_rows.9 = bf16[512,256]{1,0:T(8,128)(2,1)S(1)} custom-call(s32[2]{0:T(128)S(1)} %pad_add_fusion.where, bf16[512,4096]{1,0:T(8,128)(2,1)S(1)} %get-tuple-element.18.refs_5_.a_ref.refs_1_, bf16[512,256]{1,0:T(8,128)(2,1)S(1)} %collective-permute-done.refs_1_.refs_0_, bf16[512,256]{1,0:T(8,128)(2,1)S(1)} %collective-permute-done.4.refs_3_.refs_1_, ...), custom_call_target="tpu_custom_call" | custom-call | flops 1073741824 | bytes 4194304 | tf_op jit(solution)/shard_map/forward_rows/pallas_call | solution.py:136
  28.0 0.8 collective-permute-start.9
  28.8 1.8 %forward_rows.5.refs_0_ = f32[512,256]{1,0:T(8,128)S(1)} custom-call(s32[2]{0:T(128)S(1)} %pad_add_fusion.where, bf16[512,4096]{1,0:T(8,128)(2,1)S(1)} %get-tuple-element.14.refs_6_.a_ref.refs_0_, bf16[512,256]{1,0:T(8,128)(2,1)S(1)} %get-tuple-element.15.refs_0_, bf16[512,256]{1,0:T(8,128)(2,1)S(1)} %collective-permute-done.refs_1_.refs_0_, ...), custom_call_target="tpu_custom_call" | custom-call | flops 1073741824 | bytes 4194304 | tf_op jit(solution)/shard_map/forward_rows/pallas_call | solution.py:136
  30.6 1.6 %collective-permute-done.7.refs_1_ = bf16[512,256]{1,0:T(8,128)(2,1)S(1)} collective-permute-done((bf16[512,256]{1,0:T(8,128)(2,1)S(1)}, bf16[512,256]{1,0:T(8,128)(2,1)S(1)}, u32[]{:S(2)}, u32[]{:S(2)}) %collective-permute-start.7) | collective-permute-done | bytes 262176 | tf_op jit(solution)/shard_map/ppermute | solution.py:278
  32.2 15.2 %collective-permute-done.8.refs_2_ = bf16[512,256]{1,0:T(8,128)(2,1)S(1)} collective-permute-done((bf16[512,256]{1,0:T(8,128)(2,1)S(1)}, bf16[512,256]{1,0:T(8,128)(2,1)S(1)}, u32[]{:S(2)}, u32[]{:S(2)}) %collective-permute-start.8) | collective-permute-done | bytes 262176 | tf_op jit(solution)/shard_map/ppermute | solution.py:278
  47.4 1.1 %middle.1 = (bf16[512,256]{1,0:T(8,128)(2,1)}, bf16[256,512]{1,0:T(8,128)(2,1)S(1)}, f32[256,256]{1,0:T(8,128)S(1)}) custom-call(f32[512,256]{1,0:T(8,128)S(1)} %forward_rows.5.refs_0_, bf16[512,256]{1,0:T(8,128)(2,1)S(1)} %collective-permute-done.7.refs_1_, bf16[512,256]{1,0:T(8,128)(2,1)S(1)} %collective-permute-done.8.refs_2_, ...), custom_call_target="tpu_custom_call" | custom-call | flops 201326592 | bytes 1310720 | tf_op jit(solution)/shard_map/middle/pallas_call | solution.py:169
  48.5 3.0 %collective-permute-start.13 = (bf16[256,512]{1,0:T(8,128)(2,1)S(1)}, bf16[256,512]{1,0:T(8,128)(2,1)S(1)}, u32[]{:S(2)}, u32[]{:S(2)}) collective-permute-start(bf16[256,512]{1,0:T(8,128)(2,1)S(1)} %get-tuple-element.24.refs_2_), channel_id=1, source_target_pairs={{0,2},{1,3},{2,0},{3,1},{4,6},{5,7},{6,4},{7,5},{8,10},{9,11},{10,... | collective-permute-start | bytes 786440 | tf_op jit(solution)/shard_map/ppermute | solution.py:278
  51.5 1.3 %collective-permute-start.12 = (bf16[256,512]{1,0:T(8,128)(2,1)S(1)}, bf16[256,512]{1,0:T(8,128)(2,1)S(1)}, u32[]{:S(2)}, u32[]{:S(2)}) collective-permute-start(bf16[256,512]{1,0:T(8,128)(2,1)S(1)} %get-tuple-element.24.refs_2_), channel_id=1, source_target_pairs={{0,3},{1,2},{2,1},{3,0},{4,7},{5,6},{6,5},{7,4},{8,11},{9,10},{10,... | collective-permute-start | bytes 786440 | tf_op jit(solution)/shard_map/ppermute | solution.py:278
  52.9 10.0 %all_gather.3.refs_0_ = bf16[1024,256]{1,0:T(8,128)(2,1)S(1)} all-gather(bf16[256,256]{1,0:T(8,128)(2,1)S(1)} %add_convert_fusion), channel_id=1, replica_groups={{0,8,16,24},{4,12,20,28},{1,9,17,25},{5,13,21,29},{2,10,18,26},{6,14,22..., dimensions={0}, use_global_device_ids=true | all-gather | bytes 655360 | tf_op jit(solution)/shard_map/all_gather | solution.py:311
  63.0 4.1 %backward_cols.4.refs_2_ = f32[8,256,512]{2,1,0:T(8,128)S(1)} custom-call(s32[2]{0:T(128)S(1)} %pad_add_fusion.where, bf16[512,4096]{1,0:T(8,128)(2,1)S(1)} %get-tuple-element.14.refs_6_.a_ref.refs_0_, bf16[512,4096]{1,0:T(8,128)(2,1)S(1)} %get-tuple-element.18.refs_5_.a_ref.refs_1_, bf16[256,512]{1,0:T(8,128)(2,1)S(1)} %get-tuple-element.24.refs_2_, ...), custom_call_target="tpu_custom_call" | custom-call | tf_op jit(solution)/shard_map/backward_cols/pallas_call | solution.py:206
  67.1 2.8 %collective-permute-done.13.refs_1_ = bf16[256,512]{1,0:T(8,128)(2,1)S(1)} collective-permute-done((bf16[256,512]{1,0:T(8,128)(2,1)S(1)}, bf16[256,512]{1,0:T(8,128)(2,1)S(1)}, u32[]{:S(2)}, u32[]{:S(2)}) %collective-permute-start.13) | collective-permute-done | bytes 262176 | tf_op jit(solution)/shard_map/ppermute | solution.py:278
  69.9 3.0 %backward_cols.5.refs_2_ = f32[8,256,512]{2,1,0:T(8,128)S(1)} custom-call(s32[2]{0:T(128)S(1)} %pad_add_fusion.where, bf16[512,4096]{1,0:T(8,128)(2,1)S(1)} %get-tuple-element.17.refs_4_.a_ref.refs_0_, bf16[256,512]{1,0:T(8,128)(2,1)S(1)} %collective-permute-done.13.refs_1_, f32[8,256,512]{2,1,0:T(8,128)S(1)} %backward_cols.4.refs_2_), custom_call_target="tpu_custom_call" | custom-call | tf_op jit(solution)/shard_map/backward_cols/pallas_call | solution.py:206
  72.9 1.8 %backward_cols.7 = bf16[4,256,512]{2,1,0:T(8,128)(2,1)S(1)} custom-call(s32[2]{0:T(128)S(1)} %pad_add_fusion.where, bf16[512,4096]{1,0:T(8,128)(2,1)S(1)} %get-tuple-element.16.refs_3_.a_ref.refs_0_, bf16[256,512]{1,0:T(8,128)(2,1)S(1)} %collective-permute-done.12.refs_1_, f32[8,256,512]{2,1,0:T(8,128)S(1)} %backward_cols.5.refs_2_, ...), custom_call_target="tpu_custom_call" | custom-call | tf_op jit(solution)/shard_map/backward_cols/pallas_call | solution.py:206
  74.7 2.8 %collective-permute-start.11 = (bf16[256,256]{1,0:T(8,128)(2,1)S(1)}, bf16[256,256]{1,0:T(8,128)(2,1)S(1)}, u32[]{:S(2)}, u32[]{:S(2)}) collective-permute-start(bf16[256,256]{1,0:T(8,128)(2,1)S(1)} %total.3.refs_0_.refs_3_), channel_id=1, source_target_pairs={{0,1},{1,0},{2,3},{3,2},{4,5},{5,4},{6,7},{7,6},{8,9},{9,8},{10,11... | collective-permute-start | bytes 393224 | tf_op jit(solution)/shard_map/ppermute | solution.py:278
  77.6 1.8 %backward_cols.6.refs_2_.refs_0_ = f32[4,256,512]{2,1,0:T(8,128)S(1)} custom-call(s32[2]{0:T(128)S(1)} %pad_add_fusion.where, bf16[512,4096]{1,0:T(8,128)(2,1)S(1)} %get-tuple-element.16.refs_3_.a_ref.refs_0_, bf16[256,512]{1,0:T(8,128)(2,1)S(1)} %collective-permute-done.12.refs_1_, f32[8,256,512]{2,1,0:T(8,128)S(1)} %backward_cols.5.refs_2_), custom_call_target="tpu_custom_call" | custom-call | tf_op jit(solution)/shard_map/backward_cols/pallas_call | solution.py:206
  79.6 2.4 %collective-permute-start.19 = (bf16[256,512]{1,0:T(8,128)(2,1)S(1)}, bf16[256,512]{1,0:T(8,128)(2,1)S(1)}, u32[]{:S(2)}, u32[]{:S(2)}) collective-permute-start(bf16[256,512]{1,0:T(8,128)(2,1)S(1)} %get-tuple-element.25), channel_id=1, source_target_pairs={{0,24},{4,28},{8,16},{12,20},{16,8},{20,12},{24,0},{28,4},{1,25},{... | collective-permute-start | bytes 786440 | tf_op jit(solution)/shard_map/ppermute | solution.py:278
  82.0 0.6 collective-permute-start.18
  82.7 0.5 collective-permute-start.17
  83.2 1.8 %collective-permute-start.15 = (bf16[256,256]{1,0:T(8,128)(2,1)S(1)}, bf16[256,256]{1,0:T(8,128)(2,1)S(1)}, u32[]{:S(2)}, u32[]{:S(2)}) collective-permute-start(bf16[256,256]{1,0:T(8,128)(2,1)S(1)} %total.4.refs_0_), channel_id=1, source_target_pairs={{0,2},{1,3},{2,0},{3,1},{4,6},{5,7},{6,4},{7,5},{8,10},{9,11},{10,... | collective-permute-start | bytes 393224 | tf_op jit(solution)/shard_map/ppermute | solution.py:278
  85.0 6.7 %collective-permute-done.15.refs_1_ = bf16[256,256]{1,0:T(8,128)(2,1)S(1)} collective-permute-done((bf16[256,256]{1,0:T(8,128)(2,1)S(1)}, bf16[256,256]{1,0:T(8,128)(2,1)S(1)}, u32[]{:S(2)}, u32[]{:S(2)}) %collective-permute-start.15) | collective-permute-done | bytes 131104 | tf_op jit(solution)/shard_map/ppermute | solution.py:278
  91.7 0.7 total.5
  92.5 2.1 %collective-permute-done.18.refs_3_ = bf16[256,512]{1,0:T(8,128)(2,1)S(1)} collective-permute-done((bf16[256,512]{1,0:T(8,128)(2,1)S(1)}, bf16[256,512]{1,0:T(8,128)(2,1)S(1)}, u32[]{:S(2)}, u32[]{:S(2)}) %collective-permute-start.18) | collective-permute-done | bytes 262176 | tf_op jit(solution)/shard_map/ppermute | solution.py:278
  94.6 0.9 finish.1
  (32 shorter events, 1.3 us)
Async XLA Ops:
  0.6 12.1 %collective-permute-start.1 = (bf16[512,256]{1,0:T(8,128)(2,1)}, bf16[512,256]{1,0:T(8,128)(2,1)S(1)}, u32[]{:S(2)}, u32[]{:S(2)}) collective-permute-start(bf16[512,256]{1,0:T(8,128)(2,1)} %features_ref.1), channel_id=1, source_target_pairs={{0,24},{4,28},{8,16},{12,20},{16,8},{20,12},{24,0},{28,4},{1,25},{... | collective-permute-start | bytes 786440 | tf_op jit(solution)/shard_map/ppermute | solution.py:278
  4.6 12.4 %collective-permute-start.3 = (bf16[512,256]{1,0:T(8,128)(2,1)}, bf16[512,256]{1,0:T(8,128)(2,1)S(1)}, u32[]{:S(2)}, u32[]{:S(2)}) collective-permute-start(bf16[512,256]{1,0:T(8,128)(2,1)} %features_ref.1), channel_id=1, source_target_pairs={{0,8},{4,12},{8,0},{12,4},{16,24},{20,28},{24,16},{28,20},{1,9},{5... | collective-permute-start | bytes 786440 | tf_op jit(solution)/shard_map/ppermute | solution.py:278
  5.1 11.9 %collective-permute-start.2 = (bf16[512,256]{1,0:T(8,128)(2,1)}, bf16[512,256]{1,0:T(8,128)(2,1)S(1)}, u32[]{:S(2)}, u32[]{:S(2)}) collective-permute-start(bf16[512,256]{1,0:T(8,128)(2,1)} %features_ref.1), channel_id=1, source_target_pairs={{0,16},{4,20},{8,24},{12,28},{16,0},{20,4},{24,8},{28,12},{1,17},{... | collective-permute-start | bytes 786440 | tf_op jit(solution)/shard_map/ppermute | solution.py:278
  5.2 13.6 %collective-permute-start = (bf16[512,256]{1,0:T(8,128)(2,1)}, bf16[512,256]{1,0:T(8,128)(2,1)S(1)}, u32[]{:S(2)}, u32[]{:S(2)}) collective-permute-start(bf16[512,256]{1,0:T(8,128)(2,1)} %features_ref.1), channel_id=1, source_target_pairs={{0,4},{4,0},{8,12},{12,8},{16,20},{20,16},{24,28},{28,24},{1,5},{5... | collective-permute-start | bytes 786440 | tf_op jit(solution)/shard_map/ppermute | solution.py:278
  17.0 1.8 %collective-permute-start.4 = (bf16[512,256]{1,0:T(8,128)(2,1)S(1)}, bf16[512,256]{1,0:T(8,128)(2,1)S(1)}, u32[]{:S(2)}, u32[]{:S(2)}) collective-permute-start(bf16[512,256]{1,0:T(8,128)(2,1)S(1)} %get-tuple-element.19.refs_2_.refs_1_), channel_id=1, source_target_pairs={{0,4},{4,0},{8,12},{12,8},{16,20},{20,16},{24,28},{28,24},{1,5},{5... | collective-permute-start | bytes 786440 | tf_op jit(solution)/shard_map/ppermute | solution.py:278
  17.0 1.9 %collective-permute-start.5 = (bf16[512,256]{1,0:T(8,128)(2,1)S(1)}, bf16[512,256]{1,0:T(8,128)(2,1)S(1)}, u32[]{:S(2)}, u32[]{:S(2)}) collective-permute-start(bf16[512,256]{1,0:T(8,128)(2,1)S(1)} %get-tuple-element.20.refs_4_.refs_2_), channel_id=1, source_target_pairs={{0,4},{4,0},{8,12},{12,8},{16,20},{20,16},{24,28},{28,24},{1,5},{5... | collective-permute-start | bytes 786440 | tf_op jit(solution)/shard_map/ppermute | solution.py:278
  17.5 1.8 %collective-permute-start.6 = (bf16[512,256]{1,0:T(8,128)(2,1)S(1)}, bf16[512,256]{1,0:T(8,128)(2,1)S(1)}, u32[]{:S(2)}, u32[]{:S(2)}) collective-permute-start(bf16[512,256]{1,0:T(8,128)(2,1)S(1)} %get-tuple-element.21.refs_6_.refs_3_), channel_id=1, source_target_pairs={{0,4},{4,0},{8,12},{12,8},{16,20},{20,16},{24,28},{28,24},{1,5},{5... | collective-permute-start | bytes 786440 | tf_op jit(solution)/shard_map/ppermute | solution.py:278
  21.1 11.1 %collective-permute-start.7 = (bf16[512,256]{1,0:T(8,128)(2,1)S(1)}, bf16[512,256]{1,0:T(8,128)(2,1)S(1)}, u32[]{:S(2)}, u32[]{:S(2)}) collective-permute-start(bf16[512,256]{1,0:T(8,128)(2,1)S(1)} %forward_rows.6), channel_id=1, source_target_pairs={{0,3},{1,2},{2,1},{3,0},{4,7},{5,6},{6,5},{7,4},{8,11},{9,10},{10,... | collective-permute-start | bytes 786440 | tf_op jit(solution)/shard_map/ppermute | solution.py:278
  26.6 20.8 %collective-permute-start.8 = (bf16[512,256]{1,0:T(8,128)(2,1)S(1)}, bf16[512,256]{1,0:T(8,128)(2,1)S(1)}, u32[]{:S(2)}, u32[]{:S(2)}) collective-permute-start(bf16[512,256]{1,0:T(8,128)(2,1)S(1)} %forward_rows.7), channel_id=1, source_target_pairs={{0,2},{1,3},{2,0},{3,1},{4,6},{5,7},{6,4},{7,5},{8,10},{9,11},{10,... | collective-permute-start | bytes 786440 | tf_op jit(solution)/shard_map/ppermute | solution.py:278
  28.0 19.4 %copy-start = (bf16[512,256]{1,0:T(8,128)(2,1)S(1)}, bf16[512,256]{1,0:T(8,128)(2,1)}, u32[]{:S(2)}) copy-start(bf16[512,256]{1,0:T(8,128)(2,1)} %refs_5_.1) | copy-start | bytes 786436
  28.0 19.4 %copy-start.1 = (bf16[256,256]{1,0:T(8,128)(2,1)S(1)}, bf16[256,256]{1,0:T(8,128)(2,1)}, u32[]{:S(2)}) copy-start(bf16[256,256]{1,0:T(8,128)(2,1)} %refs_4_.1) | copy-start | bytes 393220
  28.0 19.4 %collective-permute-start.9 = (bf16[512,256]{1,0:T(8,128)(2,1)S(1)}, bf16[512,256]{1,0:T(8,128)(2,1)S(1)}, u32[]{:S(2)}, u32[]{:S(2)}) collective-permute-start(bf16[512,256]{1,0:T(8,128)(2,1)S(1)} %forward_rows.9), channel_id=1, source_target_pairs={{0,1},{1,0},{2,3},{3,2},{4,5},{5,4},{6,7},{7,6},{8,9},{9,8},{10,11... | collective-permute-start | bytes 786440 | tf_op jit(solution)/shard_map/ppermute | solution.py:278
  48.5 4.4 %collective-permute-start.10 = (f32[256,256]{1,0:T(8,128)S(1)}, f32[256,256]{1,0:T(8,128)S(1)}, u32[]{:S(2)}, u32[]{:S(2)}) collective-permute-start(f32[256,256]{1,0:T(8,128)S(1)} %get-tuple-element.23), channel_id=1, source_target_pairs={{0,4},{4,0},{8,12},{12,8},{16,20},{20,16},{24,28},{28,24},{1,5},{5... | collective-permute-start | bytes 786440 | tf_op jit(solution)/shard_map/ppermute | solution.py:278
  48.5 14.5 %collective-permute-start.14 = (bf16[256,512]{1,0:T(8,128)(2,1)S(1)}, bf16[256,512]{1,0:T(8,128)(2,1)S(1)}, u32[]{:S(2)}, u32[]{:S(2)}) collective-permute-start(bf16[256,512]{1,0:T(8,128)(2,1)S(1)} %get-tuple-element.24.refs_2_), channel_id=1, source_target_pairs={{0,1},{1,0},{2,3},{3,2},{4,5},{5,4},{6,7},{7,6},{8,9},{9,8},{10,11... | collective-permute-start | bytes 786440 | tf_op jit(solution)/shard_map/ppermute | solution.py:278
  48.5 21.4 %collective-permute-start.13 = (bf16[256,512]{1,0:T(8,128)(2,1)S(1)}, bf16[256,512]{1,0:T(8,128)(2,1)S(1)}, u32[]{:S(2)}, u32[]{:S(2)}) collective-permute-start(bf16[256,512]{1,0:T(8,128)(2,1)S(1)} %get-tuple-element.24.refs_2_), channel_id=1, source_target_pairs={{0,2},{1,3},{2,0},{3,1},{4,6},{5,7},{6,4},{7,5},{8,10},{9,11},{10,... | collective-permute-start | bytes 786440 | tf_op jit(solution)/shard_map/ppermute | solution.py:278
  51.5 21.4 %collective-permute-start.12 = (bf16[256,512]{1,0:T(8,128)(2,1)S(1)}, bf16[256,512]{1,0:T(8,128)(2,1)S(1)}, u32[]{:S(2)}, u32[]{:S(2)}) collective-permute-start(bf16[256,512]{1,0:T(8,128)(2,1)S(1)} %get-tuple-element.24.refs_2_), channel_id=1, source_target_pairs={{0,3},{1,2},{2,1},{3,0},{4,7},{5,6},{6,5},{7,4},{8,11},{9,10},{10,... | collective-permute-start | bytes 786440 | tf_op jit(solution)/shard_map/ppermute | solution.py:278
  74.7 4.7 %collective-permute-start.16 = (bf16[4,256,512]{2,1,0:T(8,128)(2,1)S(1)}, bf16[4,256,512]{2,1,0:T(8,128)(2,1)S(1)}, u32[]{:S(2)}, u32[]{:S(2)}) collective-permute-start(bf16[4,256,512]{2,1,0:T(8,128)(2,1)S(1)} %backward_cols.7), channel_id=1, source_target_pairs={{0,4},{4,0},{8,12},{12,8},{16,20},{20,16},{24,28},{28,24},{1,5},{5... | collective-permute-start | bytes 3145736 | tf_op jit(solution)/shard_map/ppermute | solution.py:278
  74.7 8.5 %collective-permute-start.11 = (bf16[256,256]{1,0:T(8,128)(2,1)S(1)}, bf16[256,256]{1,0:T(8,128)(2,1)S(1)}, u32[]{:S(2)}, u32[]{:S(2)}) collective-permute-start(bf16[256,256]{1,0:T(8,128)(2,1)S(1)} %total.3.refs_0_.refs_3_), channel_id=1, source_target_pairs={{0,1},{1,0},{2,3},{3,2},{4,5},{5,4},{6,7},{7,6},{8,9},{9,8},{10,11... | collective-permute-start | bytes 393224 | tf_op jit(solution)/shard_map/ppermute | solution.py:278
  79.6 12.8 %collective-permute-start.19 = (bf16[256,512]{1,0:T(8,128)(2,1)S(1)}, bf16[256,512]{1,0:T(8,128)(2,1)S(1)}, u32[]{:S(2)}, u32[]{:S(2)}) collective-permute-start(bf16[256,512]{1,0:T(8,128)(2,1)S(1)} %get-tuple-element.25), channel_id=1, source_target_pairs={{0,24},{4,28},{8,16},{12,20},{16,8},{20,12},{24,0},{28,4},{1,25},{... | collective-permute-start | bytes 786440 | tf_op jit(solution)/shard_map/ppermute | solution.py:278
  82.0 12.6 %collective-permute-start.18 = (bf16[256,512]{1,0:T(8,128)(2,1)S(1)}, bf16[256,512]{1,0:T(8,128)(2,1)S(1)}, u32[]{:S(2)}, u32[]{:S(2)}) collective-permute-start(bf16[256,512]{1,0:T(8,128)(2,1)S(1)} %get-tuple-element.26), channel_id=1, source_target_pairs={{0,16},{4,20},{8,24},{12,28},{16,0},{20,4},{24,8},{28,12},{1,17},{... | collective-permute-start | bytes 786440 | tf_op jit(solution)/shard_map/ppermute | solution.py:278
  82.7 11.9 %collective-permute-start.17 = (bf16[256,512]{1,0:T(8,128)(2,1)S(1)}, bf16[256,512]{1,0:T(8,128)(2,1)S(1)}, u32[]{:S(2)}, u32[]{:S(2)}) collective-permute-start(bf16[256,512]{1,0:T(8,128)(2,1)S(1)} %get-tuple-element.27), channel_id=1, source_target_pairs={{0,8},{4,12},{8,0},{12,4},{16,24},{20,28},{24,16},{28,20},{1,9},{5... | collective-permute-start | bytes 786440 | tf_op jit(solution)/shard_map/ppermute | solution.py:278
  83.2 8.5 %collective-permute-start.15 = (bf16[256,256]{1,0:T(8,128)(2,1)S(1)}, bf16[256,256]{1,0:T(8,128)(2,1)S(1)}, u32[]{:S(2)}, u32[]{:S(2)}) collective-permute-start(bf16[256,256]{1,0:T(8,128)(2,1)S(1)} %total.4.refs_0_), channel_id=1, source_target_pairs={{0,2},{1,3},{2,0},{3,1},{4,6},{5,7},{6,4},{7,5},{8,10},{9,11},{10,... | collective-permute-start | bytes 393224 | tf_op jit(solution)/shard_map/ppermute | solution.py:278

commit v10 on v9

--- a/solution.py
+++ b/solution.py
@@ -286,6 +286,7 @@
     col_tiles = depth * n_row // adj.shape[1]
     chips = n_row // 2
     where = jnp.stack([lax.axis_index("row"), lax.axis_index("col")]).astype(jnp.int32)
+    line = n_col == 4
     steps = [*range(n_col - 1, 0, -1), 0]
 
     *blocks, near_features = dense_rows(where, steps, counts, cols, adj, features, rows, col_tiles)
@@ -296,24 +297,37 @@
     even = [near_features, *away[::-1]]
     parts = [shard for pair in zip(even, odd) for shard in pair]
 
-    half = forward(where, blocks[2], even, 0, 2, [], jnp.float32)
-    shares = [forward(where, block, parts, 0, 1, [], jnp.bfloat16) for block in blocks[:-1]]
-    shares[2] = forward(where, blocks[2], odd, 1, 2, [half], jnp.bfloat16)
-    came = [swap(share, "col", n_col, s) for s, share in zip(steps, shares)]
-    mine = forward(where, blocks[-1], parts, 0, 1, [], jnp.float32)
+    half = forward(where, dense[n_col - 1], even, 0, 2, [], jnp.float32)
+    shares = {n_col - 1: forward(where, dense[n_col - 1], odd, 1, 2, [half], jnp.bfloat16)}
+    for s in steps[1:-1]:
+        shares[s] = forward(where, dense[s], parts, 0, 1, [], jnp.bfloat16)
+    if line:
+        relayed = lax.ppermute(shares[3], "col", [(0, 1), (3, 2)])
+        came = [lax.ppermute(shares[3], "col", [(1, 2), (2, 1)])]
+        joined = (shares[2].astype(jnp.float32) + relayed.astype(jnp.float32)).astype(jnp.bfloat16)
+        came += [swap(joined, "col", n_col, 2), swap(shares[1], "col", n_col, 1)]
+    else:
+        came = [swap(share, "col", n_col, s) for s, share in shares.items()]
+    mine = forward(where, dense[0], parts, 0, 1, [], jnp.float32)
     scale = 1.0 / math.sqrt(rows * n_row * n_col)
     hidden, piece, part = middle([mine, *came], weight, upstream, scale)
 
-    pieces = {s: swap(piece, "col", n_col, s) for s in steps[:-1]}
-    pieces[0] = piece
     cores = [[i for i in range(n_row) if i % 2 == core] for core in range(2)]
     part = (part + swap(part, "row", n_row, 1)).astype(jnp.bfloat16)
     gathered = lax.all_gather(part, "row", axis_index_groups=cores, tiled=True)
     part = total([gathered], part.shape[0], jnp.bfloat16)
+    if line:
+        pieces = {s: swap(piece, "col", n_col, s) for s in (1, 2)}
+        pieces[0], pieces[2] = gate([piece, pieces[2]], [part])
+        beside = lax.ppermute(pieces[0], "col", [(1, 2), (2, 1)])
+        pieces[3] = beside + lax.ppermute(pieces[2], "col", [(1, 0), (2, 3)])
+    else:
+        pieces = {s: swap(piece, "col", n_col, s) for s in steps[:-1]}
+        pieces[0] = piece
 
     every = list(range(n_row))
     sums, latest = None, n_col - 1
-    for group in [[0, 1], *[[s] for s in range(2, n_col - 1)]]:
+    for group in [list(range(n_col - 1))]:
         sums = backward(where, [dense[s] for s in group], [pieces[s] for s in group], every, depth, sums, jnp.float32)
     last = functools.partial(backward, where, [dense[latest]], [pieces[latest]])
     sent = last(every[1::2], depth, sums, jnp.bfloat16, [part])

time: 95.7 us -> 93.1 us (0.973)
  waiting for transfers between devices: 33.2 us -> 30.7 us
  Pallas kernels: 28.8 us -> 26.8 us
  starting transfers between devices: 22.4 us -> 24 us
    ppermute x0 -> x4, starting transfers between devices: none -> 6.31 us  [the longest x1 3.5 us: shards(): relayed = lax.ppermute(shares[3], 'col', [(0, 1), (3, 2)])]
    ppermute x20 -> x18, waiting for transfers between devices: 33.2 us -> 27.4 us  [swap(): return lax.ppermute(value, axis, [(i, i ^ step) for i in range(size)])]
    ppermute x20 -> x18, starting transfers between devices: 22.4 us -> 17.7 us  [swap(): return lax.ppermute(value, axis, [(i, i ^ step) for i in range(size)])]
    ppermute x0 -> x4, waiting for transfers between devices: none -> 3.31 us  [the longest x1 3.3 us: shards(): pieces[3] = beside + lax.ppermute(pieces[2], 'col', [(1, 0), (2, 3)])]
    pallas_call x4 -> x3, Pallas kernels: 10.6 us -> 8.74 us  [backward(): pl.pallas_call(functools.partial(backward_kernel, count=count, steps=step...]
  transfers between devices with their start and end apart: 20 -> 22, of which waited for: 8 -> 11; matrix products, arithmetic and copies ran while one was open for 0% -> 0% of each run, Pallas kernels for 24% -> 23%
where the time goes in v10:
time: 93.1 us; the launch traced here: 92.9 us
  waiting for transfers between devices  30.7 us (33%)
  Pallas kernels  26.8 us (29%)
  starting transfers between devices  24 us (26%)
  blocking collectives  10 us (11%)
    ppermute x18, waiting for transfers between devices, swap(): return lax.ppermute(value, axis, [(i, i ^ step) for i in range(size)])  27.4 us
    ppermute x18, starting transfers between devices, swap(): return lax.ppermute(value, axis, [(i, i ^ step) for i in range(size)])  17.7 us
    all_gather x1, blocking collectives, shards(): gathered = lax.all_gather(part, 'row', axis_index_groups=cores, tiled=True)  10 us
    pallas_call x3, Pallas kernels, backward(): pl.pallas_call(functools.partial(backward_kernel, count=count, steps=step...  8.74 us
    pallas_call x5, Pallas kernels, forward(): pl.pallas_call(functools.partial(forward_kernel, first=first, step=step),...  7.94 us
    pallas_call x1, Pallas kernels, dense_rows(): pl.pallas_call(functools.partial(dense_kernel, steps=steps, window=window...  7.33 us
    ppermute x1, starting transfers between devices, shards(): relayed = lax.ppermute(shares[3], 'col', [(0, 1), (3, 2)])  3.5 us
    ppermute x1, waiting for transfers between devices, shards(): pieces[3] = beside + lax.ppermute(pieces[2], 'col', [(1, 0), (2, 3)])  3.3 us
  transfers between devices with their start and end apart: 22, of which 11 were waited for; matrix products, arithmetic and copies ran while one was open for 0% of the time, Pallas kernels for 23%

profile of v10, /device:TPU:0, one launch (start us, length us, event | category | flops | bytes accessed | tf_op | source)
XLA Modules:
  0.0 92.9 jit_solution(16284034117360557754)
XLA Ops:
  0.6 4.0 %collective-permute-start.1 = (bf16[512,256]{1,0:T(8,128)(2,1)}, bf16[512,256]{1,0:T(8,128)(2,1)S(1)}, u32[]{:S(2)}, u32[]{:S(2)}) collective-permute-start(bf16[512,256]{1,0:T(8,128)(2,1)} %features_ref.1), channel_id=1, source_target_pairs={{0,24},{4,28},{8,16},{12,20},{16,8},{20,12},{24,0},{28,4},{1,25},{... | collective-permute-start | bytes 786440 | tf_op jit(solution)/shard_map/ppermute | solution.py:278
  5.3 7.3 %dense_rows.1 = (bf16[512,4096]{1,0:T(8,128)(2,1)S(1)}, bf16[512,4096]{1,0:T(8,128)(2,1)S(1)}, bf16[512,4096]{1,0:T(8,128)(2,1)S(1)}, bf16[512,4096]{1,0:T(8,128)(2,1)S(1)}, bf16[512,256]{1,0:T(8,128)(2,1)S(1)}) custom-call(s32[2]{0:T(128)S(1)} %pad_add_fusion.where, s32[16]{0:T(128)} %bitcast.13, s32[448]{0:T(512)} %bitcast.12, ...), custom_call_target="tpu_custom_call" | custom-call | bytes 41943040 | tf_op jit(solution)/shard_map/dense_rows/pallas_call | solution.py:102
  12.7 4.4 %collective-permute-done.3.refs_2_ = bf16[512,256]{1,0:T(8,128)(2,1)S(1)} collective-permute-done((bf16[512,256]{1,0:T(8,128)(2,1)}, bf16[512,256]{1,0:T(8,128)(2,1)S(1)}, u32[]{:S(2)}, u32[]{:S(2)}) %collective-permute-start.3) | collective-permute-done | bytes 262176 | tf_op jit(solution)/shard_map/ppermute | solution.py:278
  17.6 1.2 %forward_rows.6.refs_4_ = f32[512,256]{1,0:T(8,128)S(1)} custom-call(s32[2]{0:T(128)S(1)} %pad_add_fusion.where, bf16[512,4096]{1,0:T(8,128)(2,1)S(1)} %get-tuple-element.18.refs_3_.a_ref.refs_0_, bf16[512,256]{1,0:T(8,128)(2,1)S(1)} %get-tuple-element.17.refs_0_, bf16[512,256]{1,0:T(8,128)(2,1)S(1)} %get-tuple-element.21.refs_2_.refs_1_, ...), custom_call_target="tpu_custom_call" | custom-call | flops 1073741824 | bytes 4194304 | tf_op jit(solution)/shard_map/forward_rows/pallas_call | solution.py:136
  19.3 1.3 %forward_rows.7 = bf16[512,256]{1,0:T(8,128)(2,1)S(1)} custom-call(s32[2]{0:T(128)S(1)} %pad_add_fusion.where, bf16[512,4096]{1,0:T(8,128)(2,1)S(1)} %get-tuple-element.18.refs_3_.a_ref.refs_0_, bf16[512,256]{1,0:T(8,128)(2,1)S(1)} %collective-permute-done.refs_1_.refs_0_, bf16[512,256]{1,0:T(8,128)(2,1)S(1)} %collective-permute-done.4.refs_3_.refs_1_, ...), custom_call_target="tpu_custom_call" | custom-call | flops 1073741824 | bytes 4194304 | tf_op jit(solution)/shard_map/forward_rows/pallas_call | solution.py:136
  20.6 3.5 %collective-permute-start.8 = (bf16[512,256]{1,0:T(8,128)(2,1)S(1)}, bf16[512,256]{1,0:T(8,128)(2,1)S(1)}, u32[]{:S(2)}, u32[]{:S(2)}) collective-permute-start(bf16[512,256]{1,0:T(8,128)(2,1)S(1)} %forward_rows.7), channel_id=1, source_target_pairs={{0,1},{3,2},{4,5},{7,6},{8,9},{11,10},{12,13},{15,14},{16,17},{19,... | collective-permute-start | bytes 786440 | tf_op jit(solution)/shard_map/ppermute | solution.py:305
  24.1 0.9 collective-permute-start.7
  25.0 1.8 %forward_rows.9 = bf16[512,256]{1,0:T(8,128)(2,1)S(1)} custom-call(s32[2]{0:T(128)S(1)} %pad_add_fusion.where, bf16[512,4096]{1,0:T(8,128)(2,1)S(1)} %get-tuple-element.20.refs_5_.a_ref.refs_1_, bf16[512,256]{1,0:T(8,128)(2,1)S(1)} %get-tuple-element.17.refs_0_, bf16[512,256]{1,0:T(8,128)(2,1)S(1)} %collective-permute-done.refs_1_.refs_0_, ...), custom_call_target="tpu_custom_call" | custom-call | flops 1073741824 | bytes 4194304 | tf_op jit(solution)/shard_map/forward_rows/pallas_call | solution.py:136
  26.8 2.2 %collective-permute-start.10 = (bf16[512,256]{1,0:T(8,128)(2,1)S(1)}, bf16[512,256]{1,0:T(8,128)(2,1)S(1)}, u32[]{:S(2)}, u32[]{:S(2)}) collective-permute-start(bf16[512,256]{1,0:T(8,128)(2,1)S(1)} %forward_rows.9), channel_id=1, source_target_pairs={{0,1},{1,0},{2,3},{3,2},{4,5},{5,4},{6,7},{7,6},{8,9},{9,8},{10,11... | collective-permute-start | bytes 786440 | tf_op jit(solution)/shard_map/ppermute | solution.py:278
  29.0 1.8 %forward_rows.8 = bf16[512,256]{1,0:T(8,128)(2,1)S(1)} custom-call(s32[2]{0:T(128)S(1)} %pad_add_fusion.where, bf16[512,4096]{1,0:T(8,128)(2,1)S(1)} %get-tuple-element.19.refs_4_.a_ref.refs_2_, bf16[512,256]{1,0:T(8,128)(2,1)S(1)} %get-tuple-element.17.refs_0_, bf16[512,256]{1,0:T(8,128)(2,1)S(1)} %collective-permute-done.refs_1_.refs_0_, ...), custom_call_target="tpu_custom_call" | custom-call | flops 1073741824 | bytes 4194304 | tf_op jit(solution)/shard_map/forward_rows/pallas_call | solution.py:136
  30.9 3.4 %collective-permute-start.9 = (bf16[512,256]{1,0:T(8,128)(2,1)S(1)}, bf16[512,256]{1,0:T(8,128)(2,1)S(1)}, u32[]{:S(2)}, u32[]{:S(2)}) collective-permute-start(bf16[512,256]{1,0:T(8,128)(2,1)S(1)} %add_convert_fusion), channel_id=1, source_target_pairs={{0,2},{1,3},{2,0},{3,1},{4,6},{5,7},{6,4},{7,5},{8,10},{9,11},{10,... | collective-permute-start | bytes 786440 | tf_op jit(solution)/shard_map/ppermute | solution.py:278
  34.4 1.8 %forward_rows.5.refs_0_ = f32[512,256]{1,0:T(8,128)S(1)} custom-call(s32[2]{0:T(128)S(1)} %pad_add_fusion.where, bf16[512,4096]{1,0:T(8,128)(2,1)S(1)} %get-tuple-element.16.refs_6_.a_ref.refs_0_, bf16[512,256]{1,0:T(8,128)(2,1)S(1)} %get-tuple-element.17.refs_0_, bf16[512,256]{1,0:T(8,128)(2,1)S(1)} %collective-permute-done.refs_1_.refs_0_, ...), custom_call_target="tpu_custom_call" | custom-call | flops 1073741824 | bytes 4194304 | tf_op jit(solution)/shard_map/forward_rows/pallas_call | solution.py:136
  36.2 3.6 %collective-permute-done.10.refs_3_ = bf16[512,256]{1,0:T(8,128)(2,1)S(1)} collective-permute-done((bf16[512,256]{1,0:T(8,128)(2,1)S(1)}, bf16[512,256]{1,0:T(8,128)(2,1)S(1)}, u32[]{:S(2)}, u32[]{:S(2)}) %collective-permute-start.10) | collective-permute-done | bytes 262176 | tf_op jit(solution)/shard_map/ppermute | solution.py:278
  39.8 5.6 %collective-permute-done.9.refs_2_ = bf16[512,256]{1,0:T(8,128)(2,1)S(1)} collective-permute-done((bf16[512,256]{1,0:T(8,128)(2,1)S(1)}, bf16[512,256]{1,0:T(8,128)(2,1)S(1)}, u32[]{:S(2)}, u32[]{:S(2)}) %collective-permute-start.9) | collective-permute-done | bytes 262176 | tf_op jit(solution)/shard_map/ppermute | solution.py:278
  45.3 1.1 %middle.1 = (bf16[512,256]{1,0:T(8,128)(2,1)}, bf16[256,512]{1,0:T(8,128)(2,1)S(1)}, f32[256,256]{1,0:T(8,128)S(1)}) custom-call(f32[512,256]{1,0:T(8,128)S(1)} %forward_rows.5.refs_0_, bf16[512,256]{1,0:T(8,128)(2,1)S(1)} %collective-permute-done.7.refs_1_, bf16[512,256]{1,0:T(8,128)(2,1)S(1)} %collective-permute-done.9.refs_2_, ...), custom_call_target="tpu_custom_call" | custom-call | flops 201326592 | bytes 1310720 | tf_op jit(solution)/shard_map/middle/pallas_call | solution.py:169
  46.4 2.1 %collective-permute-start.13 = (bf16[256,512]{1,0:T(8,128)(2,1)S(1)}, bf16[256,512]{1,0:T(8,128)(2,1)S(1)}, u32[]{:S(2)}, u32[]{:S(2)}) collective-permute-start(bf16[256,512]{1,0:T(8,128)(2,1)S(1)} %get-tuple-element.26.refs_0_), channel_id=1, source_target_pairs={{0,2},{1,3},{2,0},{3,1},{4,6},{5,7},{6,4},{7,5},{8,10},{9,11},{10,... | collective-permute-start | bytes 786440 | tf_op jit(solution)/shard_map/ppermute | solution.py:278
  48.6 10.0 %all_gather.3.refs_0_ = bf16[1024,256]{1,0:T(8,128)(2,1)S(1)} all-gather(bf16[256,256]{1,0:T(8,128)(2,1)S(1)} %add_convert_fusion.1), channel_id=1, replica_groups={{0,8,16,24},{4,12,20,28},{1,9,17,25},{5,13,21,29},{2,10,18,26},{6,14,22..., dimensions={0}, use_global_device_ids=true | all-gather | bytes 655360 | tf_op jit(solution)/shard_map/all_gather | solution.py:317
  58.7 1.0 %collective-permute-done.16.refs_4_ = bf16[256,512]{1,0:T(8,128)(2,1)S(1)} collective-permute-done((bf16[256,512]{1,0:T(8,128)(2,1)S(1)}, bf16[256,512]{1,0:T(8,128)(2,1)S(1)}, u32[]{:S(2)}, u32[]{:S(2)}) %collective-permute-start.16) | collective-permute-done | bytes 262176 | tf_op jit(solution)/shard_map/ppermute | solution.py:278
  59.7 2.0 %collective-permute-done.13.refs_1_ = bf16[256,512]{1,0:T(8,128)(2,1)S(1)} collective-permute-done((bf16[256,512]{1,0:T(8,128)(2,1)S(1)}, bf16[256,512]{1,0:T(8,128)(2,1)S(1)}, u32[]{:S(2)}, u32[]{:S(2)}) %collective-permute-start.13) | collective-permute-done | bytes 262176 | tf_op jit(solution)/shard_map/ppermute | solution.py:278
  61.7 0.7 collective-permute-start.14
  62.4 1.3 %collective-permute-start.15 = (bf16[256,512]{1,0:T(8,128)(2,1)S(1)}, bf16[256,512]{1,0:T(8,128)(2,1)S(1)}, u32[]{:S(2)}, u32[]{:S(2)}) collective-permute-start(bf16[256,512]{1,0:T(8,128)(2,1)S(1)} %get-tuple-element.28.refs_5_), channel_id=1, source_target_pairs={{1,0},{2,3},{5,4},{6,7},{9,8},{10,11},{13,12},{14,15},{17,16},{18,... | collective-permute-start | bytes 786440 | tf_op jit(solution)/shard_map/ppermute | solution.py:323
  63.7 5.2 %backward_cols.3.refs_2_ = f32[8,256,512]{2,1,0:T(8,128)S(1)} custom-call(s32[2]{0:T(128)S(1)} %pad_add_fusion.where, bf16[512,4096]{1,0:T(8,128)(2,1)S(1)} %get-tuple-element.16.refs_6_.a_ref.refs_0_, bf16[512,4096]{1,0:T(8,128)(2,1)S(1)} %get-tuple-element.20.refs_5_.a_ref.refs_1_, bf16[512,4096]{1,0:T(8,128)(2,1)S(1)} %get-tuple-element.19.refs_4_.a_ref.refs_2_, ...), custom_call_target="tpu_custom_call" | custom-call | tf_op jit(solution)/shard_map/backward_cols/pallas_call | solution.py:206
  68.9 3.3 %collective-permute-done.15 = bf16[256,512]{1,0:T(8,128)(2,1)S(1)} collective-permute-done((bf16[256,512]{1,0:T(8,128)(2,1)S(1)}, bf16[256,512]{1,0:T(8,128)(2,1)S(1)}, u32[]{:S(2)}, u32[]{:S(2)}) %collective-permute-start.15) | collective-permute-done | bytes 262176 | tf_op jit(solution)/shard_map/ppermute | solution.py:323
  72.3 1.8 %backward_cols.5 = bf16[4,256,512]{2,1,0:T(8,128)(2,1)S(1)} custom-call(s32[2]{0:T(128)S(1)} %pad_add_fusion.where, bf16[512,4096]{1,0:T(8,128)(2,1)S(1)} %get-tuple-element.18.refs_3_.a_ref.refs_0_, bf16[256,512]{1,0:T(8,128)(2,1)S(1)} %add.23.refs_1_, f32[8,256,512]{2,1,0:T(8,128)S(1)} %backward_cols.3.refs_2_, ...), custom_call_target="tpu_custom_call" | custom-call | tf_op jit(solution)/shard_map/backward_cols/pallas_call | solution.py:206
  74.2 1.8 %backward_cols.4.refs_2_.refs_0_ = f32[4,256,512]{2,1,0:T(8,128)S(1)} custom-call(s32[2]{0:T(128)S(1)} %pad_add_fusion.where, bf16[512,4096]{1,0:T(8,128)(2,1)S(1)} %get-tuple-element.18.refs_3_.a_ref.refs_0_, bf16[256,512]{1,0:T(8,128)(2,1)S(1)} %add.23.refs_1_, f32[8,256,512]{2,1,0:T(8,128)S(1)} %backward_cols.3.refs_2_), custom_call_target="tpu_custom_call" | custom-call | tf_op jit(solution)/shard_map/backward_cols/pallas_call | solution.py:206
  76.0 0.8 collective-permute-done.18.refs_1_
  77.0 2.4 %collective-permute-start.21 = (bf16[256,512]{1,0:T(8,128)(2,1)S(1)}, bf16[256,512]{1,0:T(8,128)(2,1)S(1)}, u32[]{:S(2)}, u32[]{:S(2)}) collective-permute-start(bf16[256,512]{1,0:T(8,128)(2,1)S(1)} %get-tuple-element.29), channel_id=1, source_target_pairs={{0,24},{4,28},{8,16},{12,20},{16,8},{20,12},{24,0},{28,4},{1,25},{... | collective-permute-start | bytes 786440 | tf_op jit(solution)/shard_map/ppermute | solution.py:278
  80.6 1.0 %collective-permute-start.17 = (bf16[256,256]{1,0:T(8,128)(2,1)S(1)}, bf16[256,256]{1,0:T(8,128)(2,1)S(1)}, u32[]{:S(2)}, u32[]{:S(2)}) collective-permute-start(bf16[256,256]{1,0:T(8,128)(2,1)S(1)} %total.4.refs_0_), channel_id=1, source_target_pairs={{0,2},{1,3},{2,0},{3,1},{4,6},{5,7},{6,4},{7,5},{8,10},{9,11},{10,... | collective-permute-start | bytes 393224 | tf_op jit(solution)/shard_map/ppermute | solution.py:278
  81.6 7.5 %collective-permute-done.17.refs_1_ = bf16[256,256]{1,0:T(8,128)(2,1)S(1)} collective-permute-done((bf16[256,256]{1,0:T(8,128)(2,1)S(1)}, bf16[256,256]{1,0:T(8,128)(2,1)S(1)}, u32[]{:S(2)}, u32[]{:S(2)}) %collective-permute-start.17) | collective-permute-done | bytes 131104 | tf_op jit(solution)/shard_map/ppermute | solution.py:278
  89.1 0.7 total.5
  89.8 2.1 %collective-permute-done.20.refs_3_ = bf16[256,512]{1,0:T(8,128)(2,1)S(1)} collective-permute-done((bf16[256,512]{1,0:T(8,128)(2,1)S(1)}, bf16[256,512]{1,0:T(8,128)(2,1)S(1)}, u32[]{:S(2)}, u32[]{:S(2)}) %collective-permute-start.20) | collective-permute-done | bytes 262176 | tf_op jit(solution)/shard_map/ppermute | solution.py:278
  92.0 0.9 finish.1
  (38 shorter events, 3.6 us)
Async XLA Ops:
  0.6 12.0 %collective-permute-start.1 = (bf16[512,256]{1,0:T(8,128)(2,1)}, bf16[512,256]{1,0:T(8,128)(2,1)S(1)}, u32[]{:S(2)}, u32[]{:S(2)}) collective-permute-start(bf16[512,256]{1,0:T(8,128)(2,1)} %features_ref.1), channel_id=1, source_target_pairs={{0,24},{4,28},{8,16},{12,20},{16,8},{20,12},{24,0},{28,4},{1,25},{... | collective-permute-start | bytes 786440 | tf_op jit(solution)/shard_map/ppermute | solution.py:278
  4.6 12.4 %collective-permute-start.3 = (bf16[512,256]{1,0:T(8,128)(2,1)}, bf16[512,256]{1,0:T(8,128)(2,1)S(1)}, u32[]{:S(2)}, u32[]{:S(2)}) collective-permute-start(bf16[512,256]{1,0:T(8,128)(2,1)} %features_ref.1), channel_id=1, source_target_pairs={{0,8},{4,12},{8,0},{12,4},{16,24},{20,28},{24,16},{28,20},{1,9},{5... | collective-permute-start | bytes 786440 | tf_op jit(solution)/shard_map/ppermute | solution.py:278
  5.1 11.9 %collective-permute-start.2 = (bf16[512,256]{1,0:T(8,128)(2,1)}, bf16[512,256]{1,0:T(8,128)(2,1)S(1)}, u32[]{:S(2)}, u32[]{:S(2)}) collective-permute-start(bf16[512,256]{1,0:T(8,128)(2,1)} %features_ref.1), channel_id=1, source_target_pairs={{0,16},{4,20},{8,24},{12,28},{16,0},{20,4},{24,8},{28,12},{1,17},{... | collective-permute-start | bytes 786440 | tf_op jit(solution)/shard_map/ppermute | solution.py:278
  5.2 13.6 %collective-permute-start = (bf16[512,256]{1,0:T(8,128)(2,1)}, bf16[512,256]{1,0:T(8,128)(2,1)S(1)}, u32[]{:S(2)}, u32[]{:S(2)}) collective-permute-start(bf16[512,256]{1,0:T(8,128)(2,1)} %features_ref.1), channel_id=1, source_target_pairs={{0,4},{4,0},{8,12},{12,8},{16,20},{20,16},{24,28},{28,24},{1,5},{5... | collective-permute-start | bytes 786440 | tf_op jit(solution)/shard_map/ppermute | solution.py:278
  17.0 1.8 %collective-permute-start.4 = (bf16[512,256]{1,0:T(8,128)(2,1)S(1)}, bf16[512,256]{1,0:T(8,128)(2,1)S(1)}, u32[]{:S(2)}, u32[]{:S(2)}) collective-permute-start(bf16[512,256]{1,0:T(8,128)(2,1)S(1)} %get-tuple-element.21.refs_2_.refs_1_), channel_id=1, source_target_pairs={{0,4},{4,0},{8,12},{12,8},{16,20},{20,16},{24,28},{28,24},{1,5},{5... | collective-permute-start | bytes 786440 | tf_op jit(solution)/shard_map/ppermute | solution.py:278
  17.0 1.9 %collective-permute-start.5 = (bf16[512,256]{1,0:T(8,128)(2,1)S(1)}, bf16[512,256]{1,0:T(8,128)(2,1)S(1)}, u32[]{:S(2)}, u32[]{:S(2)}) collective-permute-start(bf16[512,256]{1,0:T(8,128)(2,1)S(1)} %get-tuple-element.22.refs_4_.refs_2_), channel_id=1, source_target_pairs={{0,4},{4,0},{8,12},{12,8},{16,20},{20,16},{24,28},{28,24},{1,5},{5... | collective-permute-start | bytes 786440 | tf_op jit(solution)/shard_map/ppermute | solution.py:278
  17.5 1.8 %collective-permute-start.6 = (bf16[512,256]{1,0:T(8,128)(2,1)S(1)}, bf16[512,256]{1,0:T(8,128)(2,1)S(1)}, u32[]{:S(2)}, u32[]{:S(2)}) collective-permute-start(bf16[512,256]{1,0:T(8,128)(2,1)S(1)} %get-tuple-element.23.refs_6_.refs_3_), channel_id=1, source_target_pairs={{0,4},{4,0},{8,12},{12,8},{16,20},{20,16},{24,28},{28,24},{1,5},{5... | collective-permute-start | bytes 786440 | tf_op jit(solution)/shard_map/ppermute | solution.py:278
  20.6 10.3 %collective-permute-start.8 = (bf16[512,256]{1,0:T(8,128)(2,1)S(1)}, bf16[512,256]{1,0:T(8,128)(2,1)S(1)}, u32[]{:S(2)}, u32[]{:S(2)}) collective-permute-start(bf16[512,256]{1,0:T(8,128)(2,1)S(1)} %forward_rows.7), channel_id=1, source_target_pairs={{0,1},{3,2},{4,5},{7,6},{8,9},{11,10},{12,13},{15,14},{16,17},{19,... | collective-permute-start | bytes 786440 | tf_op jit(solution)/shard_map/ppermute | solution.py:305
  24.1 15.7 %collective-permute-start.7 = (bf16[512,256]{1,0:T(8,128)(2,1)S(1)}, bf16[512,256]{1,0:T(8,128)(2,1)S(1)}, u32[]{:S(2)}, u32[]{:S(2)}) collective-permute-start(bf16[512,256]{1,0:T(8,128)(2,1)S(1)} %forward_rows.7), channel_id=1, source_target_pairs={{1,2},{2,1},{5,6},{6,5},{9,10},{10,9},{13,14},{14,13},{17,18},{18,... | collective-permute-start | bytes 786440 | tf_op jit(solution)/shard_map/ppermute | solution.py:306
  26.8 13.0 %collective-permute-start.10 = (bf16[512,256]{1,0:T(8,128)(2,1)S(1)}, bf16[512,256]{1,0:T(8,128)(2,1)S(1)}, u32[]{:S(2)}, u32[]{:S(2)}) collective-permute-start(bf16[512,256]{1,0:T(8,128)(2,1)S(1)} %forward_rows.9), channel_id=1, source_target_pairs={{0,1},{1,0},{2,3},{3,2},{4,5},{5,4},{6,7},{7,6},{8,9},{9,8},{10,11... | collective-permute-start | bytes 786440 | tf_op jit(solution)/shard_map/ppermute | solution.py:278
  30.8 14.5 %copy-start = (bf16[512,256]{1,0:T(8,128)(2,1)S(1)}, bf16[512,256]{1,0:T(8,128)(2,1)}, u32[]{:S(2)}) copy-start(bf16[512,256]{1,0:T(8,128)(2,1)} %refs_5_.1) | copy-start | bytes 786436
  30.8 14.5 %copy-start.1 = (bf16[256,256]{1,0:T(8,128)(2,1)S(1)}, bf16[256,256]{1,0:T(8,128)(2,1)}, u32[]{:S(2)}) copy-start(bf16[256,256]{1,0:T(8,128)(2,1)} %refs_4_.1) | copy-start | bytes 393220
  30.9 14.4 %collective-permute-start.9 = (bf16[512,256]{1,0:T(8,128)(2,1)S(1)}, bf16[512,256]{1,0:T(8,128)(2,1)S(1)}, u32[]{:S(2)}, u32[]{:S(2)}) collective-permute-start(bf16[512,256]{1,0:T(8,128)(2,1)S(1)} %add_convert_fusion), channel_id=1, source_target_pairs={{0,2},{1,3},{2,0},{3,1},{4,6},{5,7},{6,4},{7,5},{8,10},{9,11},{10,... | collective-permute-start | bytes 786440 | tf_op jit(solution)/shard_map/ppermute | solution.py:278
  46.4 2.1 %collective-permute-start.11 = (f32[256,256]{1,0:T(8,128)S(1)}, f32[256,256]{1,0:T(8,128)S(1)}, u32[]{:S(2)}, u32[]{:S(2)}) collective-permute-start(f32[256,256]{1,0:T(8,128)S(1)} %get-tuple-element.25), channel_id=1, source_target_pairs={{0,4},{4,0},{8,12},{12,8},{16,20},{20,16},{24,28},{28,24},{1,5},{5... | collective-permute-start | bytes 786440 | tf_op jit(solution)/shard_map/ppermute | solution.py:278
  46.4 13.3 %collective-permute-start.16 = (bf16[256,512]{1,0:T(8,128)(2,1)S(1)}, bf16[256,512]{1,0:T(8,128)(2,1)S(1)}, u32[]{:S(2)}, u32[]{:S(2)}) collective-permute-start(bf16[256,512]{1,0:T(8,128)(2,1)S(1)} %get-tuple-element.26.refs_0_), channel_id=1, source_target_pairs={{0,1},{1,0},{2,3},{3,2},{4,5},{5,4},{6,7},{7,6},{8,9},{9,8},{10,11... | collective-permute-start | bytes 786440 | tf_op jit(solution)/shard_map/ppermute | solution.py:278
  46.4 15.3 %collective-permute-start.13 = (bf16[256,512]{1,0:T(8,128)(2,1)S(1)}, bf16[256,512]{1,0:T(8,128)(2,1)S(1)}, u32[]{:S(2)}, u32[]{:S(2)}) collective-permute-start(bf16[256,512]{1,0:T(8,128)(2,1)S(1)} %get-tuple-element.26.refs_0_), channel_id=1, source_target_pairs={{0,2},{1,3},{2,0},{3,1},{4,6},{5,7},{6,4},{7,5},{8,10},{9,11},{10,... | collective-permute-start | bytes 786440 | tf_op jit(solution)/shard_map/ppermute | solution.py:278
  61.7 7.2 %collective-permute-start.14 = (bf16[256,512]{1,0:T(8,128)(2,1)S(1)}, bf16[256,512]{1,0:T(8,128)(2,1)S(1)}, u32[]{:S(2)}, u32[]{:S(2)}) collective-permute-start(bf16[256,512]{1,0:T(8,128)(2,1)S(1)} %get-tuple-element.27.refs_3_), channel_id=1, source_target_pairs={{1,2},{2,1},{5,6},{6,5},{9,10},{10,9},{13,14},{14,13},{17,18},{18,... | collective-permute-start | bytes 786440 | tf_op jit(solution)/shard_map/ppermute | solution.py:322
  62.4 9.8 %collective-permute-start.15 = (bf16[256,512]{1,0:T(8,128)(2,1)S(1)}, bf16[256,512]{1,0:T(8,128)(2,1)S(1)}, u32[]{:S(2)}, u32[]{:S(2)}) collective-permute-start(bf16[256,512]{1,0:T(8,128)(2,1)S(1)} %get-tuple-element.28.refs_5_), channel_id=1, source_target_pairs={{1,0},{2,3},{5,4},{6,7},{9,8},{10,11},{13,12},{14,15},{17,16},{18,... | collective-permute-start | bytes 786440 | tf_op jit(solution)/shard_map/ppermute | solution.py:323
  74.0 2.7 %collective-permute-start.18 = (bf16[4,256,512]{2,1,0:T(8,128)(2,1)S(1)}, bf16[4,256,512]{2,1,0:T(8,128)(2,1)S(1)}, u32[]{:S(2)}, u32[]{:S(2)}) collective-permute-start(bf16[4,256,512]{2,1,0:T(8,128)(2,1)S(1)} %backward_cols.5), channel_id=1, source_target_pairs={{0,4},{4,0},{8,12},{12,8},{16,20},{20,16},{24,28},{28,24},{1,5},{5... | collective-permute-start | bytes 3145736 | tf_op jit(solution)/shard_map/ppermute | solution.py:278
  74.1 6.5 %collective-permute-start.12 = (bf16[256,256]{1,0:T(8,128)(2,1)S(1)}, bf16[256,256]{1,0:T(8,128)(2,1)S(1)}, u32[]{:S(2)}, u32[]{:S(2)}) collective-permute-start(bf16[256,256]{1,0:T(8,128)(2,1)S(1)} %total.3.refs_2_.refs_0_.refs_3_), channel_id=1, source_target_pairs={{0,1},{1,0},{2,3},{3,2},{4,5},{5,4},{6,7},{7,6},{8,9},{9,8},{10,11... | collective-permute-start | bytes 393224 | tf_op jit(solution)/shard_map/ppermute | solution.py:278
  77.0 12.8 %collective-permute-start.21 = (bf16[256,512]{1,0:T(8,128)(2,1)S(1)}, bf16[256,512]{1,0:T(8,128)(2,1)S(1)}, u32[]{:S(2)}, u32[]{:S(2)}) collective-permute-start(bf16[256,512]{1,0:T(8,128)(2,1)S(1)} %get-tuple-element.29), channel_id=1, source_target_pairs={{0,24},{4,28},{8,16},{12,20},{16,8},{20,12},{24,0},{28,4},{1,25},{... | collective-permute-start | bytes 786440 | tf_op jit(solution)/shard_map/ppermute | solution.py:278
  79.5 12.5 %collective-permute-start.20 = (bf16[256,512]{1,0:T(8,128)(2,1)S(1)}, bf16[256,512]{1,0:T(8,128)(2,1)S(1)}, u32[]{:S(2)}, u32[]{:S(2)}) collective-permute-start(bf16[256,512]{1,0:T(8,128)(2,1)S(1)} %get-tuple-element.30), channel_id=1, source_target_pairs={{0,16},{4,20},{8,24},{12,28},{16,0},{20,4},{24,8},{28,12},{1,17},{... | collective-permute-start | bytes 786440 | tf_op jit(solution)/shard_map/ppermute | solution.py:278
  80.1 11.9 %collective-permute-start.19 = (bf16[256,512]{1,0:T(8,128)(2,1)S(1)}, bf16[256,512]{1,0:T(8,128)(2,1)S(1)}, u32[]{:S(2)}, u32[]{:S(2)}) collective-permute-start(bf16[256,512]{1,0:T(8,128)(2,1)S(1)} %get-tuple-element.31), channel_id=1, source_target_pairs={{0,8},{4,12},{8,0},{12,4},{16,24},{20,28},{24,16},{28,20},{1,9},{5... | collective-permute-start | bytes 786440 | tf_op jit(solution)/shard_map/ppermute | solution.py:278
  80.6 8.5 %collective-permute-start.17 = (bf16[256,256]{1,0:T(8,128)(2,1)S(1)}, bf16[256,256]{1,0:T(8,128)(2,1)S(1)}, u32[]{:S(2)}, u32[]{:S(2)}) collective-permute-start(bf16[256,256]{1,0:T(8,128)(2,1)S(1)} %total.4.refs_0_), channel_id=1, source_target_pairs={{0,2},{1,3},{2,0},{3,1},{4,6},{5,7},{6,4},{7,5},{8,10},{9,11},{10,... | collective-permute-start | bytes 393224 | tf_op jit(solution)/shard_map/ppermute | solution.py:278

commit v11 on v10

--- a/solution.py
+++ b/solution.py
@@ -305,6 +305,7 @@
         relayed = lax.ppermute(shares[3], "col", [(0, 1), (3, 2)])
         came = [lax.ppermute(shares[3], "col", [(1, 2), (2, 1)])]
         joined = (shares[2].astype(jnp.float32) + relayed.astype(jnp.float32)).astype(jnp.bfloat16)
+        joined, shares[1] = gate([joined, shares[1]], [])
         came += [swap(joined, "col", n_col, 2), swap(shares[1], "col", n_col, 1)]
     else:
         came = [swap(share, "col", n_col, s) for s, share in shares.items()]
@@ -317,10 +318,10 @@
     gathered = lax.all_gather(part, "row", axis_index_groups=cores, tiled=True)
     part = total([gathered], part.shape[0], jnp.bfloat16)
     if line:
-        pieces = {s: swap(piece, "col", n_col, s) for s in (1, 2)}
+        pieces = {s: swap(piece, "col", n_col, s) for s in (2, 1)}
         pieces[0], pieces[2] = gate([piece, pieces[2]], [part])
-        beside = lax.ppermute(pieces[0], "col", [(1, 2), (2, 1)])
-        pieces[3] = beside + lax.ppermute(pieces[2], "col", [(1, 0), (2, 3)])
+        relayed = lax.ppermute(pieces[2], "col", [(1, 0), (2, 3)])
+        pieces[3] = relayed + lax.ppermute(pieces[0], "col", [(1, 2), (2, 1)])
     else:
         pieces = {s: swap(piece, "col", n_col, s) for s in steps[:-1]}
         pieces[0] = piece

time: 93.1 us -> 96.1 us (1.032)
  waiting for transfers between devices: 30.7 us -> 32.6 us
  starting transfers between devices: 24 us -> 25.2 us
    ppermute x18, waiting for transfers between devices: 27.4 us -> 29 us  [swap(): return lax.ppermute(value, axis, [(i, i ^ step) for i in range(size)])]
    ppermute x1, waiting for transfers between devices: 0.01 us -> 1.3 us  [shards(): relayed = lax.ppermute(shares[3], 'col', [(0, 1), (3, 2)])]
    ppermute x18, starting transfers between devices: 17.7 us -> 18.9 us  [swap(): return lax.ppermute(value, axis, [(i, i ^ step) for i in range(size)])]
    ppermute x2, waiting for transfers between devices: 3.3 us -> 2.31 us  [the longest x1 2.31 us: shards(): relayed = lax.ppermute(pieces[2], 'col', [(1, 0), (2, 3)])]
where the time goes in v11:
time: 96.1 us; the launch traced here: 95.9 us
  waiting for transfers between devices  32.6 us (34%)
  Pallas kernels  26.7 us (28%)
  starting transfers between devices  25.2 us (26%)
  blocking collectives  10 us (10%)
    ppermute x18, waiting for transfers between devices, swap(): return lax.ppermute(value, axis, [(i, i ^ step) for i in range(size)])  29 us
    ppermute x18, starting transfers between devices, swap(): return lax.ppermute(value, axis, [(i, i ^ step) for i in range(size)])  18.9 us
    all_gather x1, blocking collectives, shards(): gathered = lax.all_gather(part, 'row', axis_index_groups=cores, tiled=True)  10 us
    pallas_call x3, Pallas kernels, backward(): pl.pallas_call(functools.partial(backward_kernel, count=count, steps=step...  8.74 us
    pallas_call x5, Pallas kernels, forward(): pl.pallas_call(functools.partial(forward_kernel, first=first, step=step),...  7.94 us
    pallas_call x1, Pallas kernels, dense_rows(): pl.pallas_call(functools.partial(dense_kernel, steps=steps, window=window...  7.14 us
    ppermute x1, starting transfers between devices, shards(): relayed = lax.ppermute(shares[3], 'col', [(0, 1), (3, 2)])  3.5 us
    ppermute x1, waiting for transfers between devices, shards(): relayed = lax.ppermute(pieces[2], 'col', [(1, 0), (2, 3)])  2.31 us
  transfers between devices with their start and end apart: 22, of which 11 were waited for; matrix products, arithmetic and copies ran while one was open for 0% of the time, Pallas kernels for 23%

profile of v11, /device:TPU:0, one launch (start us, length us, event | category | flops | bytes accessed | tf_op | source)
XLA Modules:
  0.0 95.9 jit_solution(8397515682087492766)
XLA Ops:
  0.6 4.0 %collective-permute-start.1 = (bf16[512,256]{1,0:T(8,128)(2,1)}, bf16[512,256]{1,0:T(8,128)(2,1)S(1)}, u32[]{:S(2)}, u32[]{:S(2)}) collective-permute-start(bf16[512,256]{1,0:T(8,128)(2,1)} %features_ref.1), channel_id=1, source_target_pairs={{0,24},{4,28},{8,16},{12,20},{16,8},{20,12},{24,0},{28,4},{1,25},{... | collective-permute-start | bytes 786440 | tf_op jit(solution)/shard_map/ppermute | solution.py:278
  5.3 7.1 %dense_rows.1 = (bf16[512,4096]{1,0:T(8,128)(2,1)S(1)}, bf16[512,4096]{1,0:T(8,128)(2,1)S(1)}, bf16[512,4096]{1,0:T(8,128)(2,1)S(1)}, bf16[512,4096]{1,0:T(8,128)(2,1)S(1)}, bf16[512,256]{1,0:T(8,128)(2,1)S(1)}) custom-call(s32[2]{0:T(128)S(1)} %pad_add_fusion.where, s32[16]{0:T(128)} %bitcast.13, s32[448]{0:T(512)} %bitcast.12, ...), custom_call_target="tpu_custom_call" | custom-call | bytes 41943040 | tf_op jit(solution)/shard_map/dense_rows/pallas_call | solution.py:102
  12.5 4.5 %collective-permute-done.3.refs_2_ = bf16[512,256]{1,0:T(8,128)(2,1)S(1)} collective-permute-done((bf16[512,256]{1,0:T(8,128)(2,1)}, bf16[512,256]{1,0:T(8,128)(2,1)S(1)}, u32[]{:S(2)}, u32[]{:S(2)}) %collective-permute-start.3) | collective-permute-done | bytes 262176 | tf_op jit(solution)/shard_map/ppermute | solution.py:278
  17.6 1.2 %forward_rows.6.refs_4_ = f32[512,256]{1,0:T(8,128)S(1)} custom-call(s32[2]{0:T(128)S(1)} %pad_add_fusion.where, bf16[512,4096]{1,0:T(8,128)(2,1)S(1)} %get-tuple-element.20.refs_3_.a_ref.refs_0_, bf16[512,256]{1,0:T(8,128)(2,1)S(1)} %get-tuple-element.19.refs_0_, bf16[512,256]{1,0:T(8,128)(2,1)S(1)} %get-tuple-element.23.refs_2_.refs_1_, ...), custom_call_target="tpu_custom_call" | custom-call | flops 1073741824 | bytes 4194304 | tf_op jit(solution)/shard_map/forward_rows/pallas_call | solution.py:136
  19.3 1.3 %forward_rows.7 = bf16[512,256]{1,0:T(8,128)(2,1)S(1)} custom-call(s32[2]{0:T(128)S(1)} %pad_add_fusion.where, bf16[512,4096]{1,0:T(8,128)(2,1)S(1)} %get-tuple-element.20.refs_3_.a_ref.refs_0_, bf16[512,256]{1,0:T(8,128)(2,1)S(1)} %collective-permute-done.refs_1_.refs_0_, bf16[512,256]{1,0:T(8,128)(2,1)S(1)} %collective-permute-done.4.refs_3_.refs_1_, ...), custom_call_target="tpu_custom_call" | custom-call | flops 1073741824 | bytes 4194304 | tf_op jit(solution)/shard_map/forward_rows/pallas_call | solution.py:136
  20.6 3.5 %collective-permute-start.8 = (bf16[512,256]{1,0:T(8,128)(2,1)S(1)}, bf16[512,256]{1,0:T(8,128)(2,1)S(1)}, u32[]{:S(2)}, u32[]{:S(2)}) collective-permute-start(bf16[512,256]{1,0:T(8,128)(2,1)S(1)} %forward_rows.7), channel_id=1, source_target_pairs={{0,1},{3,2},{4,5},{7,6},{8,9},{11,10},{12,13},{15,14},{16,17},{19,... | collective-permute-start | bytes 786440 | tf_op jit(solution)/shard_map/ppermute | solution.py:305
  24.1 0.9 collective-permute-start.7
  25.0 1.8 %forward_rows.9.refs_1_ = bf16[512,256]{1,0:T(8,128)(2,1)S(1)} custom-call(s32[2]{0:T(128)S(1)} %pad_add_fusion.where, bf16[512,4096]{1,0:T(8,128)(2,1)S(1)} %get-tuple-element.22.refs_5_.a_ref.refs_1_, bf16[512,256]{1,0:T(8,128)(2,1)S(1)} %get-tuple-element.19.refs_0_, bf16[512,256]{1,0:T(8,128)(2,1)S(1)} %collective-permute-done.refs_1_.refs_0_, ...), custom_call_target="tpu_custom_call" | custom-call | flops 1073741824 | bytes 4194304 | tf_op jit(solution)/shard_map/forward_rows/pallas_call | solution.py:136
  26.8 1.8 %forward_rows.8 = bf16[512,256]{1,0:T(8,128)(2,1)S(1)} custom-call(s32[2]{0:T(128)S(1)} %pad_add_fusion.where, bf16[512,4096]{1,0:T(8,128)(2,1)S(1)} %get-tuple-element.21.refs_4_.a_ref.refs_2_, bf16[512,256]{1,0:T(8,128)(2,1)S(1)} %get-tuple-element.19.refs_0_, bf16[512,256]{1,0:T(8,128)(2,1)S(1)} %collective-permute-done.refs_1_.refs_0_, ...), custom_call_target="tpu_custom_call" | custom-call | flops 1073741824 | bytes 4194304 | tf_op jit(solution)/shard_map/forward_rows/pallas_call | solution.py:136
  28.6 1.3 %collective-permute-done.8 = bf16[512,256]{1,0:T(8,128)(2,1)S(1)} collective-permute-done((bf16[512,256]{1,0:T(8,128)(2,1)S(1)}, bf16[512,256]{1,0:T(8,128)(2,1)S(1)}, u32[]{:S(2)}, u32[]{:S(2)}) %collective-permute-start.8) | collective-permute-done | bytes 262176 | tf_op jit(solution)/shard_map/ppermute | solution.py:305
  30.0 3.6 %collective-permute-start.9 = (bf16[512,256]{1,0:T(8,128)(2,1)S(1)}, bf16[512,256]{1,0:T(8,128)(2,1)S(1)}, u32[]{:S(2)}, u32[]{:S(2)}) collective-permute-start(bf16[512,256]{1,0:T(8,128)(2,1)S(1)} %get-tuple-element.26), channel_id=1, source_target_pairs={{0,2},{1,3},{2,0},{3,1},{4,6},{5,7},{6,4},{7,5},{8,10},{9,11},{10,... | collective-permute-start | bytes 786440 | tf_op jit(solution)/shard_map/ppermute | solution.py:278
  33.6 1.8 %forward_rows.5.refs_0_ = f32[512,256]{1,0:T(8,128)S(1)} custom-call(s32[2]{0:T(128)S(1)} %pad_add_fusion.where, bf16[512,4096]{1,0:T(8,128)(2,1)S(1)} %get-tuple-element.18.refs_6_.a_ref.refs_0_, bf16[512,256]{1,0:T(8,128)(2,1)S(1)} %get-tuple-element.19.refs_0_, bf16[512,256]{1,0:T(8,128)(2,1)S(1)} %collective-permute-done.refs_1_.refs_0_, ...), custom_call_target="tpu_custom_call" | custom-call | flops 1073741824 | bytes 4194304 | tf_op jit(solution)/shard_map/forward_rows/pallas_call | solution.py:136
  35.4 9.7 %collective-permute-done.9.refs_2_ = bf16[512,256]{1,0:T(8,128)(2,1)S(1)} collective-permute-done((bf16[512,256]{1,0:T(8,128)(2,1)S(1)}, bf16[512,256]{1,0:T(8,128)(2,1)S(1)}, u32[]{:S(2)}, u32[]{:S(2)}) %collective-permute-start.9) | collective-permute-done | bytes 262176 | tf_op jit(solution)/shard_map/ppermute | solution.py:278
  45.2 1.1 %middle.1 = (bf16[512,256]{1,0:T(8,128)(2,1)}, bf16[256,512]{1,0:T(8,128)(2,1)S(1)}, f32[256,256]{1,0:T(8,128)S(1)}) custom-call(f32[512,256]{1,0:T(8,128)S(1)} %forward_rows.5.refs_0_, bf16[512,256]{1,0:T(8,128)(2,1)S(1)} %collective-permute-done.7.refs_1_, bf16[512,256]{1,0:T(8,128)(2,1)S(1)} %collective-permute-done.9.refs_2_, ...), custom_call_target="tpu_custom_call" | custom-call | flops 201326592 | bytes 1310720 | tf_op jit(solution)/shard_map/middle/pallas_call | solution.py:169
  46.3 1.5 %collective-permute-start.16 = (bf16[256,512]{1,0:T(8,128)(2,1)S(1)}, bf16[256,512]{1,0:T(8,128)(2,1)S(1)}, u32[]{:S(2)}, u32[]{:S(2)}) collective-permute-start(bf16[256,512]{1,0:T(8,128)(2,1)S(1)} %get-tuple-element.30.refs_0_), channel_id=1, source_target_pairs={{0,1},{1,0},{2,3},{3,2},{4,5},{5,4},{6,7},{7,6},{8,9},{9,8},{10,11... | collective-permute-start | bytes 786440 | tf_op jit(solution)/shard_map/ppermute | solution.py:278
  47.8 0.7 collective-permute-start.13
  48.5 10.0 %all_gather.3.refs_0_ = bf16[1024,256]{1,0:T(8,128)(2,1)S(1)} all-gather(bf16[256,256]{1,0:T(8,128)(2,1)S(1)} %add_convert_fusion.1), channel_id=1, replica_groups={{0,8,16,24},{4,12,20,28},{1,9,17,25},{5,13,21,29},{2,10,18,26},{6,14,22..., dimensions={0}, use_global_device_ids=true | all-gather | bytes 655360 | tf_op jit(solution)/shard_map/all_gather | solution.py:318
  58.6 0.8 collective-permute-done.16.refs_4_
  59.4 3.4 %collective-permute-done.13.refs_1_ = bf16[256,512]{1,0:T(8,128)(2,1)S(1)} collective-permute-done((bf16[256,512]{1,0:T(8,128)(2,1)S(1)}, bf16[256,512]{1,0:T(8,128)(2,1)S(1)}, u32[]{:S(2)}, u32[]{:S(2)}) %collective-permute-start.13) | collective-permute-done | bytes 262176 | tf_op jit(solution)/shard_map/ppermute | solution.py:278
  62.8 1.3 %collective-permute-start.14 = (bf16[256,512]{1,0:T(8,128)(2,1)S(1)}, bf16[256,512]{1,0:T(8,128)(2,1)S(1)}, u32[]{:S(2)}, u32[]{:S(2)}) collective-permute-start(bf16[256,512]{1,0:T(8,128)(2,1)S(1)} %get-tuple-element.31.refs_5_), channel_id=1, source_target_pairs={{1,0},{2,3},{5,4},{6,7},{9,8},{10,11},{13,12},{14,15},{17,16},{18,... | collective-permute-start | bytes 786440 | tf_op jit(solution)/shard_map/ppermute | solution.py:323
  64.1 0.7 collective-permute-start.15
  64.8 5.2 %backward_cols.3.refs_2_ = f32[8,256,512]{2,1,0:T(8,128)S(1)} custom-call(s32[2]{0:T(128)S(1)} %pad_add_fusion.where, bf16[512,4096]{1,0:T(8,128)(2,1)S(1)} %get-tuple-element.18.refs_6_.a_ref.refs_0_, bf16[512,4096]{1,0:T(8,128)(2,1)S(1)} %get-tuple-element.22.refs_5_.a_ref.refs_1_, bf16[512,4096]{1,0:T(8,128)(2,1)S(1)} %get-tuple-element.21.refs_4_.a_ref.refs_2_, ...), custom_call_target="tpu_custom_call" | custom-call | tf_op jit(solution)/shard_map/backward_cols/pallas_call | solution.py:206
  70.0 2.3 %collective-permute-done.14 = bf16[256,512]{1,0:T(8,128)(2,1)S(1)} collective-permute-done((bf16[256,512]{1,0:T(8,128)(2,1)S(1)}, bf16[256,512]{1,0:T(8,128)(2,1)S(1)}, u32[]{:S(2)}, u32[]{:S(2)}) %collective-permute-start.14) | collective-permute-done | bytes 262176 | tf_op jit(solution)/shard_map/ppermute | solution.py:323
  72.4 1.8 %backward_cols.5 = bf16[4,256,512]{2,1,0:T(8,128)(2,1)S(1)} custom-call(s32[2]{0:T(128)S(1)} %pad_add_fusion.where, bf16[512,4096]{1,0:T(8,128)(2,1)S(1)} %get-tuple-element.20.refs_3_.a_ref.refs_0_, bf16[256,512]{1,0:T(8,128)(2,1)S(1)} %add.23.refs_1_, f32[8,256,512]{2,1,0:T(8,128)S(1)} %backward_cols.3.refs_2_, ...), custom_call_target="tpu_custom_call" | custom-call | tf_op jit(solution)/shard_map/backward_cols/pallas_call | solution.py:206
  74.2 3.7 %collective-permute-start.12 = (bf16[256,256]{1,0:T(8,128)(2,1)S(1)}, bf16[256,256]{1,0:T(8,128)(2,1)S(1)}, u32[]{:S(2)}, u32[]{:S(2)}) collective-permute-start(bf16[256,256]{1,0:T(8,128)(2,1)S(1)} %total.3.refs_2_.refs_0_.refs_3_), channel_id=1, source_target_pairs={{0,1},{1,0},{2,3},{3,2},{4,5},{5,4},{6,7},{7,6},{8,9},{9,8},{10,11... | collective-permute-start | bytes 393224 | tf_op jit(solution)/shard_map/ppermute | solution.py:278
  77.9 1.8 %backward_cols.4.refs_2_.refs_0_ = f32[4,256,512]{2,1,0:T(8,128)S(1)} custom-call(s32[2]{0:T(128)S(1)} %pad_add_fusion.where, bf16[512,4096]{1,0:T(8,128)(2,1)S(1)} %get-tuple-element.20.refs_3_.a_ref.refs_0_, bf16[256,512]{1,0:T(8,128)(2,1)S(1)} %add.23.refs_1_, f32[8,256,512]{2,1,0:T(8,128)S(1)} %backward_cols.3.refs_2_), custom_call_target="tpu_custom_call" | custom-call | tf_op jit(solution)/shard_map/backward_cols/pallas_call | solution.py:206
  80.0 2.4 %collective-permute-start.21 = (bf16[256,512]{1,0:T(8,128)(2,1)S(1)}, bf16[256,512]{1,0:T(8,128)(2,1)S(1)}, u32[]{:S(2)}, u32[]{:S(2)}) collective-permute-start(bf16[256,512]{1,0:T(8,128)(2,1)S(1)} %get-tuple-element.33), channel_id=1, source_target_pairs={{0,24},{4,28},{8,16},{12,20},{16,8},{20,12},{24,0},{28,4},{1,25},{... | collective-permute-start | bytes 786440 | tf_op jit(solution)/shard_map/ppermute | solution.py:278
  82.4 0.6 collective-permute-start.20
  84.2 7.9 %collective-permute-done.17.refs_1_ = bf16[256,256]{1,0:T(8,128)(2,1)S(1)} collective-permute-done((bf16[256,256]{1,0:T(8,128)(2,1)S(1)}, bf16[256,256]{1,0:T(8,128)(2,1)S(1)}, u32[]{:S(2)}, u32[]{:S(2)}) %collective-permute-start.17) | collective-permute-done | bytes 131104 | tf_op jit(solution)/shard_map/ppermute | solution.py:278
  92.1 0.7 total.5
  92.8 2.1 %collective-permute-done.20.refs_3_ = bf16[256,512]{1,0:T(8,128)(2,1)S(1)} collective-permute-done((bf16[256,512]{1,0:T(8,128)(2,1)S(1)}, bf16[256,512]{1,0:T(8,128)(2,1)S(1)}, u32[]{:S(2)}, u32[]{:S(2)}) %collective-permute-start.20) | collective-permute-done | bytes 262176 | tf_op jit(solution)/shard_map/ppermute | solution.py:278
  95.0 0.9 finish.1
  (39 shorter events, 3.7 us)
Async XLA Ops:
  0.6 11.8 %collective-permute-start.1 = (bf16[512,256]{1,0:T(8,128)(2,1)}, bf16[512,256]{1,0:T(8,128)(2,1)S(1)}, u32[]{:S(2)}, u32[]{:S(2)}) collective-permute-start(bf16[512,256]{1,0:T(8,128)(2,1)} %features_ref.1), channel_id=1, source_target_pairs={{0,24},{4,28},{8,16},{12,20},{16,8},{20,12},{24,0},{28,4},{1,25},{... | collective-permute-start | bytes 786440 | tf_op jit(solution)/shard_map/ppermute | solution.py:278
  4.6 12.4 %collective-permute-start.3 = (bf16[512,256]{1,0:T(8,128)(2,1)}, bf16[512,256]{1,0:T(8,128)(2,1)S(1)}, u32[]{:S(2)}, u32[]{:S(2)}) collective-permute-start(bf16[512,256]{1,0:T(8,128)(2,1)} %features_ref.1), channel_id=1, source_target_pairs={{0,8},{4,12},{8,0},{12,4},{16,24},{20,28},{24,16},{28,20},{1,9},{5... | collective-permute-start | bytes 786440 | tf_op jit(solution)/shard_map/ppermute | solution.py:278
  5.1 11.9 %collective-permute-start.2 = (bf16[512,256]{1,0:T(8,128)(2,1)}, bf16[512,256]{1,0:T(8,128)(2,1)S(1)}, u32[]{:S(2)}, u32[]{:S(2)}) collective-permute-start(bf16[512,256]{1,0:T(8,128)(2,1)} %features_ref.1), channel_id=1, source_target_pairs={{0,16},{4,20},{8,24},{12,28},{16,0},{20,4},{24,8},{28,12},{1,17},{... | collective-permute-start | bytes 786440 | tf_op jit(solution)/shard_map/ppermute | solution.py:278
  5.2 13.6 %collective-permute-start = (bf16[512,256]{1,0:T(8,128)(2,1)}, bf16[512,256]{1,0:T(8,128)(2,1)S(1)}, u32[]{:S(2)}, u32[]{:S(2)}) collective-permute-start(bf16[512,256]{1,0:T(8,128)(2,1)} %features_ref.1), channel_id=1, source_target_pairs={{0,4},{4,0},{8,12},{12,8},{16,20},{20,16},{24,28},{28,24},{1,5},{5... | collective-permute-start | bytes 786440 | tf_op jit(solution)/shard_map/ppermute | solution.py:278
  17.0 1.8 %collective-permute-start.4 = (bf16[512,256]{1,0:T(8,128)(2,1)S(1)}, bf16[512,256]{1,0:T(8,128)(2,1)S(1)}, u32[]{:S(2)}, u32[]{:S(2)}) collective-permute-start(bf16[512,256]{1,0:T(8,128)(2,1)S(1)} %get-tuple-element.23.refs_2_.refs_1_), channel_id=1, source_target_pairs={{0,4},{4,0},{8,12},{12,8},{16,20},{20,16},{24,28},{28,24},{1,5},{5... | collective-permute-start | bytes 786440 | tf_op jit(solution)/shard_map/ppermute | solution.py:278
  17.0 1.9 %collective-permute-start.5 = (bf16[512,256]{1,0:T(8,128)(2,1)S(1)}, bf16[512,256]{1,0:T(8,128)(2,1)S(1)}, u32[]{:S(2)}, u32[]{:S(2)}) collective-permute-start(bf16[512,256]{1,0:T(8,128)(2,1)S(1)} %get-tuple-element.24.refs_4_.refs_2_), channel_id=1, source_target_pairs={{0,4},{4,0},{8,12},{12,8},{16,20},{20,16},{24,28},{28,24},{1,5},{5... | collective-permute-start | bytes 786440 | tf_op jit(solution)/shard_map/ppermute | solution.py:278
  17.5 1.8 %collective-permute-start.6 = (bf16[512,256]{1,0:T(8,128)(2,1)S(1)}, bf16[512,256]{1,0:T(8,128)(2,1)S(1)}, u32[]{:S(2)}, u32[]{:S(2)}) collective-permute-start(bf16[512,256]{1,0:T(8,128)(2,1)S(1)} %get-tuple-element.25.refs_6_.refs_3_), channel_id=1, source_target_pairs={{0,4},{4,0},{8,12},{12,8},{16,20},{20,16},{24,28},{28,24},{1,5},{5... | collective-permute-start | bytes 786440 | tf_op jit(solution)/shard_map/ppermute | solution.py:278
  20.6 9.3 %collective-permute-start.8 = (bf16[512,256]{1,0:T(8,128)(2,1)S(1)}, bf16[512,256]{1,0:T(8,128)(2,1)S(1)}, u32[]{:S(2)}, u32[]{:S(2)}) collective-permute-start(bf16[512,256]{1,0:T(8,128)(2,1)S(1)} %forward_rows.7), channel_id=1, source_target_pairs={{0,1},{3,2},{4,5},{7,6},{8,9},{11,10},{12,13},{15,14},{16,17},{19,... | collective-permute-start | bytes 786440 | tf_op jit(solution)/shard_map/ppermute | solution.py:305
  24.1 11.3 %collective-permute-start.7 = (bf16[512,256]{1,0:T(8,128)(2,1)S(1)}, bf16[512,256]{1,0:T(8,128)(2,1)S(1)}, u32[]{:S(2)}, u32[]{:S(2)}) collective-permute-start(bf16[512,256]{1,0:T(8,128)(2,1)S(1)} %forward_rows.7), channel_id=1, source_target_pairs={{1,2},{2,1},{5,6},{6,5},{9,10},{10,9},{13,14},{14,13},{17,18},{18,... | collective-permute-start | bytes 786440 | tf_op jit(solution)/shard_map/ppermute | solution.py:306
  28.6 16.6 %copy-start = (bf16[512,256]{1,0:T(8,128)(2,1)S(1)}, bf16[512,256]{1,0:T(8,128)(2,1)}, u32[]{:S(2)}) copy-start(bf16[512,256]{1,0:T(8,128)(2,1)} %refs_5_.1) | copy-start | bytes 786436
  28.6 16.6 %copy-start.1 = (bf16[256,256]{1,0:T(8,128)(2,1)S(1)}, bf16[256,256]{1,0:T(8,128)(2,1)}, u32[]{:S(2)}) copy-start(bf16[256,256]{1,0:T(8,128)(2,1)} %refs_4_.1) | copy-start | bytes 393220
  30.0 15.0 %collective-permute-start.9 = (bf16[512,256]{1,0:T(8,128)(2,1)S(1)}, bf16[512,256]{1,0:T(8,128)(2,1)S(1)}, u32[]{:S(2)}, u32[]{:S(2)}) collective-permute-start(bf16[512,256]{1,0:T(8,128)(2,1)S(1)} %get-tuple-element.26), channel_id=1, source_target_pairs={{0,2},{1,3},{2,0},{3,1},{4,6},{5,7},{6,4},{7,5},{8,10},{9,11},{10,... | collective-permute-start | bytes 786440 | tf_op jit(solution)/shard_map/ppermute | solution.py:278
  33.5 11.7 %collective-permute-start.10 = (bf16[512,256]{1,0:T(8,128)(2,1)S(1)}, bf16[512,256]{1,0:T(8,128)(2,1)S(1)}, u32[]{:S(2)}, u32[]{:S(2)}) collective-permute-start(bf16[512,256]{1,0:T(8,128)(2,1)S(1)} %get-tuple-element.27), channel_id=1, source_target_pairs={{0,1},{1,0},{2,3},{3,2},{4,5},{5,4},{6,7},{7,6},{8,9},{9,8},{10,11... | collective-permute-start | bytes 786440 | tf_op jit(solution)/shard_map/ppermute | solution.py:278
  46.3 2.2 %collective-permute-start.11 = (f32[256,256]{1,0:T(8,128)S(1)}, f32[256,256]{1,0:T(8,128)S(1)}, u32[]{:S(2)}, u32[]{:S(2)}) collective-permute-start(f32[256,256]{1,0:T(8,128)S(1)} %get-tuple-element.29), channel_id=1, source_target_pairs={{0,4},{4,0},{8,12},{12,8},{16,20},{20,16},{24,28},{28,24},{1,5},{5... | collective-permute-start | bytes 786440 | tf_op jit(solution)/shard_map/ppermute | solution.py:278
  46.3 13.1 %collective-permute-start.16 = (bf16[256,512]{1,0:T(8,128)(2,1)S(1)}, bf16[256,512]{1,0:T(8,128)(2,1)S(1)}, u32[]{:S(2)}, u32[]{:S(2)}) collective-permute-start(bf16[256,512]{1,0:T(8,128)(2,1)S(1)} %get-tuple-element.30.refs_0_), channel_id=1, source_target_pairs={{0,1},{1,0},{2,3},{3,2},{4,5},{5,4},{6,7},{7,6},{8,9},{9,8},{10,11... | collective-permute-start | bytes 786440 | tf_op jit(solution)/shard_map/ppermute | solution.py:278
  47.8 15.0 %collective-permute-start.13 = (bf16[256,512]{1,0:T(8,128)(2,1)S(1)}, bf16[256,512]{1,0:T(8,128)(2,1)S(1)}, u32[]{:S(2)}, u32[]{:S(2)}) collective-permute-start(bf16[256,512]{1,0:T(8,128)(2,1)S(1)} %get-tuple-element.30.refs_0_), channel_id=1, source_target_pairs={{0,2},{1,3},{2,0},{3,1},{4,6},{5,7},{6,4},{7,5},{8,10},{9,11},{10,... | collective-permute-start | bytes 786440 | tf_op jit(solution)/shard_map/ppermute | solution.py:278
  62.8 9.5 %collective-permute-start.14 = (bf16[256,512]{1,0:T(8,128)(2,1)S(1)}, bf16[256,512]{1,0:T(8,128)(2,1)S(1)}, u32[]{:S(2)}, u32[]{:S(2)}) collective-permute-start(bf16[256,512]{1,0:T(8,128)(2,1)S(1)} %get-tuple-element.31.refs_5_), channel_id=1, source_target_pairs={{1,0},{2,3},{5,4},{6,7},{9,8},{10,11},{13,12},{14,15},{17,16},{18,... | collective-permute-start | bytes 786440 | tf_op jit(solution)/shard_map/ppermute | solution.py:323
  64.1 8.2 %collective-permute-start.15 = (bf16[256,512]{1,0:T(8,128)(2,1)S(1)}, bf16[256,512]{1,0:T(8,128)(2,1)S(1)}, u32[]{:S(2)}, u32[]{:S(2)}) collective-permute-start(bf16[256,512]{1,0:T(8,128)(2,1)S(1)} %get-tuple-element.32.refs_3_), channel_id=1, source_target_pairs={{1,2},{2,1},{5,6},{6,5},{9,10},{10,9},{13,14},{14,13},{17,18},{18,... | collective-permute-start | bytes 786440 | tf_op jit(solution)/shard_map/ppermute | solution.py:324
  74.1 5.6 %collective-permute-start.18 = (bf16[4,256,512]{2,1,0:T(8,128)(2,1)S(1)}, bf16[4,256,512]{2,1,0:T(8,128)(2,1)S(1)}, u32[]{:S(2)}, u32[]{:S(2)}) collective-permute-start(bf16[4,256,512]{2,1,0:T(8,128)(2,1)S(1)} %backward_cols.5), channel_id=1, source_target_pairs={{0,4},{4,0},{8,12},{12,8},{16,20},{20,16},{24,28},{28,24},{1,5},{5... | collective-permute-start | bytes 3145736 | tf_op jit(solution)/shard_map/ppermute | solution.py:278
  74.2 9.3 %collective-permute-start.12 = (bf16[256,256]{1,0:T(8,128)(2,1)S(1)}, bf16[256,256]{1,0:T(8,128)(2,1)S(1)}, u32[]{:S(2)}, u32[]{:S(2)}) collective-permute-start(bf16[256,256]{1,0:T(8,128)(2,1)S(1)} %total.3.refs_2_.refs_0_.refs_3_), channel_id=1, source_target_pairs={{0,1},{1,0},{2,3},{3,2},{4,5},{5,4},{6,7},{7,6},{8,9},{9,8},{10,11... | collective-permute-start | bytes 393224 | tf_op jit(solution)/shard_map/ppermute | solution.py:278
  80.0 12.8 %collective-permute-start.21 = (bf16[256,512]{1,0:T(8,128)(2,1)S(1)}, bf16[256,512]{1,0:T(8,128)(2,1)S(1)}, u32[]{:S(2)}, u32[]{:S(2)}) collective-permute-start(bf16[256,512]{1,0:T(8,128)(2,1)S(1)} %get-tuple-element.33), channel_id=1, source_target_pairs={{0,24},{4,28},{8,16},{12,20},{16,8},{20,12},{24,0},{28,4},{1,25},{... | collective-permute-start | bytes 786440 | tf_op jit(solution)/shard_map/ppermute | solution.py:278
  82.4 12.6 %collective-permute-start.20 = (bf16[256,512]{1,0:T(8,128)(2,1)S(1)}, bf16[256,512]{1,0:T(8,128)(2,1)S(1)}, u32[]{:S(2)}, u32[]{:S(2)}) collective-permute-start(bf16[256,512]{1,0:T(8,128)(2,1)S(1)} %get-tuple-element.34), channel_id=1, source_target_pairs={{0,16},{4,20},{8,24},{12,28},{16,0},{20,4},{24,8},{28,12},{1,17},{... | collective-permute-start | bytes 786440 | tf_op jit(solution)/shard_map/ppermute | solution.py:278
  83.0 11.9 %collective-permute-start.19 = (bf16[256,512]{1,0:T(8,128)(2,1)S(1)}, bf16[256,512]{1,0:T(8,128)(2,1)S(1)}, u32[]{:S(2)}, u32[]{:S(2)}) collective-permute-start(bf16[256,512]{1,0:T(8,128)(2,1)S(1)} %get-tuple-element.35), channel_id=1, source_target_pairs={{0,8},{4,12},{8,0},{12,4},{16,24},{20,28},{24,16},{28,20},{1,9},{5... | collective-permute-start | bytes 786440 | tf_op jit(solution)/shard_map/ppermute | solution.py:278
  83.6 8.5 %collective-permute-start.17 = (bf16[256,256]{1,0:T(8,128)(2,1)S(1)}, bf16[256,256]{1,0:T(8,128)(2,1)S(1)}, u32[]{:S(2)}, u32[]{:S(2)}) collective-permute-start(bf16[256,256]{1,0:T(8,128)(2,1)S(1)} %total.4.refs_0_), channel_id=1, source_target_pairs={{0,2},{1,3},{2,0},{3,1},{4,6},{5,7},{6,4},{7,5},{8,10},{9,11},{10,... | collective-permute-start | bytes 393224 | tf_op jit(solution)/shard_map/ppermute | solution.py:278

commit v12 on v10

--- a/solution.py
+++ b/solution.py
@@ -116,30 +116,27 @@
     )(where, *[pltpu.with_memory_space_constraint(x, pltpu.HBM) for x in (counts, cols, adj, features)])
 
 
-def forward_kernel(where, a_ref, *refs, first, step):
-    shards, out_ref, before = refs[:-1], refs[-1], None
-    if first:
-        shards, before = shards[:-1], shards[-1]
+def forward_kernel(where, a_ref, *refs, steps, before):
+    shards, out_ref = refs[: len(steps)], refs[-1]
     depth = shards[0].shape[0]
-    value = None if before is None else before[...]
-    for k, shard in enumerate(shards):
-        cols = pl.ds(pl.multiple_of((where[0] ^ (first + step * k)) * depth, depth), depth)
+    value = refs[len(steps)][...] if before else None
+    for step, shard in zip(steps, shards):
+        cols = pl.ds(pl.multiple_of((where[0] ^ step) * depth, depth), depth)
         part = jnp.dot(a_ref[:, cols], shard[...], preferred_element_type=jnp.float32)
         value = part if value is None else value + part
     out_ref[...] = value.astype(out_ref.dtype)
 
 
-def forward(where, dense, shards, first, step, before, kind):
+def forward(where, dense, shards, steps, before, kind):
     rows, width = dense.shape[0], shards[0].shape[1]
-    operands = [near(x) for x in [dense, *shards, *before]]
-    flops = 2 * rows * dense.shape[1] * width
-    return pl.pallas_call(
-        functools.partial(forward_kernel, first=first, step=step),
+    operands = [near(x) for x in [dense, *[shards[s] for s in steps], *before]]
+    return pl.pallas_call(
+        functools.partial(forward_kernel, steps=steps, before=bool(before)),
         out_shape=pltpu.VMEM((rows, width), kind),
         in_specs=[SCALARS] + [WHOLE] * len(operands),
         out_specs=WHOLE,
         compiler_params=params(10),
-        cost_estimate=cost(flops, dense.size * 2),
+        cost_estimate=cost(2 * dense.size * width, dense.size * 2),
         name="forward_rows",
     )(where, *operands)
 
@@ -182,21 +179,15 @@
 def backward_kernel(where, *refs, count, steps, before):
     dense, pieces = refs[:count], refs[count : 2 * count]
     out_ref = refs[-1]
-    columns, _, depth = out_ref.shape
-
-    def one(j, carry):
-        step = jnp.int32(steps[0])
-        for i in range(1, len(steps)):
-            step = jnp.where(j == i, steps[i], step)
+    depth = out_ref.shape[2]
+
+    for j, step in enumerate(steps):
         cols = pl.ds(pl.multiple_of((where[0] ^ step) * depth, depth), depth)
         value = refs[2 * count][step] if before else None
         for a_ref, piece in zip(dense, pieces):
             part = jnp.dot(piece[...], a_ref[:, cols], preferred_element_type=jnp.float32)
             value = part if value is None else value + part
         out_ref[j] = value.astype(out_ref.dtype)
-        return carry
-
-    lax.fori_loop(0, columns, one, 0)
 
 
 def backward(where, dense, pieces, steps, depth, before, kind, after=()):
@@ -216,26 +207,21 @@
 
 def finish_kernel(*refs):
     parts, out_ref = refs[:-1], refs[-1]
-    value = parts[0][0].astype(jnp.float32) + parts[1][0].astype(jnp.float32)
-    for part in parts[2:]:
+    value = parts[0][...].astype(jnp.float32)
+    for part in parts[1:]:
         value = value + part[...].astype(jnp.float32)
     out_ref[...] = value.astype(out_ref.dtype).T
 
 
-def finish(kept, came, parts):
-    _, width, rows = kept.shape
-    own = pl.BlockSpec((1, width, rows), lambda i: (0, 0, 0))
-    part = pl.BlockSpec((width, rows), lambda i: (0, 0))
+def finish(parts):
+    width, rows = parts[0].shape
     return pl.pallas_call(
         finish_kernel,
         out_shape=jax.ShapeDtypeStruct((rows, width), jnp.bfloat16),
-        grid=(1,),
-        in_specs=[own, own] + [part] * len(parts),
-        out_specs=pl.BlockSpec((rows, width), lambda i: (0, 0)),
         compiler_params=params(12),
         cost_estimate=cost(len(parts) * rows * width, 4 * len(parts) * rows * width),
         name="finish",
-    )(kept, came, *parts)
+    )(*parts)
 
 
 def gate(values, after):
@@ -292,15 +278,18 @@
     *blocks, near_features = dense_rows(where, steps, counts, cols, adj, features, rows, col_tiles)
     dense = dict(zip(steps, blocks))
 
-    away = gate([swap(features, "row", n_row, 2 * s) for s in range(chips - 1, 0, -1)], blocks)
-    odd = [swap(shard, "row", n_row, 1) for shard in [features, *away[::-1]]]
-    even = [near_features, *away[::-1]]
-    parts = [shard for pair in zip(even, odd) for shard in pair]
-
-    half = forward(where, dense[n_col - 1], even, 0, 2, [], jnp.float32)
-    shares = {n_col - 1: forward(where, dense[n_col - 1], odd, 1, 2, [half], jnp.bfloat16)}
+    far = n_col - 1
+    every = list(range(n_row))
+    away = gate([swap(features, "row", n_row, 2 * c) for c in range(chips - 1, 0, -1)], blocks)[::-1]
+    parts = {0: near_features, 1: swap(features, "row", n_row, 1)}
+    for c, shard in enumerate(away, 1):
+        parts.update({2 * c: shard, 2 * c + 1: swap(shard, "row", n_row, 1)})
+
+    half = forward(where, dense[far], parts, every[::2], [], jnp.float32)
+    first = forward(where, dense[far], parts, every[1::2], [half], jnp.bfloat16)
+    shares = {far: first}
     for s in steps[1:-1]:
-        shares[s] = forward(where, dense[s], parts, 0, 1, [], jnp.bfloat16)
+        shares[s] = forward(where, dense[s], parts, every, [], jnp.bfloat16)
     if line:
         relayed = lax.ppermute(shares[3], "col", [(0, 1), (3, 2)])
         came = [lax.ppermute(shares[3], "col", [(1, 2), (2, 1)])]
@@ -308,7 +297,7 @@
         came += [swap(joined, "col", n_col, 2), swap(shares[1], "col", n_col, 1)]
     else:
         came = [swap(share, "col", n_col, s) for s, share in shares.items()]
-    mine = forward(where, dense[0], parts, 0, 1, [], jnp.float32)
+    mine = forward(where, dense[0], parts, every, [], jnp.float32)
     scale = 1.0 / math.sqrt(rows * n_row * n_col)
     hidden, piece, part = middle([mine, *came], weight, upstream, scale)
 
@@ -325,7 +314,6 @@
         pieces = {s: swap(piece, "col", n_col, s) for s in steps[:-1]}
         pieces[0] = piece
 
-    every = list(range(n_row))
     sums, latest = None, n_col - 1
     for group in [list(range(n_col - 1))]:
         sums = backward(where, [dense[s] for s in group], [pieces[s] for s in group], every, depth, sums, jnp.float32)
@@ -333,10 +321,11 @@
     sent = last(every[1::2], depth, sums, jnp.bfloat16, [part])
     kept = last(every[::2], depth, sums, jnp.float32)
     came = swap(sent, "row", n_row, 1)
-    summed = [(kept[c] + came[c].astype(jnp.float32)).astype(jnp.bfloat16) for c in range(1, chips)]
+    own, *summed = [kept[c] + came[c].astype(jnp.float32) for c in range(chips)]
+    summed = [value.astype(jnp.bfloat16) for value in summed]
     parts = [swap(summed[c - 1], "row", n_row, 2 * c) for c in range(1, chips)]
 
-    feature_grad = finish(kept, came, parts)
+    feature_grad = finish([own, *parts])
     for s in range(n_col.bit_length() - 2):
         part = total([part, swap(part, "col", n_col, 1 << s)], part.shape[0], jnp.bfloat16, [kept])
     came = swap(part, "col", n_col, n_col // 2)

time: 93.1 us -> 92.7 us (level)
  Pallas kernels: 26.8 us -> 24.9 us
  waiting for transfers between devices: 30.7 us -> 32.6 us
    pallas_call x3, Pallas kernels: 8.74 us -> 6.55 us  [backward(): pl.pallas_call(functools.partial(backward_kernel, count=count, steps=step...]
    ppermute x1, waiting for transfers between devices: 3.3 us -> 4.48 us  [shards(): pieces[3] = beside + lax.ppermute(pieces[2], 'col', [(1, 0), (2, 3)])]
  transfers between devices with their start and end apart: 22 -> 22, of which waited for: 11 -> 11; matrix products, arithmetic and copies ran while one was open for 0% -> 1% of each run, Pallas kernels for 23% -> 22%
where the time goes in v12:
time: 92.7 us; the launch traced here: 92.5 us
  waiting for transfers between devices  32.6 us (35%)
  Pallas kernels  24.9 us (27%)
  starting transfers between devices  23.5 us (25%)
  blocking collectives  10 us (11%)
    ppermute x18, waiting for transfers between devices, swap(): return lax.ppermute(value, axis, [(i, i ^ step) for i in range(size)])  28.1 us
    ppermute x18, starting transfers between devices, swap(): return lax.ppermute(value, axis, [(i, i ^ step) for i in range(size)])  17.1 us
    all_gather x1, blocking collectives, shards(): gathered = lax.all_gather(part, 'row', axis_index_groups=cores, tiled=True)  10 us
    pallas_call x5, Pallas kernels, forward(): pl.pallas_call(functools.partial(forward_kernel, steps=steps, before=bool...  7.94 us
    pallas_call x1, Pallas kernels, dense_rows(): pl.pallas_call(functools.partial(dense_kernel, steps=steps, window=window...  7.6 us
    pallas_call x3, Pallas kernels, backward(): pl.pallas_call(functools.partial(backward_kernel, count=count, steps=step...  6.55 us
    ppermute x1, waiting for transfers between devices, shards(): pieces[3] = beside + lax.ppermute(pieces[2], 'col', [(1, 0), (2, 3)])  4.48 us
    ppermute x1, starting transfers between devices, shards(): relayed = lax.ppermute(shares[3], 'col', [(0, 1), (3, 2)])  3.5 us
  transfers between devices with their start and end apart: 22, of which 11 were waited for; matrix products, arithmetic and copies ran while one was open for 1% of the time, Pallas kernels for 22%

profile of v12, /device:TPU:0, one launch (start us, length us, event | category | flops | bytes accessed | tf_op | source)
XLA Modules:
  0.0 92.5 jit_solution(15235151076175022021)
XLA Ops:
  0.6 4.0 %collective-permute-start.1 = (bf16[512,256]{1,0:T(8,128)(2,1)}, bf16[512,256]{1,0:T(8,128)(2,1)S(1)}, u32[]{:S(2)}, u32[]{:S(2)}) collective-permute-start(bf16[512,256]{1,0:T(8,128)(2,1)} %features_ref.1), channel_id=1, source_target_pairs={{0,24},{4,28},{8,16},{12,20},{16,8},{20,12},{24,0},{28,4},{1,25},{... | collective-permute-start | bytes 786440 | tf_op jit(solution)/shard_map/ppermute | solution.py:264
  5.3 7.6 %dense_rows.1 = (bf16[512,4096]{1,0:T(8,128)(2,1)S(1)}, bf16[512,4096]{1,0:T(8,128)(2,1)S(1)}, bf16[512,4096]{1,0:T(8,128)(2,1)S(1)}, bf16[512,4096]{1,0:T(8,128)(2,1)S(1)}, bf16[512,256]{1,0:T(8,128)(2,1)S(1)}) custom-call(s32[2]{0:T(128)S(1)} %pad_add_fusion.where, s32[16]{0:T(128)} %bitcast.15, s32[448]{0:T(512)} %bitcast.14, ...), custom_call_target="tpu_custom_call" | custom-call | bytes 41943040 | tf_op jit(solution)/shard_map/dense_rows/pallas_call | solution.py:102
  12.9 4.1 %collective-permute-done.3.refs_2_ = bf16[512,256]{1,0:T(8,128)(2,1)S(1)} collective-permute-done((bf16[512,256]{1,0:T(8,128)(2,1)}, bf16[512,256]{1,0:T(8,128)(2,1)S(1)}, u32[]{:S(2)}, u32[]{:S(2)}) %collective-permute-start.3) | collective-permute-done | bytes 262176 | tf_op jit(solution)/shard_map/ppermute | solution.py:264
  17.6 1.2 %forward_rows.6.refs_4_ = f32[512,256]{1,0:T(8,128)S(1)} custom-call(s32[2]{0:T(128)S(1)} %pad_add_fusion.where, bf16[512,4096]{1,0:T(8,128)(2,1)S(1)} %get-tuple-element.18.refs_3_.a_ref.refs_0_, bf16[512,256]{1,0:T(8,128)(2,1)S(1)} %get-tuple-element.17.refs_0_, bf16[512,256]{1,0:T(8,128)(2,1)S(1)} %get-tuple-element.21.refs_2_.refs_1_, ...), custom_call_target="tpu_custom_call" | custom-call | flops 1073741824 | bytes 4194304 | tf_op jit(solution)/shard_map/forward_rows/pallas_call | solution.py:133
  19.3 1.3 %forward_rows.7 = bf16[512,256]{1,0:T(8,128)(2,1)S(1)} custom-call(s32[2]{0:T(128)S(1)} %pad_add_fusion.where, bf16[512,4096]{1,0:T(8,128)(2,1)S(1)} %get-tuple-element.18.refs_3_.a_ref.refs_0_, bf16[512,256]{1,0:T(8,128)(2,1)S(1)} %collective-permute-done.refs_1_.refs_0_, bf16[512,256]{1,0:T(8,128)(2,1)S(1)} %collective-permute-done.4.refs_3_.refs_1_, ...), custom_call_target="tpu_custom_call" | custom-call | flops 1073741824 | bytes 4194304 | tf_op jit(solution)/shard_map/forward_rows/pallas_call | solution.py:133
  20.6 3.5 %collective-permute-start.8 = (bf16[512,256]{1,0:T(8,128)(2,1)S(1)}, bf16[512,256]{1,0:T(8,128)(2,1)S(1)}, u32[]{:S(2)}, u32[]{:S(2)}) collective-permute-start(bf16[512,256]{1,0:T(8,128)(2,1)S(1)} %forward_rows.7), channel_id=1, source_target_pairs={{0,1},{3,2},{4,5},{7,6},{8,9},{11,10},{12,13},{15,14},{16,17},{19,... | collective-permute-start | bytes 786440 | tf_op jit(solution)/shard_map/ppermute | solution.py:294
  24.1 0.9 collective-permute-start.7
  25.0 1.8 %forward_rows.9 = bf16[512,256]{1,0:T(8,128)(2,1)S(1)} custom-call(s32[2]{0:T(128)S(1)} %pad_add_fusion.where, bf16[512,4096]{1,0:T(8,128)(2,1)S(1)} %get-tuple-element.20.refs_5_.a_ref.refs_1_, bf16[512,256]{1,0:T(8,128)(2,1)S(1)} %get-tuple-element.17.refs_0_, bf16[512,256]{1,0:T(8,128)(2,1)S(1)} %collective-permute-done.refs_1_.refs_0_, ...), custom_call_target="tpu_custom_call" | custom-call | flops 1073741824 | bytes 4194304 | tf_op jit(solution)/shard_map/forward_rows/pallas_call | solution.py:133
  26.8 2.2 %collective-permute-start.10 = (bf16[512,256]{1,0:T(8,128)(2,1)S(1)}, bf16[512,256]{1,0:T(8,128)(2,1)S(1)}, u32[]{:S(2)}, u32[]{:S(2)}) collective-permute-start(bf16[512,256]{1,0:T(8,128)(2,1)S(1)} %forward_rows.9), channel_id=1, source_target_pairs={{0,1},{1,0},{2,3},{3,2},{4,5},{5,4},{6,7},{7,6},{8,9},{9,8},{10,11... | collective-permute-start | bytes 786440 | tf_op jit(solution)/shard_map/ppermute | solution.py:264
  29.0 1.8 %forward_rows.8 = bf16[512,256]{1,0:T(8,128)(2,1)S(1)} custom-call(s32[2]{0:T(128)S(1)} %pad_add_fusion.where, bf16[512,4096]{1,0:T(8,128)(2,1)S(1)} %get-tuple-element.19.refs_4_.a_ref.refs_2_, bf16[512,256]{1,0:T(8,128)(2,1)S(1)} %get-tuple-element.17.refs_0_, bf16[512,256]{1,0:T(8,128)(2,1)S(1)} %collective-permute-done.refs_1_.refs_0_, ...), custom_call_target="tpu_custom_call" | custom-call | flops 1073741824 | bytes 4194304 | tf_op jit(solution)/shard_map/forward_rows/pallas_call | solution.py:133
  30.9 3.4 %collective-permute-start.9 = (bf16[512,256]{1,0:T(8,128)(2,1)S(1)}, bf16[512,256]{1,0:T(8,128)(2,1)S(1)}, u32[]{:S(2)}, u32[]{:S(2)}) collective-permute-start(bf16[512,256]{1,0:T(8,128)(2,1)S(1)} %add_convert_fusion), channel_id=1, source_target_pairs={{0,2},{1,3},{2,0},{3,1},{4,6},{5,7},{6,4},{7,5},{8,10},{9,11},{10,... | collective-permute-start | bytes 786440 | tf_op jit(solution)/shard_map/ppermute | solution.py:264
  34.4 1.8 %forward_rows.5.refs_0_ = f32[512,256]{1,0:T(8,128)S(1)} custom-call(s32[2]{0:T(128)S(1)} %pad_add_fusion.where, bf16[512,4096]{1,0:T(8,128)(2,1)S(1)} %get-tuple-element.16.refs_6_.a_ref.refs_0_, bf16[512,256]{1,0:T(8,128)(2,1)S(1)} %get-tuple-element.17.refs_0_, bf16[512,256]{1,0:T(8,128)(2,1)S(1)} %collective-permute-done.refs_1_.refs_0_, ...), custom_call_target="tpu_custom_call" | custom-call | flops 1073741824 | bytes 4194304 | tf_op jit(solution)/shard_map/forward_rows/pallas_call | solution.py:133
  36.2 3.6 %collective-permute-done.10.refs_3_ = bf16[512,256]{1,0:T(8,128)(2,1)S(1)} collective-permute-done((bf16[512,256]{1,0:T(8,128)(2,1)S(1)}, bf16[512,256]{1,0:T(8,128)(2,1)S(1)}, u32[]{:S(2)}, u32[]{:S(2)}) %collective-permute-start.10) | collective-permute-done | bytes 262176 | tf_op jit(solution)/shard_map/ppermute | solution.py:264
  39.8 5.6 %collective-permute-done.9.refs_2_ = bf16[512,256]{1,0:T(8,128)(2,1)S(1)} collective-permute-done((bf16[512,256]{1,0:T(8,128)(2,1)S(1)}, bf16[512,256]{1,0:T(8,128)(2,1)S(1)}, u32[]{:S(2)}, u32[]{:S(2)}) %collective-permute-start.9) | collective-permute-done | bytes 262176 | tf_op jit(solution)/shard_map/ppermute | solution.py:264
  45.3 1.1 %middle.1 = (bf16[512,256]{1,0:T(8,128)(2,1)}, bf16[256,512]{1,0:T(8,128)(2,1)S(1)}, f32[256,256]{1,0:T(8,128)S(1)}) custom-call(f32[512,256]{1,0:T(8,128)S(1)} %forward_rows.5.refs_0_, bf16[512,256]{1,0:T(8,128)(2,1)S(1)} %collective-permute-done.7.refs_1_, bf16[512,256]{1,0:T(8,128)(2,1)S(1)} %collective-permute-done.9.refs_2_, ...), custom_call_target="tpu_custom_call" | custom-call | flops 201326592 | bytes 1310720 | tf_op jit(solution)/shard_map/middle/pallas_call | solution.py:166
  46.4 2.1 %collective-permute-start.13 = (bf16[256,512]{1,0:T(8,128)(2,1)S(1)}, bf16[256,512]{1,0:T(8,128)(2,1)S(1)}, u32[]{:S(2)}, u32[]{:S(2)}) collective-permute-start(bf16[256,512]{1,0:T(8,128)(2,1)S(1)} %get-tuple-element.26.refs_0_), channel_id=1, source_target_pairs={{0,2},{1,3},{2,0},{3,1},{4,6},{5,7},{6,4},{7,5},{8,10},{9,11},{10,... | collective-permute-start | bytes 786440 | tf_op jit(solution)/shard_map/ppermute | solution.py:264
  48.6 10.0 %all_gather.3.refs_0_ = bf16[1024,256]{1,0:T(8,128)(2,1)S(1)} all-gather(bf16[256,256]{1,0:T(8,128)(2,1)S(1)} %add_convert_fusion.1), channel_id=1, replica_groups={{0,8,16,24},{4,12,20,28},{1,9,17,25},{5,13,21,29},{2,10,18,26},{6,14,22..., dimensions={0}, use_global_device_ids=true | all-gather | bytes 655360 | tf_op jit(solution)/shard_map/all_gather | solution.py:306
  58.7 1.0 %collective-permute-done.16.refs_4_ = bf16[256,512]{1,0:T(8,128)(2,1)S(1)} collective-permute-done((bf16[256,512]{1,0:T(8,128)(2,1)S(1)}, bf16[256,512]{1,0:T(8,128)(2,1)S(1)}, u32[]{:S(2)}, u32[]{:S(2)}) %collective-permute-start.16) | collective-permute-done | bytes 262176 | tf_op jit(solution)/shard_map/ppermute | solution.py:264
  59.7 2.0 %collective-permute-done.13.refs_1_ = bf16[256,512]{1,0:T(8,128)(2,1)S(1)} collective-permute-done((bf16[256,512]{1,0:T(8,128)(2,1)S(1)}, bf16[256,512]{1,0:T(8,128)(2,1)S(1)}, u32[]{:S(2)}, u32[]{:S(2)}) %collective-permute-start.13) | collective-permute-done | bytes 262176 | tf_op jit(solution)/shard_map/ppermute | solution.py:264
  61.7 0.7 collective-permute-start.14
  62.4 1.3 %collective-permute-start.15 = (bf16[256,512]{1,0:T(8,128)(2,1)S(1)}, bf16[256,512]{1,0:T(8,128)(2,1)S(1)}, u32[]{:S(2)}, u32[]{:S(2)}) collective-permute-start(bf16[256,512]{1,0:T(8,128)(2,1)S(1)} %get-tuple-element.28.refs_5_), channel_id=1, source_target_pairs={{1,0},{2,3},{5,4},{6,7},{9,8},{10,11},{13,12},{14,15},{17,16},{18,... | collective-permute-start | bytes 786440 | tf_op jit(solution)/shard_map/ppermute | solution.py:312
  63.7 4.0 %backward_cols.3.refs_2_ = f32[8,256,512]{2,1,0:T(8,128)S(1)} custom-call(s32[2]{0:T(128)S(1)} %pad_add_fusion.where, bf16[512,4096]{1,0:T(8,128)(2,1)S(1)} %get-tuple-element.16.refs_6_.a_ref.refs_0_, bf16[512,4096]{1,0:T(8,128)(2,1)S(1)} %get-tuple-element.20.refs_5_.a_ref.refs_1_, bf16[512,4096]{1,0:T(8,128)(2,1)S(1)} %get-tuple-element.19.refs_4_.a_ref.refs_2_, ...), custom_call_target="tpu_custom_call" | custom-call | tf_op jit(solution)/shard_map/backward_cols/pallas_call | solution.py:197
  67.7 4.5 %collective-permute-done.15 = bf16[256,512]{1,0:T(8,128)(2,1)S(1)} collective-permute-done((bf16[256,512]{1,0:T(8,128)(2,1)S(1)}, bf16[256,512]{1,0:T(8,128)(2,1)S(1)}, u32[]{:S(2)}, u32[]{:S(2)}) %collective-permute-start.15) | collective-permute-done | bytes 262176 | tf_op jit(solution)/shard_map/ppermute | solution.py:312
  72.3 1.3 %backward_cols.5 = bf16[4,256,512]{2,1,0:T(8,128)(2,1)S(1)} custom-call(s32[2]{0:T(128)S(1)} %pad_add_fusion.where, bf16[512,4096]{1,0:T(8,128)(2,1)S(1)} %get-tuple-element.18.refs_3_.a_ref.refs_0_, bf16[256,512]{1,0:T(8,128)(2,1)S(1)} %add.28.refs_1_, f32[8,256,512]{2,1,0:T(8,128)S(1)} %backward_cols.3.refs_2_, ...), custom_call_target="tpu_custom_call" | custom-call | tf_op jit(solution)/shard_map/backward_cols/pallas_call | solution.py:197
  73.7 1.3 %backward_cols.4.refs_2_ = f32[4,256,512]{2,1,0:T(8,128)S(1)} custom-call(s32[2]{0:T(128)S(1)} %pad_add_fusion.where, bf16[512,4096]{1,0:T(8,128)(2,1)S(1)} %get-tuple-element.18.refs_3_.a_ref.refs_0_, bf16[256,512]{1,0:T(8,128)(2,1)S(1)} %add.28.refs_1_, f32[8,256,512]{2,1,0:T(8,128)S(1)} %backward_cols.3.refs_2_), custom_call_target="tpu_custom_call" | custom-call | tf_op jit(solution)/shard_map/backward_cols/pallas_call | solution.py:197
  75.0 1.3 %collective-permute-done.18 = bf16[4,256,512]{2,1,0:T(8,128)(2,1)S(1)} collective-permute-done((bf16[4,256,512]{2,1,0:T(8,128)(2,1)S(1)}, bf16[4,256,512]{2,1,0:T(8,128)(2,1)S(1)}, u32[]{:S(2)}, u32[]{:S(2)}) %collective-permute-start.18) | collective-permute-done | bytes 1048608 | tf_op jit(solution)/shard_map/ppermute | solution.py:264
  76.6 2.4 %collective-permute-start.21 = (bf16[256,512]{1,0:T(8,128)(2,1)S(1)}, bf16[256,512]{1,0:T(8,128)(2,1)S(1)}, u32[]{:S(2)}, u32[]{:S(2)}) collective-permute-start(bf16[256,512]{1,0:T(8,128)(2,1)S(1)} %get-tuple-element.29), channel_id=1, source_target_pairs={{0,24},{4,28},{8,16},{12,20},{16,8},{20,12},{24,0},{28,4},{1,25},{... | collective-permute-start | bytes 786440 | tf_op jit(solution)/shard_map/ppermute | solution.py:264
  79.0 0.6 collective-permute-start.20
  80.7 8.0 %collective-permute-done.17.refs_1_ = bf16[256,256]{1,0:T(8,128)(2,1)S(1)} collective-permute-done((bf16[256,256]{1,0:T(8,128)(2,1)S(1)}, bf16[256,256]{1,0:T(8,128)(2,1)S(1)}, u32[]{:S(2)}, u32[]{:S(2)}) %collective-permute-start.17) | collective-permute-done | bytes 131104 | tf_op jit(solution)/shard_map/ppermute | solution.py:264
  88.7 0.7 total.5
  89.4 2.1 %collective-permute-done.20.refs_2_ = bf16[256,512]{1,0:T(8,128)(2,1)S(1)} collective-permute-done((bf16[256,512]{1,0:T(8,128)(2,1)S(1)}, bf16[256,512]{1,0:T(8,128)(2,1)S(1)}, u32[]{:S(2)}, u32[]{:S(2)}) %collective-permute-start.20) | collective-permute-done | bytes 262176 | tf_op jit(solution)/shard_map/ppermute | solution.py:264
  91.6 0.9 finish.1
  (38 shorter events, 3.6 us)
Async XLA Ops:
  0.6 12.3 %collective-permute-start.1 = (bf16[512,256]{1,0:T(8,128)(2,1)}, bf16[512,256]{1,0:T(8,128)(2,1)S(1)}, u32[]{:S(2)}, u32[]{:S(2)}) collective-permute-start(bf16[512,256]{1,0:T(8,128)(2,1)} %features_ref.1), channel_id=1, source_target_pairs={{0,24},{4,28},{8,16},{12,20},{16,8},{20,12},{24,0},{28,4},{1,25},{... | collective-permute-start | bytes 786440 | tf_op jit(solution)/shard_map/ppermute | solution.py:264
  4.6 12.4 %collective-permute-start.3 = (bf16[512,256]{1,0:T(8,128)(2,1)}, bf16[512,256]{1,0:T(8,128)(2,1)S(1)}, u32[]{:S(2)}, u32[]{:S(2)}) collective-permute-start(bf16[512,256]{1,0:T(8,128)(2,1)} %features_ref.1), channel_id=1, source_target_pairs={{0,8},{4,12},{8,0},{12,4},{16,24},{20,28},{24,16},{28,20},{1,9},{5... | collective-permute-start | bytes 786440 | tf_op jit(solution)/shard_map/ppermute | solution.py:264
  5.1 11.9 %collective-permute-start.2 = (bf16[512,256]{1,0:T(8,128)(2,1)}, bf16[512,256]{1,0:T(8,128)(2,1)S(1)}, u32[]{:S(2)}, u32[]{:S(2)}) collective-permute-start(bf16[512,256]{1,0:T(8,128)(2,1)} %features_ref.1), channel_id=1, source_target_pairs={{0,16},{4,20},{8,24},{12,28},{16,0},{20,4},{24,8},{28,12},{1,17},{... | collective-permute-start | bytes 786440 | tf_op jit(solution)/shard_map/ppermute | solution.py:264
  5.2 13.6 %collective-permute-start = (bf16[512,256]{1,0:T(8,128)(2,1)}, bf16[512,256]{1,0:T(8,128)(2,1)S(1)}, u32[]{:S(2)}, u32[]{:S(2)}) collective-permute-start(bf16[512,256]{1,0:T(8,128)(2,1)} %features_ref.1), channel_id=1, source_target_pairs={{0,4},{4,0},{8,12},{12,8},{16,20},{20,16},{24,28},{28,24},{1,5},{5... | collective-permute-start | bytes 786440 | tf_op jit(solution)/shard_map/ppermute | solution.py:264
  17.0 1.8 %collective-permute-start.4 = (bf16[512,256]{1,0:T(8,128)(2,1)S(1)}, bf16[512,256]{1,0:T(8,128)(2,1)S(1)}, u32[]{:S(2)}, u32[]{:S(2)}) collective-permute-start(bf16[512,256]{1,0:T(8,128)(2,1)S(1)} %get-tuple-element.21.refs_2_.refs_1_), channel_id=1, source_target_pairs={{0,4},{4,0},{8,12},{12,8},{16,20},{20,16},{24,28},{28,24},{1,5},{5... | collective-permute-start | bytes 786440 | tf_op jit(solution)/shard_map/ppermute | solution.py:264
  17.0 1.9 %collective-permute-start.5 = (bf16[512,256]{1,0:T(8,128)(2,1)S(1)}, bf16[512,256]{1,0:T(8,128)(2,1)S(1)}, u32[]{:S(2)}, u32[]{:S(2)}) collective-permute-start(bf16[512,256]{1,0:T(8,128)(2,1)S(1)} %get-tuple-element.22.refs_4_.refs_2_), channel_id=1, source_target_pairs={{0,4},{4,0},{8,12},{12,8},{16,20},{20,16},{24,28},{28,24},{1,5},{5... | collective-permute-start | bytes 786440 | tf_op jit(solution)/shard_map/ppermute | solution.py:264
  17.5 1.8 %collective-permute-start.6 = (bf16[512,256]{1,0:T(8,128)(2,1)S(1)}, bf16[512,256]{1,0:T(8,128)(2,1)S(1)}, u32[]{:S(2)}, u32[]{:S(2)}) collective-permute-start(bf16[512,256]{1,0:T(8,128)(2,1)S(1)} %get-tuple-element.23.refs_6_.refs_3_), channel_id=1, source_target_pairs={{0,4},{4,0},{8,12},{12,8},{16,20},{20,16},{24,28},{28,24},{1,5},{5... | collective-permute-start | bytes 786440 | tf_op jit(solution)/shard_map/ppermute | solution.py:264
  20.6 10.3 %collective-permute-start.8 = (bf16[512,256]{1,0:T(8,128)(2,1)S(1)}, bf16[512,256]{1,0:T(8,128)(2,1)S(1)}, u32[]{:S(2)}, u32[]{:S(2)}) collective-permute-start(bf16[512,256]{1,0:T(8,128)(2,1)S(1)} %forward_rows.7), channel_id=1, source_target_pairs={{0,1},{3,2},{4,5},{7,6},{8,9},{11,10},{12,13},{15,14},{16,17},{19,... | collective-permute-start | bytes 786440 | tf_op jit(solution)/shard_map/ppermute | solution.py:294
  24.1 15.7 %collective-permute-start.7 = (bf16[512,256]{1,0:T(8,128)(2,1)S(1)}, bf16[512,256]{1,0:T(8,128)(2,1)S(1)}, u32[]{:S(2)}, u32[]{:S(2)}) collective-permute-start(bf16[512,256]{1,0:T(8,128)(2,1)S(1)} %forward_rows.7), channel_id=1, source_target_pairs={{1,2},{2,1},{5,6},{6,5},{9,10},{10,9},{13,14},{14,13},{17,18},{18,... | collective-permute-start | bytes 786440 | tf_op jit(solution)/shard_map/ppermute | solution.py:295
  26.8 13.0 %collective-permute-start.10 = (bf16[512,256]{1,0:T(8,128)(2,1)S(1)}, bf16[512,256]{1,0:T(8,128)(2,1)S(1)}, u32[]{:S(2)}, u32[]{:S(2)}) collective-permute-start(bf16[512,256]{1,0:T(8,128)(2,1)S(1)} %forward_rows.9), channel_id=1, source_target_pairs={{0,1},{1,0},{2,3},{3,2},{4,5},{5,4},{6,7},{7,6},{8,9},{9,8},{10,11... | collective-permute-start | bytes 786440 | tf_op jit(solution)/shard_map/ppermute | solution.py:264
  30.8 14.5 %copy-start = (bf16[512,256]{1,0:T(8,128)(2,1)S(1)}, bf16[512,256]{1,0:T(8,128)(2,1)}, u32[]{:S(2)}) copy-start(bf16[512,256]{1,0:T(8,128)(2,1)} %refs_5_.1) | copy-start | bytes 786436
  30.8 14.5 %copy-start.1 = (bf16[256,256]{1,0:T(8,128)(2,1)S(1)}, bf16[256,256]{1,0:T(8,128)(2,1)}, u32[]{:S(2)}) copy-start(bf16[256,256]{1,0:T(8,128)(2,1)} %refs_4_.1) | copy-start | bytes 393220
  30.9 14.4 %collective-permute-start.9 = (bf16[512,256]{1,0:T(8,128)(2,1)S(1)}, bf16[512,256]{1,0:T(8,128)(2,1)S(1)}, u32[]{:S(2)}, u32[]{:S(2)}) collective-permute-start(bf16[512,256]{1,0:T(8,128)(2,1)S(1)} %add_convert_fusion), channel_id=1, source_target_pairs={{0,2},{1,3},{2,0},{3,1},{4,6},{5,7},{6,4},{7,5},{8,10},{9,11},{10,... | collective-permute-start | bytes 786440 | tf_op jit(solution)/shard_map/ppermute | solution.py:264
  46.4 2.1 %collective-permute-start.11 = (f32[256,256]{1,0:T(8,128)S(1)}, f32[256,256]{1,0:T(8,128)S(1)}, u32[]{:S(2)}, u32[]{:S(2)}) collective-permute-start(f32[256,256]{1,0:T(8,128)S(1)} %get-tuple-element.25), channel_id=1, source_target_pairs={{0,4},{4,0},{8,12},{12,8},{16,20},{20,16},{24,28},{28,24},{1,5},{5... | collective-permute-start | bytes 786440 | tf_op jit(solution)/shard_map/ppermute | solution.py:264
  46.4 13.3 %collective-permute-start.16 = (bf16[256,512]{1,0:T(8,128)(2,1)S(1)}, bf16[256,512]{1,0:T(8,128)(2,1)S(1)}, u32[]{:S(2)}, u32[]{:S(2)}) collective-permute-start(bf16[256,512]{1,0:T(8,128)(2,1)S(1)} %get-tuple-element.26.refs_0_), channel_id=1, source_target_pairs={{0,1},{1,0},{2,3},{3,2},{4,5},{5,4},{6,7},{7,6},{8,9},{9,8},{10,11... | collective-permute-start | bytes 786440 | tf_op jit(solution)/shard_map/ppermute | solution.py:264
  46.4 15.3 %collective-permute-start.13 = (bf16[256,512]{1,0:T(8,128)(2,1)S(1)}, bf16[256,512]{1,0:T(8,128)(2,1)S(1)}, u32[]{:S(2)}, u32[]{:S(2)}) collective-permute-start(bf16[256,512]{1,0:T(8,128)(2,1)S(1)} %get-tuple-element.26.refs_0_), channel_id=1, source_target_pairs={{0,2},{1,3},{2,0},{3,1},{4,6},{5,7},{6,4},{7,5},{8,10},{9,11},{10,... | collective-permute-start | bytes 786440 | tf_op jit(solution)/shard_map/ppermute | solution.py:264
  61.7 6.0 %collective-permute-start.14 = (bf16[256,512]{1,0:T(8,128)(2,1)S(1)}, bf16[256,512]{1,0:T(8,128)(2,1)S(1)}, u32[]{:S(2)}, u32[]{:S(2)}) collective-permute-start(bf16[256,512]{1,0:T(8,128)(2,1)S(1)} %get-tuple-element.27.refs_3_), channel_id=1, source_target_pairs={{1,2},{2,1},{5,6},{6,5},{9,10},{10,9},{13,14},{14,13},{17,18},{18,... | collective-permute-start | bytes 786440 | tf_op jit(solution)/shard_map/ppermute | solution.py:311
  62.4 9.8 %collective-permute-start.15 = (bf16[256,512]{1,0:T(8,128)(2,1)S(1)}, bf16[256,512]{1,0:T(8,128)(2,1)S(1)}, u32[]{:S(2)}, u32[]{:S(2)}) collective-permute-start(bf16[256,512]{1,0:T(8,128)(2,1)S(1)} %get-tuple-element.28.refs_5_), channel_id=1, source_target_pairs={{1,0},{2,3},{5,4},{6,7},{9,8},{10,11},{13,12},{14,15},{17,16},{18,... | collective-permute-start | bytes 786440 | tf_op jit(solution)/shard_map/ppermute | solution.py:312
  73.5 2.7 %collective-permute-start.18 = (bf16[4,256,512]{2,1,0:T(8,128)(2,1)S(1)}, bf16[4,256,512]{2,1,0:T(8,128)(2,1)S(1)}, u32[]{:S(2)}, u32[]{:S(2)}) collective-permute-start(bf16[4,256,512]{2,1,0:T(8,128)(2,1)S(1)} %backward_cols.5), channel_id=1, source_target_pairs={{0,4},{4,0},{8,12},{12,8},{16,20},{20,16},{24,28},{28,24},{1,5},{5... | collective-permute-start | bytes 3145736 | tf_op jit(solution)/shard_map/ppermute | solution.py:264
  73.6 6.6 %collective-permute-start.12 = (bf16[256,256]{1,0:T(8,128)(2,1)S(1)}, bf16[256,256]{1,0:T(8,128)(2,1)S(1)}, u32[]{:S(2)}, u32[]{:S(2)}) collective-permute-start(bf16[256,256]{1,0:T(8,128)(2,1)S(1)} %total.3.refs_2_.refs_0_.refs_3_), channel_id=1, source_target_pairs={{0,1},{1,0},{2,3},{3,2},{4,5},{5,4},{6,7},{7,6},{8,9},{9,8},{10,11... | collective-permute-start | bytes 393224 | tf_op jit(solution)/shard_map/ppermute | solution.py:264
  76.6 12.8 %collective-permute-start.21 = (bf16[256,512]{1,0:T(8,128)(2,1)S(1)}, bf16[256,512]{1,0:T(8,128)(2,1)S(1)}, u32[]{:S(2)}, u32[]{:S(2)}) collective-permute-start(bf16[256,512]{1,0:T(8,128)(2,1)S(1)} %get-tuple-element.29), channel_id=1, source_target_pairs={{0,24},{4,28},{8,16},{12,20},{16,8},{20,12},{24,0},{28,4},{1,25},{... | collective-permute-start | bytes 786440 | tf_op jit(solution)/shard_map/ppermute | solution.py:264
  79.0 12.5 %collective-permute-start.20 = (bf16[256,512]{1,0:T(8,128)(2,1)S(1)}, bf16[256,512]{1,0:T(8,128)(2,1)S(1)}, u32[]{:S(2)}, u32[]{:S(2)}) collective-permute-start(bf16[256,512]{1,0:T(8,128)(2,1)S(1)} %get-tuple-element.30), channel_id=1, source_target_pairs={{0,16},{4,20},{8,24},{12,28},{16,0},{20,4},{24,8},{28,12},{1,17},{... | collective-permute-start | bytes 786440 | tf_op jit(solution)/shard_map/ppermute | solution.py:264
  79.6 11.9 %collective-permute-start.19 = (bf16[256,512]{1,0:T(8,128)(2,1)S(1)}, bf16[256,512]{1,0:T(8,128)(2,1)S(1)}, u32[]{:S(2)}, u32[]{:S(2)}) collective-permute-start(bf16[256,512]{1,0:T(8,128)(2,1)S(1)} %get-tuple-element.31), channel_id=1, source_target_pairs={{0,8},{4,12},{8,0},{12,4},{16,24},{20,28},{24,16},{28,20},{1,9},{5... | collective-permute-start | bytes 786440 | tf_op jit(solution)/shard_map/ppermute | solution.py:264
  80.2 8.5 %collective-permute-start.17 = (bf16[256,256]{1,0:T(8,128)(2,1)S(1)}, bf16[256,256]{1,0:T(8,128)(2,1)S(1)}, u32[]{:S(2)}, u32[]{:S(2)}) collective-permute-start(bf16[256,256]{1,0:T(8,128)(2,1)S(1)} %total.4.refs_0_), channel_id=1, source_target_pairs={{0,2},{1,3},{2,0},{3,1},{4,6},{5,7},{6,4},{7,5},{8,10},{9,11},{10,... | collective-permute-start | bytes 393224 | tf_op jit(solution)/shard_map/ppermute | solution.py:264

commit v13 on v12

--- a/solution.py
+++ b/solution.py
@@ -205,6 +205,28 @@
     )(where, *operands, *after)
 
 
+def meet_kernel(where, kept_ref, came_ref, own_ref, corner_ref, first_ref, second_ref):
+    core = where[0] & 1
+    own_ref[...] = kept_ref[0] + came_ref[0].astype(jnp.float32)
+    corner_ref[...] = (kept_ref[3] + came_ref[3].astype(jnp.float32)).astype(corner_ref.dtype)
+    first_ref[...] = (kept_ref[1 + core] + came_ref[1 + core].astype(jnp.float32)).astype(first_ref.dtype)
+    second_ref[...] = kept_ref[2 - core] + came_ref[2 - core].astype(jnp.float32)
+
+
+def meet(where, kept, came):
+    shape = kept.shape[1:]
+    kinds = [jnp.float32, came.dtype, came.dtype, jnp.float32]
+    return pl.pallas_call(
+        meet_kernel,
+        out_shape=[pltpu.VMEM(shape, kind) for kind in kinds],
+        in_specs=[SCALARS, WHOLE, WHOLE],
+        out_specs=[WHOLE] * 4,
+        compiler_params=params(10),
+        cost_estimate=cost(0, 0),
+        name="meet",
+    )(where, near(kept), near(came))
+
+
 def finish_kernel(*refs):
     parts, out_ref = refs[:-1], refs[-1]
     value = parts[0][...].astype(jnp.float32)
@@ -321,9 +343,16 @@
     sent = last(every[1::2], depth, sums, jnp.bfloat16, [part])
     kept = last(every[::2], depth, sums, jnp.float32)
     came = swap(sent, "row", n_row, 1)
-    own, *summed = [kept[c] + came[c].astype(jnp.float32) for c in range(chips)]
-    summed = [value.astype(jnp.bfloat16) for value in summed]
-    parts = [swap(summed[c - 1], "row", n_row, 2 * c) for c in range(1, chips)]
+    if chips == 4:
+        own, corner, first, second = meet(where, kept, came)
+        there = [(i, i ^ (2 if i % 2 == 0 else 4)) for i in range(n_row)]
+        across = [(i, i ^ (4 if i % 2 == 0 else 2)) for i in range(n_row)]
+        corner = lax.ppermute(corner, "row", there)
+        second = (second + corner.astype(jnp.float32)).astype(jnp.bfloat16)
+        parts = [lax.ppermute(first, "row", there), lax.ppermute(second, "row", across)]
+    else:
+        own, *summed = [kept[c] + came[c].astype(jnp.float32) for c in range(chips)]
+        parts = [swap(summed[c - 1].astype(jnp.bfloat16), "row", n_row, 2 * c) for c in range(1, chips)]
 
     feature_grad = finish([own, *parts])
     for s in range(n_col.bit_length() - 2):

time: 92.7 us -> 94.1 us (1.015)
  waiting for transfers between devices: 32.6 us -> 34.5 us
    ppermute x0 -> x3, waiting for transfers between devices: none -> 4.35 us  [the longest x1 4.34 us: shards(): corner = lax.ppermute(corner, 'row', there)]
    ppermute x18 -> x15, starting transfers between devices: 17.1 us -> 13.1 us  [swap(): return lax.ppermute(value, axis, [(i, i ^ step) for i in range(size)])]
    ppermute x0 -> x3, starting transfers between devices: none -> 3.57 us  [the longest x1 1.55 us: shards(): corner = lax.ppermute(corner, 'row', there)]
    ppermute x18 -> x15, waiting for transfers between devices: 28.1 us -> 25.7 us  [swap(): return lax.ppermute(value, axis, [(i, i ^ step) for i in range(size)])]
  transfers between devices with their start and end apart: 22 -> 22, of which waited for: 11 -> 11; matrix products, arithmetic and copies ran while one was open for 1% -> 0% of each run, Pallas kernels for 22% -> 21%
where the time goes in v13:
time: 94.1 us; the launch traced here: 93.8 us
  waiting for transfers between devices  34.5 us (37%)
  Pallas kernels  25.1 us (27%)
  starting transfers between devices  23 us (24%)
  blocking collectives  10 us (11%)
    ppermute x15, waiting for transfers between devices, swap(): return lax.ppermute(value, axis, [(i, i ^ step) for i in range(size)])  25.7 us
    ppermute x15, starting transfers between devices, swap(): return lax.ppermute(value, axis, [(i, i ^ step) for i in range(size)])  13.1 us
    all_gather x1, blocking collectives, shards(): gathered = lax.all_gather(part, 'row', axis_index_groups=cores, tiled=True)  10 us
    pallas_call x5, Pallas kernels, forward(): pl.pallas_call(functools.partial(forward_kernel, steps=steps, before=bool...  7.94 us
    pallas_call x1, Pallas kernels, dense_rows(): pl.pallas_call(functools.partial(dense_kernel, steps=steps, window=window...  7.19 us
    pallas_call x3, Pallas kernels, backward(): pl.pallas_call(functools.partial(backward_kernel, count=count, steps=step...  6.55 us
    ppermute x1, waiting for transfers between devices, shards(): pieces[3] = beside + lax.ppermute(pieces[2], 'col', [(1, 0), (2, 3)])  4.48 us
    ppermute x1, waiting for transfers between devices, shards(): corner = lax.ppermute(corner, 'row', there)  4.34 us
  transfers between devices with their start and end apart: 22, of which 11 were waited for; matrix products, arithmetic and copies ran while one was open for 0% of the time, Pallas kernels for 21%

profile of v13, /device:TPU:0, one launch (start us, length us, event | category | flops | bytes accessed | tf_op | source)
XLA Modules:
  0.0 93.8 jit_solution(15328179820198055902)
XLA Ops:
  0.6 4.0 %collective-permute-start.1 = (bf16[512,256]{1,0:T(8,128)(2,1)}, bf16[512,256]{1,0:T(8,128)(2,1)S(1)}, u32[]{:S(2)}, u32[]{:S(2)}) collective-permute-start(bf16[512,256]{1,0:T(8,128)(2,1)} %features_ref.1), channel_id=1, source_target_pairs={{0,24},{4,28},{8,16},{12,20},{16,8},{20,12},{24,0},{28,4},{1,25},{... | collective-permute-start | bytes 786440 | tf_op jit(solution)/shard_map/ppermute | solution.py:286
  5.3 7.2 %dense_rows.1 = (bf16[512,4096]{1,0:T(8,128)(2,1)S(1)}, bf16[512,4096]{1,0:T(8,128)(2,1)S(1)}, bf16[512,4096]{1,0:T(8,128)(2,1)S(1)}, bf16[512,4096]{1,0:T(8,128)(2,1)S(1)}, bf16[512,256]{1,0:T(8,128)(2,1)S(1)}) custom-call(s32[2]{0:T(128)S(1)} %pad_add_fusion.where, s32[16]{0:T(128)} %bitcast.7, s32[448]{0:T(512)} %bitcast.6, ...), custom_call_target="tpu_custom_call" | custom-call | bytes 41943040 | tf_op jit(solution)/shard_map/dense_rows/pallas_call | solution.py:102
  12.5 4.5 %collective-permute-done.3.refs_2_ = bf16[512,256]{1,0:T(8,128)(2,1)S(1)} collective-permute-done((bf16[512,256]{1,0:T(8,128)(2,1)}, bf16[512,256]{1,0:T(8,128)(2,1)S(1)}, u32[]{:S(2)}, u32[]{:S(2)}) %collective-permute-start.3) | collective-permute-done | bytes 262176 | tf_op jit(solution)/shard_map/ppermute | solution.py:286
  17.6 1.2 %forward_rows.6.refs_4_ = f32[512,256]{1,0:T(8,128)S(1)} custom-call(s32[2]{0:T(128)S(1)} %pad_add_fusion.where, bf16[512,4096]{1,0:T(8,128)(2,1)S(1)} %get-tuple-element.22.refs_3_.a_ref.refs_0_, bf16[512,256]{1,0:T(8,128)(2,1)S(1)} %get-tuple-element.21.refs_0_, bf16[512,256]{1,0:T(8,128)(2,1)S(1)} %get-tuple-element.25.refs_2_.refs_1_, ...), custom_call_target="tpu_custom_call" | custom-call | flops 1073741824 | bytes 4194304 | tf_op jit(solution)/shard_map/forward_rows/pallas_call | solution.py:133
  19.3 1.3 %forward_rows.7 = bf16[512,256]{1,0:T(8,128)(2,1)S(1)} custom-call(s32[2]{0:T(128)S(1)} %pad_add_fusion.where, bf16[512,4096]{1,0:T(8,128)(2,1)S(1)} %get-tuple-element.22.refs_3_.a_ref.refs_0_, bf16[512,256]{1,0:T(8,128)(2,1)S(1)} %collective-permute-done.refs_1_.refs_0_, bf16[512,256]{1,0:T(8,128)(2,1)S(1)} %collective-permute-done.4.refs_3_.refs_1_, ...), custom_call_target="tpu_custom_call" | custom-call | flops 1073741824 | bytes 4194304 | tf_op jit(solution)/shard_map/forward_rows/pallas_call | solution.py:133
  20.6 3.5 %collective-permute-start.8 = (bf16[512,256]{1,0:T(8,128)(2,1)S(1)}, bf16[512,256]{1,0:T(8,128)(2,1)S(1)}, u32[]{:S(2)}, u32[]{:S(2)}) collective-permute-start(bf16[512,256]{1,0:T(8,128)(2,1)S(1)} %forward_rows.7), channel_id=1, source_target_pairs={{0,1},{3,2},{4,5},{7,6},{8,9},{11,10},{12,13},{15,14},{16,17},{19,... | collective-permute-start | bytes 786440 | tf_op jit(solution)/shard_map/ppermute | solution.py:316
  24.1 0.9 collective-permute-start.7
  25.0 1.8 %forward_rows.9 = bf16[512,256]{1,0:T(8,128)(2,1)S(1)} custom-call(s32[2]{0:T(128)S(1)} %pad_add_fusion.where, bf16[512,4096]{1,0:T(8,128)(2,1)S(1)} %get-tuple-element.24.refs_5_.a_ref.refs_1_, bf16[512,256]{1,0:T(8,128)(2,1)S(1)} %get-tuple-element.21.refs_0_, bf16[512,256]{1,0:T(8,128)(2,1)S(1)} %collective-permute-done.refs_1_.refs_0_, ...), custom_call_target="tpu_custom_call" | custom-call | flops 1073741824 | bytes 4194304 | tf_op jit(solution)/shard_map/forward_rows/pallas_call | solution.py:133
  26.8 2.2 %collective-permute-start.10 = (bf16[512,256]{1,0:T(8,128)(2,1)S(1)}, bf16[512,256]{1,0:T(8,128)(2,1)S(1)}, u32[]{:S(2)}, u32[]{:S(2)}) collective-permute-start(bf16[512,256]{1,0:T(8,128)(2,1)S(1)} %forward_rows.9), channel_id=1, source_target_pairs={{0,1},{1,0},{2,3},{3,2},{4,5},{5,4},{6,7},{7,6},{8,9},{9,8},{10,11... | collective-permute-start | bytes 786440 | tf_op jit(solution)/shard_map/ppermute | solution.py:286
  29.0 1.8 %forward_rows.8 = bf16[512,256]{1,0:T(8,128)(2,1)S(1)} custom-call(s32[2]{0:T(128)S(1)} %pad_add_fusion.where, bf16[512,4096]{1,0:T(8,128)(2,1)S(1)} %get-tuple-element.23.refs_4_.a_ref.refs_2_, bf16[512,256]{1,0:T(8,128)(2,1)S(1)} %get-tuple-element.21.refs_0_, bf16[512,256]{1,0:T(8,128)(2,1)S(1)} %collective-permute-done.refs_1_.refs_0_, ...), custom_call_target="tpu_custom_call" | custom-call | flops 1073741824 | bytes 4194304 | tf_op jit(solution)/shard_map/forward_rows/pallas_call | solution.py:133
  30.9 3.4 %collective-permute-start.9 = (bf16[512,256]{1,0:T(8,128)(2,1)S(1)}, bf16[512,256]{1,0:T(8,128)(2,1)S(1)}, u32[]{:S(2)}, u32[]{:S(2)}) collective-permute-start(bf16[512,256]{1,0:T(8,128)(2,1)S(1)} %add_convert_fusion.1), channel_id=1, source_target_pairs={{0,2},{1,3},{2,0},{3,1},{4,6},{5,7},{6,4},{7,5},{8,10},{9,11},{10,... | collective-permute-start | bytes 786440 | tf_op jit(solution)/shard_map/ppermute | solution.py:286
  34.4 1.8 %forward_rows.5.refs_0_ = f32[512,256]{1,0:T(8,128)S(1)} custom-call(s32[2]{0:T(128)S(1)} %pad_add_fusion.where, bf16[512,4096]{1,0:T(8,128)(2,1)S(1)} %get-tuple-element.20.refs_6_.a_ref.refs_0_, bf16[512,256]{1,0:T(8,128)(2,1)S(1)} %get-tuple-element.21.refs_0_, bf16[512,256]{1,0:T(8,128)(2,1)S(1)} %collective-permute-done.refs_1_.refs_0_, ...), custom_call_target="tpu_custom_call" | custom-call | flops 1073741824 | bytes 4194304 | tf_op jit(solution)/shard_map/forward_rows/pallas_call | solution.py:133
  36.2 3.6 %collective-permute-done.10.refs_3_ = bf16[512,256]{1,0:T(8,128)(2,1)S(1)} collective-permute-done((bf16[512,256]{1,0:T(8,128)(2,1)S(1)}, bf16[512,256]{1,0:T(8,128)(2,1)S(1)}, u32[]{:S(2)}, u32[]{:S(2)}) %collective-permute-start.10) | collective-permute-done | bytes 262176 | tf_op jit(solution)/shard_map/ppermute | solution.py:286
  39.8 5.6 %collective-permute-done.9.refs_2_ = bf16[512,256]{1,0:T(8,128)(2,1)S(1)} collective-permute-done((bf16[512,256]{1,0:T(8,128)(2,1)S(1)}, bf16[512,256]{1,0:T(8,128)(2,1)S(1)}, u32[]{:S(2)}, u32[]{:S(2)}) %collective-permute-start.9) | collective-permute-done | bytes 262176 | tf_op jit(solution)/shard_map/ppermute | solution.py:286
  45.3 1.1 %middle.1 = (bf16[512,256]{1,0:T(8,128)(2,1)}, bf16[256,512]{1,0:T(8,128)(2,1)S(1)}, f32[256,256]{1,0:T(8,128)S(1)}) custom-call(f32[512,256]{1,0:T(8,128)S(1)} %forward_rows.5.refs_0_, bf16[512,256]{1,0:T(8,128)(2,1)S(1)} %collective-permute-done.7.refs_1_, bf16[512,256]{1,0:T(8,128)(2,1)S(1)} %collective-permute-done.9.refs_2_, ...), custom_call_target="tpu_custom_call" | custom-call | flops 201326592 | bytes 1310720 | tf_op jit(solution)/shard_map/middle/pallas_call | solution.py:166
  46.4 2.1 %collective-permute-start.13 = (bf16[256,512]{1,0:T(8,128)(2,1)S(1)}, bf16[256,512]{1,0:T(8,128)(2,1)S(1)}, u32[]{:S(2)}, u32[]{:S(2)}) collective-permute-start(bf16[256,512]{1,0:T(8,128)(2,1)S(1)} %get-tuple-element.30.refs_0_), channel_id=1, source_target_pairs={{0,2},{1,3},{2,0},{3,1},{4,6},{5,7},{6,4},{7,5},{8,10},{9,11},{10,... | collective-permute-start | bytes 786440 | tf_op jit(solution)/shard_map/ppermute | solution.py:286
  48.6 10.0 %all_gather.3.refs_0_ = bf16[1024,256]{1,0:T(8,128)(2,1)S(1)} all-gather(bf16[256,256]{1,0:T(8,128)(2,1)S(1)} %add_convert_fusion.2), channel_id=1, replica_groups={{0,8,16,24},{4,12,20,28},{1,9,17,25},{5,13,21,29},{2,10,18,26},{6,14,22..., dimensions={0}, use_global_device_ids=true | all-gather | bytes 655360 | tf_op jit(solution)/shard_map/all_gather | solution.py:328
  58.7 1.0 %collective-permute-done.16.refs_4_ = bf16[256,512]{1,0:T(8,128)(2,1)S(1)} collective-permute-done((bf16[256,512]{1,0:T(8,128)(2,1)S(1)}, bf16[256,512]{1,0:T(8,128)(2,1)S(1)}, u32[]{:S(2)}, u32[]{:S(2)}) %collective-permute-start.16) | collective-permute-done | bytes 262176 | tf_op jit(solution)/shard_map/ppermute | solution.py:286
  59.7 2.0 %collective-permute-done.13.refs_1_ = bf16[256,512]{1,0:T(8,128)(2,1)S(1)} collective-permute-done((bf16[256,512]{1,0:T(8,128)(2,1)S(1)}, bf16[256,512]{1,0:T(8,128)(2,1)S(1)}, u32[]{:S(2)}, u32[]{:S(2)}) %collective-permute-start.13) | collective-permute-done | bytes 262176 | tf_op jit(solution)/shard_map/ppermute | solution.py:286
  62.4 1.3 %collective-permute-start.15 = (bf16[256,512]{1,0:T(8,128)(2,1)S(1)}, bf16[256,512]{1,0:T(8,128)(2,1)S(1)}, u32[]{:S(2)}, u32[]{:S(2)}) collective-permute-start(bf16[256,512]{1,0:T(8,128)(2,1)S(1)} %get-tuple-element.32.refs_5_), channel_id=1, source_target_pairs={{1,0},{2,3},{5,4},{6,7},{9,8},{10,11},{13,12},{14,15},{17,16},{18,... | collective-permute-start | bytes 786440 | tf_op jit(solution)/shard_map/ppermute | solution.py:334
  63.7 4.0 %backward_cols.3.refs_2_ = f32[8,256,512]{2,1,0:T(8,128)S(1)} custom-call(s32[2]{0:T(128)S(1)} %pad_add_fusion.where, bf16[512,4096]{1,0:T(8,128)(2,1)S(1)} %get-tuple-element.20.refs_6_.a_ref.refs_0_, bf16[512,4096]{1,0:T(8,128)(2,1)S(1)} %get-tuple-element.24.refs_5_.a_ref.refs_1_, bf16[512,4096]{1,0:T(8,128)(2,1)S(1)} %get-tuple-element.23.refs_4_.a_ref.refs_2_, ...), custom_call_target="tpu_custom_call" | custom-call | tf_op jit(solution)/shard_map/backward_cols/pallas_call | solution.py:197
  67.7 4.5 %collective-permute-done.15 = bf16[256,512]{1,0:T(8,128)(2,1)S(1)} collective-permute-done((bf16[256,512]{1,0:T(8,128)(2,1)S(1)}, bf16[256,512]{1,0:T(8,128)(2,1)S(1)}, u32[]{:S(2)}, u32[]{:S(2)}) %collective-permute-start.15) | collective-permute-done | bytes 262176 | tf_op jit(solution)/shard_map/ppermute | solution.py:334
  72.3 1.3 %backward_cols.5 = bf16[4,256,512]{2,1,0:T(8,128)(2,1)S(1)} custom-call(s32[2]{0:T(128)S(1)} %pad_add_fusion.where, bf16[512,4096]{1,0:T(8,128)(2,1)S(1)} %get-tuple-element.22.refs_3_.a_ref.refs_0_, bf16[256,512]{1,0:T(8,128)(2,1)S(1)} %add.14.refs_1_, f32[8,256,512]{2,1,0:T(8,128)S(1)} %backward_cols.3.refs_2_, ...), custom_call_target="tpu_custom_call" | custom-call | tf_op jit(solution)/shard_map/backward_cols/pallas_call | solution.py:197
  73.6 1.3 %backward_cols.4.refs_2_.kept_ref = f32[4,256,512]{2,1,0:T(8,128)S(1)} custom-call(s32[2]{0:T(128)S(1)} %pad_add_fusion.where, bf16[512,4096]{1,0:T(8,128)(2,1)S(1)} %get-tuple-element.22.refs_3_.a_ref.refs_0_, bf16[256,512]{1,0:T(8,128)(2,1)S(1)} %add.14.refs_1_, f32[8,256,512]{2,1,0:T(8,128)S(1)} %backward_cols.3.refs_2_), custom_call_target="tpu_custom_call" | custom-call | tf_op jit(solution)/shard_map/backward_cols/pallas_call | solution.py:197
  74.9 1.4 %collective-permute-done.18.came_ref = bf16[4,256,512]{2,1,0:T(8,128)(2,1)S(1)} collective-permute-done((bf16[4,256,512]{2,1,0:T(8,128)(2,1)S(1)}, bf16[4,256,512]{2,1,0:T(8,128)(2,1)S(1)}, u32[]{:S(2)}, u32[]{:S(2)}) %collective-permute-start.18) | collective-permute-done | bytes 1048608 | tf_op jit(solution)/shard_map/ppermute | solution.py:286
  76.3 0.7 meet.1
  77.0 1.6 %collective-permute-start.20 = (bf16[256,512]{1,0:T(8,128)(2,1)S(1)}, bf16[256,512]{1,0:T(8,128)(2,1)S(1)}, u32[]{:S(2)}, u32[]{:S(2)}) collective-permute-start(bf16[256,512]{1,0:T(8,128)(2,1)S(1)} %get-tuple-element.36), channel_id=1, source_target_pairs={{0,8},{4,20},{8,0},{12,28},{16,24},{20,4},{24,16},{28,12},{1,9},{5... | collective-permute-start | bytes 786440 | tf_op jit(solution)/shard_map/ppermute | solution.py:350
  79.1 4.3 %collective-permute-done.20 = bf16[256,512]{1,0:T(8,128)(2,1)S(1)} collective-permute-done((bf16[256,512]{1,0:T(8,128)(2,1)S(1)}, bf16[256,512]{1,0:T(8,128)(2,1)S(1)}, u32[]{:S(2)}, u32[]{:S(2)}) %collective-permute-start.20) | collective-permute-done | bytes 262176 | tf_op jit(solution)/shard_map/ppermute | solution.py:350
  83.5 1.5 %collective-permute-start.21 = (bf16[256,512]{1,0:T(8,128)(2,1)S(1)}, bf16[256,512]{1,0:T(8,128)(2,1)S(1)}, u32[]{:S(2)}, u32[]{:S(2)}) collective-permute-start(bf16[256,512]{1,0:T(8,128)(2,1)S(1)} %add_convert_fusion), channel_id=1, source_target_pairs={{0,16},{4,12},{8,24},{12,4},{16,0},{20,28},{24,8},{28,20},{1,17},{... | collective-permute-start | bytes 786440 | tf_op jit(solution)/shard_map/ppermute | solution.py:352
  85.1 7.2 %collective-permute-done.17.refs_1_ = bf16[256,256]{1,0:T(8,128)(2,1)S(1)} collective-permute-done((bf16[256,256]{1,0:T(8,128)(2,1)S(1)}, bf16[256,256]{1,0:T(8,128)(2,1)S(1)}, u32[]{:S(2)}, u32[]{:S(2)}) %collective-permute-start.17) | collective-permute-done | bytes 131104 | tf_op jit(solution)/shard_map/ppermute | solution.py:286
  92.3 0.7 total.5
  93.0 0.8 finish.1
  (39 shorter events, 3.5 us)
Async XLA Ops:
  0.6 11.9 %collective-permute-start.1 = (bf16[512,256]{1,0:T(8,128)(2,1)}, bf16[512,256]{1,0:T(8,128)(2,1)S(1)}, u32[]{:S(2)}, u32[]{:S(2)}) collective-permute-start(bf16[512,256]{1,0:T(8,128)(2,1)} %features_ref.1), channel_id=1, source_target_pairs={{0,24},{4,28},{8,16},{12,20},{16,8},{20,12},{24,0},{28,4},{1,25},{... | collective-permute-start | bytes 786440 | tf_op jit(solution)/shard_map/ppermute | solution.py:286
  4.6 12.4 %collective-permute-start.3 = (bf16[512,256]{1,0:T(8,128)(2,1)}, bf16[512,256]{1,0:T(8,128)(2,1)S(1)}, u32[]{:S(2)}, u32[]{:S(2)}) collective-permute-start(bf16[512,256]{1,0:T(8,128)(2,1)} %features_ref.1), channel_id=1, source_target_pairs={{0,8},{4,12},{8,0},{12,4},{16,24},{20,28},{24,16},{28,20},{1,9},{5... | collective-permute-start | bytes 786440 | tf_op jit(solution)/shard_map/ppermute | solution.py:286
  5.1 11.9 %collective-permute-start.2 = (bf16[512,256]{1,0:T(8,128)(2,1)}, bf16[512,256]{1,0:T(8,128)(2,1)S(1)}, u32[]{:S(2)}, u32[]{:S(2)}) collective-permute-start(bf16[512,256]{1,0:T(8,128)(2,1)} %features_ref.1), channel_id=1, source_target_pairs={{0,16},{4,20},{8,24},{12,28},{16,0},{20,4},{24,8},{28,12},{1,17},{... | collective-permute-start | bytes 786440 | tf_op jit(solution)/shard_map/ppermute | solution.py:286
  5.2 13.6 %collective-permute-start = (bf16[512,256]{1,0:T(8,128)(2,1)}, bf16[512,256]{1,0:T(8,128)(2,1)S(1)}, u32[]{:S(2)}, u32[]{:S(2)}) collective-permute-start(bf16[512,256]{1,0:T(8,128)(2,1)} %features_ref.1), channel_id=1, source_target_pairs={{0,4},{4,0},{8,12},{12,8},{16,20},{20,16},{24,28},{28,24},{1,5},{5... | collective-permute-start | bytes 786440 | tf_op jit(solution)/shard_map/ppermute | solution.py:286
  17.0 1.8 %collective-permute-start.4 = (bf16[512,256]{1,0:T(8,128)(2,1)S(1)}, bf16[512,256]{1,0:T(8,128)(2,1)S(1)}, u32[]{:S(2)}, u32[]{:S(2)}) collective-permute-start(bf16[512,256]{1,0:T(8,128)(2,1)S(1)} %get-tuple-element.25.refs_2_.refs_1_), channel_id=1, source_target_pairs={{0,4},{4,0},{8,12},{12,8},{16,20},{20,16},{24,28},{28,24},{1,5},{5... | collective-permute-start | bytes 786440 | tf_op jit(solution)/shard_map/ppermute | solution.py:286
  17.0 1.9 %collective-permute-start.5 = (bf16[512,256]{1,0:T(8,128)(2,1)S(1)}, bf16[512,256]{1,0:T(8,128)(2,1)S(1)}, u32[]{:S(2)}, u32[]{:S(2)}) collective-permute-start(bf16[512,256]{1,0:T(8,128)(2,1)S(1)} %get-tuple-element.26.refs_4_.refs_2_), channel_id=1, source_target_pairs={{0,4},{4,0},{8,12},{12,8},{16,20},{20,16},{24,28},{28,24},{1,5},{5... | collective-permute-start | bytes 786440 | tf_op jit(solution)/shard_map/ppermute | solution.py:286
  17.5 1.8 %collective-permute-start.6 = (bf16[512,256]{1,0:T(8,128)(2,1)S(1)}, bf16[512,256]{1,0:T(8,128)(2,1)S(1)}, u32[]{:S(2)}, u32[]{:S(2)}) collective-permute-start(bf16[512,256]{1,0:T(8,128)(2,1)S(1)} %get-tuple-element.27.refs_6_.refs_3_), channel_id=1, source_target_pairs={{0,4},{4,0},{8,12},{12,8},{16,20},{20,16},{24,28},{28,24},{1,5},{5... | collective-permute-start | bytes 786440 | tf_op jit(solution)/shard_map/ppermute | solution.py:286
  20.6 10.3 %collective-permute-start.8 = (bf16[512,256]{1,0:T(8,128)(2,1)S(1)}, bf16[512,256]{1,0:T(8,128)(2,1)S(1)}, u32[]{:S(2)}, u32[]{:S(2)}) collective-permute-start(bf16[512,256]{1,0:T(8,128)(2,1)S(1)} %forward_rows.7), channel_id=1, source_target_pairs={{0,1},{3,2},{4,5},{7,6},{8,9},{11,10},{12,13},{15,14},{16,17},{19,... | collective-permute-start | bytes 786440 | tf_op jit(solution)/shard_map/ppermute | solution.py:316
  24.1 15.7 %collective-permute-start.7 = (bf16[512,256]{1,0:T(8,128)(2,1)S(1)}, bf16[512,256]{1,0:T(8,128)(2,1)S(1)}, u32[]{:S(2)}, u32[]{:S(2)}) collective-permute-start(bf16[512,256]{1,0:T(8,128)(2,1)S(1)} %forward_rows.7), channel_id=1, source_target_pairs={{1,2},{2,1},{5,6},{6,5},{9,10},{10,9},{13,14},{14,13},{17,18},{18,... | collective-permute-start | bytes 786440 | tf_op jit(solution)/shard_map/ppermute | solution.py:317
  26.8 13.0 %collective-permute-start.10 = (bf16[512,256]{1,0:T(8,128)(2,1)S(1)}, bf16[512,256]{1,0:T(8,128)(2,1)S(1)}, u32[]{:S(2)}, u32[]{:S(2)}) collective-permute-start(bf16[512,256]{1,0:T(8,128)(2,1)S(1)} %forward_rows.9), channel_id=1, source_target_pairs={{0,1},{1,0},{2,3},{3,2},{4,5},{5,4},{6,7},{7,6},{8,9},{9,8},{10,11... | collective-permute-start | bytes 786440 | tf_op jit(solution)/shard_map/ppermute | solution.py:286
  30.8 14.5 %copy-start = (bf16[512,256]{1,0:T(8,128)(2,1)S(1)}, bf16[512,256]{1,0:T(8,128)(2,1)}, u32[]{:S(2)}) copy-start(bf16[512,256]{1,0:T(8,128)(2,1)} %refs_5_.1) | copy-start | bytes 786436
  30.8 14.5 %copy-start.1 = (bf16[256,256]{1,0:T(8,128)(2,1)S(1)}, bf16[256,256]{1,0:T(8,128)(2,1)}, u32[]{:S(2)}) copy-start(bf16[256,256]{1,0:T(8,128)(2,1)} %refs_4_.1) | copy-start | bytes 393220
  30.9 14.4 %collective-permute-start.9 = (bf16[512,256]{1,0:T(8,128)(2,1)S(1)}, bf16[512,256]{1,0:T(8,128)(2,1)S(1)}, u32[]{:S(2)}, u32[]{:S(2)}) collective-permute-start(bf16[512,256]{1,0:T(8,128)(2,1)S(1)} %add_convert_fusion.1), channel_id=1, source_target_pairs={{0,2},{1,3},{2,0},{3,1},{4,6},{5,7},{6,4},{7,5},{8,10},{9,11},{10,... | collective-permute-start | bytes 786440 | tf_op jit(solution)/shard_map/ppermute | solution.py:286
  46.4 2.1 %collective-permute-start.11 = (f32[256,256]{1,0:T(8,128)S(1)}, f32[256,256]{1,0:T(8,128)S(1)}, u32[]{:S(2)}, u32[]{:S(2)}) collective-permute-start(f32[256,256]{1,0:T(8,128)S(1)} %get-tuple-element.29), channel_id=1, source_target_pairs={{0,4},{4,0},{8,12},{12,8},{16,20},{20,16},{24,28},{28,24},{1,5},{5... | collective-permute-start | bytes 786440 | tf_op jit(solution)/shard_map/ppermute | solution.py:286
  46.4 13.3 %collective-permute-start.16 = (bf16[256,512]{1,0:T(8,128)(2,1)S(1)}, bf16[256,512]{1,0:T(8,128)(2,1)S(1)}, u32[]{:S(2)}, u32[]{:S(2)}) collective-permute-start(bf16[256,512]{1,0:T(8,128)(2,1)S(1)} %get-tuple-element.30.refs_0_), channel_id=1, source_target_pairs={{0,1},{1,0},{2,3},{3,2},{4,5},{5,4},{6,7},{7,6},{8,9},{9,8},{10,11... | collective-permute-start | bytes 786440 | tf_op jit(solution)/shard_map/ppermute | solution.py:286
  46.4 15.3 %collective-permute-start.13 = (bf16[256,512]{1,0:T(8,128)(2,1)S(1)}, bf16[256,512]{1,0:T(8,128)(2,1)S(1)}, u32[]{:S(2)}, u32[]{:S(2)}) collective-permute-start(bf16[256,512]{1,0:T(8,128)(2,1)S(1)} %get-tuple-element.30.refs_0_), channel_id=1, source_target_pairs={{0,2},{1,3},{2,0},{3,1},{4,6},{5,7},{6,4},{7,5},{8,10},{9,11},{10,... | collective-permute-start | bytes 786440 | tf_op jit(solution)/shard_map/ppermute | solution.py:286
  61.7 6.0 %collective-permute-start.14 = (bf16[256,512]{1,0:T(8,128)(2,1)S(1)}, bf16[256,512]{1,0:T(8,128)(2,1)S(1)}, u32[]{:S(2)}, u32[]{:S(2)}) collective-permute-start(bf16[256,512]{1,0:T(8,128)(2,1)S(1)} %get-tuple-element.31.refs_3_), channel_id=1, source_target_pairs={{1,2},{2,1},{5,6},{6,5},{9,10},{10,9},{13,14},{14,13},{17,18},{18,... | collective-permute-start | bytes 786440 | tf_op jit(solution)/shard_map/ppermute | solution.py:333
  62.4 9.8 %collective-permute-start.15 = (bf16[256,512]{1,0:T(8,128)(2,1)S(1)}, bf16[256,512]{1,0:T(8,128)(2,1)S(1)}, u32[]{:S(2)}, u32[]{:S(2)}) collective-permute-start(bf16[256,512]{1,0:T(8,128)(2,1)S(1)} %get-tuple-element.32.refs_5_), channel_id=1, source_target_pairs={{1,0},{2,3},{5,4},{6,7},{9,8},{10,11},{13,12},{14,15},{17,16},{18,... | collective-permute-start | bytes 786440 | tf_op jit(solution)/shard_map/ppermute | solution.py:334
  73.5 2.7 %collective-permute-start.18 = (bf16[4,256,512]{2,1,0:T(8,128)(2,1)S(1)}, bf16[4,256,512]{2,1,0:T(8,128)(2,1)S(1)}, u32[]{:S(2)}, u32[]{:S(2)}) collective-permute-start(bf16[4,256,512]{2,1,0:T(8,128)(2,1)S(1)} %backward_cols.5), channel_id=1, source_target_pairs={{0,4},{4,0},{8,12},{12,8},{16,20},{20,16},{24,28},{28,24},{1,5},{5... | collective-permute-start | bytes 3145736 | tf_op jit(solution)/shard_map/ppermute | solution.py:286
  77.0 6.4 %collective-permute-start.20 = (bf16[256,512]{1,0:T(8,128)(2,1)S(1)}, bf16[256,512]{1,0:T(8,128)(2,1)S(1)}, u32[]{:S(2)}, u32[]{:S(2)}) collective-permute-start(bf16[256,512]{1,0:T(8,128)(2,1)S(1)} %get-tuple-element.36), channel_id=1, source_target_pairs={{0,8},{4,20},{8,0},{12,28},{16,24},{20,4},{24,16},{28,12},{1,9},{5... | collective-permute-start | bytes 786440 | tf_op jit(solution)/shard_map/ppermute | solution.py:350
  78.5 6.4 %collective-permute-start.12 = (bf16[256,256]{1,0:T(8,128)(2,1)S(1)}, bf16[256,256]{1,0:T(8,128)(2,1)S(1)}, u32[]{:S(2)}, u32[]{:S(2)}) collective-permute-start(bf16[256,256]{1,0:T(8,128)(2,1)S(1)} %total.3.refs_2_.refs_0_.refs_3_), channel_id=1, source_target_pairs={{0,1},{1,0},{2,3},{3,2},{4,5},{5,4},{6,7},{7,6},{8,9},{9,8},{10,11... | collective-permute-start | bytes 393224 | tf_op jit(solution)/shard_map/ppermute | solution.py:286
  78.5 14.4 %collective-permute-start.19 = (bf16[256,512]{1,0:T(8,128)(2,1)S(1)}, bf16[256,512]{1,0:T(8,128)(2,1)S(1)}, u32[]{:S(2)}, u32[]{:S(2)}) collective-permute-start(bf16[256,512]{1,0:T(8,128)(2,1)S(1)} %get-tuple-element.34), channel_id=1, source_target_pairs={{0,8},{4,20},{8,0},{12,28},{16,24},{20,4},{24,16},{28,12},{1,9},{5... | collective-permute-start | bytes 786440 | tf_op jit(solution)/shard_map/ppermute | solution.py:352
  83.5 9.5 %collective-permute-start.21 = (bf16[256,512]{1,0:T(8,128)(2,1)S(1)}, bf16[256,512]{1,0:T(8,128)(2,1)S(1)}, u32[]{:S(2)}, u32[]{:S(2)}) collective-permute-start(bf16[256,512]{1,0:T(8,128)(2,1)S(1)} %add_convert_fusion), channel_id=1, source_target_pairs={{0,16},{4,12},{8,24},{12,4},{16,0},{20,28},{24,8},{28,20},{1,17},{... | collective-permute-start | bytes 786440 | tf_op jit(solution)/shard_map/ppermute | solution.py:352
  85.0 7.2 %collective-permute-start.17 = (bf16[256,256]{1,0:T(8,128)(2,1)S(1)}, bf16[256,256]{1,0:T(8,128)(2,1)S(1)}, u32[]{:S(2)}, u32[]{:S(2)}) collective-permute-start(bf16[256,256]{1,0:T(8,128)(2,1)S(1)} %total.4.refs_0_), channel_id=1, source_target_pairs={{0,2},{1,3},{2,0},{3,1},{4,6},{5,7},{6,4},{7,5},{8,10},{9,11},{10,... | collective-permute-start | bytes 393224 | tf_op jit(solution)/shard_map/ppermute | solution.py:286

commit v14 on v13

--- a/solution.py
+++ b/solution.py
@@ -205,7 +205,8 @@
     )(where, *operands, *after)
 
 
-def meet_kernel(where, kept_ref, came_ref, own_ref, corner_ref, first_ref, second_ref):
+def meet_kernel(where, kept_ref, came_ref, *refs):
+    own_ref, corner_ref, first_ref, second_ref = refs[-4:]
     core = where[0] & 1
     own_ref[...] = kept_ref[0] + came_ref[0].astype(jnp.float32)
     corner_ref[...] = (kept_ref[3] + came_ref[3].astype(jnp.float32)).astype(corner_ref.dtype)
@@ -213,18 +214,18 @@
     second_ref[...] = kept_ref[2 - core] + came_ref[2 - core].astype(jnp.float32)
 
 
-def meet(where, kept, came):
+def meet(where, kept, came, after):
     shape = kept.shape[1:]
     kinds = [jnp.float32, came.dtype, came.dtype, jnp.float32]
     return pl.pallas_call(
         meet_kernel,
         out_shape=[pltpu.VMEM(shape, kind) for kind in kinds],
-        in_specs=[SCALARS, WHOLE, WHOLE],
+        in_specs=[SCALARS, WHOLE, WHOLE] + [UNREAD] * len(after),
         out_specs=[WHOLE] * 4,
         compiler_params=params(10),
         cost_estimate=cost(0, 0),
         name="meet",
-    )(where, near(kept), near(came))
+    )(where, near(kept), near(came), *after)
 
 
 def finish_kernel(*refs):
@@ -280,6 +281,49 @@
         cost_estimate=cost(0, 0),
         name="total",
     )(*parts, *after)
+
+
+def half_kernel(where, values_ref, out_ref):
+    rows = out_ref.shape[0]
+    value = None
+    for i in range(values_ref.shape[0] // (2 * rows)):
+        at = pl.ds(pl.multiple_of((2 * i + (where[0] & 1)) * rows, rows), rows)
+        term = values_ref[at, :].astype(jnp.float32)
+        value = term if value is None else value + term
+    out_ref[...] = value.astype(out_ref.dtype)
+
+
+def half_total(where, values, rows):
+    return pl.pallas_call(
+        half_kernel,
+        out_shape=jax.ShapeDtypeStruct((rows, values.shape[1]), values.dtype),
+        in_specs=[SCALARS, WHOLE],
+        compiler_params=params(10),
+        cost_estimate=cost(0, 0),
+        name="half_total",
+    )(where, values)
+
+
+def join_kernel(where, own_ref, *refs):
+    others, out_ref = refs[:-1], refs[-1]
+    rows = own_ref.shape[0]
+    core = where[0] & 1
+    out_ref[pl.ds(pl.multiple_of(core * rows, rows), rows), :] = own_ref[...]
+    part = rows // len(others)
+    for i, other_ref in enumerate(others):
+        out_ref[pl.ds(pl.multiple_of((1 - core) * rows + i * part, part), part), :] = other_ref[...]
+
+
+def join(where, own, *others):
+    rows, width = own.shape
+    return pl.pallas_call(
+        join_kernel,
+        out_shape=jax.ShapeDtypeStruct((2 * rows, width), own.dtype),
+        in_specs=[SCALARS] + [WHOLE] * (1 + len(others)),
+        compiler_params=params(10),
+        cost_estimate=cost(0, 0),
+        name="join",
+    )(where, own, *others)
 
 
 def swap(value, axis, size, step):
@@ -326,7 +370,7 @@
     cores = [[i for i in range(n_row) if i % 2 == core] for core in range(2)]
     part = (part + swap(part, "row", n_row, 1)).astype(jnp.bfloat16)
     gathered = lax.all_gather(part, "row", axis_index_groups=cores, tiled=True)
-    part = total([gathered], part.shape[0], jnp.bfloat16)
+    part = half_total(where, gathered, part.shape[0] // 2)
     if line:
         pieces = {s: swap(piece, "col", n_col, s) for s in (1, 2)}
         pieces[0], pieces[2] = gate([piece, pieces[2]], [part])
@@ -343,22 +387,27 @@
     sent = last(every[1::2], depth, sums, jnp.bfloat16, [part])
     kept = last(every[::2], depth, sums, jnp.float32)
     came = swap(sent, "row", n_row, 1)
+    for s in range(n_col.bit_length() - 2):
+        part = total([part, swap(part, "col", n_col, 1 << s)], part.shape[0], jnp.bfloat16, [sent])
+    after = []
     if chips == 4:
-        own, corner, first, second = meet(where, kept, came)
+        own, corner, first, second = meet(where, kept, came, [part])
         there = [(i, i ^ (2 if i % 2 == 0 else 4)) for i in range(n_row)]
         across = [(i, i ^ (4 if i % 2 == 0 else 2)) for i in range(n_row)]
         corner = lax.ppermute(corner, "row", there)
         second = (second + corner.astype(jnp.float32)).astype(jnp.bfloat16)
+        after = [second]
         parts = [lax.ppermute(first, "row", there), lax.ppermute(second, "row", across)]
     else:
         own, *summed = [kept[c] + came[c].astype(jnp.float32) for c in range(chips)]
         parts = [swap(summed[c - 1].astype(jnp.bfloat16), "row", n_row, 2 * c) for c in range(1, chips)]
 
     feature_grad = finish([own, *parts])
-    for s in range(n_col.bit_length() - 2):
-        part = total([part, swap(part, "col", n_col, 1 << s)], part.shape[0], jnp.bfloat16, [kept])
-    came = swap(part, "col", n_col, n_col // 2)
-    weight_grad = total([part, came], part.shape[0], jnp.float32)
+    part = total([part, swap(part, "col", n_col, n_col // 2)], part.shape[0], jnp.float32, after)
+    top, low = part[: part.shape[0] // 2], part[part.shape[0] // 2 :]
+    top_came = swap(top, "row", n_row, 1)
+    low_came = swap(gate([low], [top_came])[0], "row", n_row, 1)
+    weight_grad = join(where, part, top_came, low_came)
     return hidden, weight_grad, feature_grad
 
 

time: 94.1 us -> 92.9 us (0.987)
  waiting for transfers between devices: 34.5 us -> 32.2 us
    ppermute x15 -> x17, waiting for transfers between devices: 25.7 us -> 22.3 us  [swap(): return lax.ppermute(value, axis, [(i, i ^ step) for i in range(size)])]
    pallas_call x0 -> x2, Pallas kernels: none -> 1.85 us  [the longest x1 1.26 us: join(): pl.pallas_call(join_kernel, out_shape=jax.ShapeDtypeStruct((2 * rows, wid...]
    ppermute x1, waiting for transfers between devices: 0.01 us -> 1.07 us  [shards(): lax.ppermute(second, 'row', across)]
    ppermute x15 -> x17, starting transfers between devices: 13.1 us -> 13.3 us  [swap(): return lax.ppermute(value, axis, [(i, i ^ step) for i in range(size)])]
  transfers between devices with their start and end apart: 22 -> 24, of which waited for: 11 -> 13; matrix products, arithmetic and copies ran while one was open for 0% -> 0% of each run, Pallas kernels for 21% -> 23%
where the time goes in v14:
time: 92.9 us; the launch traced here: 92.7 us
  waiting for transfers between devices  32.2 us (35%)
  Pallas kernels  26 us (28%)
  starting transfers between devices  23.2 us (25%)
  blocking collectives  10 us (11%)
    ppermute x17, waiting for transfers between devices, swap(): return lax.ppermute(value, axis, [(i, i ^ step) for i in range(size)])  22.3 us
    ppermute x17, starting transfers between devices, swap(): return lax.ppermute(value, axis, [(i, i ^ step) for i in range(size)])  13.3 us
    all_gather x1, blocking collectives, shards(): gathered = lax.all_gather(part, 'row', axis_index_groups=cores, tiled=True)  10 us
    pallas_call x5, Pallas kernels, forward(): pl.pallas_call(functools.partial(forward_kernel, steps=steps, before=bool...  7.94 us
    pallas_call x1, Pallas kernels, dense_rows(): pl.pallas_call(functools.partial(dense_kernel, steps=steps, window=window...  7.05 us
    pallas_call x3, Pallas kernels, backward(): pl.pallas_call(functools.partial(backward_kernel, count=count, steps=step...  6.55 us
    ppermute x1, waiting for transfers between devices, shards(): pieces[3] = beside + lax.ppermute(pieces[2], 'col', [(1, 0), (2, 3)])  4.48 us
    ppermute x1, waiting for transfers between devices, shards(): corner = lax.ppermute(corner, 'row', there)  4.34 us
  transfers between devices with their start and end apart: 24, of which 13 were waited for; matrix products, arithmetic and copies ran while one was open for 0% of the time, Pallas kernels for 23%

profile of v14, /device:TPU:0, one launch (start us, length us, event | category | flops | bytes accessed | tf_op | source)
XLA Modules:
  0.0 92.7 jit_solution(7582904366740669930)
XLA Ops:
  0.6 4.0 %collective-permute-start.1 = (bf16[512,256]{1,0:T(8,128)(2,1)}, bf16[512,256]{1,0:T(8,128)(2,1)S(1)}, u32[]{:S(2)}, u32[]{:S(2)}) collective-permute-start(bf16[512,256]{1,0:T(8,128)(2,1)} %features_ref.1), channel_id=1, source_target_pairs={{0,24},{4,28},{8,16},{12,20},{16,8},{20,12},{24,0},{28,4},{1,25},{... | collective-permute-start | bytes 786440 | tf_op jit(solution)/shard_map/ppermute | solution.py:330
  5.3 7.1 %dense_rows.1 = (bf16[512,4096]{1,0:T(8,128)(2,1)S(1)}, bf16[512,4096]{1,0:T(8,128)(2,1)S(1)}, bf16[512,4096]{1,0:T(8,128)(2,1)S(1)}, bf16[512,4096]{1,0:T(8,128)(2,1)S(1)}, bf16[512,256]{1,0:T(8,128)(2,1)S(1)}) custom-call(s32[2]{0:T(128)S(1)} %pad_add_fusion.where, s32[16]{0:T(128)} %bitcast.7, s32[448]{0:T(512)} %bitcast.6, ...), custom_call_target="tpu_custom_call" | custom-call | bytes 41943040 | tf_op jit(solution)/shard_map/dense_rows/pallas_call | solution.py:102
  12.4 4.6 %collective-permute-done.3.refs_2_ = bf16[512,256]{1,0:T(8,128)(2,1)S(1)} collective-permute-done((bf16[512,256]{1,0:T(8,128)(2,1)}, bf16[512,256]{1,0:T(8,128)(2,1)S(1)}, u32[]{:S(2)}, u32[]{:S(2)}) %collective-permute-start.3) | collective-permute-done | bytes 262176 | tf_op jit(solution)/shard_map/ppermute | solution.py:330
  17.6 1.2 %forward_rows.6.refs_4_ = f32[512,256]{1,0:T(8,128)S(1)} custom-call(s32[2]{0:T(128)S(1)} %pad_add_fusion.where, bf16[512,4096]{1,0:T(8,128)(2,1)S(1)} %get-tuple-element.22.refs_3_.a_ref.refs_0_, bf16[512,256]{1,0:T(8,128)(2,1)S(1)} %get-tuple-element.21.refs_0_, bf16[512,256]{1,0:T(8,128)(2,1)S(1)} %get-tuple-element.25.refs_2_.refs_1_, ...), custom_call_target="tpu_custom_call" | custom-call | flops 1073741824 | bytes 4194304 | tf_op jit(solution)/shard_map/forward_rows/pallas_call | solution.py:133
  19.3 1.3 %forward_rows.7 = bf16[512,256]{1,0:T(8,128)(2,1)S(1)} custom-call(s32[2]{0:T(128)S(1)} %pad_add_fusion.where, bf16[512,4096]{1,0:T(8,128)(2,1)S(1)} %get-tuple-element.22.refs_3_.a_ref.refs_0_, bf16[512,256]{1,0:T(8,128)(2,1)S(1)} %collective-permute-done.refs_1_.refs_0_, bf16[512,256]{1,0:T(8,128)(2,1)S(1)} %collective-permute-done.4.refs_3_.refs_1_, ...), custom_call_target="tpu_custom_call" | custom-call | flops 1073741824 | bytes 4194304 | tf_op jit(solution)/shard_map/forward_rows/pallas_call | solution.py:133
  20.6 3.5 %collective-permute-start.8 = (bf16[512,256]{1,0:T(8,128)(2,1)S(1)}, bf16[512,256]{1,0:T(8,128)(2,1)S(1)}, u32[]{:S(2)}, u32[]{:S(2)}) collective-permute-start(bf16[512,256]{1,0:T(8,128)(2,1)S(1)} %forward_rows.7), channel_id=1, source_target_pairs={{0,1},{3,2},{4,5},{7,6},{8,9},{11,10},{12,13},{15,14},{16,17},{19,... | collective-permute-start | bytes 786440 | tf_op jit(solution)/shard_map/ppermute | solution.py:360
  24.1 0.9 collective-permute-start.7
  25.0 1.8 %forward_rows.9 = bf16[512,256]{1,0:T(8,128)(2,1)S(1)} custom-call(s32[2]{0:T(128)S(1)} %pad_add_fusion.where, bf16[512,4096]{1,0:T(8,128)(2,1)S(1)} %get-tuple-element.24.refs_5_.a_ref.refs_1_, bf16[512,256]{1,0:T(8,128)(2,1)S(1)} %get-tuple-element.21.refs_0_, bf16[512,256]{1,0:T(8,128)(2,1)S(1)} %collective-permute-done.refs_1_.refs_0_, ...), custom_call_target="tpu_custom_call" | custom-call | flops 1073741824 | bytes 4194304 | tf_op jit(solution)/shard_map/forward_rows/pallas_call | solution.py:133
  26.8 2.2 %collective-permute-start.10 = (bf16[512,256]{1,0:T(8,128)(2,1)S(1)}, bf16[512,256]{1,0:T(8,128)(2,1)S(1)}, u32[]{:S(2)}, u32[]{:S(2)}) collective-permute-start(bf16[512,256]{1,0:T(8,128)(2,1)S(1)} %forward_rows.9), channel_id=1, source_target_pairs={{0,1},{1,0},{2,3},{3,2},{4,5},{5,4},{6,7},{7,6},{8,9},{9,8},{10,11... | collective-permute-start | bytes 786440 | tf_op jit(solution)/shard_map/ppermute | solution.py:330
  29.0 1.8 %forward_rows.8 = bf16[512,256]{1,0:T(8,128)(2,1)S(1)} custom-call(s32[2]{0:T(128)S(1)} %pad_add_fusion.where, bf16[512,4096]{1,0:T(8,128)(2,1)S(1)} %get-tuple-element.23.refs_4_.a_ref.refs_2_, bf16[512,256]{1,0:T(8,128)(2,1)S(1)} %get-tuple-element.21.refs_0_, bf16[512,256]{1,0:T(8,128)(2,1)S(1)} %collective-permute-done.refs_1_.refs_0_, ...), custom_call_target="tpu_custom_call" | custom-call | flops 1073741824 | bytes 4194304 | tf_op jit(solution)/shard_map/forward_rows/pallas_call | solution.py:133
  30.9 3.4 %collective-permute-start.9 = (bf16[512,256]{1,0:T(8,128)(2,1)S(1)}, bf16[512,256]{1,0:T(8,128)(2,1)S(1)}, u32[]{:S(2)}, u32[]{:S(2)}) collective-permute-start(bf16[512,256]{1,0:T(8,128)(2,1)S(1)} %add_convert_fusion.1), channel_id=1, source_target_pairs={{0,2},{1,3},{2,0},{3,1},{4,6},{5,7},{6,4},{7,5},{8,10},{9,11},{10,... | collective-permute-start | bytes 786440 | tf_op jit(solution)/shard_map/ppermute | solution.py:330
  34.4 1.8 %forward_rows.5.refs_0_ = f32[512,256]{1,0:T(8,128)S(1)} custom-call(s32[2]{0:T(128)S(1)} %pad_add_fusion.where, bf16[512,4096]{1,0:T(8,128)(2,1)S(1)} %get-tuple-element.20.refs_6_.a_ref.refs_0_, bf16[512,256]{1,0:T(8,128)(2,1)S(1)} %get-tuple-element.21.refs_0_, bf16[512,256]{1,0:T(8,128)(2,1)S(1)} %collective-permute-done.refs_1_.refs_0_, ...), custom_call_target="tpu_custom_call" | custom-call | flops 1073741824 | bytes 4194304 | tf_op jit(solution)/shard_map/forward_rows/pallas_call | solution.py:133
  36.2 3.6 %collective-permute-done.10.refs_3_ = bf16[512,256]{1,0:T(8,128)(2,1)S(1)} collective-permute-done((bf16[512,256]{1,0:T(8,128)(2,1)S(1)}, bf16[512,256]{1,0:T(8,128)(2,1)S(1)}, u32[]{:S(2)}, u32[]{:S(2)}) %collective-permute-start.10) | collective-permute-done | bytes 262176 | tf_op jit(solution)/shard_map/ppermute | solution.py:330
  39.8 5.6 %collective-permute-done.9.refs_2_ = bf16[512,256]{1,0:T(8,128)(2,1)S(1)} collective-permute-done((bf16[512,256]{1,0:T(8,128)(2,1)S(1)}, bf16[512,256]{1,0:T(8,128)(2,1)S(1)}, u32[]{:S(2)}, u32[]{:S(2)}) %collective-permute-start.9) | collective-permute-done | bytes 262176 | tf_op jit(solution)/shard_map/ppermute | solution.py:330
  45.3 1.1 %middle.1 = (bf16[512,256]{1,0:T(8,128)(2,1)}, bf16[256,512]{1,0:T(8,128)(2,1)S(1)}, f32[256,256]{1,0:T(8,128)S(1)}) custom-call(f32[512,256]{1,0:T(8,128)S(1)} %forward_rows.5.refs_0_, bf16[512,256]{1,0:T(8,128)(2,1)S(1)} %collective-permute-done.7.refs_1_, bf16[512,256]{1,0:T(8,128)(2,1)S(1)} %collective-permute-done.9.refs_2_, ...), custom_call_target="tpu_custom_call" | custom-call | flops 201326592 | bytes 1310720 | tf_op jit(solution)/shard_map/middle/pallas_call | solution.py:166
  46.4 2.1 %collective-permute-start.13 = (bf16[256,512]{1,0:T(8,128)(2,1)S(1)}, bf16[256,512]{1,0:T(8,128)(2,1)S(1)}, u32[]{:S(2)}, u32[]{:S(2)}) collective-permute-start(bf16[256,512]{1,0:T(8,128)(2,1)S(1)} %get-tuple-element.30.refs_0_), channel_id=1, source_target_pairs={{0,2},{1,3},{2,0},{3,1},{4,6},{5,7},{6,4},{7,5},{8,10},{9,11},{10,... | collective-permute-start | bytes 786440 | tf_op jit(solution)/shard_map/ppermute | solution.py:330
  48.6 10.0 %all_gather.3.values_ref = bf16[1024,256]{1,0:T(8,128)(2,1)S(1)} all-gather(bf16[256,256]{1,0:T(8,128)(2,1)S(1)} %add_convert_fusion.2), channel_id=1, replica_groups={{0,8,16,24},{4,12,20,28},{1,9,17,25},{5,13,21,29},{2,10,18,26},{6,14,22..., dimensions={0}, use_global_device_ids=true | all-gather | bytes 655360 | tf_op jit(solution)/shard_map/all_gather | solution.py:372
  59.7 2.0 %collective-permute-done.13.refs_1_ = bf16[256,512]{1,0:T(8,128)(2,1)S(1)} collective-permute-done((bf16[256,512]{1,0:T(8,128)(2,1)S(1)}, bf16[256,512]{1,0:T(8,128)(2,1)S(1)}, u32[]{:S(2)}, u32[]{:S(2)}) %collective-permute-start.13) | collective-permute-done | bytes 262176 | tf_op jit(solution)/shard_map/ppermute | solution.py:330
  62.4 1.3 %collective-permute-start.15 = (bf16[256,512]{1,0:T(8,128)(2,1)S(1)}, bf16[256,512]{1,0:T(8,128)(2,1)S(1)}, u32[]{:S(2)}, u32[]{:S(2)}) collective-permute-start(bf16[256,512]{1,0:T(8,128)(2,1)S(1)} %get-tuple-element.32.refs_5_), channel_id=1, source_target_pairs={{1,0},{2,3},{5,4},{6,7},{9,8},{10,11},{13,12},{14,15},{17,16},{18,... | collective-permute-start | bytes 786440 | tf_op jit(solution)/shard_map/ppermute | solution.py:378
  63.7 4.0 %backward_cols.3.refs_2_ = f32[8,256,512]{2,1,0:T(8,128)S(1)} custom-call(s32[2]{0:T(128)S(1)} %pad_add_fusion.where, bf16[512,4096]{1,0:T(8,128)(2,1)S(1)} %get-tuple-element.20.refs_6_.a_ref.refs_0_, bf16[512,4096]{1,0:T(8,128)(2,1)S(1)} %get-tuple-element.24.refs_5_.a_ref.refs_1_, bf16[512,4096]{1,0:T(8,128)(2,1)S(1)} %get-tuple-element.23.refs_4_.a_ref.refs_2_, ...), custom_call_target="tpu_custom_call" | custom-call | tf_op jit(solution)/shard_map/backward_cols/pallas_call | solution.py:197
  67.7 4.5 %collective-permute-done.15 = bf16[256,512]{1,0:T(8,128)(2,1)S(1)} collective-permute-done((bf16[256,512]{1,0:T(8,128)(2,1)S(1)}, bf16[256,512]{1,0:T(8,128)(2,1)S(1)}, u32[]{:S(2)}, u32[]{:S(2)}) %collective-permute-start.15) | collective-permute-done | bytes 262176 | tf_op jit(solution)/shard_map/ppermute | solution.py:378
  72.3 1.3 %backward_cols.4.refs_2_ = bf16[4,256,512]{2,1,0:T(8,128)(2,1)S(1)} custom-call(s32[2]{0:T(128)S(1)} %pad_add_fusion.where, bf16[512,4096]{1,0:T(8,128)(2,1)S(1)} %get-tuple-element.22.refs_3_.a_ref.refs_0_, bf16[256,512]{1,0:T(8,128)(2,1)S(1)} %add.14.refs_1_, f32[8,256,512]{2,1,0:T(8,128)S(1)} %backward_cols.3.refs_2_, ...), custom_call_target="tpu_custom_call" | custom-call | tf_op jit(solution)/shard_map/backward_cols/pallas_call | solution.py:197
  73.7 1.3 %backward_cols.5.kept_ref = f32[4,256,512]{2,1,0:T(8,128)S(1)} custom-call(s32[2]{0:T(128)S(1)} %pad_add_fusion.where, bf16[512,4096]{1,0:T(8,128)(2,1)S(1)} %get-tuple-element.22.refs_3_.a_ref.refs_0_, bf16[256,512]{1,0:T(8,128)(2,1)S(1)} %add.14.refs_1_, f32[8,256,512]{2,1,0:T(8,128)S(1)} %backward_cols.3.refs_2_), custom_call_target="tpu_custom_call" | custom-call | tf_op jit(solution)/shard_map/backward_cols/pallas_call | solution.py:197
  75.0 3.2 %collective-permute-done.12.refs_1_ = bf16[128,256]{1,0:T(8,128)(2,1)S(1)} collective-permute-done((bf16[128,256]{1,0:T(8,128)(2,1)S(1)}, bf16[128,256]{1,0:T(8,128)(2,1)S(1)}, u32[]{:S(2)}, u32[]{:S(2)}) %collective-permute-start.12) | collective-permute-done | bytes 65568 | tf_op jit(solution)/shard_map/ppermute | solution.py:330
  78.9 1.6 %collective-permute-start.19 = (bf16[256,512]{1,0:T(8,128)(2,1)S(1)}, bf16[256,512]{1,0:T(8,128)(2,1)S(1)}, u32[]{:S(2)}, u32[]{:S(2)}) collective-permute-start(bf16[256,512]{1,0:T(8,128)(2,1)S(1)} %get-tuple-element.34), channel_id=1, source_target_pairs={{0,8},{4,20},{8,0},{12,28},{16,24},{20,4},{24,16},{28,12},{1,9},{5... | collective-permute-start | bytes 786440 | tf_op jit(solution)/shard_map/ppermute | solution.py:397
  81.0 4.3 %collective-permute-done.19 = bf16[256,512]{1,0:T(8,128)(2,1)S(1)} collective-permute-done((bf16[256,512]{1,0:T(8,128)(2,1)S(1)}, bf16[256,512]{1,0:T(8,128)(2,1)S(1)}, u32[]{:S(2)}, u32[]{:S(2)}) %collective-permute-start.19) | collective-permute-done | bytes 262176 | tf_op jit(solution)/shard_map/ppermute | solution.py:397
  85.4 1.5 %collective-permute-start.23 = (bf16[256,512]{1,0:T(8,128)(2,1)S(1)}, bf16[256,512]{1,0:T(8,128)(2,1)S(1)}, u32[]{:S(2)}, u32[]{:S(2)}) collective-permute-start(bf16[256,512]{1,0:T(8,128)(2,1)S(1)} %add_convert_fusion.refs_2_), channel_id=1, source_target_pairs={{0,16},{4,12},{8,24},{12,4},{16,0},{20,28},{24,8},{28,20},{1,17},{... | collective-permute-start | bytes 786440 | tf_op jit(solution)/shard_map/ppermute | solution.py:400
  87.0 1.2 %collective-permute-done.20.refs_1_.refs_0_ = f32[64,256]{1,0:T(8,128)S(1)} collective-permute-done((f32[64,256]{1,0:T(8,128)S(1)}, f32[64,256]{1,0:T(8,128)S(1)}, u32[]{:S(2)}, u32[]{:S(2)}) %collective-permute-start.20) | collective-permute-done | bytes 65568 | tf_op jit(solution)/shard_map/ppermute | solution.py:330
  88.4 1.1 %collective-permute-done.21.refs_1_ = f32[64,256]{1,0:T(8,128)S(1)} collective-permute-done((f32[64,256]{1,0:T(8,128)S(1)}, f32[64,256]{1,0:T(8,128)S(1)}, u32[]{:S(2)}, u32[]{:S(2)}) %collective-permute-start.21) | collective-permute-done | bytes 65568 | tf_op jit(solution)/shard_map/ppermute | solution.py:330
  89.5 1.3 %join.1 = f32[256,256]{1,0:T(8,128)} custom-call(s32[2]{0:T(128)S(1)} %pad_add_fusion.where, f32[128,256]{1,0:T(8,128)S(1)} %total.3.own_ref, f32[64,256]{1,0:T(8,128)S(1)} %collective-permute-done.20.refs_1_.refs_0_, f32[64,256]{1,0:T(8,128)S(1)} %collective-permute-done.21.refs_1_), custom_call_target="tpu_custom_call" | custom-call | tf_op jit(solution)/shard_map/join/pallas_call | solution.py:319
  90.8 1.1 %collective-permute-done.23.refs_2_ = bf16[256,512]{1,0:T(8,128)(2,1)S(1)} collective-permute-done((bf16[256,512]{1,0:T(8,128)(2,1)S(1)}, bf16[256,512]{1,0:T(8,128)(2,1)S(1)}, u32[]{:S(2)}, u32[]{:S(2)}) %collective-permute-start.23) | collective-permute-done | bytes 262176 | tf_op jit(solution)/shard_map/ppermute | solution.py:400
  91.8 0.8 finish.1
  (46 shorter events, 5.5 us)
Async XLA Ops:
  0.6 11.7 %collective-permute-start.1 = (bf16[512,256]{1,0:T(8,128)(2,1)}, bf16[512,256]{1,0:T(8,128)(2,1)S(1)}, u32[]{:S(2)}, u32[]{:S(2)}) collective-permute-start(bf16[512,256]{1,0:T(8,128)(2,1)} %features_ref.1), channel_id=1, source_target_pairs={{0,24},{4,28},{8,16},{12,20},{16,8},{20,12},{24,0},{28,4},{1,25},{... | collective-permute-start | bytes 786440 | tf_op jit(solution)/shard_map/ppermute | solution.py:330
  4.6 12.4 %collective-permute-start.3 = (bf16[512,256]{1,0:T(8,128)(2,1)}, bf16[512,256]{1,0:T(8,128)(2,1)S(1)}, u32[]{:S(2)}, u32[]{:S(2)}) collective-permute-start(bf16[512,256]{1,0:T(8,128)(2,1)} %features_ref.1), channel_id=1, source_target_pairs={{0,8},{4,12},{8,0},{12,4},{16,24},{20,28},{24,16},{28,20},{1,9},{5... | collective-permute-start | bytes 786440 | tf_op jit(solution)/shard_map/ppermute | solution.py:330
  5.1 11.9 %collective-permute-start.2 = (bf16[512,256]{1,0:T(8,128)(2,1)}, bf16[512,256]{1,0:T(8,128)(2,1)S(1)}, u32[]{:S(2)}, u32[]{:S(2)}) collective-permute-start(bf16[512,256]{1,0:T(8,128)(2,1)} %features_ref.1), channel_id=1, source_target_pairs={{0,16},{4,20},{8,24},{12,28},{16,0},{20,4},{24,8},{28,12},{1,17},{... | collective-permute-start | bytes 786440 | tf_op jit(solution)/shard_map/ppermute | solution.py:330
  5.2 13.6 %collective-permute-start = (bf16[512,256]{1,0:T(8,128)(2,1)}, bf16[512,256]{1,0:T(8,128)(2,1)S(1)}, u32[]{:S(2)}, u32[]{:S(2)}) collective-permute-start(bf16[512,256]{1,0:T(8,128)(2,1)} %features_ref.1), channel_id=1, source_target_pairs={{0,4},{4,0},{8,12},{12,8},{16,20},{20,16},{24,28},{28,24},{1,5},{5... | collective-permute-start | bytes 786440 | tf_op jit(solution)/shard_map/ppermute | solution.py:330
  17.0 1.8 %collective-permute-start.4 = (bf16[512,256]{1,0:T(8,128)(2,1)S(1)}, bf16[512,256]{1,0:T(8,128)(2,1)S(1)}, u32[]{:S(2)}, u32[]{:S(2)}) collective-permute-start(bf16[512,256]{1,0:T(8,128)(2,1)S(1)} %get-tuple-element.25.refs_2_.refs_1_), channel_id=1, source_target_pairs={{0,4},{4,0},{8,12},{12,8},{16,20},{20,16},{24,28},{28,24},{1,5},{5... | collective-permute-start | bytes 786440 | tf_op jit(solution)/shard_map/ppermute | solution.py:330
  17.0 1.9 %collective-permute-start.5 = (bf16[512,256]{1,0:T(8,128)(2,1)S(1)}, bf16[512,256]{1,0:T(8,128)(2,1)S(1)}, u32[]{:S(2)}, u32[]{:S(2)}) collective-permute-start(bf16[512,256]{1,0:T(8,128)(2,1)S(1)} %get-tuple-element.26.refs_4_.refs_2_), channel_id=1, source_target_pairs={{0,4},{4,0},{8,12},{12,8},{16,20},{20,16},{24,28},{28,24},{1,5},{5... | collective-permute-start | bytes 786440 | tf_op jit(solution)/shard_map/ppermute | solution.py:330
  17.5 1.8 %collective-permute-start.6 = (bf16[512,256]{1,0:T(8,128)(2,1)S(1)}, bf16[512,256]{1,0:T(8,128)(2,1)S(1)}, u32[]{:S(2)}, u32[]{:S(2)}) collective-permute-start(bf16[512,256]{1,0:T(8,128)(2,1)S(1)} %get-tuple-element.27.refs_6_.refs_3_), channel_id=1, source_target_pairs={{0,4},{4,0},{8,12},{12,8},{16,20},{20,16},{24,28},{28,24},{1,5},{5... | collective-permute-start | bytes 786440 | tf_op jit(solution)/shard_map/ppermute | solution.py:330
  20.6 10.3 %collective-permute-start.8 = (bf16[512,256]{1,0:T(8,128)(2,1)S(1)}, bf16[512,256]{1,0:T(8,128)(2,1)S(1)}, u32[]{:S(2)}, u32[]{:S(2)}) collective-permute-start(bf16[512,256]{1,0:T(8,128)(2,1)S(1)} %forward_rows.7), channel_id=1, source_target_pairs={{0,1},{3,2},{4,5},{7,6},{8,9},{11,10},{12,13},{15,14},{16,17},{19,... | collective-permute-start | bytes 786440 | tf_op jit(solution)/shard_map/ppermute | solution.py:360
  24.1 15.7 %collective-permute-start.7 = (bf16[512,256]{1,0:T(8,128)(2,1)S(1)}, bf16[512,256]{1,0:T(8,128)(2,1)S(1)}, u32[]{:S(2)}, u32[]{:S(2)}) collective-permute-start(bf16[512,256]{1,0:T(8,128)(2,1)S(1)} %forward_rows.7), channel_id=1, source_target_pairs={{1,2},{2,1},{5,6},{6,5},{9,10},{10,9},{13,14},{14,13},{17,18},{18,... | collective-permute-start | bytes 786440 | tf_op jit(solution)/shard_map/ppermute | solution.py:361
  26.8 13.0 %collective-permute-start.10 = (bf16[512,256]{1,0:T(8,128)(2,1)S(1)}, bf16[512,256]{1,0:T(8,128)(2,1)S(1)}, u32[]{:S(2)}, u32[]{:S(2)}) collective-permute-start(bf16[512,256]{1,0:T(8,128)(2,1)S(1)} %forward_rows.9), channel_id=1, source_target_pairs={{0,1},{1,0},{2,3},{3,2},{4,5},{5,4},{6,7},{7,6},{8,9},{9,8},{10,11... | collective-permute-start | bytes 786440 | tf_op jit(solution)/shard_map/ppermute | solution.py:330
  30.8 14.5 %copy-start = (bf16[512,256]{1,0:T(8,128)(2,1)S(1)}, bf16[512,256]{1,0:T(8,128)(2,1)}, u32[]{:S(2)}) copy-start(bf16[512,256]{1,0:T(8,128)(2,1)} %refs_5_.1) | copy-start | bytes 786436
  30.8 14.5 %copy-start.1 = (bf16[256,256]{1,0:T(8,128)(2,1)S(1)}, bf16[256,256]{1,0:T(8,128)(2,1)}, u32[]{:S(2)}) copy-start(bf16[256,256]{1,0:T(8,128)(2,1)} %refs_4_.1) | copy-start | bytes 393220
  30.9 14.4 %collective-permute-start.9 = (bf16[512,256]{1,0:T(8,128)(2,1)S(1)}, bf16[512,256]{1,0:T(8,128)(2,1)S(1)}, u32[]{:S(2)}, u32[]{:S(2)}) collective-permute-start(bf16[512,256]{1,0:T(8,128)(2,1)S(1)} %add_convert_fusion.1), channel_id=1, source_target_pairs={{0,2},{1,3},{2,0},{3,1},{4,6},{5,7},{6,4},{7,5},{8,10},{9,11},{10,... | collective-permute-start | bytes 786440 | tf_op jit(solution)/shard_map/ppermute | solution.py:330
  46.4 2.1 %collective-permute-start.11 = (f32[256,256]{1,0:T(8,128)S(1)}, f32[256,256]{1,0:T(8,128)S(1)}, u32[]{:S(2)}, u32[]{:S(2)}) collective-permute-start(f32[256,256]{1,0:T(8,128)S(1)} %get-tuple-element.29), channel_id=1, source_target_pairs={{0,4},{4,0},{8,12},{12,8},{16,20},{20,16},{24,28},{28,24},{1,5},{5... | collective-permute-start | bytes 786440 | tf_op jit(solution)/shard_map/ppermute | solution.py:330
  46.4 13.3 %collective-permute-start.16 = (bf16[256,512]{1,0:T(8,128)(2,1)S(1)}, bf16[256,512]{1,0:T(8,128)(2,1)S(1)}, u32[]{:S(2)}, u32[]{:S(2)}) collective-permute-start(bf16[256,512]{1,0:T(8,128)(2,1)S(1)} %get-tuple-element.30.refs_0_), channel_id=1, source_target_pairs={{0,1},{1,0},{2,3},{3,2},{4,5},{5,4},{6,7},{7,6},{8,9},{9,8},{10,11... | collective-permute-start | bytes 786440 | tf_op jit(solution)/shard_map/ppermute | solution.py:330
  46.4 15.3 %collective-permute-start.13 = (bf16[256,512]{1,0:T(8,128)(2,1)S(1)}, bf16[256,512]{1,0:T(8,128)(2,1)S(1)}, u32[]{:S(2)}, u32[]{:S(2)}) collective-permute-start(bf16[256,512]{1,0:T(8,128)(2,1)S(1)} %get-tuple-element.30.refs_0_), channel_id=1, source_target_pairs={{0,2},{1,3},{2,0},{3,1},{4,6},{5,7},{6,4},{7,5},{8,10},{9,11},{10,... | collective-permute-start | bytes 786440 | tf_op jit(solution)/shard_map/ppermute | solution.py:330
  61.7 6.0 %collective-permute-start.14 = (bf16[256,512]{1,0:T(8,128)(2,1)S(1)}, bf16[256,512]{1,0:T(8,128)(2,1)S(1)}, u32[]{:S(2)}, u32[]{:S(2)}) collective-permute-start(bf16[256,512]{1,0:T(8,128)(2,1)S(1)} %get-tuple-element.31.refs_3_), channel_id=1, source_target_pairs={{1,2},{2,1},{5,6},{6,5},{9,10},{10,9},{13,14},{14,13},{17,18},{18,... | collective-permute-start | bytes 786440 | tf_op jit(solution)/shard_map/ppermute | solution.py:377
  62.4 9.8 %collective-permute-start.15 = (bf16[256,512]{1,0:T(8,128)(2,1)S(1)}, bf16[256,512]{1,0:T(8,128)(2,1)S(1)}, u32[]{:S(2)}, u32[]{:S(2)}) collective-permute-start(bf16[256,512]{1,0:T(8,128)(2,1)S(1)} %get-tuple-element.32.refs_5_), channel_id=1, source_target_pairs={{1,0},{2,3},{5,4},{6,7},{9,8},{10,11},{13,12},{14,15},{17,16},{18,... | collective-permute-start | bytes 786440 | tf_op jit(solution)/shard_map/ppermute | solution.py:378
  73.5 4.6 %collective-permute-start.18 = (bf16[4,256,512]{2,1,0:T(8,128)(2,1)S(1)}, bf16[4,256,512]{2,1,0:T(8,128)(2,1)S(1)}, u32[]{:S(2)}, u32[]{:S(2)}) collective-permute-start(bf16[4,256,512]{2,1,0:T(8,128)(2,1)S(1)} %backward_cols.4.refs_2_), channel_id=1, source_target_pairs={{0,4},{4,0},{8,12},{12,8},{16,20},{20,16},{24,28},{28,24},{1,5},{5... | collective-permute-start | bytes 3145736 | tf_op jit(solution)/shard_map/ppermute | solution.py:330
  73.6 4.5 %collective-permute-start.12 = (bf16[128,256]{1,0:T(8,128)(2,1)S(1)}, bf16[128,256]{1,0:T(8,128)(2,1)S(1)}, u32[]{:S(2)}, u32[]{:S(2)}) collective-permute-start(bf16[128,256]{1,0:T(8,128)(2,1)S(1)} %half_total.1.refs_2_.refs_3_.refs_0_), channel_id=1, source_target_pairs={{0,1},{1,0},{2,3},{3,2},{4,5},{5,4},{6,7},{7,6},{8,9},{9,8},{10,11... | collective-permute-start | bytes 196616 | tf_op jit(solution)/shard_map/ppermute | solution.py:330
  78.9 6.4 %collective-permute-start.19 = (bf16[256,512]{1,0:T(8,128)(2,1)S(1)}, bf16[256,512]{1,0:T(8,128)(2,1)S(1)}, u32[]{:S(2)}, u32[]{:S(2)}) collective-permute-start(bf16[256,512]{1,0:T(8,128)(2,1)S(1)} %get-tuple-element.34), channel_id=1, source_target_pairs={{0,8},{4,20},{8,0},{12,28},{16,24},{20,4},{24,16},{28,12},{1,9},{5... | collective-permute-start | bytes 786440 | tf_op jit(solution)/shard_map/ppermute | solution.py:397
  80.4 6.4 %collective-permute-start.17 = (bf16[128,256]{1,0:T(8,128)(2,1)S(1)}, bf16[128,256]{1,0:T(8,128)(2,1)S(1)}, u32[]{:S(2)}, u32[]{:S(2)}) collective-permute-start(bf16[128,256]{1,0:T(8,128)(2,1)S(1)} %total.2.refs_0_), channel_id=1, source_target_pairs={{0,2},{1,3},{2,0},{3,1},{4,6},{5,7},{6,4},{7,5},{8,10},{9,11},{10,... | collective-permute-start | bytes 196616 | tf_op jit(solution)/shard_map/ppermute | solution.py:330
  80.4 10.3 %collective-permute-start.22 = (bf16[256,512]{1,0:T(8,128)(2,1)S(1)}, bf16[256,512]{1,0:T(8,128)(2,1)S(1)}, u32[]{:S(2)}, u32[]{:S(2)}) collective-permute-start(bf16[256,512]{1,0:T(8,128)(2,1)S(1)} %get-tuple-element.36), channel_id=1, source_target_pairs={{0,8},{4,20},{8,0},{12,28},{16,24},{20,4},{24,16},{28,12},{1,9},{5... | collective-permute-start | bytes 786440 | tf_op jit(solution)/shard_map/ppermute | solution.py:400
  85.4 6.4 %collective-permute-start.23 = (bf16[256,512]{1,0:T(8,128)(2,1)S(1)}, bf16[256,512]{1,0:T(8,128)(2,1)S(1)}, u32[]{:S(2)}, u32[]{:S(2)}) collective-permute-start(bf16[256,512]{1,0:T(8,128)(2,1)S(1)} %add_convert_fusion.refs_2_), channel_id=1, source_target_pairs={{0,16},{4,12},{8,24},{12,4},{16,0},{20,28},{24,8},{28,20},{1,17},{... | collective-permute-start | bytes 786440 | tf_op jit(solution)/shard_map/ppermute | solution.py:400
  86.9 1.3 %collective-permute-start.20 = (f32[64,256]{1,0:T(8,128)S(1)}, f32[64,256]{1,0:T(8,128)S(1)}, u32[]{:S(2)}, u32[]{:S(2)}) collective-permute-start(f32[64,256]{1,0:T(8,128)S(1)} %get-tuple-element.38), channel_id=1, source_target_pairs={{0,4},{4,0},{8,12},{12,8},{16,20},{20,16},{24,28},{28,24},{1,5},{5... | collective-permute-start | bytes 196616 | tf_op jit(solution)/shard_map/ppermute | solution.py:330
  88.2 1.3 %collective-permute-start.21 = (f32[64,256]{1,0:T(8,128)S(1)}, f32[64,256]{1,0:T(8,128)S(1)}, u32[]{:S(2)}, u32[]{:S(2)}) collective-permute-start(f32[64,256]{1,0:T(8,128)S(1)} %gate.5), channel_id=1, source_target_pairs={{0,4},{4,0},{8,12},{12,8},{16,20},{20,16},{24,28},{28,24},{1,5},{5... | collective-permute-start | bytes 196616 | tf_op jit(solution)/shard_map/ppermute | solution.py:330

commit v15 on v14

--- a/solution.py
+++ b/solution.py
@@ -373,7 +373,7 @@
     part = half_total(where, gathered, part.shape[0] // 2)
     if line:
         pieces = {s: swap(piece, "col", n_col, s) for s in (1, 2)}
-        pieces[0], pieces[2] = gate([piece, pieces[2]], [part])
+        pieces[0], pieces[2], part = gate([piece, pieces[2], part], [])
         beside = lax.ppermute(pieces[0], "col", [(1, 2), (2, 1)])
         pieces[3] = beside + lax.ppermute(pieces[2], "col", [(1, 0), (2, 3)])
     else:
@@ -383,15 +383,15 @@
     sums, latest = None, n_col - 1
     for group in [list(range(n_col - 1))]:
         sums = backward(where, [dense[s] for s in group], [pieces[s] for s in group], every, depth, sums, jnp.float32)
+    for s in range(n_col.bit_length() - 2):
+        part = total([part, swap(part, "col", n_col, 1 << s)], part.shape[0], jnp.bfloat16)
     last = functools.partial(backward, where, [dense[latest]], [pieces[latest]])
     sent = last(every[1::2], depth, sums, jnp.bfloat16, [part])
     kept = last(every[::2], depth, sums, jnp.float32)
     came = swap(sent, "row", n_row, 1)
-    for s in range(n_col.bit_length() - 2):
-        part = total([part, swap(part, "col", n_col, 1 << s)], part.shape[0], jnp.bfloat16, [sent])
     after = []
     if chips == 4:
-        own, corner, first, second = meet(where, kept, came, [part])
+        own, corner, first, second = meet(where, kept, came, [])
         there = [(i, i ^ (2 if i % 2 == 0 else 4)) for i in range(n_row)]
         across = [(i, i ^ (4 if i % 2 == 0 else 2)) for i in range(n_row)]
         corner = lax.ppermute(corner, "row", there)

time: 92.9 us -> 92.5 us (level)
  waiting for transfers between devices: 32.2 us -> 28.4 us
  starting transfers between devices: 23.2 us -> 25.9 us
    ppermute x1, waiting for transfers between devices: 4.48 us -> 0.01 us  [shards(): pieces[3] = beside + lax.ppermute(pieces[2], 'col', [(1, 0), (2, 3)])]
    ppermute x17, starting transfers between devices: 13.3 us -> 16 us  [swap(): return lax.ppermute(value, axis, [(i, i ^ step) for i in range(size)])]
where the time goes in v15:
time: 92.5 us; the launch traced here: 92.2 us
  waiting for transfers between devices  28.4 us (31%)
  Pallas kernels  26.7 us (29%)
  starting transfers between devices  25.9 us (28%)
  blocking collectives  10 us (11%)
    ppermute x17, waiting for transfers between devices, swap(): return lax.ppermute(value, axis, [(i, i ^ step) for i in range(size)])  23 us
    ppermute x17, starting transfers between devices, swap(): return lax.ppermute(value, axis, [(i, i ^ step) for i in range(size)])  16 us
    all_gather x1, blocking collectives, shards(): gathered = lax.all_gather(part, 'row', axis_index_groups=cores, tiled=True)  10 us
    pallas_call x5, Pallas kernels, forward(): pl.pallas_call(functools.partial(forward_kernel, steps=steps, before=bool...  7.94 us
    pallas_call x1, Pallas kernels, dense_rows(): pl.pallas_call(functools.partial(dense_kernel, steps=steps, window=window...  7.69 us
    pallas_call x3, Pallas kernels, backward(): pl.pallas_call(functools.partial(backward_kernel, count=count, steps=step...  6.55 us
    ppermute x1, waiting for transfers between devices, shards(): corner = lax.ppermute(corner, 'row', there)  4.34 us
    ppermute x1, starting transfers between devices, shards(): relayed = lax.ppermute(shares[3], 'col', [(0, 1), (3, 2)])  3.5 us
  transfers between devices with their start and end apart: 24, of which 13 were waited for; matrix products, arithmetic and copies ran while one was open for 0% of the time, Pallas kernels for 23%

profile of v15, /device:TPU:0, one launch (start us, length us, event | category | flops | bytes accessed | tf_op | source)
XLA Modules:
  0.0 92.2 jit_solution(1337424460963482885)
XLA Ops:
  0.6 4.0 %collective-permute-start.1 = (bf16[512,256]{1,0:T(8,128)(2,1)}, bf16[512,256]{1,0:T(8,128)(2,1)S(1)}, u32[]{:S(2)}, u32[]{:S(2)}) collective-permute-start(bf16[512,256]{1,0:T(8,128)(2,1)} %features_ref.1), channel_id=1, source_target_pairs={{0,24},{4,28},{8,16},{12,20},{16,8},{20,12},{24,0},{28,4},{1,25},{... | collective-permute-start | bytes 786440 | tf_op jit(solution)/shard_map/ppermute | solution.py:330
  5.3 7.7 %dense_rows.1 = (bf16[512,4096]{1,0:T(8,128)(2,1)S(1)}, bf16[512,4096]{1,0:T(8,128)(2,1)S(1)}, bf16[512,4096]{1,0:T(8,128)(2,1)S(1)}, bf16[512,4096]{1,0:T(8,128)(2,1)S(1)}, bf16[512,256]{1,0:T(8,128)(2,1)S(1)}) custom-call(s32[2]{0:T(128)S(1)} %pad_add_fusion.where, s32[16]{0:T(128)} %bitcast.7, s32[448]{0:T(512)} %bitcast.6, ...), custom_call_target="tpu_custom_call" | custom-call | bytes 41943040 | tf_op jit(solution)/shard_map/dense_rows/pallas_call | solution.py:102
  13.0 4.0 %collective-permute-done.3.refs_2_ = bf16[512,256]{1,0:T(8,128)(2,1)S(1)} collective-permute-done((bf16[512,256]{1,0:T(8,128)(2,1)}, bf16[512,256]{1,0:T(8,128)(2,1)S(1)}, u32[]{:S(2)}, u32[]{:S(2)}) %collective-permute-start.3) | collective-permute-done | bytes 262176 | tf_op jit(solution)/shard_map/ppermute | solution.py:330
  17.6 1.2 %forward_rows.6.refs_4_ = f32[512,256]{1,0:T(8,128)S(1)} custom-call(s32[2]{0:T(128)S(1)} %pad_add_fusion.where, bf16[512,4096]{1,0:T(8,128)(2,1)S(1)} %get-tuple-element.23.refs_3_.a_ref.refs_0_, bf16[512,256]{1,0:T(8,128)(2,1)S(1)} %get-tuple-element.22.refs_0_, bf16[512,256]{1,0:T(8,128)(2,1)S(1)} %get-tuple-element.26.refs_2_.refs_1_, ...), custom_call_target="tpu_custom_call" | custom-call | flops 1073741824 | bytes 4194304 | tf_op jit(solution)/shard_map/forward_rows/pallas_call | solution.py:133
  19.3 1.3 %forward_rows.7 = bf16[512,256]{1,0:T(8,128)(2,1)S(1)} custom-call(s32[2]{0:T(128)S(1)} %pad_add_fusion.where, bf16[512,4096]{1,0:T(8,128)(2,1)S(1)} %get-tuple-element.23.refs_3_.a_ref.refs_0_, bf16[512,256]{1,0:T(8,128)(2,1)S(1)} %collective-permute-done.refs_1_.refs_0_, bf16[512,256]{1,0:T(8,128)(2,1)S(1)} %collective-permute-done.4.refs_3_.refs_1_, ...), custom_call_target="tpu_custom_call" | custom-call | flops 1073741824 | bytes 4194304 | tf_op jit(solution)/shard_map/forward_rows/pallas_call | solution.py:133
  20.6 3.5 %collective-permute-start.8 = (bf16[512,256]{1,0:T(8,128)(2,1)S(1)}, bf16[512,256]{1,0:T(8,128)(2,1)S(1)}, u32[]{:S(2)}, u32[]{:S(2)}) collective-permute-start(bf16[512,256]{1,0:T(8,128)(2,1)S(1)} %forward_rows.7), channel_id=1, source_target_pairs={{0,1},{3,2},{4,5},{7,6},{8,9},{11,10},{12,13},{15,14},{16,17},{19,... | collective-permute-start | bytes 786440 | tf_op jit(solution)/shard_map/ppermute | solution.py:360
  24.1 0.9 collective-permute-start.7
  25.0 1.8 %forward_rows.9 = bf16[512,256]{1,0:T(8,128)(2,1)S(1)} custom-call(s32[2]{0:T(128)S(1)} %pad_add_fusion.where, bf16[512,4096]{1,0:T(8,128)(2,1)S(1)} %get-tuple-element.25.refs_5_.a_ref.refs_1_, bf16[512,256]{1,0:T(8,128)(2,1)S(1)} %get-tuple-element.22.refs_0_, bf16[512,256]{1,0:T(8,128)(2,1)S(1)} %collective-permute-done.refs_1_.refs_0_, ...), custom_call_target="tpu_custom_call" | custom-call | flops 1073741824 | bytes 4194304 | tf_op jit(solution)/shard_map/forward_rows/pallas_call | solution.py:133
  26.8 2.2 %collective-permute-start.10 = (bf16[512,256]{1,0:T(8,128)(2,1)S(1)}, bf16[512,256]{1,0:T(8,128)(2,1)S(1)}, u32[]{:S(2)}, u32[]{:S(2)}) collective-permute-start(bf16[512,256]{1,0:T(8,128)(2,1)S(1)} %forward_rows.9), channel_id=1, source_target_pairs={{0,1},{1,0},{2,3},{3,2},{4,5},{5,4},{6,7},{7,6},{8,9},{9,8},{10,11... | collective-permute-start | bytes 786440 | tf_op jit(solution)/shard_map/ppermute | solution.py:330
  29.0 1.8 %forward_rows.8 = bf16[512,256]{1,0:T(8,128)(2,1)S(1)} custom-call(s32[2]{0:T(128)S(1)} %pad_add_fusion.where, bf16[512,4096]{1,0:T(8,128)(2,1)S(1)} %get-tuple-element.24.refs_4_.a_ref.refs_2_, bf16[512,256]{1,0:T(8,128)(2,1)S(1)} %get-tuple-element.22.refs_0_, bf16[512,256]{1,0:T(8,128)(2,1)S(1)} %collective-permute-done.refs_1_.refs_0_, ...), custom_call_target="tpu_custom_call" | custom-call | flops 1073741824 | bytes 4194304 | tf_op jit(solution)/shard_map/forward_rows/pallas_call | solution.py:133
  30.9 3.4 %collective-permute-start.9 = (bf16[512,256]{1,0:T(8,128)(2,1)S(1)}, bf16[512,256]{1,0:T(8,128)(2,1)S(1)}, u32[]{:S(2)}, u32[]{:S(2)}) collective-permute-start(bf16[512,256]{1,0:T(8,128)(2,1)S(1)} %add_convert_fusion.1), channel_id=1, source_target_pairs={{0,2},{1,3},{2,0},{3,1},{4,6},{5,7},{6,4},{7,5},{8,10},{9,11},{10,... | collective-permute-start | bytes 786440 | tf_op jit(solution)/shard_map/ppermute | solution.py:330
  34.4 1.8 %forward_rows.5.refs_0_ = f32[512,256]{1,0:T(8,128)S(1)} custom-call(s32[2]{0:T(128)S(1)} %pad_add_fusion.where, bf16[512,4096]{1,0:T(8,128)(2,1)S(1)} %get-tuple-element.21.refs_6_.a_ref.refs_0_, bf16[512,256]{1,0:T(8,128)(2,1)S(1)} %get-tuple-element.22.refs_0_, bf16[512,256]{1,0:T(8,128)(2,1)S(1)} %collective-permute-done.refs_1_.refs_0_, ...), custom_call_target="tpu_custom_call" | custom-call | flops 1073741824 | bytes 4194304 | tf_op jit(solution)/shard_map/forward_rows/pallas_call | solution.py:133
  36.2 3.6 %collective-permute-done.10.refs_3_ = bf16[512,256]{1,0:T(8,128)(2,1)S(1)} collective-permute-done((bf16[512,256]{1,0:T(8,128)(2,1)S(1)}, bf16[512,256]{1,0:T(8,128)(2,1)S(1)}, u32[]{:S(2)}, u32[]{:S(2)}) %collective-permute-start.10) | collective-permute-done | bytes 262176 | tf_op jit(solution)/shard_map/ppermute | solution.py:330
  39.8 5.6 %collective-permute-done.9.refs_2_ = bf16[512,256]{1,0:T(8,128)(2,1)S(1)} collective-permute-done((bf16[512,256]{1,0:T(8,128)(2,1)S(1)}, bf16[512,256]{1,0:T(8,128)(2,1)S(1)}, u32[]{:S(2)}, u32[]{:S(2)}) %collective-permute-start.9) | collective-permute-done | bytes 262176 | tf_op jit(solution)/shard_map/ppermute | solution.py:330
  45.3 1.1 %middle.1 = (bf16[512,256]{1,0:T(8,128)(2,1)}, bf16[256,512]{1,0:T(8,128)(2,1)S(1)}, f32[256,256]{1,0:T(8,128)S(1)}) custom-call(f32[512,256]{1,0:T(8,128)S(1)} %forward_rows.5.refs_0_, bf16[512,256]{1,0:T(8,128)(2,1)S(1)} %collective-permute-done.7.refs_1_, bf16[512,256]{1,0:T(8,128)(2,1)S(1)} %collective-permute-done.9.refs_2_, ...), custom_call_target="tpu_custom_call" | custom-call | flops 201326592 | bytes 1310720 | tf_op jit(solution)/shard_map/middle/pallas_call | solution.py:166
  46.4 2.1 %collective-permute-start.11 = (bf16[256,512]{1,0:T(8,128)(2,1)S(1)}, bf16[256,512]{1,0:T(8,128)(2,1)S(1)}, u32[]{:S(2)}, u32[]{:S(2)}) collective-permute-start(bf16[256,512]{1,0:T(8,128)(2,1)S(1)} %get-tuple-element.30.refs_0_), channel_id=1, source_target_pairs={{0,2},{1,3},{2,0},{3,1},{4,6},{5,7},{6,4},{7,5},{8,10},{9,11},{10,... | collective-permute-start | bytes 786440 | tf_op jit(solution)/shard_map/ppermute | solution.py:330
  48.6 10.0 %all_gather.3.values_ref = bf16[1024,256]{1,0:T(8,128)(2,1)S(1)} all-gather(bf16[256,256]{1,0:T(8,128)(2,1)S(1)} %add_convert_fusion.2), channel_id=1, replica_groups={{0,8,16,24},{4,12,20,28},{1,9,17,25},{5,13,21,29},{2,10,18,26},{6,14,22..., dimensions={0}, use_global_device_ids=true | all-gather | bytes 655360 | tf_op jit(solution)/shard_map/all_gather | solution.py:372
  59.7 2.0 %collective-permute-done.11.refs_1_ = bf16[256,512]{1,0:T(8,128)(2,1)S(1)} collective-permute-done((bf16[256,512]{1,0:T(8,128)(2,1)S(1)}, bf16[256,512]{1,0:T(8,128)(2,1)S(1)}, u32[]{:S(2)}, u32[]{:S(2)}) %collective-permute-start.11) | collective-permute-done | bytes 262176 | tf_op jit(solution)/shard_map/ppermute | solution.py:330
  62.4 1.3 %collective-permute-start.16 = (bf16[256,512]{1,0:T(8,128)(2,1)S(1)}, bf16[256,512]{1,0:T(8,128)(2,1)S(1)}, u32[]{:S(2)}, u32[]{:S(2)}) collective-permute-start(bf16[256,512]{1,0:T(8,128)(2,1)S(1)} %get-tuple-element.34.refs_5_), channel_id=1, source_target_pairs={{1,0},{2,3},{5,4},{6,7},{9,8},{10,11},{13,12},{14,15},{17,16},{18,... | collective-permute-start | bytes 786440 | tf_op jit(solution)/shard_map/ppermute | solution.py:378
  63.7 2.7 %collective-permute-start.13 = (bf16[128,256]{1,0:T(8,128)(2,1)S(1)}, bf16[128,256]{1,0:T(8,128)(2,1)S(1)}, u32[]{:S(2)}, u32[]{:S(2)}) collective-permute-start(bf16[128,256]{1,0:T(8,128)(2,1)S(1)} %get-tuple-element.32.refs_0_), channel_id=1, source_target_pairs={{0,1},{1,0},{2,3},{3,2},{4,5},{5,4},{6,7},{7,6},{8,9},{9,8},{10,11... | collective-permute-start | bytes 196616 | tf_op jit(solution)/shard_map/ppermute | solution.py:330
  66.4 4.0 %backward_cols.3.refs_2_ = f32[8,256,512]{2,1,0:T(8,128)S(1)} custom-call(s32[2]{0:T(128)S(1)} %pad_add_fusion.where, bf16[512,4096]{1,0:T(8,128)(2,1)S(1)} %get-tuple-element.21.refs_6_.a_ref.refs_0_, bf16[512,4096]{1,0:T(8,128)(2,1)S(1)} %get-tuple-element.25.refs_5_.a_ref.refs_1_, bf16[512,4096]{1,0:T(8,128)(2,1)S(1)} %get-tuple-element.24.refs_4_.a_ref.refs_2_, ...), custom_call_target="tpu_custom_call" | custom-call | tf_op jit(solution)/shard_map/backward_cols/pallas_call | solution.py:197
  70.4 3.2 %collective-permute-done.13.refs_1_ = bf16[128,256]{1,0:T(8,128)(2,1)S(1)} collective-permute-done((bf16[128,256]{1,0:T(8,128)(2,1)S(1)}, bf16[128,256]{1,0:T(8,128)(2,1)S(1)}, u32[]{:S(2)}, u32[]{:S(2)}) %collective-permute-start.13) | collective-permute-done | bytes 65568 | tf_op jit(solution)/shard_map/ppermute | solution.py:330
  73.7 1.3 %backward_cols.5 = bf16[4,256,512]{2,1,0:T(8,128)(2,1)S(1)} custom-call(s32[2]{0:T(128)S(1)} %pad_add_fusion.where, bf16[512,4096]{1,0:T(8,128)(2,1)S(1)} %get-tuple-element.23.refs_3_.a_ref.refs_0_, bf16[256,512]{1,0:T(8,128)(2,1)S(1)} %add.14.refs_1_, f32[8,256,512]{2,1,0:T(8,128)S(1)} %backward_cols.3.refs_2_, bf16[128,256]{1,0:T(8,128)(2,1)S(1)} %total.2.refs_3_.refs_0_), custom_call_target="tpu_custom_call" | custom-call | tf_op jit(solution)/shard_map/backward_cols/pallas_call | solution.py:197
  75.1 1.3 %backward_cols.4.kept_ref = f32[4,256,512]{2,1,0:T(8,128)S(1)} custom-call(s32[2]{0:T(128)S(1)} %pad_add_fusion.where, bf16[512,4096]{1,0:T(8,128)(2,1)S(1)} %get-tuple-element.23.refs_3_.a_ref.refs_0_, bf16[256,512]{1,0:T(8,128)(2,1)S(1)} %add.14.refs_1_, f32[8,256,512]{2,1,0:T(8,128)S(1)} %backward_cols.3.refs_2_), custom_call_target="tpu_custom_call" | custom-call | tf_op jit(solution)/shard_map/backward_cols/pallas_call | solution.py:197
  76.3 1.4 %collective-permute-done.18.came_ref = bf16[4,256,512]{2,1,0:T(8,128)(2,1)S(1)} collective-permute-done((bf16[4,256,512]{2,1,0:T(8,128)(2,1)S(1)}, bf16[4,256,512]{2,1,0:T(8,128)(2,1)S(1)}, u32[]{:S(2)}, u32[]{:S(2)}) %collective-permute-start.18) | collective-permute-done | bytes 1048608 | tf_op jit(solution)/shard_map/ppermute | solution.py:330
  78.4 1.6 %collective-permute-start.19 = (bf16[256,512]{1,0:T(8,128)(2,1)S(1)}, bf16[256,512]{1,0:T(8,128)(2,1)S(1)}, u32[]{:S(2)}, u32[]{:S(2)}) collective-permute-start(bf16[256,512]{1,0:T(8,128)(2,1)S(1)} %get-tuple-element.36), channel_id=1, source_target_pairs={{0,8},{4,20},{8,0},{12,28},{16,24},{20,4},{24,16},{28,12},{1,9},{5... | collective-permute-start | bytes 786440 | tf_op jit(solution)/shard_map/ppermute | solution.py:397
  80.5 4.3 %collective-permute-done.19 = bf16[256,512]{1,0:T(8,128)(2,1)S(1)} collective-permute-done((bf16[256,512]{1,0:T(8,128)(2,1)S(1)}, bf16[256,512]{1,0:T(8,128)(2,1)S(1)}, u32[]{:S(2)}, u32[]{:S(2)}) %collective-permute-start.19) | collective-permute-done | bytes 262176 | tf_op jit(solution)/shard_map/ppermute | solution.py:397
  84.9 1.5 %collective-permute-start.23 = (bf16[256,512]{1,0:T(8,128)(2,1)S(1)}, bf16[256,512]{1,0:T(8,128)(2,1)S(1)}, u32[]{:S(2)}, u32[]{:S(2)}) collective-permute-start(bf16[256,512]{1,0:T(8,128)(2,1)S(1)} %add_convert_fusion.refs_2_), channel_id=1, source_target_pairs={{0,16},{4,12},{8,24},{12,4},{16,0},{20,28},{24,8},{28,20},{1,17},{... | collective-permute-start | bytes 786440 | tf_op jit(solution)/shard_map/ppermute | solution.py:400
  86.5 1.2 %collective-permute-done.20.refs_1_.refs_0_ = f32[64,256]{1,0:T(8,128)S(1)} collective-permute-done((f32[64,256]{1,0:T(8,128)S(1)}, f32[64,256]{1,0:T(8,128)S(1)}, u32[]{:S(2)}, u32[]{:S(2)}) %collective-permute-start.20) | collective-permute-done | bytes 65568 | tf_op jit(solution)/shard_map/ppermute | solution.py:330
  88.0 1.1 %collective-permute-done.21.refs_1_ = f32[64,256]{1,0:T(8,128)S(1)} collective-permute-done((f32[64,256]{1,0:T(8,128)S(1)}, f32[64,256]{1,0:T(8,128)S(1)}, u32[]{:S(2)}, u32[]{:S(2)}) %collective-permute-start.21) | collective-permute-done | bytes 65568 | tf_op jit(solution)/shard_map/ppermute | solution.py:330
  89.0 1.3 %join.1 = f32[256,256]{1,0:T(8,128)} custom-call(s32[2]{0:T(128)S(1)} %pad_add_fusion.where, f32[128,256]{1,0:T(8,128)S(1)} %total.3.own_ref, f32[64,256]{1,0:T(8,128)S(1)} %collective-permute-done.20.refs_1_.refs_0_, f32[64,256]{1,0:T(8,128)S(1)} %collective-permute-done.21.refs_1_), custom_call_target="tpu_custom_call" | custom-call | tf_op jit(solution)/shard_map/join/pallas_call | solution.py:319
  90.3 1.1 %collective-permute-done.23.refs_2_ = bf16[256,512]{1,0:T(8,128)(2,1)S(1)} collective-permute-done((bf16[256,512]{1,0:T(8,128)(2,1)S(1)}, bf16[256,512]{1,0:T(8,128)(2,1)S(1)}, u32[]{:S(2)}, u32[]{:S(2)}) %collective-permute-start.23) | collective-permute-done | bytes 262176 | tf_op jit(solution)/shard_map/ppermute | solution.py:400
  (46 shorter events, 6.2 us)
Async XLA Ops:
  0.6 12.4 %collective-permute-start.1 = (bf16[512,256]{1,0:T(8,128)(2,1)}, bf16[512,256]{1,0:T(8,128)(2,1)S(1)}, u32[]{:S(2)}, u32[]{:S(2)}) collective-permute-start(bf16[512,256]{1,0:T(8,128)(2,1)} %features_ref.1), channel_id=1, source_target_pairs={{0,24},{4,28},{8,16},{12,20},{16,8},{20,12},{24,0},{28,4},{1,25},{... | collective-permute-start | bytes 786440 | tf_op jit(solution)/shard_map/ppermute | solution.py:330
  4.6 12.4 %collective-permute-start.3 = (bf16[512,256]{1,0:T(8,128)(2,1)}, bf16[512,256]{1,0:T(8,128)(2,1)S(1)}, u32[]{:S(2)}, u32[]{:S(2)}) collective-permute-start(bf16[512,256]{1,0:T(8,128)(2,1)} %features_ref.1), channel_id=1, source_target_pairs={{0,8},{4,12},{8,0},{12,4},{16,24},{20,28},{24,16},{28,20},{1,9},{5... | collective-permute-start | bytes 786440 | tf_op jit(solution)/shard_map/ppermute | solution.py:330
  5.1 11.9 %collective-permute-start.2 = (bf16[512,256]{1,0:T(8,128)(2,1)}, bf16[512,256]{1,0:T(8,128)(2,1)S(1)}, u32[]{:S(2)}, u32[]{:S(2)}) collective-permute-start(bf16[512,256]{1,0:T(8,128)(2,1)} %features_ref.1), channel_id=1, source_target_pairs={{0,16},{4,20},{8,24},{12,28},{16,0},{20,4},{24,8},{28,12},{1,17},{... | collective-permute-start | bytes 786440 | tf_op jit(solution)/shard_map/ppermute | solution.py:330
  5.2 13.6 %collective-permute-start = (bf16[512,256]{1,0:T(8,128)(2,1)}, bf16[512,256]{1,0:T(8,128)(2,1)S(1)}, u32[]{:S(2)}, u32[]{:S(2)}) collective-permute-start(bf16[512,256]{1,0:T(8,128)(2,1)} %features_ref.1), channel_id=1, source_target_pairs={{0,4},{4,0},{8,12},{12,8},{16,20},{20,16},{24,28},{28,24},{1,5},{5... | collective-permute-start | bytes 786440 | tf_op jit(solution)/shard_map/ppermute | solution.py:330
  17.0 1.8 %collective-permute-start.4 = (bf16[512,256]{1,0:T(8,128)(2,1)S(1)}, bf16[512,256]{1,0:T(8,128)(2,1)S(1)}, u32[]{:S(2)}, u32[]{:S(2)}) collective-permute-start(bf16[512,256]{1,0:T(8,128)(2,1)S(1)} %get-tuple-element.26.refs_2_.refs_1_), channel_id=1, source_target_pairs={{0,4},{4,0},{8,12},{12,8},{16,20},{20,16},{24,28},{28,24},{1,5},{5... | collective-permute-start | bytes 786440 | tf_op jit(solution)/shard_map/ppermute | solution.py:330
  17.0 1.9 %collective-permute-start.5 = (bf16[512,256]{1,0:T(8,128)(2,1)S(1)}, bf16[512,256]{1,0:T(8,128)(2,1)S(1)}, u32[]{:S(2)}, u32[]{:S(2)}) collective-permute-start(bf16[512,256]{1,0:T(8,128)(2,1)S(1)} %get-tuple-element.27.refs_4_.refs_2_), channel_id=1, source_target_pairs={{0,4},{4,0},{8,12},{12,8},{16,20},{20,16},{24,28},{28,24},{1,5},{5... | collective-permute-start | bytes 786440 | tf_op jit(solution)/shard_map/ppermute | solution.py:330
  17.5 1.8 %collective-permute-start.6 = (bf16[512,256]{1,0:T(8,128)(2,1)S(1)}, bf16[512,256]{1,0:T(8,128)(2,1)S(1)}, u32[]{:S(2)}, u32[]{:S(2)}) collective-permute-start(bf16[512,256]{1,0:T(8,128)(2,1)S(1)} %get-tuple-element.28.refs_6_.refs_3_), channel_id=1, source_target_pairs={{0,4},{4,0},{8,12},{12,8},{16,20},{20,16},{24,28},{28,24},{1,5},{5... | collective-permute-start | bytes 786440 | tf_op jit(solution)/shard_map/ppermute | solution.py:330
  20.6 10.3 %collective-permute-start.8 = (bf16[512,256]{1,0:T(8,128)(2,1)S(1)}, bf16[512,256]{1,0:T(8,128)(2,1)S(1)}, u32[]{:S(2)}, u32[]{:S(2)}) collective-permute-start(bf16[512,256]{1,0:T(8,128)(2,1)S(1)} %forward_rows.7), channel_id=1, source_target_pairs={{0,1},{3,2},{4,5},{7,6},{8,9},{11,10},{12,13},{15,14},{16,17},{19,... | collective-permute-start | bytes 786440 | tf_op jit(solution)/shard_map/ppermute | solution.py:360
  24.1 15.7 %collective-permute-start.7 = (bf16[512,256]{1,0:T(8,128)(2,1)S(1)}, bf16[512,256]{1,0:T(8,128)(2,1)S(1)}, u32[]{:S(2)}, u32[]{:S(2)}) collective-permute-start(bf16[512,256]{1,0:T(8,128)(2,1)S(1)} %forward_rows.7), channel_id=1, source_target_pairs={{1,2},{2,1},{5,6},{6,5},{9,10},{10,9},{13,14},{14,13},{17,18},{18,... | collective-permute-start | bytes 786440 | tf_op jit(solution)/shard_map/ppermute | solution.py:361
  26.8 13.0 %collective-permute-start.10 = (bf16[512,256]{1,0:T(8,128)(2,1)S(1)}, bf16[512,256]{1,0:T(8,128)(2,1)S(1)}, u32[]{:S(2)}, u32[]{:S(2)}) collective-permute-start(bf16[512,256]{1,0:T(8,128)(2,1)S(1)} %forward_rows.9), channel_id=1, source_target_pairs={{0,1},{1,0},{2,3},{3,2},{4,5},{5,4},{6,7},{7,6},{8,9},{9,8},{10,11... | collective-permute-start | bytes 786440 | tf_op jit(solution)/shard_map/ppermute | solution.py:330
  30.8 14.5 %copy-start = (bf16[512,256]{1,0:T(8,128)(2,1)S(1)}, bf16[512,256]{1,0:T(8,128)(2,1)}, u32[]{:S(2)}) copy-start(bf16[512,256]{1,0:T(8,128)(2,1)} %refs_5_.1) | copy-start | bytes 786436
  30.8 14.5 %copy-start.1 = (bf16[256,256]{1,0:T(8,128)(2,1)S(1)}, bf16[256,256]{1,0:T(8,128)(2,1)}, u32[]{:S(2)}) copy-start(bf16[256,256]{1,0:T(8,128)(2,1)} %refs_4_.1) | copy-start | bytes 393220
  30.9 14.4 %collective-permute-start.9 = (bf16[512,256]{1,0:T(8,128)(2,1)S(1)}, bf16[512,256]{1,0:T(8,128)(2,1)S(1)}, u32[]{:S(2)}, u32[]{:S(2)}) collective-permute-start(bf16[512,256]{1,0:T(8,128)(2,1)S(1)} %add_convert_fusion.1), channel_id=1, source_target_pairs={{0,2},{1,3},{2,0},{3,1},{4,6},{5,7},{6,4},{7,5},{8,10},{9,11},{10,... | collective-permute-start | bytes 786440 | tf_op jit(solution)/shard_map/ppermute | solution.py:330
  46.4 2.1 %collective-permute-start.12 = (f32[256,256]{1,0:T(8,128)S(1)}, f32[256,256]{1,0:T(8,128)S(1)}, u32[]{:S(2)}, u32[]{:S(2)}) collective-permute-start(f32[256,256]{1,0:T(8,128)S(1)} %get-tuple-element.31), channel_id=1, source_target_pairs={{0,4},{4,0},{8,12},{12,8},{16,20},{20,16},{24,28},{28,24},{1,5},{5... | collective-permute-start | bytes 786440 | tf_op jit(solution)/shard_map/ppermute | solution.py:330
  46.4 13.3 %collective-permute-start.17 = (bf16[256,512]{1,0:T(8,128)(2,1)S(1)}, bf16[256,512]{1,0:T(8,128)(2,1)S(1)}, u32[]{:S(2)}, u32[]{:S(2)}) collective-permute-start(bf16[256,512]{1,0:T(8,128)(2,1)S(1)} %get-tuple-element.30.refs_0_), channel_id=1, source_target_pairs={{0,1},{1,0},{2,3},{3,2},{4,5},{5,4},{6,7},{7,6},{8,9},{9,8},{10,11... | collective-permute-start | bytes 786440 | tf_op jit(solution)/shard_map/ppermute | solution.py:330
  46.4 15.3 %collective-permute-start.11 = (bf16[256,512]{1,0:T(8,128)(2,1)S(1)}, bf16[256,512]{1,0:T(8,128)(2,1)S(1)}, u32[]{:S(2)}, u32[]{:S(2)}) collective-permute-start(bf16[256,512]{1,0:T(8,128)(2,1)S(1)} %get-tuple-element.30.refs_0_), channel_id=1, source_target_pairs={{0,2},{1,3},{2,0},{3,1},{4,6},{5,7},{6,4},{7,5},{8,10},{9,11},{10,... | collective-permute-start | bytes 786440 | tf_op jit(solution)/shard_map/ppermute | solution.py:330
  61.7 11.9 %collective-permute-start.15 = (bf16[256,512]{1,0:T(8,128)(2,1)S(1)}, bf16[256,512]{1,0:T(8,128)(2,1)S(1)}, u32[]{:S(2)}, u32[]{:S(2)}) collective-permute-start(bf16[256,512]{1,0:T(8,128)(2,1)S(1)} %get-tuple-element.33.refs_3_), channel_id=1, source_target_pairs={{1,2},{2,1},{5,6},{6,5},{9,10},{10,9},{13,14},{14,13},{17,18},{18,... | collective-permute-start | bytes 786440 | tf_op jit(solution)/shard_map/ppermute | solution.py:377
  62.4 11.3 %collective-permute-start.16 = (bf16[256,512]{1,0:T(8,128)(2,1)S(1)}, bf16[256,512]{1,0:T(8,128)(2,1)S(1)}, u32[]{:S(2)}, u32[]{:S(2)}) collective-permute-start(bf16[256,512]{1,0:T(8,128)(2,1)S(1)} %get-tuple-element.34.refs_5_), channel_id=1, source_target_pairs={{1,0},{2,3},{5,4},{6,7},{9,8},{10,11},{13,12},{14,15},{17,16},{18,... | collective-permute-start | bytes 786440 | tf_op jit(solution)/shard_map/ppermute | solution.py:378
  63.7 9.9 %collective-permute-start.13 = (bf16[128,256]{1,0:T(8,128)(2,1)S(1)}, bf16[128,256]{1,0:T(8,128)(2,1)S(1)}, u32[]{:S(2)}, u32[]{:S(2)}) collective-permute-start(bf16[128,256]{1,0:T(8,128)(2,1)S(1)} %get-tuple-element.32.refs_0_), channel_id=1, source_target_pairs={{0,1},{1,0},{2,3},{3,2},{4,5},{5,4},{6,7},{7,6},{8,9},{9,8},{10,11... | collective-permute-start | bytes 196616 | tf_op jit(solution)/shard_map/ppermute | solution.py:330
  75.0 2.7 %collective-permute-start.18 = (bf16[4,256,512]{2,1,0:T(8,128)(2,1)S(1)}, bf16[4,256,512]{2,1,0:T(8,128)(2,1)S(1)}, u32[]{:S(2)}, u32[]{:S(2)}) collective-permute-start(bf16[4,256,512]{2,1,0:T(8,128)(2,1)S(1)} %backward_cols.5), channel_id=1, source_target_pairs={{0,4},{4,0},{8,12},{12,8},{16,20},{20,16},{24,28},{28,24},{1,5},{5... | collective-permute-start | bytes 3145736 | tf_op jit(solution)/shard_map/ppermute | solution.py:330
  78.4 6.4 %collective-permute-start.19 = (bf16[256,512]{1,0:T(8,128)(2,1)S(1)}, bf16[256,512]{1,0:T(8,128)(2,1)S(1)}, u32[]{:S(2)}, u32[]{:S(2)}) collective-permute-start(bf16[256,512]{1,0:T(8,128)(2,1)S(1)} %get-tuple-element.36), channel_id=1, source_target_pairs={{0,8},{4,20},{8,0},{12,28},{16,24},{20,4},{24,16},{28,12},{1,9},{5... | collective-permute-start | bytes 786440 | tf_op jit(solution)/shard_map/ppermute | solution.py:397
  80.0 6.4 %collective-permute-start.14 = (bf16[128,256]{1,0:T(8,128)(2,1)S(1)}, bf16[128,256]{1,0:T(8,128)(2,1)S(1)}, u32[]{:S(2)}, u32[]{:S(2)}) collective-permute-start(bf16[128,256]{1,0:T(8,128)(2,1)S(1)} %total.2.refs_3_.refs_0_), channel_id=1, source_target_pairs={{0,2},{1,3},{2,0},{3,1},{4,6},{5,7},{6,4},{7,5},{8,10},{9,11},{10,... | collective-permute-start | bytes 196616 | tf_op jit(solution)/shard_map/ppermute | solution.py:330
  80.0 10.3 %collective-permute-start.22 = (bf16[256,512]{1,0:T(8,128)(2,1)S(1)}, bf16[256,512]{1,0:T(8,128)(2,1)S(1)}, u32[]{:S(2)}, u32[]{:S(2)}) collective-permute-start(bf16[256,512]{1,0:T(8,128)(2,1)S(1)} %get-tuple-element.38), channel_id=1, source_target_pairs={{0,8},{4,20},{8,0},{12,28},{16,24},{20,4},{24,16},{28,12},{1,9},{5... | collective-permute-start | bytes 786440 | tf_op jit(solution)/shard_map/ppermute | solution.py:400
  84.9 6.4 %collective-permute-start.23 = (bf16[256,512]{1,0:T(8,128)(2,1)S(1)}, bf16[256,512]{1,0:T(8,128)(2,1)S(1)}, u32[]{:S(2)}, u32[]{:S(2)}) collective-permute-start(bf16[256,512]{1,0:T(8,128)(2,1)S(1)} %add_convert_fusion.refs_2_), channel_id=1, source_target_pairs={{0,16},{4,12},{8,24},{12,4},{16,0},{20,28},{24,8},{28,20},{1,17},{... | collective-permute-start | bytes 786440 | tf_op jit(solution)/shard_map/ppermute | solution.py:400
  86.5 1.3 %collective-permute-start.20 = (f32[64,256]{1,0:T(8,128)S(1)}, f32[64,256]{1,0:T(8,128)S(1)}, u32[]{:S(2)}, u32[]{:S(2)}) collective-permute-start(f32[64,256]{1,0:T(8,128)S(1)} %get-tuple-element.40), channel_id=1, source_target_pairs={{0,4},{4,0},{8,12},{12,8},{16,20},{20,16},{24,28},{28,24},{1,5},{5... | collective-permute-start | bytes 196616 | tf_op jit(solution)/shard_map/ppermute | solution.py:330
  87.8 1.3 %collective-permute-start.21 = (f32[64,256]{1,0:T(8,128)S(1)}, f32[64,256]{1,0:T(8,128)S(1)}, u32[]{:S(2)}, u32[]{:S(2)}) collective-permute-start(f32[64,256]{1,0:T(8,128)S(1)} %gate.5), channel_id=1, source_target_pairs={{0,4},{4,0},{8,12},{12,8},{16,20},{20,16},{24,28},{28,24},{1,5},{5... | collective-permute-start | bytes 196616 | tf_op jit(solution)/shard_map/ppermute | solution.py:330

commit v16 on v15

--- a/solution.py
+++ b/solution.py
@@ -176,56 +176,55 @@
     )(*parts, weight, upstream)
 
 
-def backward_kernel(where, *refs, count, steps, before):
+def backward_kernel(where, *refs, count, groups, before):
     dense, pieces = refs[:count], refs[count : 2 * count]
-    out_ref = refs[-1]
-    depth = out_ref.shape[2]
-
-    for j, step in enumerate(steps):
-        cols = pl.ds(pl.multiple_of((where[0] ^ step) * depth, depth), depth)
-        value = refs[2 * count][step] if before else None
-        for a_ref, piece in zip(dense, pieces):
-            part = jnp.dot(piece[...], a_ref[:, cols], preferred_element_type=jnp.float32)
-            value = part if value is None else value + part
-        out_ref[j] = value.astype(out_ref.dtype)
-
-
-def backward(where, dense, pieces, steps, depth, before, kind, after=()):
+    outs = refs[-len(groups) :]
+    depth = outs[0].shape[2]
+
+    for out_ref, steps in zip(outs, groups):
+        for j, step in enumerate(steps):
+            cols = pl.ds(pl.multiple_of((where[0] ^ step) * depth, depth), depth)
+            value = refs[2 * count][step] if before else None
+            for a_ref, piece in zip(dense, pieces):
+                part = jnp.dot(piece[...], a_ref[:, cols], preferred_element_type=jnp.float32)
+                value = part if value is None else value + part
+            out_ref[j] = value.astype(out_ref.dtype)
+
+
+def backward(where, dense, pieces, groups, depth, before, kind, after=()):
     count = len(pieces)
     width, _ = pieces[0].shape
     operands = [near(x) for x in [*dense, *pieces] + ([] if before is None else [before])]
     return pl.pallas_call(
-        functools.partial(backward_kernel, count=count, steps=steps, before=before is not None),
-        out_shape=pltpu.VMEM((len(steps), width, depth), kind),
+        functools.partial(backward_kernel, count=count, groups=groups, before=before is not None),
+        out_shape=[pltpu.VMEM((len(steps), width, depth), kind) for steps in groups],
         in_specs=[SCALARS] + [WHOLE] * len(operands) + [UNREAD] * len(after),
-        out_specs=WHOLE,
+        out_specs=[WHOLE] * len(groups),
         compiler_params=params(10),
         cost_estimate=cost(0, 0),
         name="backward_cols",
     )(where, *operands, *after)
 
 
-def meet_kernel(where, kept_ref, came_ref, *refs):
-    own_ref, corner_ref, first_ref, second_ref = refs[-4:]
+def meet_kernel(where, kept_ref, came_ref, own_ref, first_ref, second_ref):
     core = where[0] & 1
     own_ref[...] = kept_ref[0] + came_ref[0].astype(jnp.float32)
-    corner_ref[...] = (kept_ref[3] + came_ref[3].astype(jnp.float32)).astype(corner_ref.dtype)
     first_ref[...] = (kept_ref[1 + core] + came_ref[1 + core].astype(jnp.float32)).astype(first_ref.dtype)
     second_ref[...] = kept_ref[2 - core] + came_ref[2 - core].astype(jnp.float32)
 
 
-def meet(where, kept, came, after):
+def meet(where, kept, came):
     shape = kept.shape[1:]
-    kinds = [jnp.float32, came.dtype, came.dtype, jnp.float32]
+    kinds = [jnp.float32, came.dtype, jnp.float32]
     return pl.pallas_call(
         meet_kernel,
         out_shape=[pltpu.VMEM(shape, kind) for kind in kinds],
-        in_specs=[SCALARS, WHOLE, WHOLE] + [UNREAD] * len(after),
-        out_specs=[WHOLE] * 4,
+        in_specs=[SCALARS, WHOLE, WHOLE],
+        out_specs=[WHOLE] * len(kinds),
         compiler_params=params(10),
         cost_estimate=cost(0, 0),
         name="meet",
-    )(where, near(kept), near(came), *after)
+    )(where, near(kept), near(came))
 
 
 def finish_kernel(*refs):
@@ -382,24 +381,28 @@
 
     sums, latest = None, n_col - 1
     for group in [list(range(n_col - 1))]:
-        sums = backward(where, [dense[s] for s in group], [pieces[s] for s in group], every, depth, sums, jnp.float32)
+        sums = backward(where, [dense[s] for s in group], [pieces[s] for s in group], [every], depth, sums, jnp.float32)[0]
     for s in range(n_col.bit_length() - 2):
         part = total([part, swap(part, "col", n_col, 1 << s)], part.shape[0], jnp.bfloat16)
     last = functools.partial(backward, where, [dense[latest]], [pieces[latest]])
-    sent = last(every[1::2], depth, sums, jnp.bfloat16, [part])
-    kept = last(every[::2], depth, sums, jnp.float32)
-    came = swap(sent, "row", n_row, 1)
+    groups = [every[-2:], every[:-2]]
+    sent = last([group[1::2] for group in groups], depth, sums, jnp.bfloat16, [part])
+    kept = last([group[::2] for group in groups], depth, sums, jnp.float32)
+    came = [swap(block, "row", n_row, 1) for block in sent]
+    corner = kept[0][0] + came[0][0].astype(jnp.float32)
     after = []
     if chips == 4:
-        own, corner, first, second = meet(where, kept, came, [])
+        own, first, second = meet(where, kept[1], came[1])
         there = [(i, i ^ (2 if i % 2 == 0 else 4)) for i in range(n_row)]
         across = [(i, i ^ (4 if i % 2 == 0 else 2)) for i in range(n_row)]
-        corner = lax.ppermute(corner, "row", there)
+        corner = lax.ppermute(corner.astype(jnp.bfloat16), "row", there)
         second = (second + corner.astype(jnp.float32)).astype(jnp.bfloat16)
         after = [second]
+        first = gate([first], [])[0]
         parts = [lax.ppermute(first, "row", there), lax.ppermute(second, "row", across)]
     else:
-        own, *summed = [kept[c] + came[c].astype(jnp.float32) for c in range(chips)]
+        own, *summed = [kept[1][c] + came[1][c].astype(jnp.float32) for c in range(chips - 1)]
+        summed.append(corner)
         parts = [swap(summed[c - 1].astype(jnp.bfloat16), "row", n_row, 2 * c) for c in range(1, chips)]
 
     feature_grad = finish([own, *parts])

time: 92.5 us -> 91.8 us (level)
  waiting for transfers between devices: 28.4 us -> 27.3 us
    ppermute x17 -> x18, starting transfers between devices: 16 us -> 16.5 us  [swap(): return lax.ppermute(value, axis, [(i, i ^ step) for i in range(size)])]
    ppermute x17 -> x18, waiting for transfers between devices: 23 us -> 22.6 us  [swap(): return lax.ppermute(value, axis, [(i, i ^ step) for i in range(size)])]
  transfers between devices with their start and end apart: 24 -> 25, of which waited for: 13 -> 13; matrix products, arithmetic and copies ran while one was open for 0% -> 0% of each run, Pallas kernels for 23% -> 24%
where the time goes in v16:
time: 91.8 us; the launch traced here: 91.6 us
  waiting for transfers between devices  27.3 us (30%)
  Pallas kernels  26.6 us (29%)
  starting transfers between devices  26.4 us (29%)
  blocking collectives  10 us (11%)
    ppermute x18, waiting for transfers between devices, swap(): return lax.ppermute(value, axis, [(i, i ^ step) for i in range(size)])  22.6 us
    ppermute x18, starting transfers between devices, swap(): return lax.ppermute(value, axis, [(i, i ^ step) for i in range(size)])  16.5 us
    all_gather x1, blocking collectives, shards(): gathered = lax.all_gather(part, 'row', axis_index_groups=cores, tiled=True)  10 us
    pallas_call x5, Pallas kernels, forward(): pl.pallas_call(functools.partial(forward_kernel, steps=steps, before=bool...  7.94 us
    pallas_call x1, Pallas kernels, dense_rows(): pl.pallas_call(functools.partial(dense_kernel, steps=steps, window=window...  7.6 us
    pallas_call x3, Pallas kernels, backward(): pl.pallas_call(functools.partial(backward_kernel, count=count, groups=gro...  6.55 us
    ppermute x1, waiting for transfers between devices, shards(): corner = lax.ppermute(corner.astype(jnp.bfloat16), 'row', there)  3.59 us
    ppermute x1, starting transfers between devices, shards(): relayed = lax.ppermute(shares[3], 'col', [(0, 1), (3, 2)])  3.5 us
  transfers between devices with their start and end apart: 25, of which 13 were waited for; matrix products, arithmetic and copies ran while one was open for 0% of the time, Pallas kernels for 24%

profile of v16, /device:TPU:0, one launch (start us, length us, event | category | flops | bytes accessed | tf_op | source)
XLA Modules:
  0.0 91.6 jit_solution(2505970211959713862)
XLA Ops:
  0.6 4.0 %collective-permute-start.1 = (bf16[512,256]{1,0:T(8,128)(2,1)}, bf16[512,256]{1,0:T(8,128)(2,1)S(1)}, u32[]{:S(2)}, u32[]{:S(2)}) collective-permute-start(bf16[512,256]{1,0:T(8,128)(2,1)} %features_ref.1), channel_id=1, source_target_pairs={{0,24},{4,28},{8,16},{12,20},{16,8},{20,12},{24,0},{28,4},{1,25},{... | collective-permute-start | bytes 786440 | tf_op jit(solution)/shard_map/ppermute | solution.py:329
  5.3 7.6 %dense_rows.1 = (bf16[512,4096]{1,0:T(8,128)(2,1)S(1)}, bf16[512,4096]{1,0:T(8,128)(2,1)S(1)}, bf16[512,4096]{1,0:T(8,128)(2,1)S(1)}, bf16[512,4096]{1,0:T(8,128)(2,1)S(1)}, bf16[512,256]{1,0:T(8,128)(2,1)S(1)}) custom-call(s32[2]{0:T(128)S(1)} %pad_add_fusion.where, s32[16]{0:T(128)} %bitcast.9, s32[448]{0:T(512)} %bitcast.8, ...), custom_call_target="tpu_custom_call" | custom-call | bytes 41943040 | tf_op jit(solution)/shard_map/dense_rows/pallas_call | solution.py:102
  12.9 4.1 %collective-permute-done.3.refs_2_ = bf16[512,256]{1,0:T(8,128)(2,1)S(1)} collective-permute-done((bf16[512,256]{1,0:T(8,128)(2,1)}, bf16[512,256]{1,0:T(8,128)(2,1)S(1)}, u32[]{:S(2)}, u32[]{:S(2)}) %collective-permute-start.3) | collective-permute-done | bytes 262176 | tf_op jit(solution)/shard_map/ppermute | solution.py:329
  17.6 1.2 %forward_rows.6.refs_4_ = f32[512,256]{1,0:T(8,128)S(1)} custom-call(s32[2]{0:T(128)S(1)} %pad_add_fusion.where, bf16[512,4096]{1,0:T(8,128)(2,1)S(1)} %get-tuple-element.26.refs_3_.a_ref.refs_0_, bf16[512,256]{1,0:T(8,128)(2,1)S(1)} %get-tuple-element.25.refs_0_, bf16[512,256]{1,0:T(8,128)(2,1)S(1)} %get-tuple-element.29.refs_2_.refs_1_, ...), custom_call_target="tpu_custom_call" | custom-call | flops 1073741824 | bytes 4194304 | tf_op jit(solution)/shard_map/forward_rows/pallas_call | solution.py:133
  19.3 1.3 %forward_rows.7 = bf16[512,256]{1,0:T(8,128)(2,1)S(1)} custom-call(s32[2]{0:T(128)S(1)} %pad_add_fusion.where, bf16[512,4096]{1,0:T(8,128)(2,1)S(1)} %get-tuple-element.26.refs_3_.a_ref.refs_0_, bf16[512,256]{1,0:T(8,128)(2,1)S(1)} %collective-permute-done.refs_1_.refs_0_, bf16[512,256]{1,0:T(8,128)(2,1)S(1)} %collective-permute-done.4.refs_3_.refs_1_, ...), custom_call_target="tpu_custom_call" | custom-call | flops 1073741824 | bytes 4194304 | tf_op jit(solution)/shard_map/forward_rows/pallas_call | solution.py:133
  20.6 3.5 %collective-permute-start.8 = (bf16[512,256]{1,0:T(8,128)(2,1)S(1)}, bf16[512,256]{1,0:T(8,128)(2,1)S(1)}, u32[]{:S(2)}, u32[]{:S(2)}) collective-permute-start(bf16[512,256]{1,0:T(8,128)(2,1)S(1)} %forward_rows.7), channel_id=1, source_target_pairs={{0,1},{3,2},{4,5},{7,6},{8,9},{11,10},{12,13},{15,14},{16,17},{19,... | collective-permute-start | bytes 786440 | tf_op jit(solution)/shard_map/ppermute | solution.py:359
  24.1 0.9 collective-permute-start.7
  25.0 1.8 %forward_rows.9 = bf16[512,256]{1,0:T(8,128)(2,1)S(1)} custom-call(s32[2]{0:T(128)S(1)} %pad_add_fusion.where, bf16[512,4096]{1,0:T(8,128)(2,1)S(1)} %get-tuple-element.28.refs_5_.a_ref.refs_1_, bf16[512,256]{1,0:T(8,128)(2,1)S(1)} %get-tuple-element.25.refs_0_, bf16[512,256]{1,0:T(8,128)(2,1)S(1)} %collective-permute-done.refs_1_.refs_0_, ...), custom_call_target="tpu_custom_call" | custom-call | flops 1073741824 | bytes 4194304 | tf_op jit(solution)/shard_map/forward_rows/pallas_call | solution.py:133
  26.8 2.2 %collective-permute-start.10 = (bf16[512,256]{1,0:T(8,128)(2,1)S(1)}, bf16[512,256]{1,0:T(8,128)(2,1)S(1)}, u32[]{:S(2)}, u32[]{:S(2)}) collective-permute-start(bf16[512,256]{1,0:T(8,128)(2,1)S(1)} %forward_rows.9), channel_id=1, source_target_pairs={{0,1},{1,0},{2,3},{3,2},{4,5},{5,4},{6,7},{7,6},{8,9},{9,8},{10,11... | collective-permute-start | bytes 786440 | tf_op jit(solution)/shard_map/ppermute | solution.py:329
  29.0 1.8 %forward_rows.8 = bf16[512,256]{1,0:T(8,128)(2,1)S(1)} custom-call(s32[2]{0:T(128)S(1)} %pad_add_fusion.where, bf16[512,4096]{1,0:T(8,128)(2,1)S(1)} %get-tuple-element.27.refs_4_.a_ref.refs_2_, bf16[512,256]{1,0:T(8,128)(2,1)S(1)} %get-tuple-element.25.refs_0_, bf16[512,256]{1,0:T(8,128)(2,1)S(1)} %collective-permute-done.refs_1_.refs_0_, ...), custom_call_target="tpu_custom_call" | custom-call | flops 1073741824 | bytes 4194304 | tf_op jit(solution)/shard_map/forward_rows/pallas_call | solution.py:133
  30.9 3.4 %collective-permute-start.9 = (bf16[512,256]{1,0:T(8,128)(2,1)S(1)}, bf16[512,256]{1,0:T(8,128)(2,1)S(1)}, u32[]{:S(2)}, u32[]{:S(2)}) collective-permute-start(bf16[512,256]{1,0:T(8,128)(2,1)S(1)} %add_convert_fusion.2), channel_id=1, source_target_pairs={{0,2},{1,3},{2,0},{3,1},{4,6},{5,7},{6,4},{7,5},{8,10},{9,11},{10,... | collective-permute-start | bytes 786440 | tf_op jit(solution)/shard_map/ppermute | solution.py:329
  34.4 1.8 %forward_rows.5.refs_0_ = f32[512,256]{1,0:T(8,128)S(1)} custom-call(s32[2]{0:T(128)S(1)} %pad_add_fusion.where, bf16[512,4096]{1,0:T(8,128)(2,1)S(1)} %get-tuple-element.24.refs_6_.a_ref.refs_0_, bf16[512,256]{1,0:T(8,128)(2,1)S(1)} %get-tuple-element.25.refs_0_, bf16[512,256]{1,0:T(8,128)(2,1)S(1)} %collective-permute-done.refs_1_.refs_0_, ...), custom_call_target="tpu_custom_call" | custom-call | flops 1073741824 | bytes 4194304 | tf_op jit(solution)/shard_map/forward_rows/pallas_call | solution.py:133
  36.2 3.6 %collective-permute-done.10.refs_3_ = bf16[512,256]{1,0:T(8,128)(2,1)S(1)} collective-permute-done((bf16[512,256]{1,0:T(8,128)(2,1)S(1)}, bf16[512,256]{1,0:T(8,128)(2,1)S(1)}, u32[]{:S(2)}, u32[]{:S(2)}) %collective-permute-start.10) | collective-permute-done | bytes 262176 | tf_op jit(solution)/shard_map/ppermute | solution.py:329
  39.8 5.6 %collective-permute-done.9.refs_2_ = bf16[512,256]{1,0:T(8,128)(2,1)S(1)} collective-permute-done((bf16[512,256]{1,0:T(8,128)(2,1)S(1)}, bf16[512,256]{1,0:T(8,128)(2,1)S(1)}, u32[]{:S(2)}, u32[]{:S(2)}) %collective-permute-start.9) | collective-permute-done | bytes 262176 | tf_op jit(solution)/shard_map/ppermute | solution.py:329
  45.3 1.1 %middle.1 = (bf16[512,256]{1,0:T(8,128)(2,1)}, bf16[256,512]{1,0:T(8,128)(2,1)S(1)}, f32[256,256]{1,0:T(8,128)S(1)}) custom-call(f32[512,256]{1,0:T(8,128)S(1)} %forward_rows.5.refs_0_, bf16[512,256]{1,0:T(8,128)(2,1)S(1)} %collective-permute-done.7.refs_1_, bf16[512,256]{1,0:T(8,128)(2,1)S(1)} %collective-permute-done.9.refs_2_, ...), custom_call_target="tpu_custom_call" | custom-call | flops 201326592 | bytes 1310720 | tf_op jit(solution)/shard_map/middle/pallas_call | solution.py:166
  46.4 2.1 %collective-permute-start.11 = (bf16[256,512]{1,0:T(8,128)(2,1)S(1)}, bf16[256,512]{1,0:T(8,128)(2,1)S(1)}, u32[]{:S(2)}, u32[]{:S(2)}) collective-permute-start(bf16[256,512]{1,0:T(8,128)(2,1)S(1)} %get-tuple-element.33.refs_0_), channel_id=1, source_target_pairs={{0,2},{1,3},{2,0},{3,1},{4,6},{5,7},{6,4},{7,5},{8,10},{9,11},{10,... | collective-permute-start | bytes 786440 | tf_op jit(solution)/shard_map/ppermute | solution.py:329
  48.6 10.0 %all_gather.3.values_ref = bf16[1024,256]{1,0:T(8,128)(2,1)S(1)} all-gather(bf16[256,256]{1,0:T(8,128)(2,1)S(1)} %add_convert_fusion.3), channel_id=1, replica_groups={{0,8,16,24},{4,12,20,28},{1,9,17,25},{5,13,21,29},{2,10,18,26},{6,14,22..., dimensions={0}, use_global_device_ids=true | all-gather | bytes 655360 | tf_op jit(solution)/shard_map/all_gather | solution.py:371
  59.7 2.0 %collective-permute-done.11.refs_1_ = bf16[256,512]{1,0:T(8,128)(2,1)S(1)} collective-permute-done((bf16[256,512]{1,0:T(8,128)(2,1)S(1)}, bf16[256,512]{1,0:T(8,128)(2,1)S(1)}, u32[]{:S(2)}, u32[]{:S(2)}) %collective-permute-start.11) | collective-permute-done | bytes 262176 | tf_op jit(solution)/shard_map/ppermute | solution.py:329
  62.4 1.3 %collective-permute-start.16 = (bf16[256,512]{1,0:T(8,128)(2,1)S(1)}, bf16[256,512]{1,0:T(8,128)(2,1)S(1)}, u32[]{:S(2)}, u32[]{:S(2)}) collective-permute-start(bf16[256,512]{1,0:T(8,128)(2,1)S(1)} %get-tuple-element.37.refs_5_), channel_id=1, source_target_pairs={{1,0},{2,3},{5,4},{6,7},{9,8},{10,11},{13,12},{14,15},{17,16},{18,... | collective-permute-start | bytes 786440 | tf_op jit(solution)/shard_map/ppermute | solution.py:377
  63.7 2.7 %collective-permute-start.13 = (bf16[128,256]{1,0:T(8,128)(2,1)S(1)}, bf16[128,256]{1,0:T(8,128)(2,1)S(1)}, u32[]{:S(2)}, u32[]{:S(2)}) collective-permute-start(bf16[128,256]{1,0:T(8,128)(2,1)S(1)} %get-tuple-element.35.refs_0_), channel_id=1, source_target_pairs={{0,1},{1,0},{2,3},{3,2},{4,5},{5,4},{6,7},{7,6},{8,9},{9,8},{10,11... | collective-permute-start | bytes 196616 | tf_op jit(solution)/shard_map/ppermute | solution.py:329
  66.4 4.0 %backward_cols.3.refs_2_ = f32[8,256,512]{2,1,0:T(8,128)S(1)} custom-call(s32[2]{0:T(128)S(1)} %pad_add_fusion.where, bf16[512,4096]{1,0:T(8,128)(2,1)S(1)} %get-tuple-element.24.refs_6_.a_ref.refs_0_, bf16[512,4096]{1,0:T(8,128)(2,1)S(1)} %get-tuple-element.28.refs_5_.a_ref.refs_1_, bf16[512,4096]{1,0:T(8,128)(2,1)S(1)} %get-tuple-element.27.refs_4_.a_ref.refs_2_, ...), custom_call_target="tpu_custom_call" | custom-call | tf_op jit(solution)/shard_map/backward_cols/pallas_call | solution.py:198
  70.4 3.2 %collective-permute-done.13.refs_1_ = bf16[128,256]{1,0:T(8,128)(2,1)S(1)} collective-permute-done((bf16[128,256]{1,0:T(8,128)(2,1)S(1)}, bf16[128,256]{1,0:T(8,128)(2,1)S(1)}, u32[]{:S(2)}, u32[]{:S(2)}) %collective-permute-start.13) | collective-permute-done | bytes 65568 | tf_op jit(solution)/shard_map/ppermute | solution.py:329
  73.7 1.3 %backward_cols.5 = (bf16[1,256,512]{2,1,0:T(8,128)(2,1)S(1)}, bf16[3,256,512]{2,1,0:T(8,128)(2,1)S(1)}) custom-call(s32[2]{0:T(128)S(1)} %pad_add_fusion.where, bf16[512,4096]{1,0:T(8,128)(2,1)S(1)} %get-tuple-element.26.refs_3_.a_ref.refs_0_, bf16[256,512]{1,0:T(8,128)(2,1)S(1)} %add.18.refs_1_, f32[8,256,512]{2,1,0:T(8,128)S(1)} %backward_cols.3.refs_2_, ...), custom_call_target="tpu_custom_call" | custom-call | tf_op jit(solution)/shard_map/backward_cols/pallas_call | solution.py:198
  75.6 1.3 %backward_cols.4 = (f32[1,256,512]{2,1,0:T(8,128)S(1)}, f32[3,256,512]{2,1,0:T(8,128)S(1)}) custom-call(s32[2]{0:T(128)S(1)} %pad_add_fusion.where, bf16[512,4096]{1,0:T(8,128)(2,1)S(1)} %get-tuple-element.26.refs_3_.a_ref.refs_0_, bf16[256,512]{1,0:T(8,128)(2,1)S(1)} %add.18.refs_1_, f32[8,256,512]{2,1,0:T(8,128)S(1)} %backward_cols.3.refs_2_), custom_call_target="tpu_custom_call" | custom-call | tf_op jit(solution)/shard_map/backward_cols/pallas_call | solution.py:198
  76.8 0.9 collective-permute-done.19
  77.8 1.6 %collective-permute-start.20 = (bf16[256,512]{1,0:T(8,128)(2,1)S(1)}, bf16[256,512]{1,0:T(8,128)(2,1)S(1)}, u32[]{:S(2)}, u32[]{:S(2)}) collective-permute-start(bf16[256,512]{1,0:T(8,128)(2,1)S(1)} %fusion), channel_id=1, source_target_pairs={{0,8},{4,20},{8,0},{12,28},{16,24},{20,4},{24,16},{28,12},{1,9},{5... | collective-permute-start | bytes 786440 | tf_op jit(solution)/shard_map/ppermute | solution.py:398
  80.7 3.6 %collective-permute-done.20 = bf16[256,512]{1,0:T(8,128)(2,1)S(1)} collective-permute-done((bf16[256,512]{1,0:T(8,128)(2,1)S(1)}, bf16[256,512]{1,0:T(8,128)(2,1)S(1)}, u32[]{:S(2)}, u32[]{:S(2)}) %collective-permute-start.20) | collective-permute-done | bytes 262176 | tf_op jit(solution)/shard_map/ppermute | solution.py:398
  84.3 1.5 %collective-permute-start.24 = (bf16[256,512]{1,0:T(8,128)(2,1)S(1)}, bf16[256,512]{1,0:T(8,128)(2,1)S(1)}, u32[]{:S(2)}, u32[]{:S(2)}) collective-permute-start(bf16[256,512]{1,0:T(8,128)(2,1)S(1)} %add_convert_fusion.refs_2_), channel_id=1, source_target_pairs={{0,16},{4,12},{8,24},{12,4},{16,0},{20,28},{24,8},{28,20},{1,17},{... | collective-permute-start | bytes 786440 | tf_op jit(solution)/shard_map/ppermute | solution.py:402
  85.9 1.2 %collective-permute-done.21.refs_1_.refs_0_ = f32[64,256]{1,0:T(8,128)S(1)} collective-permute-done((f32[64,256]{1,0:T(8,128)S(1)}, f32[64,256]{1,0:T(8,128)S(1)}, u32[]{:S(2)}, u32[]{:S(2)}) %collective-permute-start.21) | collective-permute-done | bytes 65568 | tf_op jit(solution)/shard_map/ppermute | solution.py:329
  87.3 1.1 %collective-permute-done.22.refs_1_ = f32[64,256]{1,0:T(8,128)S(1)} collective-permute-done((f32[64,256]{1,0:T(8,128)S(1)}, f32[64,256]{1,0:T(8,128)S(1)}, u32[]{:S(2)}, u32[]{:S(2)}) %collective-permute-start.22) | collective-permute-done | bytes 65568 | tf_op jit(solution)/shard_map/ppermute | solution.py:329
  88.4 1.3 %join.1 = f32[256,256]{1,0:T(8,128)} custom-call(s32[2]{0:T(128)S(1)} %pad_add_fusion.where, f32[128,256]{1,0:T(8,128)S(1)} %total.3.own_ref, f32[64,256]{1,0:T(8,128)S(1)} %collective-permute-done.21.refs_1_.refs_0_, f32[64,256]{1,0:T(8,128)S(1)} %collective-permute-done.22.refs_1_), custom_call_target="tpu_custom_call" | custom-call | tf_op jit(solution)/shard_map/join/pallas_call | solution.py:318
  89.7 1.1 %collective-permute-done.24.refs_2_ = bf16[256,512]{1,0:T(8,128)(2,1)S(1)} collective-permute-done((bf16[256,512]{1,0:T(8,128)(2,1)S(1)}, bf16[256,512]{1,0:T(8,128)(2,1)S(1)}, u32[]{:S(2)}, u32[]{:S(2)}) %collective-permute-start.24) | collective-permute-done | bytes 262176 | tf_op jit(solution)/shard_map/ppermute | solution.py:402
  (50 shorter events, 6.8 us)
Async XLA Ops:
  0.6 12.3 %collective-permute-start.1 = (bf16[512,256]{1,0:T(8,128)(2,1)}, bf16[512,256]{1,0:T(8,128)(2,1)S(1)}, u32[]{:S(2)}, u32[]{:S(2)}) collective-permute-start(bf16[512,256]{1,0:T(8,128)(2,1)} %features_ref.1), channel_id=1, source_target_pairs={{0,24},{4,28},{8,16},{12,20},{16,8},{20,12},{24,0},{28,4},{1,25},{... | collective-permute-start | bytes 786440 | tf_op jit(solution)/shard_map/ppermute | solution.py:329
  4.6 12.4 %collective-permute-start.3 = (bf16[512,256]{1,0:T(8,128)(2,1)}, bf16[512,256]{1,0:T(8,128)(2,1)S(1)}, u32[]{:S(2)}, u32[]{:S(2)}) collective-permute-start(bf16[512,256]{1,0:T(8,128)(2,1)} %features_ref.1), channel_id=1, source_target_pairs={{0,8},{4,12},{8,0},{12,4},{16,24},{20,28},{24,16},{28,20},{1,9},{5... | collective-permute-start | bytes 786440 | tf_op jit(solution)/shard_map/ppermute | solution.py:329
  5.1 11.9 %collective-permute-start.2 = (bf16[512,256]{1,0:T(8,128)(2,1)}, bf16[512,256]{1,0:T(8,128)(2,1)S(1)}, u32[]{:S(2)}, u32[]{:S(2)}) collective-permute-start(bf16[512,256]{1,0:T(8,128)(2,1)} %features_ref.1), channel_id=1, source_target_pairs={{0,16},{4,20},{8,24},{12,28},{16,0},{20,4},{24,8},{28,12},{1,17},{... | collective-permute-start | bytes 786440 | tf_op jit(solution)/shard_map/ppermute | solution.py:329
  5.2 13.6 %collective-permute-start = (bf16[512,256]{1,0:T(8,128)(2,1)}, bf16[512,256]{1,0:T(8,128)(2,1)S(1)}, u32[]{:S(2)}, u32[]{:S(2)}) collective-permute-start(bf16[512,256]{1,0:T(8,128)(2,1)} %features_ref.1), channel_id=1, source_target_pairs={{0,4},{4,0},{8,12},{12,8},{16,20},{20,16},{24,28},{28,24},{1,5},{5... | collective-permute-start | bytes 786440 | tf_op jit(solution)/shard_map/ppermute | solution.py:329
  17.0 1.8 %collective-permute-start.4 = (bf16[512,256]{1,0:T(8,128)(2,1)S(1)}, bf16[512,256]{1,0:T(8,128)(2,1)S(1)}, u32[]{:S(2)}, u32[]{:S(2)}) collective-permute-start(bf16[512,256]{1,0:T(8,128)(2,1)S(1)} %get-tuple-element.29.refs_2_.refs_1_), channel_id=1, source_target_pairs={{0,4},{4,0},{8,12},{12,8},{16,20},{20,16},{24,28},{28,24},{1,5},{5... | collective-permute-start | bytes 786440 | tf_op jit(solution)/shard_map/ppermute | solution.py:329
  17.0 1.9 %collective-permute-start.5 = (bf16[512,256]{1,0:T(8,128)(2,1)S(1)}, bf16[512,256]{1,0:T(8,128)(2,1)S(1)}, u32[]{:S(2)}, u32[]{:S(2)}) collective-permute-start(bf16[512,256]{1,0:T(8,128)(2,1)S(1)} %get-tuple-element.30.refs_4_.refs_2_), channel_id=1, source_target_pairs={{0,4},{4,0},{8,12},{12,8},{16,20},{20,16},{24,28},{28,24},{1,5},{5... | collective-permute-start | bytes 786440 | tf_op jit(solution)/shard_map/ppermute | solution.py:329
  17.5 1.8 %collective-permute-start.6 = (bf16[512,256]{1,0:T(8,128)(2,1)S(1)}, bf16[512,256]{1,0:T(8,128)(2,1)S(1)}, u32[]{:S(2)}, u32[]{:S(2)}) collective-permute-start(bf16[512,256]{1,0:T(8,128)(2,1)S(1)} %get-tuple-element.31.refs_6_.refs_3_), channel_id=1, source_target_pairs={{0,4},{4,0},{8,12},{12,8},{16,20},{20,16},{24,28},{28,24},{1,5},{5... | collective-permute-start | bytes 786440 | tf_op jit(solution)/shard_map/ppermute | solution.py:329
  20.6 10.3 %collective-permute-start.8 = (bf16[512,256]{1,0:T(8,128)(2,1)S(1)}, bf16[512,256]{1,0:T(8,128)(2,1)S(1)}, u32[]{:S(2)}, u32[]{:S(2)}) collective-permute-start(bf16[512,256]{1,0:T(8,128)(2,1)S(1)} %forward_rows.7), channel_id=1, source_target_pairs={{0,1},{3,2},{4,5},{7,6},{8,9},{11,10},{12,13},{15,14},{16,17},{19,... | collective-permute-start | bytes 786440 | tf_op jit(solution)/shard_map/ppermute | solution.py:359
  24.1 15.7 %collective-permute-start.7 = (bf16[512,256]{1,0:T(8,128)(2,1)S(1)}, bf16[512,256]{1,0:T(8,128)(2,1)S(1)}, u32[]{:S(2)}, u32[]{:S(2)}) collective-permute-start(bf16[512,256]{1,0:T(8,128)(2,1)S(1)} %forward_rows.7), channel_id=1, source_target_pairs={{1,2},{2,1},{5,6},{6,5},{9,10},{10,9},{13,14},{14,13},{17,18},{18,... | collective-permute-start | bytes 786440 | tf_op jit(solution)/shard_map/ppermute | solution.py:360
  26.8 13.0 %collective-permute-start.10 = (bf16[512,256]{1,0:T(8,128)(2,1)S(1)}, bf16[512,256]{1,0:T(8,128)(2,1)S(1)}, u32[]{:S(2)}, u32[]{:S(2)}) collective-permute-start(bf16[512,256]{1,0:T(8,128)(2,1)S(1)} %forward_rows.9), channel_id=1, source_target_pairs={{0,1},{1,0},{2,3},{3,2},{4,5},{5,4},{6,7},{7,6},{8,9},{9,8},{10,11... | collective-permute-start | bytes 786440 | tf_op jit(solution)/shard_map/ppermute | solution.py:329
  30.8 14.5 %copy-start = (bf16[512,256]{1,0:T(8,128)(2,1)S(1)}, bf16[512,256]{1,0:T(8,128)(2,1)}, u32[]{:S(2)}) copy-start(bf16[512,256]{1,0:T(8,128)(2,1)} %refs_5_.1) | copy-start | bytes 786436
  30.8 14.5 %copy-start.1 = (bf16[256,256]{1,0:T(8,128)(2,1)S(1)}, bf16[256,256]{1,0:T(8,128)(2,1)}, u32[]{:S(2)}) copy-start(bf16[256,256]{1,0:T(8,128)(2,1)} %refs_4_.1) | copy-start | bytes 393220
  30.9 14.4 %collective-permute-start.9 = (bf16[512,256]{1,0:T(8,128)(2,1)S(1)}, bf16[512,256]{1,0:T(8,128)(2,1)S(1)}, u32[]{:S(2)}, u32[]{:S(2)}) collective-permute-start(bf16[512,256]{1,0:T(8,128)(2,1)S(1)} %add_convert_fusion.2), channel_id=1, source_target_pairs={{0,2},{1,3},{2,0},{3,1},{4,6},{5,7},{6,4},{7,5},{8,10},{9,11},{10,... | collective-permute-start | bytes 786440 | tf_op jit(solution)/shard_map/ppermute | solution.py:329
  46.4 2.1 %collective-permute-start.12 = (f32[256,256]{1,0:T(8,128)S(1)}, f32[256,256]{1,0:T(8,128)S(1)}, u32[]{:S(2)}, u32[]{:S(2)}) collective-permute-start(f32[256,256]{1,0:T(8,128)S(1)} %get-tuple-element.34), channel_id=1, source_target_pairs={{0,4},{4,0},{8,12},{12,8},{16,20},{20,16},{24,28},{28,24},{1,5},{5... | collective-permute-start | bytes 786440 | tf_op jit(solution)/shard_map/ppermute | solution.py:329
  46.4 13.3 %collective-permute-start.17 = (bf16[256,512]{1,0:T(8,128)(2,1)S(1)}, bf16[256,512]{1,0:T(8,128)(2,1)S(1)}, u32[]{:S(2)}, u32[]{:S(2)}) collective-permute-start(bf16[256,512]{1,0:T(8,128)(2,1)S(1)} %get-tuple-element.33.refs_0_), channel_id=1, source_target_pairs={{0,1},{1,0},{2,3},{3,2},{4,5},{5,4},{6,7},{7,6},{8,9},{9,8},{10,11... | collective-permute-start | bytes 786440 | tf_op jit(solution)/shard_map/ppermute | solution.py:329
  46.4 15.3 %collective-permute-start.11 = (bf16[256,512]{1,0:T(8,128)(2,1)S(1)}, bf16[256,512]{1,0:T(8,128)(2,1)S(1)}, u32[]{:S(2)}, u32[]{:S(2)}) collective-permute-start(bf16[256,512]{1,0:T(8,128)(2,1)S(1)} %get-tuple-element.33.refs_0_), channel_id=1, source_target_pairs={{0,2},{1,3},{2,0},{3,1},{4,6},{5,7},{6,4},{7,5},{8,10},{9,11},{10,... | collective-permute-start | bytes 786440 | tf_op jit(solution)/shard_map/ppermute | solution.py:329
  61.7 11.9 %collective-permute-start.15 = (bf16[256,512]{1,0:T(8,128)(2,1)S(1)}, bf16[256,512]{1,0:T(8,128)(2,1)S(1)}, u32[]{:S(2)}, u32[]{:S(2)}) collective-permute-start(bf16[256,512]{1,0:T(8,128)(2,1)S(1)} %get-tuple-element.36.refs_3_), channel_id=1, source_target_pairs={{1,2},{2,1},{5,6},{6,5},{9,10},{10,9},{13,14},{14,13},{17,18},{18,... | collective-permute-start | bytes 786440 | tf_op jit(solution)/shard_map/ppermute | solution.py:376
  62.4 11.3 %collective-permute-start.16 = (bf16[256,512]{1,0:T(8,128)(2,1)S(1)}, bf16[256,512]{1,0:T(8,128)(2,1)S(1)}, u32[]{:S(2)}, u32[]{:S(2)}) collective-permute-start(bf16[256,512]{1,0:T(8,128)(2,1)S(1)} %get-tuple-element.37.refs_5_), channel_id=1, source_target_pairs={{1,0},{2,3},{5,4},{6,7},{9,8},{10,11},{13,12},{14,15},{17,16},{18,... | collective-permute-start | bytes 786440 | tf_op jit(solution)/shard_map/ppermute | solution.py:377
  63.7 9.9 %collective-permute-start.13 = (bf16[128,256]{1,0:T(8,128)(2,1)S(1)}, bf16[128,256]{1,0:T(8,128)(2,1)S(1)}, u32[]{:S(2)}, u32[]{:S(2)}) collective-permute-start(bf16[128,256]{1,0:T(8,128)(2,1)S(1)} %get-tuple-element.35.refs_0_), channel_id=1, source_target_pairs={{0,1},{1,0},{2,3},{3,2},{4,5},{5,4},{6,7},{7,6},{8,9},{9,8},{10,11... | collective-permute-start | bytes 196616 | tf_op jit(solution)/shard_map/ppermute | solution.py:329
  75.0 4.4 %collective-permute-start.18 = (bf16[3,256,512]{2,1,0:T(8,128)(2,1)S(1)}, bf16[3,256,512]{2,1,0:T(8,128)(2,1)S(1)}, u32[]{:S(2)}, u32[]{:S(2)}) collective-permute-start(bf16[3,256,512]{2,1,0:T(8,128)(2,1)S(1)} %get-tuple-element.39), channel_id=1, source_target_pairs={{0,4},{4,0},{8,12},{12,8},{16,20},{20,16},{24,28},{28,24},{1,5},{5... | collective-permute-start | bytes 2359304 | tf_op jit(solution)/shard_map/ppermute | solution.py:329
  75.1 2.6 %collective-permute-start.19 = (bf16[1,256,512]{2,1,0:T(8,128)(2,1)S(1)}, bf16[1,256,512]{2,1,0:T(8,128)(2,1)S(1)}, u32[]{:S(2)}, u32[]{:S(2)}) collective-permute-start(bf16[1,256,512]{2,1,0:T(8,128)(2,1)S(1)} %get-tuple-element.42), channel_id=1, source_target_pairs={{0,4},{4,0},{8,12},{12,8},{16,20},{20,16},{24,28},{28,24},{1,5},{5... | collective-permute-start | bytes 786440 | tf_op jit(solution)/shard_map/ppermute | solution.py:329
  77.8 6.4 %collective-permute-start.20 = (bf16[256,512]{1,0:T(8,128)(2,1)S(1)}, bf16[256,512]{1,0:T(8,128)(2,1)S(1)}, u32[]{:S(2)}, u32[]{:S(2)}) collective-permute-start(bf16[256,512]{1,0:T(8,128)(2,1)S(1)} %fusion), channel_id=1, source_target_pairs={{0,8},{4,20},{8,0},{12,28},{16,24},{20,4},{24,16},{28,12},{1,9},{5... | collective-permute-start | bytes 786440 | tf_op jit(solution)/shard_map/ppermute | solution.py:398
  79.4 6.4 %collective-permute-start.14 = (bf16[128,256]{1,0:T(8,128)(2,1)S(1)}, bf16[128,256]{1,0:T(8,128)(2,1)S(1)}, u32[]{:S(2)}, u32[]{:S(2)}) collective-permute-start(bf16[128,256]{1,0:T(8,128)(2,1)S(1)} %total.2.refs_3_.refs_0_), channel_id=1, source_target_pairs={{0,2},{1,3},{2,0},{3,1},{4,6},{5,7},{6,4},{7,5},{8,10},{9,11},{10,... | collective-permute-start | bytes 196616 | tf_op jit(solution)/shard_map/ppermute | solution.py:329
  80.0 9.6 %collective-permute-start.23 = (bf16[256,512]{1,0:T(8,128)(2,1)S(1)}, bf16[256,512]{1,0:T(8,128)(2,1)S(1)}, u32[]{:S(2)}, u32[]{:S(2)}) collective-permute-start(bf16[256,512]{1,0:T(8,128)(2,1)S(1)} %gate.7), channel_id=1, source_target_pairs={{0,8},{4,20},{8,0},{12,28},{16,24},{20,4},{24,16},{28,12},{1,9},{5... | collective-permute-start | bytes 786440 | tf_op jit(solution)/shard_map/ppermute | solution.py:402
  84.3 6.4 %collective-permute-start.24 = (bf16[256,512]{1,0:T(8,128)(2,1)S(1)}, bf16[256,512]{1,0:T(8,128)(2,1)S(1)}, u32[]{:S(2)}, u32[]{:S(2)}) collective-permute-start(bf16[256,512]{1,0:T(8,128)(2,1)S(1)} %add_convert_fusion.refs_2_), channel_id=1, source_target_pairs={{0,16},{4,12},{8,24},{12,4},{16,0},{20,28},{24,8},{28,20},{1,17},{... | collective-permute-start | bytes 786440 | tf_op jit(solution)/shard_map/ppermute | solution.py:402
  85.8 1.3 %collective-permute-start.21 = (f32[64,256]{1,0:T(8,128)S(1)}, f32[64,256]{1,0:T(8,128)S(1)}, u32[]{:S(2)}, u32[]{:S(2)}) collective-permute-start(f32[64,256]{1,0:T(8,128)S(1)} %get-tuple-element.46), channel_id=1, source_target_pairs={{0,4},{4,0},{8,12},{12,8},{16,20},{20,16},{24,28},{28,24},{1,5},{5... | collective-permute-start | bytes 196616 | tf_op jit(solution)/shard_map/ppermute | solution.py:329
  87.2 1.3 %collective-permute-start.22 = (f32[64,256]{1,0:T(8,128)S(1)}, f32[64,256]{1,0:T(8,128)S(1)}, u32[]{:S(2)}, u32[]{:S(2)}) collective-permute-start(f32[64,256]{1,0:T(8,128)S(1)} %gate.6), channel_id=1, source_target_pairs={{0,4},{4,0},{8,12},{12,8},{16,20},{20,16},{24,28},{28,24},{1,5},{5... | collective-permute-start | bytes 196616 | tf_op jit(solution)/shard_map/ppermute | solution.py:329

commit v17 on v16

--- a/solution.py
+++ b/solution.py
@@ -359,7 +359,8 @@
         relayed = lax.ppermute(shares[3], "col", [(0, 1), (3, 2)])
         came = [lax.ppermute(shares[3], "col", [(1, 2), (2, 1)])]
         joined = (shares[2].astype(jnp.float32) + relayed.astype(jnp.float32)).astype(jnp.bfloat16)
-        came += [swap(joined, "col", n_col, 2), swap(shares[1], "col", n_col, 1)]
+        came += [lax.ppermute(shares[2], "col", [(0, 2), (3, 1)]), lax.ppermute(joined, "col", [(1, 3), (2, 0)])]
+        came.append(swap(shares[1], "col", n_col, 1))
     else:
         came = [swap(share, "col", n_col, s) for s, share in shares.items()]
     mine = forward(where, dense[0], parts, every, [], jnp.float32)

time: 91.8 us -> 95.8 us (1.044)
  waiting for transfers between devices: 27.3 us -> 30.5 us
    ppermute x0 -> x2, waiting for transfers between devices: none -> 12.2 us  [the longest x1 8.03 us: shards(): lax.ppermute(joined, 'col', [(1, 3), (2, 0)])]
    ppermute x18 -> x17, waiting for transfers between devices: 22.6 us -> 13.6 us  [swap(): return lax.ppermute(value, axis, [(i, i ^ step) for i in range(size)])]
    ppermute x0 -> x2, starting transfers between devices: none -> 4.38 us  [the longest x1 2.91 us: shards(): lax.ppermute(shares[2], 'col', [(0, 2), (3, 1)])]
    ppermute x18 -> x17, starting transfers between devices: 16.5 us -> 13.1 us  [swap(): return lax.ppermute(value, axis, [(i, i ^ step) for i in range(size)])]
  transfers between devices with their start and end apart: 25 -> 26, of which waited for: 13 -> 13; matrix products, arithmetic and copies ran while one was open for 0% -> 0% of each run, Pallas kernels for 24% -> 23%
where the time goes in v17:
time: 95.8 us; the launch traced here: 95.5 us
  waiting for transfers between devices  30.5 us (32%)
  starting transfers between devices  27.2 us (28%)
  Pallas kernels  26.4 us (28%)
  blocking collectives  10 us (10%)
    ppermute x17, waiting for transfers between devices, swap(): return lax.ppermute(value, axis, [(i, i ^ step) for i in range(size)])  13.6 us
    ppermute x17, starting transfers between devices, swap(): return lax.ppermute(value, axis, [(i, i ^ step) for i in range(size)])  13.1 us
    all_gather x1, blocking collectives, shards(): gathered = lax.all_gather(part, 'row', axis_index_groups=cores, tiled=True)  10 us
    ppermute x1, waiting for transfers between devices, shards(): lax.ppermute(joined, 'col', [(1, 3), (2, 0)])  8.03 us
    pallas_call x5, Pallas kernels, forward(): pl.pallas_call(functools.partial(forward_kernel, steps=steps, before=bool...  7.94 us
    pallas_call x1, Pallas kernels, dense_rows(): pl.pallas_call(functools.partial(dense_kernel, steps=steps, window=window...  7.39 us
    pallas_call x3, Pallas kernels, backward(): pl.pallas_call(functools.partial(backward_kernel, count=count, groups=gro...  6.55 us
    ppermute x1, waiting for transfers between devices, shards(): lax.ppermute(shares[2], 'col', [(0, 2), (3, 1)])  4.2 us
  transfers between devices with their start and end apart: 26, of which 13 were waited for; matrix products, arithmetic and copies ran while one was open for 0% of the time, Pallas kernels for 23%

profile of v17, /device:TPU:0, one launch (start us, length us, event | category | flops | bytes accessed | tf_op | source)
XLA Modules:
  0.0 95.5 jit_solution(10210649377138160918)
XLA Ops:
  0.6 4.0 %collective-permute-start.1 = (bf16[512,256]{1,0:T(8,128)(2,1)}, bf16[512,256]{1,0:T(8,128)(2,1)S(1)}, u32[]{:S(2)}, u32[]{:S(2)}) collective-permute-start(bf16[512,256]{1,0:T(8,128)(2,1)} %features_ref.1), channel_id=1, source_target_pairs={{0,24},{4,28},{8,16},{12,20},{16,8},{20,12},{24,0},{28,4},{1,25},{... | collective-permute-start | bytes 786440 | tf_op jit(solution)/shard_map/ppermute | solution.py:329
  5.3 7.4 %dense_rows.1 = (bf16[512,4096]{1,0:T(8,128)(2,1)S(1)}, bf16[512,4096]{1,0:T(8,128)(2,1)S(1)}, bf16[512,4096]{1,0:T(8,128)(2,1)S(1)}, bf16[512,4096]{1,0:T(8,128)(2,1)S(1)}, bf16[512,256]{1,0:T(8,128)(2,1)S(1)}) custom-call(s32[2]{0:T(128)S(1)} %pad_add_fusion.where, s32[16]{0:T(128)} %bitcast.9, s32[448]{0:T(512)} %bitcast.8, ...), custom_call_target="tpu_custom_call" | custom-call | bytes 41943040 | tf_op jit(solution)/shard_map/dense_rows/pallas_call | solution.py:102
  12.7 4.3 %collective-permute-done.3.refs_2_ = bf16[512,256]{1,0:T(8,128)(2,1)S(1)} collective-permute-done((bf16[512,256]{1,0:T(8,128)(2,1)}, bf16[512,256]{1,0:T(8,128)(2,1)S(1)}, u32[]{:S(2)}, u32[]{:S(2)}) %collective-permute-start.3) | collective-permute-done | bytes 262176 | tf_op jit(solution)/shard_map/ppermute | solution.py:329
  17.6 1.2 %forward_rows.6.refs_4_ = f32[512,256]{1,0:T(8,128)S(1)} custom-call(s32[2]{0:T(128)S(1)} %pad_add_fusion.where, bf16[512,4096]{1,0:T(8,128)(2,1)S(1)} %get-tuple-element.26.refs_3_.a_ref.refs_0_, bf16[512,256]{1,0:T(8,128)(2,1)S(1)} %get-tuple-element.25.refs_0_, bf16[512,256]{1,0:T(8,128)(2,1)S(1)} %get-tuple-element.29.refs_2_.refs_1_, ...), custom_call_target="tpu_custom_call" | custom-call | flops 1073741824 | bytes 4194304 | tf_op jit(solution)/shard_map/forward_rows/pallas_call | solution.py:133
  19.3 1.3 %forward_rows.7 = bf16[512,256]{1,0:T(8,128)(2,1)S(1)} custom-call(s32[2]{0:T(128)S(1)} %pad_add_fusion.where, bf16[512,4096]{1,0:T(8,128)(2,1)S(1)} %get-tuple-element.26.refs_3_.a_ref.refs_0_, bf16[512,256]{1,0:T(8,128)(2,1)S(1)} %collective-permute-done.refs_1_.refs_0_, bf16[512,256]{1,0:T(8,128)(2,1)S(1)} %collective-permute-done.4.refs_3_.refs_1_, ...), custom_call_target="tpu_custom_call" | custom-call | flops 1073741824 | bytes 4194304 | tf_op jit(solution)/shard_map/forward_rows/pallas_call | solution.py:133
  20.6 3.5 %collective-permute-start.9 = (bf16[512,256]{1,0:T(8,128)(2,1)S(1)}, bf16[512,256]{1,0:T(8,128)(2,1)S(1)}, u32[]{:S(2)}, u32[]{:S(2)}) collective-permute-start(bf16[512,256]{1,0:T(8,128)(2,1)S(1)} %forward_rows.7), channel_id=1, source_target_pairs={{0,1},{3,2},{4,5},{7,6},{8,9},{11,10},{12,13},{15,14},{16,17},{19,... | collective-permute-start | bytes 786440 | tf_op jit(solution)/shard_map/ppermute | solution.py:359
  24.8 1.8 %forward_rows.9 = bf16[512,256]{1,0:T(8,128)(2,1)S(1)} custom-call(s32[2]{0:T(128)S(1)} %pad_add_fusion.where, bf16[512,4096]{1,0:T(8,128)(2,1)S(1)} %get-tuple-element.28.refs_5_.a_ref.refs_1_, bf16[512,256]{1,0:T(8,128)(2,1)S(1)} %get-tuple-element.25.refs_0_, bf16[512,256]{1,0:T(8,128)(2,1)S(1)} %collective-permute-done.refs_1_.refs_0_, ...), custom_call_target="tpu_custom_call" | custom-call | flops 1073741824 | bytes 4194304 | tf_op jit(solution)/shard_map/forward_rows/pallas_call | solution.py:133
  26.6 2.2 %collective-permute-start.11 = (bf16[512,256]{1,0:T(8,128)(2,1)S(1)}, bf16[512,256]{1,0:T(8,128)(2,1)S(1)}, u32[]{:S(2)}, u32[]{:S(2)}) collective-permute-start(bf16[512,256]{1,0:T(8,128)(2,1)S(1)} %forward_rows.9), channel_id=1, source_target_pairs={{0,1},{1,0},{2,3},{3,2},{4,5},{5,4},{6,7},{7,6},{8,9},{9,8},{10,11... | collective-permute-start | bytes 786440 | tf_op jit(solution)/shard_map/ppermute | solution.py:329
  28.8 1.8 %forward_rows.8 = bf16[512,256]{1,0:T(8,128)(2,1)S(1)} custom-call(s32[2]{0:T(128)S(1)} %pad_add_fusion.where, bf16[512,4096]{1,0:T(8,128)(2,1)S(1)} %get-tuple-element.27.refs_4_.a_ref.refs_2_, bf16[512,256]{1,0:T(8,128)(2,1)S(1)} %get-tuple-element.25.refs_0_, bf16[512,256]{1,0:T(8,128)(2,1)S(1)} %collective-permute-done.refs_1_.refs_0_, ...), custom_call_target="tpu_custom_call" | custom-call | flops 1073741824 | bytes 4194304 | tf_op jit(solution)/shard_map/forward_rows/pallas_call | solution.py:133
  30.7 2.9 %collective-permute-start.8 = (bf16[512,256]{1,0:T(8,128)(2,1)S(1)}, bf16[512,256]{1,0:T(8,128)(2,1)S(1)}, u32[]{:S(2)}, u32[]{:S(2)}) collective-permute-start(bf16[512,256]{1,0:T(8,128)(2,1)S(1)} %forward_rows.8), channel_id=1, source_target_pairs={{0,2},{3,1},{4,6},{7,5},{8,10},{11,9},{12,14},{15,13},{16,18},{19,... | collective-permute-start | bytes 786440 | tf_op jit(solution)/shard_map/ppermute | solution.py:362
  33.7 1.5 %collective-permute-start.10 = (bf16[512,256]{1,0:T(8,128)(2,1)S(1)}, bf16[512,256]{1,0:T(8,128)(2,1)S(1)}, u32[]{:S(2)}, u32[]{:S(2)}) collective-permute-start(bf16[512,256]{1,0:T(8,128)(2,1)S(1)} %add_convert_fusion.2), channel_id=1, source_target_pairs={{1,3},{2,0},{5,7},{6,4},{9,11},{10,8},{13,15},{14,12},{17,19},{18,... | collective-permute-start | bytes 786440 | tf_op jit(solution)/shard_map/ppermute | solution.py:362
  35.2 1.8 %forward_rows.5.refs_0_ = f32[512,256]{1,0:T(8,128)S(1)} custom-call(s32[2]{0:T(128)S(1)} %pad_add_fusion.where, bf16[512,4096]{1,0:T(8,128)(2,1)S(1)} %get-tuple-element.24.refs_6_.a_ref.refs_0_, bf16[512,256]{1,0:T(8,128)(2,1)S(1)} %get-tuple-element.25.refs_0_, bf16[512,256]{1,0:T(8,128)(2,1)S(1)} %collective-permute-done.refs_1_.refs_0_, ...), custom_call_target="tpu_custom_call" | custom-call | flops 1073741824 | bytes 4194304 | tf_op jit(solution)/shard_map/forward_rows/pallas_call | solution.py:133
  37.0 4.2 %collective-permute-done.8.refs_2_ = bf16[512,256]{1,0:T(8,128)(2,1)S(1)} collective-permute-done((bf16[512,256]{1,0:T(8,128)(2,1)S(1)}, bf16[512,256]{1,0:T(8,128)(2,1)S(1)}, u32[]{:S(2)}, u32[]{:S(2)}) %collective-permute-start.8) | collective-permute-done | bytes 262176 | tf_op jit(solution)/shard_map/ppermute | solution.py:362
  41.2 8.0 %collective-permute-done.10.refs_3_ = bf16[512,256]{1,0:T(8,128)(2,1)S(1)} collective-permute-done((bf16[512,256]{1,0:T(8,128)(2,1)S(1)}, bf16[512,256]{1,0:T(8,128)(2,1)S(1)}, u32[]{:S(2)}, u32[]{:S(2)}) %collective-permute-start.10) | collective-permute-done | bytes 262176 | tf_op jit(solution)/shard_map/ppermute | solution.py:362
  49.2 1.1 %middle.1 = (bf16[512,256]{1,0:T(8,128)(2,1)}, bf16[256,512]{1,0:T(8,128)(2,1)S(1)}, f32[256,256]{1,0:T(8,128)S(1)}) custom-call(f32[512,256]{1,0:T(8,128)S(1)} %forward_rows.5.refs_0_, bf16[512,256]{1,0:T(8,128)(2,1)S(1)} %collective-permute-done.7.refs_1_, bf16[512,256]{1,0:T(8,128)(2,1)S(1)} %collective-permute-done.8.refs_2_, ...), custom_call_target="tpu_custom_call" | custom-call | flops 201326592 | bytes 1310720 | tf_op jit(solution)/shard_map/middle/pallas_call | solution.py:166
  50.3 2.1 %collective-permute-start.12 = (bf16[256,512]{1,0:T(8,128)(2,1)S(1)}, bf16[256,512]{1,0:T(8,128)(2,1)S(1)}, u32[]{:S(2)}, u32[]{:S(2)}) collective-permute-start(bf16[256,512]{1,0:T(8,128)(2,1)S(1)} %get-tuple-element.33.refs_0_), channel_id=1, source_target_pairs={{0,2},{1,3},{2,0},{3,1},{4,6},{5,7},{6,4},{7,5},{8,10},{9,11},{10,... | collective-permute-start | bytes 786440 | tf_op jit(solution)/shard_map/ppermute | solution.py:329
  52.5 10.0 %all_gather.3.values_ref = bf16[1024,256]{1,0:T(8,128)(2,1)S(1)} all-gather(bf16[256,256]{1,0:T(8,128)(2,1)S(1)} %add_convert_fusion.3), channel_id=1, replica_groups={{0,8,16,24},{4,12,20,28},{1,9,17,25},{5,13,21,29},{2,10,18,26},{6,14,22..., dimensions={0}, use_global_device_ids=true | all-gather | bytes 655360 | tf_op jit(solution)/shard_map/all_gather | solution.py:372
  63.6 2.0 %collective-permute-done.12.refs_1_ = bf16[256,512]{1,0:T(8,128)(2,1)S(1)} collective-permute-done((bf16[256,512]{1,0:T(8,128)(2,1)S(1)}, bf16[256,512]{1,0:T(8,128)(2,1)S(1)}, u32[]{:S(2)}, u32[]{:S(2)}) %collective-permute-start.12) | collective-permute-done | bytes 262176 | tf_op jit(solution)/shard_map/ppermute | solution.py:329
  66.3 1.3 %collective-permute-start.17 = (bf16[256,512]{1,0:T(8,128)(2,1)S(1)}, bf16[256,512]{1,0:T(8,128)(2,1)S(1)}, u32[]{:S(2)}, u32[]{:S(2)}) collective-permute-start(bf16[256,512]{1,0:T(8,128)(2,1)S(1)} %get-tuple-element.37.refs_5_), channel_id=1, source_target_pairs={{1,0},{2,3},{5,4},{6,7},{9,8},{10,11},{13,12},{14,15},{17,16},{18,... | collective-permute-start | bytes 786440 | tf_op jit(solution)/shard_map/ppermute | solution.py:378
  67.6 2.7 %collective-permute-start.14 = (bf16[128,256]{1,0:T(8,128)(2,1)S(1)}, bf16[128,256]{1,0:T(8,128)(2,1)S(1)}, u32[]{:S(2)}, u32[]{:S(2)}) collective-permute-start(bf16[128,256]{1,0:T(8,128)(2,1)S(1)} %get-tuple-element.35.refs_0_), channel_id=1, source_target_pairs={{0,1},{1,0},{2,3},{3,2},{4,5},{5,4},{6,7},{7,6},{8,9},{9,8},{10,11... | collective-permute-start | bytes 196616 | tf_op jit(solution)/shard_map/ppermute | solution.py:329
  70.3 4.0 %backward_cols.3.refs_2_ = f32[8,256,512]{2,1,0:T(8,128)S(1)} custom-call(s32[2]{0:T(128)S(1)} %pad_add_fusion.where, bf16[512,4096]{1,0:T(8,128)(2,1)S(1)} %get-tuple-element.24.refs_6_.a_ref.refs_0_, bf16[512,4096]{1,0:T(8,128)(2,1)S(1)} %get-tuple-element.28.refs_5_.a_ref.refs_1_, bf16[512,4096]{1,0:T(8,128)(2,1)S(1)} %get-tuple-element.27.refs_4_.a_ref.refs_2_, ...), custom_call_target="tpu_custom_call" | custom-call | tf_op jit(solution)/shard_map/backward_cols/pallas_call | solution.py:198
  74.3 3.2 %collective-permute-done.14.refs_1_ = bf16[128,256]{1,0:T(8,128)(2,1)S(1)} collective-permute-done((bf16[128,256]{1,0:T(8,128)(2,1)S(1)}, bf16[128,256]{1,0:T(8,128)(2,1)S(1)}, u32[]{:S(2)}, u32[]{:S(2)}) %collective-permute-start.14) | collective-permute-done | bytes 65568 | tf_op jit(solution)/shard_map/ppermute | solution.py:329
  77.6 1.3 %backward_cols.5 = (bf16[1,256,512]{2,1,0:T(8,128)(2,1)S(1)}, bf16[3,256,512]{2,1,0:T(8,128)(2,1)S(1)}) custom-call(s32[2]{0:T(128)S(1)} %pad_add_fusion.where, bf16[512,4096]{1,0:T(8,128)(2,1)S(1)} %get-tuple-element.26.refs_3_.a_ref.refs_0_, bf16[256,512]{1,0:T(8,128)(2,1)S(1)} %add.18.refs_1_, f32[8,256,512]{2,1,0:T(8,128)S(1)} %backward_cols.3.refs_2_, ...), custom_call_target="tpu_custom_call" | custom-call | tf_op jit(solution)/shard_map/backward_cols/pallas_call | solution.py:198
  79.5 1.3 %backward_cols.4 = (f32[1,256,512]{2,1,0:T(8,128)S(1)}, f32[3,256,512]{2,1,0:T(8,128)S(1)}) custom-call(s32[2]{0:T(128)S(1)} %pad_add_fusion.where, bf16[512,4096]{1,0:T(8,128)(2,1)S(1)} %get-tuple-element.26.refs_3_.a_ref.refs_0_, bf16[256,512]{1,0:T(8,128)(2,1)S(1)} %add.18.refs_1_, f32[8,256,512]{2,1,0:T(8,128)S(1)} %backward_cols.3.refs_2_), custom_call_target="tpu_custom_call" | custom-call | tf_op jit(solution)/shard_map/backward_cols/pallas_call | solution.py:198
  80.7 0.9 collective-permute-done.20
  81.7 1.6 %collective-permute-start.21 = (bf16[256,512]{1,0:T(8,128)(2,1)S(1)}, bf16[256,512]{1,0:T(8,128)(2,1)S(1)}, u32[]{:S(2)}, u32[]{:S(2)}) collective-permute-start(bf16[256,512]{1,0:T(8,128)(2,1)S(1)} %fusion), channel_id=1, source_target_pairs={{0,8},{4,20},{8,0},{12,28},{16,24},{20,4},{24,16},{28,12},{1,9},{5... | collective-permute-start | bytes 786440 | tf_op jit(solution)/shard_map/ppermute | solution.py:399
  84.5 3.6 %collective-permute-done.21 = bf16[256,512]{1,0:T(8,128)(2,1)S(1)} collective-permute-done((bf16[256,512]{1,0:T(8,128)(2,1)S(1)}, bf16[256,512]{1,0:T(8,128)(2,1)S(1)}, u32[]{:S(2)}, u32[]{:S(2)}) %collective-permute-start.21) | collective-permute-done | bytes 262176 | tf_op jit(solution)/shard_map/ppermute | solution.py:399
  88.2 1.5 %collective-permute-start.25 = (bf16[256,512]{1,0:T(8,128)(2,1)S(1)}, bf16[256,512]{1,0:T(8,128)(2,1)S(1)}, u32[]{:S(2)}, u32[]{:S(2)}) collective-permute-start(bf16[256,512]{1,0:T(8,128)(2,1)S(1)} %add_convert_fusion.refs_2_), channel_id=1, source_target_pairs={{0,16},{4,12},{8,24},{12,4},{16,0},{20,28},{24,8},{28,20},{1,17},{... | collective-permute-start | bytes 786440 | tf_op jit(solution)/shard_map/ppermute | solution.py:403
  89.8 1.2 %collective-permute-done.22.refs_1_.refs_0_ = f32[64,256]{1,0:T(8,128)S(1)} collective-permute-done((f32[64,256]{1,0:T(8,128)S(1)}, f32[64,256]{1,0:T(8,128)S(1)}, u32[]{:S(2)}, u32[]{:S(2)}) %collective-permute-start.22) | collective-permute-done | bytes 65568 | tf_op jit(solution)/shard_map/ppermute | solution.py:329
  91.2 1.1 %collective-permute-done.23.refs_1_ = f32[64,256]{1,0:T(8,128)S(1)} collective-permute-done((f32[64,256]{1,0:T(8,128)S(1)}, f32[64,256]{1,0:T(8,128)S(1)}, u32[]{:S(2)}, u32[]{:S(2)}) %collective-permute-start.23) | collective-permute-done | bytes 65568 | tf_op jit(solution)/shard_map/ppermute | solution.py:329
  92.3 1.3 %join.1 = f32[256,256]{1,0:T(8,128)} custom-call(s32[2]{0:T(128)S(1)} %pad_add_fusion.where, f32[128,256]{1,0:T(8,128)S(1)} %total.3.own_ref, f32[64,256]{1,0:T(8,128)S(1)} %collective-permute-done.22.refs_1_.refs_0_, f32[64,256]{1,0:T(8,128)S(1)} %collective-permute-done.23.refs_1_), custom_call_target="tpu_custom_call" | custom-call | tf_op jit(solution)/shard_map/join/pallas_call | solution.py:318
  93.6 1.1 %collective-permute-done.25.refs_2_ = bf16[256,512]{1,0:T(8,128)(2,1)S(1)} collective-permute-done((bf16[256,512]{1,0:T(8,128)(2,1)S(1)}, bf16[256,512]{1,0:T(8,128)(2,1)S(1)}, u32[]{:S(2)}, u32[]{:S(2)}) %collective-permute-start.25) | collective-permute-done | bytes 262176 | tf_op jit(solution)/shard_map/ppermute | solution.py:403
  (52 shorter events, 7.5 us)
Async XLA Ops:
  0.6 12.1 %collective-permute-start.1 = (bf16[512,256]{1,0:T(8,128)(2,1)}, bf16[512,256]{1,0:T(8,128)(2,1)S(1)}, u32[]{:S(2)}, u32[]{:S(2)}) collective-permute-start(bf16[512,256]{1,0:T(8,128)(2,1)} %features_ref.1), channel_id=1, source_target_pairs={{0,24},{4,28},{8,16},{12,20},{16,8},{20,12},{24,0},{28,4},{1,25},{... | collective-permute-start | bytes 786440 | tf_op jit(solution)/shard_map/ppermute | solution.py:329
  4.6 12.4 %collective-permute-start.3 = (bf16[512,256]{1,0:T(8,128)(2,1)}, bf16[512,256]{1,0:T(8,128)(2,1)S(1)}, u32[]{:S(2)}, u32[]{:S(2)}) collective-permute-start(bf16[512,256]{1,0:T(8,128)(2,1)} %features_ref.1), channel_id=1, source_target_pairs={{0,8},{4,12},{8,0},{12,4},{16,24},{20,28},{24,16},{28,20},{1,9},{5... | collective-permute-start | bytes 786440 | tf_op jit(solution)/shard_map/ppermute | solution.py:329
  5.1 11.9 %collective-permute-start.2 = (bf16[512,256]{1,0:T(8,128)(2,1)}, bf16[512,256]{1,0:T(8,128)(2,1)S(1)}, u32[]{:S(2)}, u32[]{:S(2)}) collective-permute-start(bf16[512,256]{1,0:T(8,128)(2,1)} %features_ref.1), channel_id=1, source_target_pairs={{0,16},{4,20},{8,24},{12,28},{16,0},{20,4},{24,8},{28,12},{1,17},{... | collective-permute-start | bytes 786440 | tf_op jit(solution)/shard_map/ppermute | solution.py:329
  5.2 13.6 %collective-permute-start = (bf16[512,256]{1,0:T(8,128)(2,1)}, bf16[512,256]{1,0:T(8,128)(2,1)S(1)}, u32[]{:S(2)}, u32[]{:S(2)}) collective-permute-start(bf16[512,256]{1,0:T(8,128)(2,1)} %features_ref.1), channel_id=1, source_target_pairs={{0,4},{4,0},{8,12},{12,8},{16,20},{20,16},{24,28},{28,24},{1,5},{5... | collective-permute-start | bytes 786440 | tf_op jit(solution)/shard_map/ppermute | solution.py:329
  17.0 1.8 %collective-permute-start.4 = (bf16[512,256]{1,0:T(8,128)(2,1)S(1)}, bf16[512,256]{1,0:T(8,128)(2,1)S(1)}, u32[]{:S(2)}, u32[]{:S(2)}) collective-permute-start(bf16[512,256]{1,0:T(8,128)(2,1)S(1)} %get-tuple-element.29.refs_2_.refs_1_), channel_id=1, source_target_pairs={{0,4},{4,0},{8,12},{12,8},{16,20},{20,16},{24,28},{28,24},{1,5},{5... | collective-permute-start | bytes 786440 | tf_op jit(solution)/shard_map/ppermute | solution.py:329
  17.0 1.9 %collective-permute-start.5 = (bf16[512,256]{1,0:T(8,128)(2,1)S(1)}, bf16[512,256]{1,0:T(8,128)(2,1)S(1)}, u32[]{:S(2)}, u32[]{:S(2)}) collective-permute-start(bf16[512,256]{1,0:T(8,128)(2,1)S(1)} %get-tuple-element.30.refs_4_.refs_2_), channel_id=1, source_target_pairs={{0,4},{4,0},{8,12},{12,8},{16,20},{20,16},{24,28},{28,24},{1,5},{5... | collective-permute-start | bytes 786440 | tf_op jit(solution)/shard_map/ppermute | solution.py:329
  17.5 1.8 %collective-permute-start.6 = (bf16[512,256]{1,0:T(8,128)(2,1)S(1)}, bf16[512,256]{1,0:T(8,128)(2,1)S(1)}, u32[]{:S(2)}, u32[]{:S(2)}) collective-permute-start(bf16[512,256]{1,0:T(8,128)(2,1)S(1)} %get-tuple-element.31.refs_6_.refs_3_), channel_id=1, source_target_pairs={{0,4},{4,0},{8,12},{12,8},{16,20},{20,16},{24,28},{28,24},{1,5},{5... | collective-permute-start | bytes 786440 | tf_op jit(solution)/shard_map/ppermute | solution.py:329
  20.6 13.0 %collective-permute-start.9 = (bf16[512,256]{1,0:T(8,128)(2,1)S(1)}, bf16[512,256]{1,0:T(8,128)(2,1)S(1)}, u32[]{:S(2)}, u32[]{:S(2)}) collective-permute-start(bf16[512,256]{1,0:T(8,128)(2,1)S(1)} %forward_rows.7), channel_id=1, source_target_pairs={{0,1},{3,2},{4,5},{7,6},{8,9},{11,10},{12,13},{15,14},{16,17},{19,... | collective-permute-start | bytes 786440 | tf_op jit(solution)/shard_map/ppermute | solution.py:359
  24.1 17.1 %collective-permute-start.7 = (bf16[512,256]{1,0:T(8,128)(2,1)S(1)}, bf16[512,256]{1,0:T(8,128)(2,1)S(1)}, u32[]{:S(2)}, u32[]{:S(2)}) collective-permute-start(bf16[512,256]{1,0:T(8,128)(2,1)S(1)} %forward_rows.7), channel_id=1, source_target_pairs={{1,2},{2,1},{5,6},{6,5},{9,10},{10,9},{13,14},{14,13},{17,18},{18,... | collective-permute-start | bytes 786440 | tf_op jit(solution)/shard_map/ppermute | solution.py:360
  26.6 10.4 %collective-permute-start.11 = (bf16[512,256]{1,0:T(8,128)(2,1)S(1)}, bf16[512,256]{1,0:T(8,128)(2,1)S(1)}, u32[]{:S(2)}, u32[]{:S(2)}) collective-permute-start(bf16[512,256]{1,0:T(8,128)(2,1)S(1)} %forward_rows.9), channel_id=1, source_target_pairs={{0,1},{1,0},{2,3},{3,2},{4,5},{5,4},{6,7},{7,6},{8,9},{9,8},{10,11... | collective-permute-start | bytes 786440 | tf_op jit(solution)/shard_map/ppermute | solution.py:329
  30.6 18.6 %copy-start = (bf16[512,256]{1,0:T(8,128)(2,1)S(1)}, bf16[512,256]{1,0:T(8,128)(2,1)}, u32[]{:S(2)}) copy-start(bf16[512,256]{1,0:T(8,128)(2,1)} %refs_6_.1) | copy-start | bytes 786436
  30.7 18.6 %copy-start.1 = (bf16[256,256]{1,0:T(8,128)(2,1)S(1)}, bf16[256,256]{1,0:T(8,128)(2,1)}, u32[]{:S(2)}) copy-start(bf16[256,256]{1,0:T(8,128)(2,1)} %refs_5_.1) | copy-start | bytes 393220
  30.7 10.5 %collective-permute-start.8 = (bf16[512,256]{1,0:T(8,128)(2,1)S(1)}, bf16[512,256]{1,0:T(8,128)(2,1)S(1)}, u32[]{:S(2)}, u32[]{:S(2)}) collective-permute-start(bf16[512,256]{1,0:T(8,128)(2,1)S(1)} %forward_rows.8), channel_id=1, source_target_pairs={{0,2},{3,1},{4,6},{7,5},{8,10},{11,9},{12,14},{15,13},{16,18},{19,... | collective-permute-start | bytes 786440 | tf_op jit(solution)/shard_map/ppermute | solution.py:362
  33.7 15.5 %collective-permute-start.10 = (bf16[512,256]{1,0:T(8,128)(2,1)S(1)}, bf16[512,256]{1,0:T(8,128)(2,1)S(1)}, u32[]{:S(2)}, u32[]{:S(2)}) collective-permute-start(bf16[512,256]{1,0:T(8,128)(2,1)S(1)} %add_convert_fusion.2), channel_id=1, source_target_pairs={{1,3},{2,0},{5,7},{6,4},{9,11},{10,8},{13,15},{14,12},{17,19},{18,... | collective-permute-start | bytes 786440 | tf_op jit(solution)/shard_map/ppermute | solution.py:362
  50.3 2.1 %collective-permute-start.13 = (f32[256,256]{1,0:T(8,128)S(1)}, f32[256,256]{1,0:T(8,128)S(1)}, u32[]{:S(2)}, u32[]{:S(2)}) collective-permute-start(f32[256,256]{1,0:T(8,128)S(1)} %get-tuple-element.34), channel_id=1, source_target_pairs={{0,4},{4,0},{8,12},{12,8},{16,20},{20,16},{24,28},{28,24},{1,5},{5... | collective-permute-start | bytes 786440 | tf_op jit(solution)/shard_map/ppermute | solution.py:329
  50.3 13.3 %collective-permute-start.18 = (bf16[256,512]{1,0:T(8,128)(2,1)S(1)}, bf16[256,512]{1,0:T(8,128)(2,1)S(1)}, u32[]{:S(2)}, u32[]{:S(2)}) collective-permute-start(bf16[256,512]{1,0:T(8,128)(2,1)S(1)} %get-tuple-element.33.refs_0_), channel_id=1, source_target_pairs={{0,1},{1,0},{2,3},{3,2},{4,5},{5,4},{6,7},{7,6},{8,9},{9,8},{10,11... | collective-permute-start | bytes 786440 | tf_op jit(solution)/shard_map/ppermute | solution.py:329
  50.3 15.3 %collective-permute-start.12 = (bf16[256,512]{1,0:T(8,128)(2,1)S(1)}, bf16[256,512]{1,0:T(8,128)(2,1)S(1)}, u32[]{:S(2)}, u32[]{:S(2)}) collective-permute-start(bf16[256,512]{1,0:T(8,128)(2,1)S(1)} %get-tuple-element.33.refs_0_), channel_id=1, source_target_pairs={{0,2},{1,3},{2,0},{3,1},{4,6},{5,7},{6,4},{7,5},{8,10},{9,11},{10,... | collective-permute-start | bytes 786440 | tf_op jit(solution)/shard_map/ppermute | solution.py:329
  65.6 11.9 %collective-permute-start.16 = (bf16[256,512]{1,0:T(8,128)(2,1)S(1)}, bf16[256,512]{1,0:T(8,128)(2,1)S(1)}, u32[]{:S(2)}, u32[]{:S(2)}) collective-permute-start(bf16[256,512]{1,0:T(8,128)(2,1)S(1)} %get-tuple-element.36.refs_3_), channel_id=1, source_target_pairs={{1,2},{2,1},{5,6},{6,5},{9,10},{10,9},{13,14},{14,13},{17,18},{18,... | collective-permute-start | bytes 786440 | tf_op jit(solution)/shard_map/ppermute | solution.py:377
  66.3 11.3 %collective-permute-start.17 = (bf16[256,512]{1,0:T(8,128)(2,1)S(1)}, bf16[256,512]{1,0:T(8,128)(2,1)S(1)}, u32[]{:S(2)}, u32[]{:S(2)}) collective-permute-start(bf16[256,512]{1,0:T(8,128)(2,1)S(1)} %get-tuple-element.37.refs_5_), channel_id=1, source_target_pairs={{1,0},{2,3},{5,4},{6,7},{9,8},{10,11},{13,12},{14,15},{17,16},{18,... | collective-permute-start | bytes 786440 | tf_op jit(solution)/shard_map/ppermute | solution.py:378
  67.6 9.9 %collective-permute-start.14 = (bf16[128,256]{1,0:T(8,128)(2,1)S(1)}, bf16[128,256]{1,0:T(8,128)(2,1)S(1)}, u32[]{:S(2)}, u32[]{:S(2)}) collective-permute-start(bf16[128,256]{1,0:T(8,128)(2,1)S(1)} %get-tuple-element.35.refs_0_), channel_id=1, source_target_pairs={{0,1},{1,0},{2,3},{3,2},{4,5},{5,4},{6,7},{7,6},{8,9},{9,8},{10,11... | collective-permute-start | bytes 196616 | tf_op jit(solution)/shard_map/ppermute | solution.py:329
  78.9 4.4 %collective-permute-start.19 = (bf16[3,256,512]{2,1,0:T(8,128)(2,1)S(1)}, bf16[3,256,512]{2,1,0:T(8,128)(2,1)S(1)}, u32[]{:S(2)}, u32[]{:S(2)}) collective-permute-start(bf16[3,256,512]{2,1,0:T(8,128)(2,1)S(1)} %get-tuple-element.39), channel_id=1, source_target_pairs={{0,4},{4,0},{8,12},{12,8},{16,20},{20,16},{24,28},{28,24},{1,5},{5... | collective-permute-start | bytes 2359304 | tf_op jit(solution)/shard_map/ppermute | solution.py:329
  79.0 2.6 %collective-permute-start.20 = (bf16[1,256,512]{2,1,0:T(8,128)(2,1)S(1)}, bf16[1,256,512]{2,1,0:T(8,128)(2,1)S(1)}, u32[]{:S(2)}, u32[]{:S(2)}) collective-permute-start(bf16[1,256,512]{2,1,0:T(8,128)(2,1)S(1)} %get-tuple-element.42), channel_id=1, source_target_pairs={{0,4},{4,0},{8,12},{12,8},{16,20},{20,16},{24,28},{28,24},{1,5},{5... | collective-permute-start | bytes 786440 | tf_op jit(solution)/shard_map/ppermute | solution.py:329
  81.7 6.4 %collective-permute-start.21 = (bf16[256,512]{1,0:T(8,128)(2,1)S(1)}, bf16[256,512]{1,0:T(8,128)(2,1)S(1)}, u32[]{:S(2)}, u32[]{:S(2)}) collective-permute-start(bf16[256,512]{1,0:T(8,128)(2,1)S(1)} %fusion), channel_id=1, source_target_pairs={{0,8},{4,20},{8,0},{12,28},{16,24},{20,4},{24,16},{28,12},{1,9},{5... | collective-permute-start | bytes 786440 | tf_op jit(solution)/shard_map/ppermute | solution.py:399
  83.2 6.4 %collective-permute-start.15 = (bf16[128,256]{1,0:T(8,128)(2,1)S(1)}, bf16[128,256]{1,0:T(8,128)(2,1)S(1)}, u32[]{:S(2)}, u32[]{:S(2)}) collective-permute-start(bf16[128,256]{1,0:T(8,128)(2,1)S(1)} %total.2.refs_3_.refs_0_), channel_id=1, source_target_pairs={{0,2},{1,3},{2,0},{3,1},{4,6},{5,7},{6,4},{7,5},{8,10},{9,11},{10,... | collective-permute-start | bytes 196616 | tf_op jit(solution)/shard_map/ppermute | solution.py:329
  83.9 9.6 %collective-permute-start.24 = (bf16[256,512]{1,0:T(8,128)(2,1)S(1)}, bf16[256,512]{1,0:T(8,128)(2,1)S(1)}, u32[]{:S(2)}, u32[]{:S(2)}) collective-permute-start(bf16[256,512]{1,0:T(8,128)(2,1)S(1)} %gate.7), channel_id=1, source_target_pairs={{0,8},{4,20},{8,0},{12,28},{16,24},{20,4},{24,16},{28,12},{1,9},{5... | collective-permute-start | bytes 786440 | tf_op jit(solution)/shard_map/ppermute | solution.py:403
  88.2 6.4 %collective-permute-start.25 = (bf16[256,512]{1,0:T(8,128)(2,1)S(1)}, bf16[256,512]{1,0:T(8,128)(2,1)S(1)}, u32[]{:S(2)}, u32[]{:S(2)}) collective-permute-start(bf16[256,512]{1,0:T(8,128)(2,1)S(1)} %add_convert_fusion.refs_2_), channel_id=1, source_target_pairs={{0,16},{4,12},{8,24},{12,4},{16,0},{20,28},{24,8},{28,20},{1,17},{... | collective-permute-start | bytes 786440 | tf_op jit(solution)/shard_map/ppermute | solution.py:403
  89.7 1.3 %collective-permute-start.22 = (f32[64,256]{1,0:T(8,128)S(1)}, f32[64,256]{1,0:T(8,128)S(1)}, u32[]{:S(2)}, u32[]{:S(2)}) collective-permute-start(f32[64,256]{1,0:T(8,128)S(1)} %get-tuple-element.46), channel_id=1, source_target_pairs={{0,4},{4,0},{8,12},{12,8},{16,20},{20,16},{24,28},{28,24},{1,5},{5... | collective-permute-start | bytes 196616 | tf_op jit(solution)/shard_map/ppermute | solution.py:329
  91.1 1.3 %collective-permute-start.23 = (f32[64,256]{1,0:T(8,128)S(1)}, f32[64,256]{1,0:T(8,128)S(1)}, u32[]{:S(2)}, u32[]{:S(2)}) collective-permute-start(f32[64,256]{1,0:T(8,128)S(1)} %gate.6), channel_id=1, source_target_pairs={{0,4},{4,0},{8,12},{12,8},{16,20},{20,16},{24,28},{28,24},{1,5},{5... | collective-permute-start | bytes 196616 | tf_op jit(solution)/shard_map/ppermute | solution.py:329

commit v18 on v16

--- a/solution.py
+++ b/solution.py
@@ -166,9 +166,9 @@
     return pl.pallas_call(
         functools.partial(middle_kernel, scale=scale, came=len(parts) - 1),
         out_shape=(
-            jax.ShapeDtypeStruct((rows, width), jnp.bfloat16),
-            jax.ShapeDtypeStruct((width, rows), jnp.bfloat16),
-            jax.ShapeDtypeStruct((width, width), jnp.float32),
+            pltpu.VMEM((rows, width), jnp.bfloat16),
+            pltpu.VMEM((width, rows), jnp.bfloat16),
+            pltpu.VMEM((width, width), jnp.float32),
         ),
         compiler_params=params(16),
         cost_estimate=cost(6 * rows * width * width, 10 * rows * width, rows * width),

time: 91.8 us -> 91.2 us (level)
  Pallas kernels: 26.6 us -> 25.5 us
  transfers between devices with their start and end apart: 25 -> 25, of which waited for: 13 -> 13; matrix products, arithmetic and copies ran while one was open for 0% -> 1% of each run, Pallas kernels for 24% -> 24%
where the time goes in v18:
time: 91.2 us; the launch traced here: 91 us
  waiting for transfers between devices  26.8 us (29%)
  starting transfers between devices  26.6 us (29%)
  Pallas kernels  25.5 us (28%)
  blocking collectives  10 us (11%)
    ppermute x18, waiting for transfers between devices, swap(): return lax.ppermute(value, axis, [(i, i ^ step) for i in range(size)])  22.2 us
    ppermute x18, starting transfers between devices, swap(): return lax.ppermute(value, axis, [(i, i ^ step) for i in range(size)])  16.6 us
    all_gather x1, blocking collectives, shards(): gathered = lax.all_gather(part, 'row', axis_index_groups=cores, tiled=True)  10 us
    pallas_call x5, Pallas kernels, forward(): pl.pallas_call(functools.partial(forward_kernel, steps=steps, before=bool...  7.94 us
    pallas_call x1, Pallas kernels, dense_rows(): pl.pallas_call(functools.partial(dense_kernel, steps=steps, window=window...  7.1 us
    pallas_call x3, Pallas kernels, backward(): pl.pallas_call(functools.partial(backward_kernel, count=count, groups=gro...  6.55 us
    ppermute x1, waiting for transfers between devices, shards(): corner = lax.ppermute(corner.astype(jnp.bfloat16), 'row', there)  3.59 us
    ppermute x1, starting transfers between devices, shards(): relayed = lax.ppermute(shares[3], 'col', [(0, 1), (3, 2)])  3.5 us
  transfers between devices with their start and end apart: 25, of which 13 were waited for; matrix products, arithmetic and copies ran while one was open for 1% of the time, Pallas kernels for 24%

profile of v18, /device:TPU:0, one launch (start us, length us, event | category | flops | bytes accessed | tf_op | source)
XLA Modules:
  0.0 91.0 jit_solution(11648701063351560591)
XLA Ops:
  0.6 4.0 %collective-permute-start.1 = (bf16[512,256]{1,0:T(8,128)(2,1)}, bf16[512,256]{1,0:T(8,128)(2,1)S(1)}, u32[]{:S(2)}, u32[]{:S(2)}) collective-permute-start(bf16[512,256]{1,0:T(8,128)(2,1)} %features_ref.1), channel_id=1, source_target_pairs={{0,24},{4,28},{8,16},{12,20},{16,8},{20,12},{24,0},{28,4},{1,25},{... | collective-permute-start | bytes 786440 | tf_op jit(solution)/shard_map/ppermute | solution.py:329
  5.3 7.1 %dense_rows.1 = (bf16[512,4096]{1,0:T(8,128)(2,1)S(1)}, bf16[512,4096]{1,0:T(8,128)(2,1)S(1)}, bf16[512,4096]{1,0:T(8,128)(2,1)S(1)}, bf16[512,4096]{1,0:T(8,128)(2,1)S(1)}, bf16[512,256]{1,0:T(8,128)(2,1)S(1)}) custom-call(s32[2]{0:T(128)S(1)} %pad_add_fusion.where, s32[16]{0:T(128)} %bitcast.9, s32[448]{0:T(512)} %bitcast.8, ...), custom_call_target="tpu_custom_call" | custom-call | bytes 41943040 | tf_op jit(solution)/shard_map/dense_rows/pallas_call | solution.py:102
  12.4 4.6 %collective-permute-done.3.refs_2_ = bf16[512,256]{1,0:T(8,128)(2,1)S(1)} collective-permute-done((bf16[512,256]{1,0:T(8,128)(2,1)}, bf16[512,256]{1,0:T(8,128)(2,1)S(1)}, u32[]{:S(2)}, u32[]{:S(2)}) %collective-permute-start.3) | collective-permute-done | bytes 262176 | tf_op jit(solution)/shard_map/ppermute | solution.py:329
  17.6 1.2 %forward_rows.6.refs_4_ = f32[512,256]{1,0:T(8,128)S(1)} custom-call(s32[2]{0:T(128)S(1)} %pad_add_fusion.where, bf16[512,4096]{1,0:T(8,128)(2,1)S(1)} %get-tuple-element.26.refs_3_.a_ref.refs_0_, bf16[512,256]{1,0:T(8,128)(2,1)S(1)} %get-tuple-element.25.refs_0_, bf16[512,256]{1,0:T(8,128)(2,1)S(1)} %get-tuple-element.29.refs_2_.refs_1_, ...), custom_call_target="tpu_custom_call" | custom-call | flops 1073741824 | bytes 4194304 | tf_op jit(solution)/shard_map/forward_rows/pallas_call | solution.py:133
  19.3 1.3 %forward_rows.7 = bf16[512,256]{1,0:T(8,128)(2,1)S(1)} custom-call(s32[2]{0:T(128)S(1)} %pad_add_fusion.where, bf16[512,4096]{1,0:T(8,128)(2,1)S(1)} %get-tuple-element.26.refs_3_.a_ref.refs_0_, bf16[512,256]{1,0:T(8,128)(2,1)S(1)} %collective-permute-done.refs_1_.refs_0_, bf16[512,256]{1,0:T(8,128)(2,1)S(1)} %collective-permute-done.4.refs_3_.refs_1_, ...), custom_call_target="tpu_custom_call" | custom-call | flops 1073741824 | bytes 4194304 | tf_op jit(solution)/shard_map/forward_rows/pallas_call | solution.py:133
  20.6 3.5 %collective-permute-start.8 = (bf16[512,256]{1,0:T(8,128)(2,1)S(1)}, bf16[512,256]{1,0:T(8,128)(2,1)S(1)}, u32[]{:S(2)}, u32[]{:S(2)}) collective-permute-start(bf16[512,256]{1,0:T(8,128)(2,1)S(1)} %forward_rows.7), channel_id=1, source_target_pairs={{0,1},{3,2},{4,5},{7,6},{8,9},{11,10},{12,13},{15,14},{16,17},{19,... | collective-permute-start | bytes 786440 | tf_op jit(solution)/shard_map/ppermute | solution.py:359
  24.1 0.9 collective-permute-start.7
  25.0 1.8 %forward_rows.9 = bf16[512,256]{1,0:T(8,128)(2,1)S(1)} custom-call(s32[2]{0:T(128)S(1)} %pad_add_fusion.where, bf16[512,4096]{1,0:T(8,128)(2,1)S(1)} %get-tuple-element.28.refs_5_.a_ref.refs_1_, bf16[512,256]{1,0:T(8,128)(2,1)S(1)} %get-tuple-element.25.refs_0_, bf16[512,256]{1,0:T(8,128)(2,1)S(1)} %collective-permute-done.refs_1_.refs_0_, ...), custom_call_target="tpu_custom_call" | custom-call | flops 1073741824 | bytes 4194304 | tf_op jit(solution)/shard_map/forward_rows/pallas_call | solution.py:133
  26.8 2.2 %collective-permute-start.10 = (bf16[512,256]{1,0:T(8,128)(2,1)S(1)}, bf16[512,256]{1,0:T(8,128)(2,1)S(1)}, u32[]{:S(2)}, u32[]{:S(2)}) collective-permute-start(bf16[512,256]{1,0:T(8,128)(2,1)S(1)} %forward_rows.9), channel_id=1, source_target_pairs={{0,1},{1,0},{2,3},{3,2},{4,5},{5,4},{6,7},{7,6},{8,9},{9,8},{10,11... | collective-permute-start | bytes 786440 | tf_op jit(solution)/shard_map/ppermute | solution.py:329
  29.0 1.8 %forward_rows.8 = bf16[512,256]{1,0:T(8,128)(2,1)S(1)} custom-call(s32[2]{0:T(128)S(1)} %pad_add_fusion.where, bf16[512,4096]{1,0:T(8,128)(2,1)S(1)} %get-tuple-element.27.refs_4_.a_ref.refs_2_, bf16[512,256]{1,0:T(8,128)(2,1)S(1)} %get-tuple-element.25.refs_0_, bf16[512,256]{1,0:T(8,128)(2,1)S(1)} %collective-permute-done.refs_1_.refs_0_, ...), custom_call_target="tpu_custom_call" | custom-call | flops 1073741824 | bytes 4194304 | tf_op jit(solution)/shard_map/forward_rows/pallas_call | solution.py:133
  30.9 3.4 %collective-permute-start.9 = (bf16[512,256]{1,0:T(8,128)(2,1)S(1)}, bf16[512,256]{1,0:T(8,128)(2,1)S(1)}, u32[]{:S(2)}, u32[]{:S(2)}) collective-permute-start(bf16[512,256]{1,0:T(8,128)(2,1)S(1)} %add_convert_fusion.2), channel_id=1, source_target_pairs={{0,2},{1,3},{2,0},{3,1},{4,6},{5,7},{6,4},{7,5},{8,10},{9,11},{10,... | collective-permute-start | bytes 786440 | tf_op jit(solution)/shard_map/ppermute | solution.py:329
  34.4 1.8 %forward_rows.5.refs_0_ = f32[512,256]{1,0:T(8,128)S(1)} custom-call(s32[2]{0:T(128)S(1)} %pad_add_fusion.where, bf16[512,4096]{1,0:T(8,128)(2,1)S(1)} %get-tuple-element.24.refs_6_.a_ref.refs_0_, bf16[512,256]{1,0:T(8,128)(2,1)S(1)} %get-tuple-element.25.refs_0_, bf16[512,256]{1,0:T(8,128)(2,1)S(1)} %collective-permute-done.refs_1_.refs_0_, ...), custom_call_target="tpu_custom_call" | custom-call | flops 1073741824 | bytes 4194304 | tf_op jit(solution)/shard_map/forward_rows/pallas_call | solution.py:133
  36.2 3.6 %collective-permute-done.10.refs_3_ = bf16[512,256]{1,0:T(8,128)(2,1)S(1)} collective-permute-done((bf16[512,256]{1,0:T(8,128)(2,1)S(1)}, bf16[512,256]{1,0:T(8,128)(2,1)S(1)}, u32[]{:S(2)}, u32[]{:S(2)}) %collective-permute-start.10) | collective-permute-done | bytes 262176 | tf_op jit(solution)/shard_map/ppermute | solution.py:329
  39.8 5.6 %collective-permute-done.9.refs_2_ = bf16[512,256]{1,0:T(8,128)(2,1)S(1)} collective-permute-done((bf16[512,256]{1,0:T(8,128)(2,1)S(1)}, bf16[512,256]{1,0:T(8,128)(2,1)S(1)}, u32[]{:S(2)}, u32[]{:S(2)}) %collective-permute-start.9) | collective-permute-done | bytes 262176 | tf_op jit(solution)/shard_map/ppermute | solution.py:329
  46.1 2.1 %collective-permute-start.11 = (bf16[256,512]{1,0:T(8,128)(2,1)S(1)}, bf16[256,512]{1,0:T(8,128)(2,1)S(1)}, u32[]{:S(2)}, u32[]{:S(2)}) collective-permute-start(bf16[256,512]{1,0:T(8,128)(2,1)S(1)} %get-tuple-element.33.refs_0_), channel_id=1, source_target_pairs={{0,2},{1,3},{2,0},{3,1},{4,6},{5,7},{6,4},{7,5},{8,10},{9,11},{10,... | collective-permute-start | bytes 786440 | tf_op jit(solution)/shard_map/ppermute | solution.py:329
  48.2 10.0 %all_gather.3.values_ref = bf16[1024,256]{1,0:T(8,128)(2,1)S(1)} all-gather(bf16[256,256]{1,0:T(8,128)(2,1)S(1)} %add_convert_fusion.3), channel_id=1, replica_groups={{0,8,16,24},{4,12,20,28},{1,9,17,25},{5,13,21,29},{2,10,18,26},{6,14,22..., dimensions={0}, use_global_device_ids=true | all-gather | bytes 655360 | tf_op jit(solution)/shard_map/all_gather | solution.py:371
  59.3 2.0 %collective-permute-done.11.refs_1_ = bf16[256,512]{1,0:T(8,128)(2,1)S(1)} collective-permute-done((bf16[256,512]{1,0:T(8,128)(2,1)S(1)}, bf16[256,512]{1,0:T(8,128)(2,1)S(1)}, u32[]{:S(2)}, u32[]{:S(2)}) %collective-permute-start.11) | collective-permute-done | bytes 262176 | tf_op jit(solution)/shard_map/ppermute | solution.py:329
  61.9 1.3 %collective-permute-start.16 = (bf16[256,512]{1,0:T(8,128)(2,1)S(1)}, bf16[256,512]{1,0:T(8,128)(2,1)S(1)}, u32[]{:S(2)}, u32[]{:S(2)}) collective-permute-start(bf16[256,512]{1,0:T(8,128)(2,1)S(1)} %get-tuple-element.37.refs_5_), channel_id=1, source_target_pairs={{1,0},{2,3},{5,4},{6,7},{9,8},{10,11},{13,12},{14,15},{17,16},{18,... | collective-permute-start | bytes 786440 | tf_op jit(solution)/shard_map/ppermute | solution.py:377
  63.2 2.7 %collective-permute-start.13 = (bf16[128,256]{1,0:T(8,128)(2,1)S(1)}, bf16[128,256]{1,0:T(8,128)(2,1)S(1)}, u32[]{:S(2)}, u32[]{:S(2)}) collective-permute-start(bf16[128,256]{1,0:T(8,128)(2,1)S(1)} %get-tuple-element.35.refs_0_), channel_id=1, source_target_pairs={{0,1},{1,0},{2,3},{3,2},{4,5},{5,4},{6,7},{7,6},{8,9},{9,8},{10,11... | collective-permute-start | bytes 196616 | tf_op jit(solution)/shard_map/ppermute | solution.py:329
  65.9 4.0 %backward_cols.3.refs_2_ = f32[8,256,512]{2,1,0:T(8,128)S(1)} custom-call(s32[2]{0:T(128)S(1)} %pad_add_fusion.where, bf16[512,4096]{1,0:T(8,128)(2,1)S(1)} %get-tuple-element.24.refs_6_.a_ref.refs_0_, bf16[512,4096]{1,0:T(8,128)(2,1)S(1)} %get-tuple-element.28.refs_5_.a_ref.refs_1_, bf16[512,4096]{1,0:T(8,128)(2,1)S(1)} %get-tuple-element.27.refs_4_.a_ref.refs_2_, ...), custom_call_target="tpu_custom_call" | custom-call | tf_op jit(solution)/shard_map/backward_cols/pallas_call | solution.py:198
  70.0 3.0 %collective-permute-done.13.refs_1_ = bf16[128,256]{1,0:T(8,128)(2,1)S(1)} collective-permute-done((bf16[128,256]{1,0:T(8,128)(2,1)S(1)}, bf16[128,256]{1,0:T(8,128)(2,1)S(1)}, u32[]{:S(2)}, u32[]{:S(2)}) %collective-permute-start.13) | collective-permute-done | bytes 65568 | tf_op jit(solution)/shard_map/ppermute | solution.py:329
  73.1 1.3 %backward_cols.5 = (bf16[1,256,512]{2,1,0:T(8,128)(2,1)S(1)}, bf16[3,256,512]{2,1,0:T(8,128)(2,1)S(1)}) custom-call(s32[2]{0:T(128)S(1)} %pad_add_fusion.where, bf16[512,4096]{1,0:T(8,128)(2,1)S(1)} %get-tuple-element.26.refs_3_.a_ref.refs_0_, bf16[256,512]{1,0:T(8,128)(2,1)S(1)} %add.18.refs_1_, f32[8,256,512]{2,1,0:T(8,128)S(1)} %backward_cols.3.refs_2_, ...), custom_call_target="tpu_custom_call" | custom-call | tf_op jit(solution)/shard_map/backward_cols/pallas_call | solution.py:198
  75.0 1.3 %backward_cols.4 = (f32[1,256,512]{2,1,0:T(8,128)S(1)}, f32[3,256,512]{2,1,0:T(8,128)S(1)}) custom-call(s32[2]{0:T(128)S(1)} %pad_add_fusion.where, bf16[512,4096]{1,0:T(8,128)(2,1)S(1)} %get-tuple-element.26.refs_3_.a_ref.refs_0_, bf16[256,512]{1,0:T(8,128)(2,1)S(1)} %add.18.refs_1_, f32[8,256,512]{2,1,0:T(8,128)S(1)} %backward_cols.3.refs_2_), custom_call_target="tpu_custom_call" | custom-call | tf_op jit(solution)/shard_map/backward_cols/pallas_call | solution.py:198
  76.2 0.9 collective-permute-done.19
  77.2 1.6 %collective-permute-start.20 = (bf16[256,512]{1,0:T(8,128)(2,1)S(1)}, bf16[256,512]{1,0:T(8,128)(2,1)S(1)}, u32[]{:S(2)}, u32[]{:S(2)}) collective-permute-start(bf16[256,512]{1,0:T(8,128)(2,1)S(1)} %fusion), channel_id=1, source_target_pairs={{0,8},{4,20},{8,0},{12,28},{16,24},{20,4},{24,16},{28,12},{1,9},{5... | collective-permute-start | bytes 786440 | tf_op jit(solution)/shard_map/ppermute | solution.py:398
  80.0 3.6 %collective-permute-done.20 = bf16[256,512]{1,0:T(8,128)(2,1)S(1)} collective-permute-done((bf16[256,512]{1,0:T(8,128)(2,1)S(1)}, bf16[256,512]{1,0:T(8,128)(2,1)S(1)}, u32[]{:S(2)}, u32[]{:S(2)}) %collective-permute-start.20) | collective-permute-done | bytes 262176 | tf_op jit(solution)/shard_map/ppermute | solution.py:398
  83.7 1.5 %collective-permute-start.24 = (bf16[256,512]{1,0:T(8,128)(2,1)S(1)}, bf16[256,512]{1,0:T(8,128)(2,1)S(1)}, u32[]{:S(2)}, u32[]{:S(2)}) collective-permute-start(bf16[256,512]{1,0:T(8,128)(2,1)S(1)} %add_convert_fusion.refs_2_), channel_id=1, source_target_pairs={{0,16},{4,12},{8,24},{12,4},{16,0},{20,28},{24,8},{28,20},{1,17},{... | collective-permute-start | bytes 786440 | tf_op jit(solution)/shard_map/ppermute | solution.py:402
  85.3 1.2 %collective-permute-done.21.refs_1_.refs_0_ = f32[64,256]{1,0:T(8,128)S(1)} collective-permute-done((f32[64,256]{1,0:T(8,128)S(1)}, f32[64,256]{1,0:T(8,128)S(1)}, u32[]{:S(2)}, u32[]{:S(2)}) %collective-permute-start.21) | collective-permute-done | bytes 65568 | tf_op jit(solution)/shard_map/ppermute | solution.py:329
  86.7 0.7 copy.25
  87.8 1.3 %join.1 = f32[256,256]{1,0:T(8,128)} custom-call(s32[2]{0:T(128)S(1)} %pad_add_fusion.where, f32[128,256]{1,0:T(8,128)S(1)} %total.3.own_ref, f32[64,256]{1,0:T(8,128)S(1)} %collective-permute-done.21.refs_1_.refs_0_, f32[64,256]{1,0:T(8,128)S(1)} %collective-permute-done.22.refs_1_), custom_call_target="tpu_custom_call" | custom-call | tf_op jit(solution)/shard_map/join/pallas_call | solution.py:318
  89.1 1.1 %collective-permute-done.24.refs_2_ = bf16[256,512]{1,0:T(8,128)(2,1)S(1)} collective-permute-done((bf16[256,512]{1,0:T(8,128)(2,1)S(1)}, bf16[256,512]{1,0:T(8,128)(2,1)S(1)}, u32[]{:S(2)}, u32[]{:S(2)}) %collective-permute-start.24) | collective-permute-done | bytes 262176 | tf_op jit(solution)/shard_map/ppermute | solution.py:402
  90.1 0.9 finish.1
  (51 shorter events, 7.0 us)
Async XLA Ops:
  0.6 11.8 %collective-permute-start.1 = (bf16[512,256]{1,0:T(8,128)(2,1)}, bf16[512,256]{1,0:T(8,128)(2,1)S(1)}, u32[]{:S(2)}, u32[]{:S(2)}) collective-permute-start(bf16[512,256]{1,0:T(8,128)(2,1)} %features_ref.1), channel_id=1, source_target_pairs={{0,24},{4,28},{8,16},{12,20},{16,8},{20,12},{24,0},{28,4},{1,25},{... | collective-permute-start | bytes 786440 | tf_op jit(solution)/shard_map/ppermute | solution.py:329
  4.6 12.4 %collective-permute-start.3 = (bf16[512,256]{1,0:T(8,128)(2,1)}, bf16[512,256]{1,0:T(8,128)(2,1)S(1)}, u32[]{:S(2)}, u32[]{:S(2)}) collective-permute-start(bf16[512,256]{1,0:T(8,128)(2,1)} %features_ref.1), channel_id=1, source_target_pairs={{0,8},{4,12},{8,0},{12,4},{16,24},{20,28},{24,16},{28,20},{1,9},{5... | collective-permute-start | bytes 786440 | tf_op jit(solution)/shard_map/ppermute | solution.py:329
  5.1 11.9 %collective-permute-start.2 = (bf16[512,256]{1,0:T(8,128)(2,1)}, bf16[512,256]{1,0:T(8,128)(2,1)S(1)}, u32[]{:S(2)}, u32[]{:S(2)}) collective-permute-start(bf16[512,256]{1,0:T(8,128)(2,1)} %features_ref.1), channel_id=1, source_target_pairs={{0,16},{4,20},{8,24},{12,28},{16,0},{20,4},{24,8},{28,12},{1,17},{... | collective-permute-start | bytes 786440 | tf_op jit(solution)/shard_map/ppermute | solution.py:329
  5.2 13.6 %collective-permute-start = (bf16[512,256]{1,0:T(8,128)(2,1)}, bf16[512,256]{1,0:T(8,128)(2,1)S(1)}, u32[]{:S(2)}, u32[]{:S(2)}) collective-permute-start(bf16[512,256]{1,0:T(8,128)(2,1)} %features_ref.1), channel_id=1, source_target_pairs={{0,4},{4,0},{8,12},{12,8},{16,20},{20,16},{24,28},{28,24},{1,5},{5... | collective-permute-start | bytes 786440 | tf_op jit(solution)/shard_map/ppermute | solution.py:329
  17.0 1.8 %collective-permute-start.4 = (bf16[512,256]{1,0:T(8,128)(2,1)S(1)}, bf16[512,256]{1,0:T(8,128)(2,1)S(1)}, u32[]{:S(2)}, u32[]{:S(2)}) collective-permute-start(bf16[512,256]{1,0:T(8,128)(2,1)S(1)} %get-tuple-element.29.refs_2_.refs_1_), channel_id=1, source_target_pairs={{0,4},{4,0},{8,12},{12,8},{16,20},{20,16},{24,28},{28,24},{1,5},{5... | collective-permute-start | bytes 786440 | tf_op jit(solution)/shard_map/ppermute | solution.py:329
  17.0 1.9 %collective-permute-start.5 = (bf16[512,256]{1,0:T(8,128)(2,1)S(1)}, bf16[512,256]{1,0:T(8,128)(2,1)S(1)}, u32[]{:S(2)}, u32[]{:S(2)}) collective-permute-start(bf16[512,256]{1,0:T(8,128)(2,1)S(1)} %get-tuple-element.30.refs_4_.refs_2_), channel_id=1, source_target_pairs={{0,4},{4,0},{8,12},{12,8},{16,20},{20,16},{24,28},{28,24},{1,5},{5... | collective-permute-start | bytes 786440 | tf_op jit(solution)/shard_map/ppermute | solution.py:329
  17.5 1.8 %collective-permute-start.6 = (bf16[512,256]{1,0:T(8,128)(2,1)S(1)}, bf16[512,256]{1,0:T(8,128)(2,1)S(1)}, u32[]{:S(2)}, u32[]{:S(2)}) collective-permute-start(bf16[512,256]{1,0:T(8,128)(2,1)S(1)} %get-tuple-element.31.refs_6_.refs_3_), channel_id=1, source_target_pairs={{0,4},{4,0},{8,12},{12,8},{16,20},{20,16},{24,28},{28,24},{1,5},{5... | collective-permute-start | bytes 786440 | tf_op jit(solution)/shard_map/ppermute | solution.py:329
  20.6 10.3 %collective-permute-start.8 = (bf16[512,256]{1,0:T(8,128)(2,1)S(1)}, bf16[512,256]{1,0:T(8,128)(2,1)S(1)}, u32[]{:S(2)}, u32[]{:S(2)}) collective-permute-start(bf16[512,256]{1,0:T(8,128)(2,1)S(1)} %forward_rows.7), channel_id=1, source_target_pairs={{0,1},{3,2},{4,5},{7,6},{8,9},{11,10},{12,13},{15,14},{16,17},{19,... | collective-permute-start | bytes 786440 | tf_op jit(solution)/shard_map/ppermute | solution.py:359
  24.1 15.7 %collective-permute-start.7 = (bf16[512,256]{1,0:T(8,128)(2,1)S(1)}, bf16[512,256]{1,0:T(8,128)(2,1)S(1)}, u32[]{:S(2)}, u32[]{:S(2)}) collective-permute-start(bf16[512,256]{1,0:T(8,128)(2,1)S(1)} %forward_rows.7), channel_id=1, source_target_pairs={{1,2},{2,1},{5,6},{6,5},{9,10},{10,9},{13,14},{14,13},{17,18},{18,... | collective-permute-start | bytes 786440 | tf_op jit(solution)/shard_map/ppermute | solution.py:360
  26.8 13.0 %collective-permute-start.10 = (bf16[512,256]{1,0:T(8,128)(2,1)S(1)}, bf16[512,256]{1,0:T(8,128)(2,1)S(1)}, u32[]{:S(2)}, u32[]{:S(2)}) collective-permute-start(bf16[512,256]{1,0:T(8,128)(2,1)S(1)} %forward_rows.9), channel_id=1, source_target_pairs={{0,1},{1,0},{2,3},{3,2},{4,5},{5,4},{6,7},{7,6},{8,9},{9,8},{10,11... | collective-permute-start | bytes 786440 | tf_op jit(solution)/shard_map/ppermute | solution.py:329
  30.8 14.5 %copy-start = (bf16[512,256]{1,0:T(8,128)(2,1)S(1)}, bf16[512,256]{1,0:T(8,128)(2,1)}, u32[]{:S(2)}) copy-start(bf16[512,256]{1,0:T(8,128)(2,1)} %refs_5_.1) | copy-start | bytes 786436
  30.8 14.5 %copy-start.1 = (bf16[256,256]{1,0:T(8,128)(2,1)S(1)}, bf16[256,256]{1,0:T(8,128)(2,1)}, u32[]{:S(2)}) copy-start(bf16[256,256]{1,0:T(8,128)(2,1)} %refs_4_.1) | copy-start | bytes 393220
  30.9 14.4 %collective-permute-start.9 = (bf16[512,256]{1,0:T(8,128)(2,1)S(1)}, bf16[512,256]{1,0:T(8,128)(2,1)S(1)}, u32[]{:S(2)}, u32[]{:S(2)}) collective-permute-start(bf16[512,256]{1,0:T(8,128)(2,1)S(1)} %add_convert_fusion.2), channel_id=1, source_target_pairs={{0,2},{1,3},{2,0},{3,1},{4,6},{5,7},{6,4},{7,5},{8,10},{9,11},{10,... | collective-permute-start | bytes 786440 | tf_op jit(solution)/shard_map/ppermute | solution.py:329
  45.9 2.3 %collective-permute-start.12 = (f32[256,256]{1,0:T(8,128)S(1)}, f32[256,256]{1,0:T(8,128)S(1)}, u32[]{:S(2)}, u32[]{:S(2)}) collective-permute-start(f32[256,256]{1,0:T(8,128)S(1)} %get-tuple-element.34), channel_id=1, source_target_pairs={{0,4},{4,0},{8,12},{12,8},{16,20},{20,16},{24,28},{28,24},{1,5},{5... | collective-permute-start | bytes 786440 | tf_op jit(solution)/shard_map/ppermute | solution.py:329
  46.0 13.3 %collective-permute-start.17 = (bf16[256,512]{1,0:T(8,128)(2,1)S(1)}, bf16[256,512]{1,0:T(8,128)(2,1)S(1)}, u32[]{:S(2)}, u32[]{:S(2)}) collective-permute-start(bf16[256,512]{1,0:T(8,128)(2,1)S(1)} %get-tuple-element.33.refs_0_), channel_id=1, source_target_pairs={{0,1},{1,0},{2,3},{3,2},{4,5},{5,4},{6,7},{7,6},{8,9},{9,8},{10,11... | collective-permute-start | bytes 786440 | tf_op jit(solution)/shard_map/ppermute | solution.py:329
  46.1 15.2 %collective-permute-start.11 = (bf16[256,512]{1,0:T(8,128)(2,1)S(1)}, bf16[256,512]{1,0:T(8,128)(2,1)S(1)}, u32[]{:S(2)}, u32[]{:S(2)}) collective-permute-start(bf16[256,512]{1,0:T(8,128)(2,1)S(1)} %get-tuple-element.33.refs_0_), channel_id=1, source_target_pairs={{0,2},{1,3},{2,0},{3,1},{4,6},{5,7},{6,4},{7,5},{8,10},{9,11},{10,... | collective-permute-start | bytes 786440 | tf_op jit(solution)/shard_map/ppermute | solution.py:329
  61.2 11.8 %collective-permute-start.15 = (bf16[256,512]{1,0:T(8,128)(2,1)S(1)}, bf16[256,512]{1,0:T(8,128)(2,1)S(1)}, u32[]{:S(2)}, u32[]{:S(2)}) collective-permute-start(bf16[256,512]{1,0:T(8,128)(2,1)S(1)} %get-tuple-element.36.refs_3_), channel_id=1, source_target_pairs={{1,2},{2,1},{5,6},{6,5},{9,10},{10,9},{13,14},{14,13},{17,18},{18,... | collective-permute-start | bytes 786440 | tf_op jit(solution)/shard_map/ppermute | solution.py:376
  61.9 11.1 %collective-permute-start.16 = (bf16[256,512]{1,0:T(8,128)(2,1)S(1)}, bf16[256,512]{1,0:T(8,128)(2,1)S(1)}, u32[]{:S(2)}, u32[]{:S(2)}) collective-permute-start(bf16[256,512]{1,0:T(8,128)(2,1)S(1)} %get-tuple-element.37.refs_5_), channel_id=1, source_target_pairs={{1,0},{2,3},{5,4},{6,7},{9,8},{10,11},{13,12},{14,15},{17,16},{18,... | collective-permute-start | bytes 786440 | tf_op jit(solution)/shard_map/ppermute | solution.py:377
  63.2 9.8 %collective-permute-start.13 = (bf16[128,256]{1,0:T(8,128)(2,1)S(1)}, bf16[128,256]{1,0:T(8,128)(2,1)S(1)}, u32[]{:S(2)}, u32[]{:S(2)}) collective-permute-start(bf16[128,256]{1,0:T(8,128)(2,1)S(1)} %get-tuple-element.35.refs_0_), channel_id=1, source_target_pairs={{0,1},{1,0},{2,3},{3,2},{4,5},{5,4},{6,7},{7,6},{8,9},{9,8},{10,11... | collective-permute-start | bytes 196616 | tf_op jit(solution)/shard_map/ppermute | solution.py:329
  74.4 4.4 %collective-permute-start.18 = (bf16[3,256,512]{2,1,0:T(8,128)(2,1)S(1)}, bf16[3,256,512]{2,1,0:T(8,128)(2,1)S(1)}, u32[]{:S(2)}, u32[]{:S(2)}) collective-permute-start(bf16[3,256,512]{2,1,0:T(8,128)(2,1)S(1)} %get-tuple-element.39), channel_id=1, source_target_pairs={{0,4},{4,0},{8,12},{12,8},{16,20},{20,16},{24,28},{28,24},{1,5},{5... | collective-permute-start | bytes 2359304 | tf_op jit(solution)/shard_map/ppermute | solution.py:329
  74.5 2.6 %collective-permute-start.19 = (bf16[1,256,512]{2,1,0:T(8,128)(2,1)S(1)}, bf16[1,256,512]{2,1,0:T(8,128)(2,1)S(1)}, u32[]{:S(2)}, u32[]{:S(2)}) collective-permute-start(bf16[1,256,512]{2,1,0:T(8,128)(2,1)S(1)} %get-tuple-element.42), channel_id=1, source_target_pairs={{0,4},{4,0},{8,12},{12,8},{16,20},{20,16},{24,28},{28,24},{1,5},{5... | collective-permute-start | bytes 786440 | tf_op jit(solution)/shard_map/ppermute | solution.py:329
  77.2 6.4 %collective-permute-start.20 = (bf16[256,512]{1,0:T(8,128)(2,1)S(1)}, bf16[256,512]{1,0:T(8,128)(2,1)S(1)}, u32[]{:S(2)}, u32[]{:S(2)}) collective-permute-start(bf16[256,512]{1,0:T(8,128)(2,1)S(1)} %fusion), channel_id=1, source_target_pairs={{0,8},{4,20},{8,0},{12,28},{16,24},{20,4},{24,16},{28,12},{1,9},{5... | collective-permute-start | bytes 786440 | tf_op jit(solution)/shard_map/ppermute | solution.py:398
  78.7 6.4 %collective-permute-start.14 = (bf16[128,256]{1,0:T(8,128)(2,1)S(1)}, bf16[128,256]{1,0:T(8,128)(2,1)S(1)}, u32[]{:S(2)}, u32[]{:S(2)}) collective-permute-start(bf16[128,256]{1,0:T(8,128)(2,1)S(1)} %total.2.refs_3_.refs_0_), channel_id=1, source_target_pairs={{0,2},{1,3},{2,0},{3,1},{4,6},{5,7},{6,4},{7,5},{8,10},{9,11},{10,... | collective-permute-start | bytes 196616 | tf_op jit(solution)/shard_map/ppermute | solution.py:329
  79.4 9.6 %collective-permute-start.23 = (bf16[256,512]{1,0:T(8,128)(2,1)S(1)}, bf16[256,512]{1,0:T(8,128)(2,1)S(1)}, u32[]{:S(2)}, u32[]{:S(2)}) collective-permute-start(bf16[256,512]{1,0:T(8,128)(2,1)S(1)} %gate.7), channel_id=1, source_target_pairs={{0,8},{4,20},{8,0},{12,28},{16,24},{20,4},{24,16},{28,12},{1,9},{5... | collective-permute-start | bytes 786440 | tf_op jit(solution)/shard_map/ppermute | solution.py:402
  83.7 6.4 %collective-permute-start.24 = (bf16[256,512]{1,0:T(8,128)(2,1)S(1)}, bf16[256,512]{1,0:T(8,128)(2,1)S(1)}, u32[]{:S(2)}, u32[]{:S(2)}) collective-permute-start(bf16[256,512]{1,0:T(8,128)(2,1)S(1)} %add_convert_fusion.refs_2_), channel_id=1, source_target_pairs={{0,16},{4,12},{8,24},{12,4},{16,0},{20,28},{24,8},{28,20},{1,17},{... | collective-permute-start | bytes 786440 | tf_op jit(solution)/shard_map/ppermute | solution.py:402
  85.2 1.3 %collective-permute-start.21 = (f32[64,256]{1,0:T(8,128)S(1)}, f32[64,256]{1,0:T(8,128)S(1)}, u32[]{:S(2)}, u32[]{:S(2)}) collective-permute-start(f32[64,256]{1,0:T(8,128)S(1)} %get-tuple-element.46), channel_id=1, source_target_pairs={{0,4},{4,0},{8,12},{12,8},{16,20},{20,16},{24,28},{28,24},{1,5},{5... | collective-permute-start | bytes 196616 | tf_op jit(solution)/shard_map/ppermute | solution.py:329
  86.5 1.3 %collective-permute-start.22 = (f32[64,256]{1,0:T(8,128)S(1)}, f32[64,256]{1,0:T(8,128)S(1)}, u32[]{:S(2)}, u32[]{:S(2)}) collective-permute-start(f32[64,256]{1,0:T(8,128)S(1)} %gate.6), channel_id=1, source_target_pairs={{0,4},{4,0},{8,12},{12,8},{16,20},{20,16},{24,28},{28,24},{1,5},{5... | collective-permute-start | bytes 196616 | tf_op jit(solution)/shard_map/ppermute | solution.py:329
